TPU v7x, 32 devices: a whole 2x2x4 slice. The times are simulated.
32 devices in a mesh: pb: 4 (over y, x), dp: 8 (over z, core).
Axes of the slice: x: 2, y: 2, z: 4, core: 2. Of those that a mesh axis runs over, the one named last changes fastest.
Arguments:
- tokens: bfloat16 [32, 100, 512], P('dp', 'pb'), may hold values from -6 to 6
- query_pos: bfloat16 [100, 512], replicated, may hold values from -6 to 6
- features: bfloat16 [32, 1200, 512], P('dp'), may hold values from -6 to 6
- camera_mask: int32 [32, 4], P('dp'), may hold values from 0 to 1, as said below
- out_grad: bfloat16 [32, 100, 512], P('dp', 'pb'), may hold values from -6 to 6
- self_proj: bfloat16 [3, 512, 512], replicated, may hold values from -0.25 to 0.25
- self_out: bfloat16 [512, 512], replicated, may hold values from -0.75 to 0.75
- self_bias: bfloat16 [3, 512], replicated, may hold values from -3 to 3
- cross_proj: bfloat16 [3, 512, 512], replicated, may hold values from -0.25 to 0.25
- cross_out: bfloat16 [512, 512], replicated, may hold values from -1 to 1
- cross_bias: bfloat16 [3, 512], replicated, may hold values from -3 to 3
- w_up: bfloat16 [512, 3200], P(None, 'pb'), may hold values from -0.25 to 0.25
- b_up: bfloat16 [3200], P('pb'), may hold values from -3 to 3
- w_down: bfloat16 [512, 3200], P(None, 'pb'), may hold values from -0.109375 to 0.109375
- b_down: bfloat16 [512], replicated, may hold values from -3 to 3
- norm_gain: bfloat16 [3, 512], replicated, may hold values from 0.5 to 1.5
- norm_bias: bfloat16 [3, 512], replicated, may hold values from -2 to 2
- in_proj: bfloat16 [512, 512], replicated, may hold values from -0.25 to 0.25
- in_bias: bfloat16 [512], replicated, may hold values from -3 to 3
Outputs:
- layer_out: bfloat16 [32, 100, 512], P('dp', 'pb')
- grad_tokens: bfloat16 [32, 100, 512], P('dp', 'pb')
- grad_features: bfloat16 [32, 1200, 512], P('dp', 'pb')
- grad_query_pos: float32 [100, 512], replicated
- grad_self_proj: float32 [3, 512, 512], replicated
- grad_self_out: float32 [512, 512], replicated
- grad_self_bias: float32 [3, 512], replicated
- grad_cross_proj: float32 [3, 512, 512], replicated
- grad_cross_out: float32 [512, 512], replicated
- grad_cross_bias: float32 [3, 512], replicated
- grad_w_up: float32 [512, 3200], P('dp', 'pb')
- grad_b_up: float32 [3200], replicated
- grad_w_down: float32 [512, 3200], P('dp', 'pb')
- grad_b_down: float32 [512], replicated
- grad_norm_gain: float32 [3, 512], replicated
- grad_norm_bias: float32 [3, 512], replicated
- grad_in_proj: float32 [512, 512], replicated
- grad_in_bias: float32 [512], replicated
Inputs may be any that keep to these rules, and one draw needn't show every extreme that they name: `camera_mask`: each episode has between 2 and 4 cameras present, in any combination of slots.
All inputs are finite; a program needn't handle non-finite values.
Results may differ from a plain program's by a relative error of at most 0.03.
Values may be sent and summed in bfloat16 or wider, within the bound.
No kernel may reach another device: no remote copies, remote signals or barrier semaphores. Data moves between devices by JAX's collectives and lax.ppermute only.
A program may use at most 128 MiB of HBM per device.

v0:
```python
import functools

import jax
import jax.numpy as jnp
import numpy as np
from jax import lax
from jax.experimental import pallas as pl
from jax.experimental.pallas import tpu as pltpu
from jax.sharding import PartitionSpec as P

BF = jnp.bfloat16
F32 = jnp.float32
HEADS = 8
LANES = 128
GROUPS = 4
FAR = -1e30


def dims(left, right, a, b):
    return lax.dot_general(left, right, (((a,), (b,)), ((), ())), preferred_element_type=F32)


def nn(left, right):
    return dims(left, right, 1, 0)


def nt(left, right):
    return dims(left, right, 1, 1)


def tn(left, right):
    return dims(left, right, 0, 0)


def lane_masks(dtype=BF):
    lane = lax.broadcasted_iota(jnp.int32, (1, LANES), 1)
    low = (lane < LANES // 2).astype(F32)
    return low.astype(dtype), (1.0 - low).astype(dtype)


def pair(value, group):
    part = value[:, group * LANES : (group + 1) * LANES]
    low, high = lane_masks()
    return jnp.concatenate([part * low, part * high], axis=0)


def unpair(value):
    rows = value.shape[0] // 2
    lane = lax.broadcasted_iota(jnp.int32, (rows, LANES), 1)
    return jnp.where(lane < LANES // 2, value[:rows], value[rows:])


def eights(value, op):
    return op(value.reshape(value.shape[0] // 8, 8, value.shape[1]), axis=0)


def norm(value):
    center = value - jnp.mean(value, -1, keepdims=True)
    rstd = lax.rsqrt(jnp.mean(center * center, -1, keepdims=True) + 1e-05)
    return center * rstd, rstd


def norm_back(xhat, rstd, gain, grad):
    scaled = grad * gain
    inner = jnp.mean(scaled, -1, keepdims=True) + xhat * jnp.mean(
        scaled * xhat, -1, keepdims=True
    )
    return (
        rstd * (scaled - inner),
        jnp.sum(grad * xhat, 0, keepdims=True),
        jnp.sum(grad, 0, keepdims=True),
    )


def column_sum(value):
    return jnp.sum(value.astype(F32), 0, keepdims=True)


def row(ref, index):
    return ref[index : index + 1, :].astype(F32)


def cdf(value):
    return 0.5 * (1.0 + lax.erf(value * np.float32(0.7071067811865476)))


def density(value):
    return jnp.exp(-0.5 * value * value) * np.float32(0.3989422804014327)


def put_halves(core, value, index, keep_ref, send_ref, scratch):
    half = value.shape[0] // 2
    scratch[...] = value
    mine = pl.multiple_of(core * half, half)
    other = pl.multiple_of((1 - core) * half, half)
    for block in range(value.shape[1] // LANES):
        lanes = slice(block * LANES, (block + 1) * LANES)
        keep_ref[index + block] = scratch[pl.ds(mine, half), lanes].astype(BF)
        send_ref[index + block] = scratch[pl.ds(other, half), lanes].astype(BF)


def memory_kernel(
    ids, feats, table, in_proj, in_bias, cross_proj, cross_bias, featp, ki, vi, k, v, buf, sem
):
    copy = pltpu.make_async_copy(feats.at[ids[0]], buf, sem)
    copy.start()
    copy.wait()
    slots = buf.shape[0]
    blocks = GROUPS
    part = slots // blocks
    padded = featp.shape[0] // blocks
    for j in range(blocks):
        here = slice(j * padded, (j + 1) * padded)
        featp[(j + 1) * padded - 16 : (j + 1) * padded] = jnp.zeros((16, featp.shape[1]), BF)
        featp[j * padded : j * padded + part] = buf[j * part : (j + 1) * part]
        memory = nn(featp[here], in_proj[...]) + in_bias[...].astype(F32)
        key_input = (memory + table[here]).astype(BF)
        value_input = memory.astype(BF)
        ki[here] = key_input
        vi[here] = value_input
        k[here] = nn(key_input, cross_proj[1]).astype(BF)
        v[here] = (nn(value_input, cross_proj[2]) + row(cross_bias, 1)).astype(BF)


def forward_kernel(
    ids,
    mask,
    own,
    got1,
    got2,
    got3,
    pos_ref,
    self_proj,
    self_out,
    self_bias,
    cross_proj,
    cross_out,
    cross_bias,
    gains,
    shifts,
    k_ref,
    v_ref,
    x_out,
    cot_out,
    ai_out,
    sq_out,
    sk_out,
    sv_out,
    ps_out,
    sm_out,
    xhat1_out,
    rstd1_out,
    ci_out,
    cq_out,
    pc_out,
    cm_out,
    h2_out,
    xhat2_out,
    rstd2_out,
    scores,
    *,
    rows_used,
):
    pb = ids[0]
    width = pos_ref.shape[1]
    block = own.shape[0]
    for k, ref in enumerate((own, got1, got2, got3)):
        at = pl.multiple_of((pb ^ k) * block, block)
        x_out[pl.ds(at, block), :] = ref[:, :width]
        cot_out[pl.ds(at, block), :] = ref[:, width:]
    rows = x_out.shape[0]
    pos = pos_ref[...].astype(F32)
    x = x_out[...].astype(F32)
    ai = (x + pos).astype(BF)
    ai_out[...] = ai
    sq_out[...] = ((nn(ai, self_proj[0]) + row(self_bias, 0)) * 0.125).astype(BF)
    sk_out[...] = nn(ai, self_proj[1]).astype(BF)
    sv_out[...] = (nn(x_out[...], self_proj[2]) + row(self_bias, 1)).astype(BF)
    key_row = lax.broadcasted_iota(jnp.int32, (rows, 2 * rows), 0)
    spare = jnp.where(lax.rem(key_row, block) < rows_used, 0.0, FAR).astype(F32)
    for g in range(GROUPS):
        lanes = slice(g * LANES, (g + 1) * LANES)
        s = nt(sk_out[:, lanes], pair(sq_out[...], g)) + spare
        e = jnp.exp(s - jnp.max(s, 0, keepdims=True))
        p = (e * (1.0 / jnp.sum(e, 0, keepdims=True))).astype(BF)
        ps_out[g] = p
        sm_out[:, lanes] = unpair(tn(p, sv_out[:, lanes])).astype(BF)
    xhat, rstd = norm(x + nn(sm_out[...], self_out[...]) + row(self_bias, 2))
    xhat1_out[...] = xhat
    rstd1_out[...] = rstd
    h1 = xhat * row(gains, 0) + row(shifts, 0)
    ci = (h1 + pos).astype(BF)
    ci_out[...] = ci
    cq_out[...] = ((nn(ci, cross_proj[0]) + row(cross_bias, 0)) * 0.125).astype(BF)

    padded = k_ref.shape[0] // GROUPS
    used = rows_used * 12
    slot_row = lax.broadcasted_iota(jnp.int32, (padded, 2 * rows), 0)
    for g in range(GROUPS):
        lanes = slice(g * LANES, (g + 1) * LANES)
        queries = pair(cq_out[...], g)
        top = jnp.full((8, 2 * rows), FAR, F32)
        for j in range(GROUPS):
            here = slice(j * padded, (j + 1) * padded)
            live = jnp.where(mask[pb, j] > 0, 0.0, -1000000000.0).astype(F32)
            s = nt(k_ref[here, lanes], queries) + jnp.where(slot_row < used, live, FAR)
            scores[here] = s
            top = jnp.maximum(top, eights(s, jnp.max))
        top = jnp.max(top, 0, keepdims=True)
        total = jnp.zeros((8, 2 * rows), F32)
        for j in range(GROUPS):
            here = slice(j * padded, (j + 1) * padded)
            e = jnp.exp(scores[here] - top)
            scores[here] = e
            total = total + eights(e, jnp.sum)
        inverse = 1.0 / jnp.sum(total, 0, keepdims=True)
        for j in range(GROUPS):
            here = slice(j * padded, (j + 1) * padded)
            pc_out[g, here] = (scores[here] * inverse).astype(BF)
        cm_out[:, lanes] = unpair(tn(pc_out[g], v_ref[:, lanes])).astype(BF)
    xhat, rstd = norm(h1 + nn(cm_out[...], cross_out[...]) + row(cross_bias, 2))
    xhat2_out[...] = xhat
    rstd2_out[...] = rstd
    h2_out[...] = xhat * row(gains, 1) + row(shifts, 1)


def ffn_kernel(
    ids,
    h2_ref,
    cot_ref,
    xhat2_ref,
    rstd2_ref,
    w_up,
    b_up,
    w_down,
    b_down,
    gains,
    shifts,
    fx,
    fy,
    fdx,
    fdy,
    sx,
    sy,
    sdx,
    sdy,
    res_out,
    ops_out,
    g2_out,
    small_out,
    weights,
    pre_ref,
    sems,
):
    core = ids[1]
    width = h2_ref.shape[1]
    half = fdx.shape[0]
    full = fx.shape[0]
    copies = []
    for side, (rx, ry, rdx, rdy) in enumerate(((fx, fy, fdx, fdy), (sx, sy, sdx, sdy))):
        to = core if side == 0 else 1 - core
        copies.append(
            [
                pltpu.make_async_copy(rx, weights.at[to, 0], sems.at[side, 0]),
                pltpu.make_async_copy(ry, weights.at[to, 1], sems.at[side, 1]),
                pltpu.make_async_copy(
                    rdx, weights.at[to, 2, pl.ds(0, half)], sems.at[side, 2]
                ),
                pltpu.make_async_copy(
                    rdy, weights.at[to, 2, pl.ds(half, full - half)], sems.at[side, 3]
                ),
            ]
        )
    for one in copies:
        for copy in one:
            copy.start()
    h2 = h2_ref[...]
    h2b = h2.astype(BF)
    ops_out[:, :width] = h2b
    down = jnp.zeros(h2.shape, F32)
    waits = ([], [0], [1], [2, 3])
    for p in range(4):
        for index in waits[p]:
            copies[0][index].wait()
            copies[1][index].wait()
        up = w_up[...] if p == 0 else weights[0, p - 1, :width]
        bias = b_up[...] if p == 0 else weights[0, p - 1, width : width + 1]
        dn = w_down[...] if p == 0 else weights[1, p - 1, :width]
        pre = nn(h2b, up) + bias.astype(F32)
        pre_ref[p] = pre
        down = down + nt((pre * cdf(pre)).astype(BF), dn)
    xhat, rstd = norm(h2 + down + b_down[...].astype(F32))
    res_out[...] = (xhat * row(gains, 2) + row(shifts, 2)).astype(BF)
    g3, dgain3, dshift3 = norm_back(xhat, rstd, row(gains, 2), cot_ref[...].astype(F32))
    gb = g3.astype(BF)
    ops_out[:, width:] = gb
    gh = g3
    for p in range(4):
        up = w_up[...] if p == 0 else weights[0, p - 1, :width]
        dn = w_down[...] if p == 0 else weights[1, p - 1, :width]
        ga = nn(gb, dn).astype(BF).astype(F32)
        pre = pre_ref[p]
        gp = (ga * (cdf(pre) + pre * density(pre))).astype(BF)
        gh = gh + nt(gp, up)
    g2, dgain2, dshift2 = norm_back(xhat2_ref[...], rstd2_ref[...], row(gains, 1), gh)
    g2_out[...] = g2
    small_out[0:1] = dgain3
    small_out[1:2] = dshift3
    small_out[2:3] = dgain2
    small_out[3:4] = dshift2
    small_out[4:5] = column_sum(gb)
    small_out[5:6] = column_sum(g2.astype(BF))
    small_out[6:8] = jnp.zeros((2, width), F32)


def backward_kernel(
    ids,
    g2_ref,
    pc_ref,
    k_ref,
    v_ref,
    cq_ref,
    ci_ref,
    cm_ref,
    xhat1_ref,
    rstd1_ref,
    x_ref,
    ai_ref,
    sq_ref,
    sk_ref,
    sv_ref,
    ps_ref,
    sm_ref,
    self_proj,
    self_out,
    cross_proj,
    cross_out,
    gains,
    ds_out,
    gcm_out,
    gx_out,
    gpos_out,
    small_out,
    keep1,
    send1,
    keep2,
    send2,
    dp_ref,
    work,
    gq_ref,
    gk_ref,
    gv_ref,
):
    core = ids[1]
    width = x_ref.shape[1]
    rows = x_ref.shape[0]
    g2 = g2_ref[...]
    branch = g2.astype(BF)
    gcm_out[...] = nt(branch, cross_out[...]).astype(BF)
    padded = k_ref.shape[0] // GROUPS
    for g in range(GROUPS):
        lanes = slice(g * LANES, (g + 1) * LANES)
        grads = pair(gcm_out[...], g)
        total = jnp.zeros((8, 2 * rows), F32)
        for j in range(GROUPS):
            here = slice(j * padded, (j + 1) * padded)
            dp = nt(v_ref[here, lanes], grads).astype(BF)
            dp_ref[here] = dp
            total = total + eights(pc_ref[g, here].astype(F32) * dp.astype(F32), jnp.sum)
        total = jnp.sum(total, 0, keepdims=True)
        for j in range(GROUPS):
            here = slice(j * padded, (j + 1) * padded)
            ds_out[g, here] = (
                pc_ref[g, here].astype(F32) * (dp_ref[here].astype(F32) - total)
            ).astype(BF)
        gq_ref[:, lanes] = unpair(tn(ds_out[g], k_ref[:, lanes])).astype(BF) * 0.125
    gcq = gq_ref[...]
    gci = nt(gcq, cross_proj[0])
    small_out[0:1] = column_sum(gcq)
    put_halves(core, tn(ci_ref[...], gcq), 0, keep1, send1, work)
    put_halves(core, tn(cm_ref[...], branch), 8, keep1, send1, work)
    g1, dgain1, dshift1 = norm_back(xhat1_ref[...], rstd1_ref[...], row(gains, 0), g2 + gci)
    small_out[1:2] = dgain1
    small_out[2:3] = dshift1
    sbranch = g1.astype(BF)
    small_out[3:4] = column_sum(sbranch)
    put_halves(core, tn(sm_ref[...], sbranch), 4, keep1, send1, work)
    gsm = nt(sbranch, self_out[...]).astype(BF)
    for g in range(GROUPS):
        lanes = slice(g * LANES, (g + 1) * LANES)
        grads = pair(gsm, g)
        p = ps_ref[g]
        dp = nt(sv_ref[:, lanes], grads).astype(BF).astype(F32)
        pf = p.astype(F32)
        ds = (pf * (dp - jnp.sum(pf * dp, 0, keepdims=True))).astype(BF)
        gq_ref[:, lanes] = unpair(tn(ds, sk_ref[:, lanes])).astype(BF) * 0.125
        gk_ref[:, lanes] = nn(ds, pair(sq_ref[...], g)).astype(BF)
        gv_ref[:, lanes] = nn(p, grads).astype(BF)
    gq, gk, gv = gq_ref[...], gk_ref[...], gv_ref[...]
    gai = nt(gq, self_proj[0]) + nt(gk, self_proj[1])
    gx_out[...] = (g1 + gai + nt(gv, self_proj[2])).astype(BF)
    gpos_out[...] = gai + gci
    small_out[4:5] = column_sum(gq)
    small_out[5:6] = column_sum(gv)
    small_out[6:8] = jnp.zeros((2, width), F32)
    put_halves(core, tn(ai_ref[...], gq), 0, keep2, send2, work)
    put_halves(core, tn(ai_ref[...], gk), 4, keep2, send2, work)
    put_halves(core, tn(x_ref[...], gv), 8, keep2, send2, work)


def ffn_grad_kernel(
    ids, own, got1, got2, got3, w_up, b_up, w_down, keep, send, bup_out, work
):
    core = ids[1]
    width = w_up.shape[0]
    ops = jnp.concatenate([ref[...] for ref in (own, got1, got2, got3)], axis=0)
    inputs, branch = ops[:, :width], ops[:, width:]
    pre = nn(inputs, w_up[...]) + b_up[...].astype(F32)
    phi = cdf(pre)
    act = (pre * phi).astype(BF)
    gact = nn(branch, w_down[...]).astype(BF).astype(F32)
    gpre = (gact * (phi + pre * density(pre))).astype(BF)
    bup_out[...] = column_sum(gpre)
    blocks, size = keep.shape[1], keep.shape[2]
    for side, grad in enumerate((tn(inputs, gpre), tn(branch, act))):
        work[...] = grad
        for block in range(blocks):
            mine = pl.multiple_of((2 * block + core) * size, size)
            other = pl.multiple_of((2 * block + 1 - core) * size, size)
            keep[side, block] = work[pl.ds(mine, size), :].astype(BF)
            send[side, block] = work[pl.ds(other, size), :].astype(BF)


def memory_back_kernel(
    ids,
    ds_ref,
    pc_ref,
    cq_ref,
    gcm_ref,
    featp,
    ki,
    vi,
    cross_proj,
    in_proj,
    res_ref,
    gx_ref,
    gpos_ref,
    small_a,
    small_b,
    bup,
    rows_out,
    keep,
    send,
    gk_ref,
    gv_ref,
    gm_ref,
    work,
    small,
    *,
    rows_used,
):
    pb, core = ids[0], ids[1]
    width = featp.shape[1]
    rows = res_ref.shape[0]
    block = rows // GROUPS
    padded = featp.shape[0] // GROUPS
    pairs_q = [pair(cq_ref[...], g) for g in range(GROUPS)]
    pairs_g = [pair(gcm_ref[...], g) for g in range(GROUPS)]
    for j in range(GROUPS):
        here = slice(j * padded, (j + 1) * padded)
        for g in range(GROUPS):
            lanes = slice(g * LANES, (g + 1) * LANES)
            gk_ref[here, lanes] = nn(ds_ref[g, here], pairs_q[g]).astype(BF)
            gv_ref[here, lanes] = nn(pc_ref[g, here], pairs_g[g]).astype(BF)
        gm = (nt(gk_ref[here], cross_proj[1]) + nt(gv_ref[here], cross_proj[2])).astype(BF)
        gm_ref[here] = gm
        to = j ^ pb
        rows_out[to, 0:padded] = nt(gm, in_proj[...]).astype(BF)
        rows_out[to, padded : padded + block] = gx_ref[j * block : (j + 1) * block]
        rows_out[to, padded + block : padded + 2 * block] = res_ref[j * block : (j + 1) * block]
    put_halves(core, tn(ki[...], gk_ref[...]), 0, keep, send, work)
    put_halves(core, tn(vi[...], gv_ref[...]), 4, keep, send, work)
    put_halves(core, tn(featp[...], gm_ref[...]), 8, keep, send, work)

    small[...] = gpos_ref[...]
    extras = [
        row(small_b, 1),
        row(small_a, 2),
        row(small_a, 0),
        row(small_b, 2),
        row(small_a, 3),
        row(small_a, 1),
        row(small_b, 4),
        row(small_b, 5),
        row(small_b, 3),
        row(small_b, 0),
        column_sum(gv_ref[...]),
        row(small_a, 5),
        row(small_a, 4),
        column_sum(gm_ref[...]),
    ]
    for index, value in enumerate(extras):
        at = spare_row(index, block, rows_used)
        small[at : at + 1] = value
    units = bup.shape[1]
    for b in range(GROUPS):
        mine = jnp.where(pb == b, 1.0, 0.0).astype(F32)
        at = b * block + rows_used + 5
        small[at : at + 1] = bup[:, :width] * mine
        small[at + 1 : at + 2] = jnp.concatenate(
            [bup[:, width:] * mine, jnp.zeros((1, 2 * width - units), F32)], axis=1
        )
    for b in range(2):
        for side, ref in ((core, keep), (1 - core, send)):
            low = small[:, b * LANES : (b + 1) * LANES]
            high = small[:, (2 + b) * LANES : (3 + b) * LANES]
            ref[12, b * rows : (b + 1) * rows] = jnp.where(side == 0, low, high).astype(BF)


def spare_row(index, block, rows_used):
    return index // 5 * block + rows_used + index % 5


def finish_kernel(
    ids, own1, got1, own3, got3, cross_out_, self_out_, ccross_, in_, small_, *, rows
):
    core = ids[1]
    half = own1.shape[1]
    mine = pl.multiple_of(core * half, half)
    other = pl.multiple_of((1 - core) * half, half)

    def put(index, refs, own, got):
        for b in range(4):
            lanes = slice(b * LANES, (b + 1) * LANES)
            refs[pl.ds(mine, half), lanes] = own[index + b].astype(F32)
            refs[pl.ds(other, half), lanes] = got[index + b].astype(F32)

    put(0, cross_out_.at[0], own1, got1)
    put(4, self_out_, own1, got1)
    put(8, ccross_, own1, got1)
    put(0, cross_out_.at[1], own3, got3)
    put(4, cross_out_.at[2], own3, got3)
    put(8, in_, own3, got3)
    for b in range(2):
        here = slice(b * rows, (b + 1) * rows)
        first = own3[12, here].astype(F32)
        second = got3[12, here].astype(F32)
        small_[:, b * LANES : (b + 1) * LANES] = jnp.where(core == 0, first, second)
        small_[:, (2 + b) * LANES : (3 + b) * LANES] = jnp.where(core == 0, second, first)


def finish_self_kernel(ids, own, got, out):
    core = ids[1]
    half = own.shape[1]
    mine = pl.multiple_of(core * half, half)
    other = pl.multiple_of((1 - core) * half, half)
    for m in range(3):
        for b in range(4):
            lanes = slice(b * LANES, (b + 1) * LANES)
            out[m, pl.ds(mine, half), lanes] = own[m * 4 + b].astype(F32)
            out[m, pl.ds(other, half), lanes] = got[m * 4 + b].astype(F32)


def call(kernel, args, outs, scratch=(), smem=1, hbm=(), flops=0):
    specs = []
    for index in range(len(args)):
        space = pltpu.SMEM if index < smem else pl.ANY if index in hbm else pltpu.VMEM
        specs.append(pl.BlockSpec(memory_space=space))
    size = lambda shape, dtype: int(np.prod(shape)) * jnp.dtype(dtype).itemsize
    moved = sum(size(a.shape, a.dtype) for a in args) + sum(size(*o) for o in outs)
    return pl.pallas_call(
        kernel,
        out_shape=[jax.ShapeDtypeStruct(*o) for o in outs],
        in_specs=specs,
        out_specs=[pl.BlockSpec(memory_space=pltpu.VMEM)] * len(outs),
        scratch_shapes=list(scratch),
        compiler_params=pltpu.CompilerParams(vmem_limit_bytes=60 * 1024 * 1024),
        cost_estimate=pl.CostEstimate(flops=flops, bytes_accessed=moved, transcendentals=0),
    )(*args)


def swap(value, axis, bit):
    size = lax.axis_size(axis)
    return lax.ppermute(value, axis, [(i, i ^ bit) for i in range(size)])


def bit_of(axis, bit):
    return (lax.axis_index(axis) // bit) % 2


def plus(left, right):
    return (left.astype(F32) + right.astype(F32)).astype(BF)


def halve(value, axis, bit, dim):
    mine = bit_of(axis, bit)
    half = value.shape[dim] // 2
    keep = lax.dynamic_slice_in_dim(value, mine * half, half, dim)
    send = lax.dynamic_slice_in_dim(value, (1 - mine) * half, half, dim)
    return plus(keep, swap(send, axis, bit))


def double(value, axis, bit, dim):
    other = swap(value, axis, bit)
    mine = bit_of(axis, bit)
    return jnp.where(
        mine == 0,
        jnp.concatenate([value, other], dim),
        jnp.concatenate([other, value], dim),
    )


def sinusoid(count, model_width):
    places = np.arange(count).astype(np.float32)[:, None]
    column = np.arange(model_width)
    exponent = (column // 2 * 2).astype(np.float32) / np.float32(model_width)
    angle = places / np.float32(10000.0) ** exponent
    return np.where(column % 2 == 0, np.sin(angle), np.cos(angle)).astype(np.float32)


def on_device(
    tokens,
    query_pos,
    features,
    camera_mask,
    out_grad,
    self_proj,
    self_out,
    self_bias,
    cross_proj,
    cross_out,
    cross_bias,
    w_up,
    b_up,
    w_down,
    b_down,
    norm_gain,
    norm_bias,
    in_proj,
    in_bias,
):
    pb = lax.axis_index("pb")
    pb_size = lax.axis_size("pb")
    dp_size = lax.axis_size("dp")
    core = bit_of("dp", 1)
    ids = jnp.stack([pb, core]).astype(jnp.int32)
    width = tokens.shape[2]
    used = tokens.shape[1]
    block = -(-used // 16) * 16
    rows = block * pb_size
    mem = features.shape[1]
    part = mem // pb_size
    padded = -(-part // 16) * 16
    slots = padded * pb_size
    units = b_up.shape[0]
    half_row = lambda value: value.reshape(1, -1)

    tail = jnp.zeros((31, units), BF)
    mine = jnp.where(
        core == 0,
        jnp.concatenate([w_up, half_row(b_up), tail]),
        jnp.concatenate([w_down, half_row(b_up), tail]),
    )
    cut = mine.shape[0] // 2
    both = jnp.pad(
        jnp.concatenate([tokens, out_grad], -1), ((0, 0), (0, block - used), (0, 0))
    )
    send = [lax.dynamic_index_in_dim(both, pb ^ k, 0, keepdims=False) for k in range(pb_size)]
    got = [send[0]] + [swap(send[k], "pb", k) for k in range(1, pb_size)]
    fx = swap(mine, "pb", 1)
    fy = swap(mine, "pb", 2)
    fdx = swap(fy[:cut], "pb", 1)
    fdy = swap(fx[cut:], "pb", 2)
    sx, sy, sdx, sdy = [swap(value, "dp", 1) for value in (fx, fy, fdx, fdy)]

    pos = jnp.pad(
        query_pos.reshape(pb_size, used, width), ((0, 0), (0, block - used), (0, 0))
    ).reshape(rows, width)
    table = np.zeros((pb_size, padded, width), np.float32)
    table[:, :part] = sinusoid(mem, width).reshape(pb_size, part, width)
    table = jnp.asarray(table.reshape(slots, width))

    wide = (slots, width)
    featp, ki, vi, ck, cv = call(
        memory_kernel,
        [ids, features, table, in_proj, half_row(in_bias), cross_proj, cross_bias],
        [(wide, BF)] * 5,
        scratch=[pltpu.VMEM((mem, width), BF), pltpu.SemaphoreType.DMA],
        hbm=(1,),
        flops=6 * slots * width * width,
    )
    flat = (rows, width)
    scores = (GROUPS, slots, 2 * rows)
    (x, cot, ai, sq, sk, sv, ps, sm, xhat1, rstd1, ci, cq, pc, cm, h2, xhat2, rstd2) = call(
        functools.partial(forward_kernel, rows_used=used),
        [
            ids,
            camera_mask,
            *got,
            pos,
            self_proj,
            self_out,
            self_bias,
            cross_proj,
            cross_out,
            cross_bias,
            norm_gain,
            norm_bias,
            ck,
            cv,
        ],
        [
            (flat, BF),
            (flat, BF),
            (flat, BF),
            (flat, BF),
            (flat, BF),
            (flat, BF),
            ((GROUPS, rows, 2 * rows), BF),
            (flat, BF),
            (flat, F32),
            ((rows, 1), F32),
            (flat, BF),
            (flat, BF),
            (scores, BF),
            (flat, BF),
            (flat, F32),
            (flat, F32),
            ((rows, 1), F32),
        ],
        scratch=[pltpu.VMEM((slots, 2 * rows), F32)],
        smem=2,
        flops=12 * rows * width * width + 8 * rows * slots * width,
    )
    res, ops, g2, small_a = call(
        ffn_kernel,
        [
            ids,
            h2,
            cot,
            xhat2,
            rstd2,
            w_up,
            half_row(b_up),
            w_down,
            half_row(b_down),
            norm_gain,
            norm_bias,
            fx,
            fy,
            fdx,
            fdy,
            sx,
            sy,
            sdx,
            sdy,
        ],
        [(flat, BF), ((rows, 2 * width), BF), (flat, F32), ((8, width), F32)],
        scratch=[
            pltpu.VMEM((2, 3, mine.shape[0], units), BF),
            pltpu.VMEM((4, rows, units), F32),
            pltpu.SemaphoreType.DMA((2, 4)),
        ],
        hbm=tuple(range(11, 19)),
        flops=32 * rows * width * units,
    )
    others = [swap(ops, "pb", k) for k in range(1, pb_size)]
    halves = ((12, width // 2, LANES), BF)
    ds, gcm, gx, gpos, small_b, keep1, send1, keep2, send2 = call(
        backward_kernel,
        [
            ids,
            g2,
            pc,
            ck,
            cv,
            cq,
            ci,
            cm,
            xhat1,
            rstd1,
            x,
            ai,
            sq,
            sk,
            sv,
            ps,
            sm,
            self_proj,
            self_out,
            cross_proj,
            cross_out,
            norm_gain,
        ],
        [
            (scores, BF),
            (flat, BF),
            (flat, BF),
            (flat, F32),
            ((8, width), F32),
            halves,
            halves,
            halves,
            halves,
        ],
        scratch=[
            pltpu.VMEM((slots, 2 * rows), BF),
            pltpu.VMEM((width, width), F32),
            pltpu.VMEM(flat, BF),
            pltpu.VMEM(flat, BF),
            pltpu.VMEM(flat, BF),
        ],
        flops=24 * rows * width * width + 8 * rows * slots * width,
    )
    piece = width // dp_size
    fhalf = ((2, dp_size // 2, piece, units), BF)
    fkeep, fsend, bup = call(
        ffn_grad_kernel,
        [ids, ops, *others, w_up, half_row(b_up), w_down],
        [fhalf, fhalf, ((1, units), F32)],
        scratch=[pltpu.VMEM((width, units), F32)],
        flops=8 * pb_size * rows * width * units,
    )
    halves3 = ((13, width // 2, LANES), BF)
    rows_out, keep3, send3 = call(
        functools.partial(memory_back_kernel, rows_used=used),
        [ids, ds, pc, cq, gcm, featp, ki, vi, cross_proj, in_proj, res, gx, gpos, small_a, small_b, bup],
        [((pb_size, padded + 2 * block, width), BF), halves3, halves3],
        scratch=[
            pltpu.VMEM(wide, BF),
            pltpu.VMEM(wide, BF),
            pltpu.VMEM(wide, BF),
            pltpu.VMEM((width, width), F32),
            pltpu.VMEM(flat, F32),
        ],
        flops=12 * slots * width * width + 8 * rows * slots * width,
    )

    later = [("dp", 1 << i) for i in range(2, dp_size.bit_length() - 1)]
    first = [("pb", 1), ("pb", 2), ("dp", 2)]
    orders = [first[i:] + first[:i] + later for i in range(3)]
    parts = [
        plus(keep, swap(send, "dp", 1))
        for keep, send in ((keep1, send1), (keep2, send2), (keep3, send3))
    ]
    for step in range(len(first + later)):
        parts = [halve(value, *order[step], 1) for value, order in zip(parts, orders)]
    ffn = plus(fkeep, swap(fsend, "dp", 1))
    for axis, bit in reversed([first[2]] + later):
        ffn = halve(ffn, axis, bit, 1)
    for step in reversed(range(len(first + later))):
        parts = [double(value, *order[step], 1) for value, order in zip(parts, orders)]
    swapped = [swap(value, "dp", 1) for value in parts]
    matrix = ((width, width), F32)
    three = ((3, width, width), F32)
    (g_self_proj,) = call(finish_self_kernel, [ids, parts[1], swapped[1]], [three])
    g_cross_proj, g_self_out, g_cross_out, g_in_proj, small = call(
        functools.partial(finish_kernel, rows=rows),
        [ids, parts[0], swapped[0], parts[2], swapped[2]],
        [three, matrix, matrix, matrix, (flat, F32)],
    )

    arrived = [rows_out[0]] + [swap(rows_out[k], "pb", k) for k in range(1, pb_size)]
    arrived = jnp.stack(arrived)
    ordered = jnp.stack(
        [lax.dynamic_index_in_dim(arrived, pb ^ e, 0, keepdims=False) for e in range(pb_size)]
    )
    spare = lambda index, count=1: jnp.stack(
        [small[spare_row(i, block, used)] for i in range(index, index + count)]
    )
    bup_rows = [
        small[b * block + used + 5 : b * block + used + 7].reshape(-1)[:units]
        for b in range(pb_size)
    ]
    return (
        ordered[:, padded + block : padded + block + used],
        ordered[:, padded : padded + used],
        ordered[:, :part],
        small.reshape(pb_size, block, width)[:, :used].reshape(query_pos.shape),
        g_self_proj,
        g_self_out,
        spare(6, 3),
        g_cross_proj,
        g_cross_out,
        spare(9, 3),
        ffn[0].reshape(piece, units).astype(F32),
        jnp.concatenate(bup_rows),
        ffn[1].reshape(piece, units).astype(F32),
        spare(12)[0],
        spare(0, 3),
        spare(3, 3),
        g_in_proj,
        spare(13)[0],
    )


def solution(mesh):
    return jax.shard_map(
        on_device,
        mesh=mesh,
        in_specs=(
            P("dp", "pb", None),
            P(),
            P("dp", None, None),
            P("dp", None),
            P("dp", "pb", None),
            P(),
            P(),
            P(),
            P(),
            P(),
            P(),
            P(None, "pb"),
            P("pb"),
            P(None, "pb"),
            P(),
            P(),
            P(),
            P(),
            P(),
        ),
        out_specs=(
            P("dp", "pb", None),
            P("dp", "pb", None),
            P("dp", "pb", None),
            P(),
            P(),
            P(),
            P(),
            P(),
            P(),
            P(),
            P("dp", "pb"),
            P(),
            P("dp", "pb"),
            P(),
            P(),
            P(),
            P(),
            P(),
        ),
        check_vma=False,
    )
```

profile of v0, /device:TPU:0, one launch (start us, length us, event | category | flops | bytes accessed | tf_op | source)
XLA Modules:
  0.0 250.0 jit_solution(6502920854634079942)
XLA Ops:
  0.7 1.6 copy.51.w_up
  3.5 3.0 %collective-permute-start.3 = (bf16[544,800]{1,0:T(8,128)(2,1)S(1)}, bf16[544,800]{1,0:T(8,128)(2,1)S(1)}, u32[]{:S(2)}, u32[]{:S(2)}) collective-permute-start(bf16[544,800]{1,0:T(8,128)(2,1)S(1)} %fusion.1), channel_id=1, source_target_pairs={{0,8},{8,0},{16,24},{24,16},{1,9},{9,1},{17,25},{25,17},{2,10},{10... | collective-permute-start | bytes 2611208 | tf_op jit(solution)/shard_map/ppermute | solution.py:584
  6.5 1.5 collective-permute-start.4
  8.1 20.1 %collective-permute-done.3.fx = bf16[544,800]{1,0:T(8,128)(2,1)S(1)} collective-permute-done((bf16[544,800]{1,0:T(8,128)(2,1)S(1)}, bf16[544,800]{1,0:T(8,128)(2,1)S(1)}, u32[]{:S(2)}, u32[]{:S(2)}) %collective-permute-start.3) | collective-permute-done | bytes 870432 | tf_op jit(solution)/shard_map/ppermute | solution.py:584
  28.1 0.9 slice.123
  29.1 1.8 collective-permute-start.6
  30.8 1.8 slice.122
  32.7 1.5 collective-permute-start.5
  36.0 5.7 %collective-permute-done.6.fdy = bf16[272,800]{1,0:T(8,128)(2,1)S(1)} collective-permute-done((bf16[272,800]{1,0:T(8,128)(2,1)}, bf16[272,800]{1,0:T(8,128)(2,1)S(1)}, u32[]{:S(2)}, u32[]{:S(2)}) %collective-permute-start.6) | collective-permute-done | bytes 435232 | tf_op jit(solution)/shard_map/ppermute | solution.py:584
  41.7 3.7 %collective-permute-done.5.fdx = bf16[272,800]{1,0:T(8,128)(2,1)S(1)} collective-permute-done((bf16[272,800]{1,0:T(8,128)(2,1)}, bf16[272,800]{1,0:T(8,128)(2,1)S(1)}, u32[]{:S(2)}, u32[]{:S(2)}) %collective-permute-start.5) | collective-permute-done | bytes 435232 | tf_op jit(solution)/shard_map/ppermute | solution.py:584
  47.3 3.3 %collective-permute-done.1.got2 = bf16[32,1024]{1,0:T(8,128)(2,1)S(1)} collective-permute-done((bf16[32,1024]{1,0:T(8,128)(2,1)S(1)}, bf16[32,1024]{1,0:T(8,128)(2,1)S(1)}, u32[]{:S(2)}, u32[]{:S(2)}) %collective-permute-start.1) | collective-permute-done | bytes 65568 | tf_op jit(solution)/shard_map/ppermute | solution.py:584
  50.6 1.4 collective-permute-start.2
  52.0 8.1 %shard_map.331 = (bf16[1216,512]{1,0:T(8,128)(2,1)}, bf16[1216,512]{1,0:T(8,128)(2,1)}, bf16[1216,512]{1,0:T(8,128)(2,1)}, bf16[1216,512]{1,0:T(8,128)(2,1)}, bf16[1216,512]{1,0:T(8,128)(2,1)}) custom-call(s32[2]{0:T(128)} %pad_add_fusion.ids, bf16[4,1200,512]{2,1,0:T(8,128)(2,1)} %feats.1, f32[1216,512]{1,0:T(8,128)} %constant.208.clone.table, ...), custom_call_target="tpu_custom_call" | custom-call | flops 1912602624 | bytes 15732744 | tf_op jit(solution)/shard_map/pallas_call | solution.py:571
  62.1 9.5 %shard_map.332 = (bf16[128,512]{1,0:T(8,128)(2,1)}, bf16[128,512]{1,0:T(8,128)(2,1)}, bf16[128,512]{1,0:T(8,128)(2,1)}, bf16[128,512]{1,0:T(8,128)(2,1)}, bf16[1...) custom-call(s32[2]{0:T(128)} %pad_add_fusion.ids, ...), custom_call_target="tpu_custom_call" | custom-call | flops 1040187392 | bytes 11940936 | tf_op jit(solution)/shard_map/pallas_call | solution.py:571
  72.5 8.8 %shard_map.333 = (bf16[128,512]{1,0:T(8,128)(2,1)}, bf16[128,1024]{1,0:T(8,128)(2,1)}, f32[128,512]{1,0:T(8,128)}, f32[8,512]{1,0:T(8,128)}) custom-call(s32[2]{0:T(128)} %pad_add_fusion.ids, f32[128,512]{1,0:T(8,128)} %get-tuple-element.66.h2_ref, bf16[128,512]{1,0:T(8,128)(2,1)} %get-tuple-element.67.cot_ref, f32[128,512]{1,0:T(8,128)} %get-tuple-element.68.xhat2_ref, ...), custom_call_target="tpu_custom_call" | custom-call | flops 1677721600 | bytes 8197192 | tf_op jit(solution)/shard_map/pallas_call | solution.py:571
  82.0 1.5 collective-permute-start.12
  83.4 1.4 collective-permute-start.13
  84.8 12.7 %shard_map.334 = (bf16[4,1216,256]{2,1,0:T(8,128)(2,1)}, bf16[128,512]{1,0:T(8,128)(2,1)}, bf16[128,512]{1,0:T(8,128)(2,1)}, f32[128,512]{1,0:T(8,128)}, f32[8,5...) custom-call(s32[2]{0:T(128)} %pad_add_fusion.ids, ...), custom_call_target="tpu_custom_call" | custom-call | flops 1442840576 | bytes 17321480 | tf_op jit(solution)/shard_map/pallas_call | solution.py:571
  99.2 5.8 %shard_map.335 = (bf16[2,4,64,800]{3,2,1,0:T(8,128)(2,1)}, bf16[2,4,64,800]{3,2,1,0:T(8,128)(2,1)}, f32[1,800]{1,0:T(1,128)}) custom-call(s32[2]{0:T(128)} %pad_add_fusion.ids, bf16[128,1024]{1,0:T(8,128)(2,1)} %get-tuple-element.94.own, bf16[128,1024]{1,0:T(8,128)(2,1)} %copy-done.26, bf16[128,1024]{1,0:T(8,128)(2,1)} %copy-done.27, ...), custom_call_target="tpu_custom_call" | custom-call | flops 1677721600 | bytes 4330184 | tf_op jit(solution)/shard_map/pallas_call | solution.py:571
  105.0 12.3 %shard_map.336 = (bf16[4,368,512]{2,1,0:T(8,128)(2,1)}, bf16[13,256,128]{2,1,0:T(8,128)(2,1)}, bf16[13,256,128]{2,1,0:T(8,128)(2,1)}) custom-call(s32[2]{0:T(128)} %pad_add_fusion.ids, bf16[4,1216,256]{2,1,0:T(8,128)(2,1)} %get-tuple-element.84.ds_ref, bf16[4,1216,256]{2,1,0:T(8,128)(2,1)} %get-tuple-element.71.pc_ref, ...), custom_call_target="tpu_custom_call" | custom-call | flops 4462739456 | bytes 14847112 | tf_op jit(solution)/shard_map/pallas_call | solution.py:571
  117.2 2.3 fusion.8
  119.5 1.5 collective-permute-start.15
  121.6 1.4 collective-permute-start.14
  123.0 16.0 %collective-permute-done.15 = bf16[368,512]{1,0:T(8,128)(2,1)S(1)} collective-permute-done((bf16[368,512]{1,0:T(8,128)(2,1)}, bf16[368,512]{1,0:T(8,128)(2,1)S(1)}, u32[]{:S(2)}, u32[]{:S(2)}) %collective-permute-start.15) | collective-permute-done | bytes 376864 | tf_op jit(solution)/shard_map/ppermute | solution.py:584
  140.5 1.0 copy-done.13
  142.9 1.6 collective-permute-start.38
  144.8 2.7 %collective-permute-start.48 = (bf16[2,2,64,800]{3,2,1,0:T(8,128)(2,1)S(1)}, bf16[2,2,64,800]{3,2,1,0:T(8,128)(2,1)S(1)}, u32[]{:S(2)}, u32[]{:S(2)}) collective-permute-start(bf16[2,2,64,800]{3,2,1,0:T(8,128)(2,1)S(1)} %constant_dynamic-slice_fusion.1), channel_id=1, source_target_pairs={{0,4},{1,5},{2,6},{3,7},{4,0},{5,1},{6,2},{7,3},{8,12},{9,13},{10,... | collective-permute-start | bytes 1228808 | tf_op jit(solution)/shard_map/ppermute | solution.py:584
  147.8 1.6 collective-permute-start.28
  149.5 2.8 %collective-permute-done.18 = bf16[12,128,128]{2,1,0:T(8,128)(2,1)S(1)} collective-permute-done((bf16[12,128,128]{2,1,0:T(8,128)(2,1)S(1)}, bf16[12,128,128]{2,1,0:T(8,128)(2,1)S(1)}, u32[]{:S(2)}, u32[]{:S(2)}) %collective-permute-start.18) | collective-permute-done | bytes 393248 | tf_op jit(solution)/shard_map/ppermute | solution.py:584
  152.4 1.6 collective-permute-start.19
  154.1 1.7 collective-permute-start.39
  155.8 2.4 collective-permute-done.19
  158.3 1.6 collective-permute-start.20
  159.9 12.5 %collective-permute-done.39 = bf16[12,64,128]{2,1,0:T(8,128)(2,1)S(1)} collective-permute-done((bf16[12,64,128]{2,1,0:T(8,128)(2,1)S(1)}, bf16[12,64,128]{2,1,0:T(8,128)(2,1)S(1)}, u32[]{:S(2)}, u32[]{:S(2)}) %collective-permute-start.39) | collective-permute-done | bytes 196640 | tf_op jit(solution)/shard_map/ppermute | solution.py:584
  172.5 1.0 collective-permute-start.40
  173.6 1.3 collective-permute-start.21
  174.9 2.3 collective-permute-done.40
  177.2 1.3 collective-permute-start.41
  178.6 1.3 collective-permute-done.21
  180.5 1.5 collective-permute-start.29
  182.3 2.6 %collective-permute-start.42 = (bf16[12,16,128]{2,1,0:T(8,128)(2,1)S(1)}, bf16[12,16,128]{2,1,0:T(8,128)(2,1)S(1)}, u32[]{:S(2)}, u32[]{:S(2)}) collective-permute-start(bf16[12,16,128]{2,1,0:T(8,128)(2,1)S(1)} %add_convert_fusion.16), channel_id=1, source_target_pairs={{0,4},{1,5},{2,6},{3,7},{4,0},{5,1},{6,2},{7,3},{8,12},{9,13},{10,... | collective-permute-start | bytes 147464 | tf_op jit(solution)/shard_map/ppermute | solution.py:584
  185.0 1.4 collective-permute-done.29
  186.5 1.2 collective-permute-start.30
  187.7 2.8 %collective-permute-start.23 = (bf16[12,32,128]{2,1,0:T(8,128)(2,1)S(1)}, bf16[12,32,128]{2,1,0:T(8,128)(2,1)S(1)}, u32[]{:S(2)}, u32[]{:S(2)}) collective-permute-start(bf16[12,32,128]{2,1,0:T(8,128)(2,1)S(1)} %maximum_select_fusion.10), channel_id=1, source_target_pairs={{0,2},{1,3},{2,0},{3,1},{4,6},{5,7},{6,4},{7,5},{8,10},{9,11},{10,... | collective-permute-start | bytes 294920 | tf_op jit(solution)/shard_map/ppermute | solution.py:584
  191.3 2.6 %collective-permute-start.31 = (bf16[13,16,128]{2,1,0:T(8,128)(2,1)S(1)}, bf16[13,16,128]{2,1,0:T(8,128)(2,1)S(1)}, u32[]{:S(2)}, u32[]{:S(2)}) collective-permute-start(bf16[13,16,128]{2,1,0:T(8,128)(2,1)S(1)} %constant_dynamic-slice_fusion.6), channel_id=1, source_target_pairs={{0,4},{1,5},{2,6},{3,7},{4,0},{5,1},{6,2},{7,3},{8,12},{9,13},{10,... | collective-permute-start | bytes 159752 | tf_op jit(solution)/shard_map/ppermute | solution.py:584
  194.0 1.8 collective-permute-start.43
  196.5 2.8 %collective-permute-start.32 = (bf16[13,16,128]{2,1,0:T(8,128)(2,1)S(1)}, bf16[13,16,128]{2,1,0:T(8,128)(2,1)S(1)}, u32[]{:S(2)}, u32[]{:S(2)}) collective-permute-start(bf16[13,16,128]{2,1,0:T(8,128)(2,1)S(1)} %add_convert_fusion.15), channel_id=1, source_target_pairs={{0,4},{1,5},{2,6},{3,7},{4,0},{5,1},{6,2},{7,3},{8,12},{9,13},{10,... | collective-permute-start | bytes 159752 | tf_op jit(solution)/shard_map/ppermute | solution.py:584
  199.5 2.1 collective-permute-done.32
  201.6 1.4 collective-permute-start.33
  203.0 2.6 %collective-permute-start.44 = (bf16[12,64,128]{2,1,0:T(8,128)(2,1)S(1)}, bf16[12,64,128]{2,1,0:T(8,128)(2,1)S(1)}, u32[]{:S(2)}, u32[]{:S(2)}) collective-permute-start(bf16[12,64,128]{2,1,0:T(8,128)(2,1)S(1)} %maximum_select_fusion.8), channel_id=1, source_target_pairs={{0,2},{1,3},{2,0},{3,1},{4,6},{5,7},{6,4},{7,5},{8,10},{9,11},{10,... | collective-permute-start | bytes 589832 | tf_op jit(solution)/shard_map/ppermute | solution.py:584
  205.6 3.6 %collective-permute-done.33 = bf16[13,32,128]{2,1,0:T(8,128)(2,1)S(1)} collective-permute-done((bf16[13,32,128]{2,1,0:T(8,128)(2,1)S(1)}, bf16[13,32,128]{2,1,0:T(8,128)(2,1)S(1)}, u32[]{:S(2)}, u32[]{:S(2)}) %collective-permute-start.33) | collective-permute-done | bytes 106528 | tf_op jit(solution)/shard_map/ppermute | solution.py:584
  209.3 1.9 collective-permute-start.34
  212.4 2.8 %collective-permute-done.34 = bf16[13,64,128]{2,1,0:T(8,128)(2,1)S(1)} collective-permute-done((bf16[13,64,128]{2,1,0:T(8,128)(2,1)S(1)}, bf16[13,64,128]{2,1,0:T(8,128)(2,1)S(1)}, u32[]{:S(2)}, u32[]{:S(2)}) %collective-permute-start.34) | collective-permute-done | bytes 213024 | tf_op jit(solution)/shard_map/ppermute | solution.py:584
  215.3 1.6 collective-permute-start.35
  217.0 2.4 collective-permute-done.25
  220.5 3.0 %collective-permute-done.35 = bf16[13,128,128]{2,1,0:T(8,128)(2,1)S(1)} collective-permute-done((bf16[13,128,128]{2,1,0:T(8,128)(2,1)S(1)}, bf16[13,128,128]{2,1,0:T(8,128)(2,1)S(1)}, u32[]{:S(2)}, u32[]{:S(2)}) %collective-permute-start.35) | collective-permute-done | bytes 426016 | tf_op jit(solution)/shard_map/ppermute | solution.py:584
  223.9 1.6 collective-permute-start.49
  225.6 2.0 copy.57
  229.0 2.9 %collective-permute-done.49 = bf16[2,1,64,800]{3,2,1,0:T(8,128)(2,1)S(1)} collective-permute-done((bf16[2,1,64,800]{3,2,1,0:T(8,128)(2,1)S(1)}, bf16[2,1,64,800]{3,2,1,0:T(8,128)(2,1)S(1)}, u32[]{:S(2)}, u32[]{:S(2)}) %collective-permute-start.49) | collective-permute-done | bytes 204832 | tf_op jit(solution)/shard_map/ppermute | solution.py:584
  233.7 3.4 %shard_map.338 = f32[3,512,512]{2,1,0:T(8,128)} custom-call(s32[2]{0:T(128)} %pad_add_fusion.ids, bf16[12,256,128]{2,1,0:T(8,128)(2,1)} %copy-done.3, bf16[12,256,128]{2,1,0:T(8,128)(2,1)} %copy-done.11), custom_call_target="tpu_custom_call" | custom-call | bytes 4718600 | tf_op jit(solution)/shard_map/pallas_call | solution.py:571
  238.0 5.4 %shard_map.337 = (f32[3,512,512]{2,1,0:T(8,128)}, f32[512,512]{1,0:T(8,128)}, f32[512,512]{1,0:T(8,128)}, f32[512,512]{1,0:T(8,128)}, f32[128,512]{1,0:T(8,128)}) custom-call(s32[2]{0:T(128)} %pad_add_fusion.ids, bf16[12,256,128]{2,1,0:T(8,128)(2,1)} %copy-done.4, bf16[12,256,128]{2,1,0:T(8,128)(2,1)} %collective-permute-done.26.got1, ...), custom_call_target="tpu_custom_call" | custom-call | bytes 9830408 | tf_op jit(solution)/shard_map/pallas_call | solution.py:571
  244.3 1.4 fusion.9
  245.7 1.3 fusion.11
  247.0 1.7 reshape.82
  (182 shorter events, 26.8 us)
Async XLA Ops:
  2.9 26.1 %copy-start.1 = (bf16[512,800]{1,0:T(8,128)(2,1)}, bf16[512,800]{1,0:T(8,128)(2,1)S(1)}, u32[]{:S(2)}) copy-start(bf16[512,800]{1,0:T(8,128)(2,1)S(1)} %copy.52.w_down) | copy-start | bytes 2457604
  3.0 26.1 %copy-start.22 = (bf16[1,800]{1,0:T(2,128)(2,1)}, bf16[1,800]{1,0:T(2,128)(2,1)S(1)}, u32[]{:S(2)}) copy-start(bf16[1,800]{1,0:T(2,128)(2,1)S(1)} %reshape.79.b_up) | copy-start | bytes 4804
  3.5 31.2 %copy-start.17 = (bf16[4,25,512]{2,0,1:T(4,128)(2,1)S(1)}, bf16[4,25,512]{2,0,1:T(4,128)(2,1)}, u32[]{:S(2)}) copy-start(bf16[4,25,512]{2,0,1:T(4,128)(2,1)} %param.20) | copy-start | bytes 307204
  3.5 31.2 %copy-start.18 = (bf16[4,25,512]{2,0,1:T(4,128)(2,1)S(1)}, bf16[4,25,512]{2,0,1:T(4,128)(2,1)}, u32[]{:S(2)}) copy-start(bf16[4,25,512]{2,0,1:T(4,128)(2,1)} %param.24) | copy-start | bytes 307204
  3.5 41.9 %copy-start.24 = (bf16[512]{0:T(512)(128)(2,1)S(1)}, bf16[512]{0:T(512)(128)(2,1)}, u32[]{:S(2)}) copy-start(bf16[512]{0:T(512)(128)(2,1)} %param.38) | copy-start | bytes 3076
  3.5 24.6 %collective-permute-start.3 = (bf16[544,800]{1,0:T(8,128)(2,1)S(1)}, bf16[544,800]{1,0:T(8,128)(2,1)S(1)}, u32[]{:S(2)}, u32[]{:S(2)}) collective-permute-start(bf16[544,800]{1,0:T(8,128)(2,1)S(1)} %fusion.1), channel_id=1, source_target_pairs={{0,8},{8,0},{16,24},{24,16},{1,9},{9,1},{17,25},{25,17},{2,10},{10... | collective-permute-start | bytes 2611208 | tf_op jit(solution)/shard_map/ppermute | solution.py:584
  6.5 24.3 %collective-permute-start.4 = (bf16[544,800]{1,0:T(8,128)(2,1)S(1)}, bf16[544,800]{1,0:T(8,128)(2,1)}, u32[]{:S(2)}, u32[]{:S(2)}) collective-permute-start(bf16[544,800]{1,0:T(8,128)(2,1)S(1)} %fusion.1), channel_id=1, source_target_pairs={{0,16},{8,24},{16,0},{24,8},{1,17},{9,25},{17,1},{25,9},{2,18},{10... | collective-permute-start | bytes 2611208 | tf_op jit(solution)/shard_map/ppermute | solution.py:584
  28.1 7.3 %copy-start.5 = (bf16[544,800]{1,0:T(8,128)(2,1)}, bf16[544,800]{1,0:T(8,128)(2,1)S(1)}, u32[]{:S(2)}) copy-start(bf16[544,800]{1,0:T(8,128)(2,1)S(1)} %collective-permute-done.3.fx) | copy-start | bytes 2611204
  29.1 12.6 %collective-permute-start.6 = (bf16[272,800]{1,0:T(8,128)(2,1)}, bf16[272,800]{1,0:T(8,128)(2,1)S(1)}, u32[]{:S(2)}, u32[]{:S(2)}) collective-permute-start(bf16[272,800]{1,0:T(8,128)(2,1)} %slice.123), channel_id=1, source_target_pairs={{0,16},{8,24},{16,0},{24,8},{1,17},{9,25},{17,1},{25,9},{2,18},{10... | collective-permute-start | bytes 1305608 | tf_op jit(solution)/shard_map/ppermute | solution.py:584
  32.7 12.7 %collective-permute-start.5 = (bf16[272,800]{1,0:T(8,128)(2,1)}, bf16[272,800]{1,0:T(8,128)(2,1)S(1)}, u32[]{:S(2)}, u32[]{:S(2)}) collective-permute-start(bf16[272,800]{1,0:T(8,128)(2,1)} %slice.122), channel_id=1, source_target_pairs={{0,8},{8,0},{16,24},{24,16},{1,9},{9,1},{17,25},{25,17},{2,10},{10... | collective-permute-start | bytes 1305608 | tf_op jit(solution)/shard_map/ppermute | solution.py:584
  34.2 37.4 %collective-permute-start.7 = (bf16[544,800]{1,0:T(8,128)(2,1)S(1)}, bf16[544,800]{1,0:T(8,128)(2,1)S(1)}, u32[]{:S(2)}, u32[]{:S(2)}) collective-permute-start(bf16[544,800]{1,0:T(8,128)(2,1)S(1)} %collective-permute-done.3.fx), channel_id=1, source_target_pairs={{0,1},{1,0},{2,3},{3,2},{4,5},{5,4},{6,7},{7,6},{8,9},{9,8},{10,11... | collective-permute-start | bytes 2611208 | tf_op jit(solution)/shard_map/ppermute | solution.py:584
  34.2 37.4 %collective-permute-start.8 = (bf16[544,800]{1,0:T(8,128)(2,1)}, bf16[544,800]{1,0:T(8,128)(2,1)}, u32[]{:S(2)}, u32[]{:S(2)}) collective-permute-start(bf16[544,800]{1,0:T(8,128)(2,1)} %collective-permute-done.4.fy), channel_id=1, source_target_pairs={{0,1},{1,0},{2,3},{3,2},{4,5},{5,4},{6,7},{7,6},{8,9},{9,8},{10,11... | collective-permute-start | bytes 2611208 | tf_op jit(solution)/shard_map/ppermute | solution.py:584
  35.5 10.7 %collective-permute-start = (bf16[32,1024]{1,0:T(8,128)(2,1)S(1)}, bf16[32,1024]{1,0:T(8,128)(2,1)S(1)}, u32[]{:S(2)}, u32[]{:S(2)}) collective-permute-start(bf16[32,1024]{1,0:T(8,128)(2,1)S(1)} %get-tuple-element.170), channel_id=1, source_target_pairs={{0,8},{8,0},{16,24},{24,16},{1,9},{9,1},{17,25},{25,17},{2,10},{10... | collective-permute-start | bytes 196616 | tf_op jit(solution)/shard_map/ppermute | solution.py:584
  41.7 18.4 %copy-start.14 = (bf16[272,800]{1,0:T(8,128)(2,1)}, bf16[272,800]{1,0:T(8,128)(2,1)S(1)}, u32[]{:S(2)}) copy-start(bf16[272,800]{1,0:T(8,128)(2,1)S(1)} %collective-permute-done.6.fdy) | copy-start | bytes 1305604
  41.7 29.9 %collective-permute-start.10 = (bf16[272,800]{1,0:T(8,128)(2,1)S(1)}, bf16[272,800]{1,0:T(8,128)(2,1)}, u32[]{:S(2)}, u32[]{:S(2)}) collective-permute-start(bf16[272,800]{1,0:T(8,128)(2,1)S(1)} %collective-permute-done.6.fdy), channel_id=1, source_target_pairs={{0,1},{1,0},{2,3},{3,2},{4,5},{5,4},{6,7},{7,6},{8,9},{9,8},{10,11... | collective-permute-start | bytes 1305608 | tf_op jit(solution)/shard_map/ppermute | solution.py:584
  45.4 14.7 %copy-start.15 = (bf16[272,800]{1,0:T(8,128)(2,1)}, bf16[272,800]{1,0:T(8,128)(2,1)S(1)}, u32[]{:S(2)}) copy-start(bf16[272,800]{1,0:T(8,128)(2,1)S(1)} %collective-permute-done.5.fdx) | copy-start | bytes 1305604
  45.4 26.1 %collective-permute-start.9 = (bf16[272,800]{1,0:T(8,128)(2,1)S(1)}, bf16[272,800]{1,0:T(8,128)(2,1)}, u32[]{:S(2)}, u32[]{:S(2)}) collective-permute-start(bf16[272,800]{1,0:T(8,128)(2,1)S(1)} %collective-permute-done.5.fdx), channel_id=1, source_target_pairs={{0,1},{1,0},{2,3},{3,2},{4,5},{5,4},{6,7},{7,6},{8,9},{9,8},{10,11... | collective-permute-start | bytes 1305608 | tf_op jit(solution)/shard_map/ppermute | solution.py:584
  46.1 14.0 %copy-start.19 = (bf16[32,1024]{1,0:T(8,128)(2,1)}, bf16[32,1024]{1,0:T(8,128)(2,1)S(1)}, u32[]{:S(2)}) copy-start(bf16[32,1024]{1,0:T(8,128)(2,1)S(1)} %collective-permute-done.got1) | copy-start | bytes 196612
  46.1 4.4 %collective-permute-start.1 = (bf16[32,1024]{1,0:T(8,128)(2,1)S(1)}, bf16[32,1024]{1,0:T(8,128)(2,1)S(1)}, u32[]{:S(2)}, u32[]{:S(2)}) collective-permute-start(bf16[32,1024]{1,0:T(8,128)(2,1)S(1)} %get-tuple-element.169), channel_id=1, source_target_pairs={{0,16},{8,24},{16,0},{24,8},{1,17},{9,25},{17,1},{25,9},{2,18},{10... | collective-permute-start | bytes 196616 | tf_op jit(solution)/shard_map/ppermute | solution.py:584
  50.5 9.5 %copy-start.20 = (bf16[32,1024]{1,0:T(8,128)(2,1)}, bf16[32,1024]{1,0:T(8,128)(2,1)S(1)}, u32[]{:S(2)}) copy-start(bf16[32,1024]{1,0:T(8,128)(2,1)S(1)} %collective-permute-done.1.got2) | copy-start | bytes 196612
  50.5 9.6 %copy-start.16 = (bf16[100,512]{1,0:T(8,128)(2,1)S(1)}, bf16[100,512]{1,0:T(8,128)(2,1)}, u32[]{:S(2)}) copy-start(bf16[100,512]{1,0:T(8,128)(2,1)} %param.21) | copy-start | bytes 307204
  50.5 10.3 %copy-start.25 = (bf16[512]{0:T(512)(128)(2,1)S(1)}, bf16[512]{0:T(512)(128)(2,1)}, u32[]{:S(2)}) copy-start(bf16[512]{0:T(512)(128)(2,1)} %param.34) | copy-start | bytes 3076
  50.6 10.9 %collective-permute-start.2 = (bf16[32,1024]{1,0:T(8,128)(2,1)S(1)}, bf16[32,1024]{1,0:T(8,128)(2,1)S(1)}, u32[]{:S(2)}, u32[]{:S(2)}) collective-permute-start(bf16[32,1024]{1,0:T(8,128)(2,1)S(1)} %get-tuple-element.168), channel_id=1, source_target_pairs={{0,24},{8,16},{16,8},{24,0},{1,25},{9,17},{17,9},{25,1},{2,26},{10... | collective-permute-start | bytes 196616 | tf_op jit(solution)/shard_map/ppermute | solution.py:584
  81.3 16.4 %collective-permute-start.11 = (bf16[128,1024]{1,0:T(8,128)(2,1)}, bf16[128,1024]{1,0:T(8,128)(2,1)S(1)}, u32[]{:S(2)}, u32[]{:S(2)}) collective-permute-start(bf16[128,1024]{1,0:T(8,128)(2,1)} %get-tuple-element.94.own), channel_id=1, source_target_pairs={{0,8},{8,0},{16,24},{24,16},{1,9},{9,1},{17,25},{25,17},{2,10},{10... | collective-permute-start | bytes 786440 | tf_op jit(solution)/shard_map/ppermute | solution.py:584
  82.0 15.7 %collective-permute-start.12 = (bf16[128,1024]{1,0:T(8,128)(2,1)}, bf16[128,1024]{1,0:T(8,128)(2,1)S(1)}, u32[]{:S(2)}, u32[]{:S(2)}) collective-permute-start(bf16[128,1024]{1,0:T(8,128)(2,1)} %get-tuple-element.94.own), channel_id=1, source_target_pairs={{0,16},{8,24},{16,0},{24,8},{1,17},{9,25},{17,1},{25,9},{2,18},{10... | collective-permute-start | bytes 786440 | tf_op jit(solution)/shard_map/ppermute | solution.py:584
  83.4 14.3 %collective-permute-start.13 = (bf16[128,1024]{1,0:T(8,128)(2,1)}, bf16[128,1024]{1,0:T(8,128)(2,1)S(1)}, u32[]{:S(2)}, u32[]{:S(2)}) collective-permute-start(bf16[128,1024]{1,0:T(8,128)(2,1)} %get-tuple-element.94.own), channel_id=1, source_target_pairs={{0,24},{8,16},{16,8},{24,0},{1,25},{9,17},{17,9},{25,1},{2,26},{10... | collective-permute-start | bytes 786440 | tf_op jit(solution)/shard_map/ppermute | solution.py:584
  97.6 43.0 %collective-permute-start.17 = (bf16[12,256,128]{2,1,0:T(8,128)(2,1)}, bf16[12,256,128]{2,1,0:T(8,128)(2,1)S(1)}, u32[]{:S(2)}, u32[]{:S(2)}) collective-permute-start(bf16[12,256,128]{2,1,0:T(8,128)(2,1)} %get-tuple-element.98), channel_id=1, source_target_pairs={{0,1},{1,0},{2,3},{3,2},{4,5},{5,4},{6,7},{7,6},{8,9},{9,8},{10,11... | collective-permute-start | bytes 2359304 | tf_op jit(solution)/shard_map/ppermute | solution.py:584
  119.5 19.4 %collective-permute-start.15 = (bf16[368,512]{1,0:T(8,128)(2,1)}, bf16[368,512]{1,0:T(8,128)(2,1)S(1)}, u32[]{:S(2)}, u32[]{:S(2)}) collective-permute-start(bf16[368,512]{1,0:T(8,128)(2,1)} %get-tuple-element.154), channel_id=1, source_target_pairs={{0,16},{8,24},{16,0},{24,8},{1,17},{9,25},{17,1},{25,9},{2,18},{10... | collective-permute-start | bytes 1130504 | tf_op jit(solution)/shard_map/ppermute | solution.py:584
  121.0 18.0 %collective-permute-start.16 = (bf16[368,512]{1,0:T(8,128)(2,1)}, bf16[368,512]{1,0:T(8,128)(2,1)S(1)}, u32[]{:S(2)}, u32[]{:S(2)}) collective-permute-start(bf16[368,512]{1,0:T(8,128)(2,1)} %get-tuple-element.153), channel_id=1, source_target_pairs={{0,24},{8,16},{16,8},{24,0},{1,25},{9,17},{17,9},{25,1},{2,26},{10... | collective-permute-start | bytes 1130504 | tf_op jit(solution)/shard_map/ppermute | solution.py:584
  121.6 18.6 %collective-permute-start.14 = (bf16[368,512]{1,0:T(8,128)(2,1)S(1)}, bf16[368,512]{1,0:T(8,128)(2,1)S(1)}, u32[]{:S(2)}, u32[]{:S(2)}) collective-permute-start(bf16[368,512]{1,0:T(8,128)(2,1)S(1)} %get-tuple-element.155), channel_id=1, source_target_pairs={{0,8},{8,0},{16,24},{24,16},{1,9},{9,1},{17,25},{25,17},{2,10},{10... | collective-permute-start | bytes 1130504 | tf_op jit(solution)/shard_map/ppermute | solution.py:584
  123.0 19.5 %collective-permute-start.37 = (bf16[12,256,128]{2,1,0:T(8,128)(2,1)}, bf16[12,256,128]{2,1,0:T(8,128)(2,1)S(1)}, u32[]{:S(2)}, u32[]{:S(2)}) collective-permute-start(bf16[12,256,128]{2,1,0:T(8,128)(2,1)} %get-tuple-element.103), channel_id=1, source_target_pairs={{0,1},{1,0},{2,3},{3,2},{4,5},{5,4},{6,7},{7,6},{8,9},{9,8},{10,11... | collective-permute-start | bytes 2359304 | tf_op jit(solution)/shard_map/ppermute | solution.py:584
  139.0 8.5 %collective-permute-start.27 = (bf16[13,256,128]{2,1,0:T(8,128)(2,1)}, bf16[13,256,128]{2,1,0:T(8,128)(2,1)S(1)}, u32[]{:S(2)}, u32[]{:S(2)}) collective-permute-start(bf16[13,256,128]{2,1,0:T(8,128)(2,1)} %get-tuple-element.100), channel_id=1, source_target_pairs={{0,1},{1,0},{2,3},{3,2},{4,5},{5,4},{6,7},{7,6},{8,9},{9,8},{10,11... | collective-permute-start | bytes 2555912 | tf_op jit(solution)/shard_map/ppermute | solution.py:584
  139.0 5.5 %collective-permute-start.47 = (bf16[2,4,64,800]{3,2,1,0:T(8,128)(2,1)}, bf16[2,4,64,800]{3,2,1,0:T(8,128)(2,1)S(1)}, u32[]{:S(2)}, u32[]{:S(2)}) collective-permute-start(bf16[2,4,64,800]{3,2,1,0:T(8,128)(2,1)} %get-tuple-element.108), channel_id=1, source_target_pairs={{0,1},{1,0},{2,3},{3,2},{4,5},{5,4},{6,7},{7,6},{8,9},{9,8},{10,11... | collective-permute-start | bytes 2457608 | tf_op jit(solution)/shard_map/ppermute | solution.py:584
  141.8 10.5 %collective-permute-start.18 = (bf16[12,128,128]{2,1,0:T(8,128)(2,1)S(1)}, bf16[12,128,128]{2,1,0:T(8,128)(2,1)S(1)}, u32[]{:S(2)}, u32[]{:S(2)}) collective-permute-start(bf16[12,128,128]{2,1,0:T(8,128)(2,1)S(1)} %constant_dynamic-slice_fusion.13), channel_id=1, source_target_pairs={{0,8},{8,0},{16,24},{24,16},{1,9},{9,1},{17,25},{25,17},{2,10},{10... | collective-permute-start | bytes 1179656 | tf_op jit(solution)/shard_map/ppermute | solution.py:584
  142.9 11.0 %collective-permute-start.38 = (bf16[12,128,128]{2,1,0:T(8,128)(2,1)S(1)}, bf16[12,128,128]{2,1,0:T(8,128)(2,1)S(1)}, u32[]{:S(2)}, u32[]{:S(2)}) collective-permute-start(bf16[12,128,128]{2,1,0:T(8,128)(2,1)S(1)} %constant_dynamic-slice_fusion.5), channel_id=1, source_target_pairs={{0,16},{8,24},{16,0},{24,8},{1,17},{9,25},{17,1},{25,9},{2,18},{10... | collective-permute-start | bytes 1179656 | tf_op jit(solution)/shard_map/ppermute | solution.py:584
  144.8 72.1 %collective-permute-start.48 = (bf16[2,2,64,800]{3,2,1,0:T(8,128)(2,1)S(1)}, bf16[2,2,64,800]{3,2,1,0:T(8,128)(2,1)S(1)}, u32[]{:S(2)}, u32[]{:S(2)}) collective-permute-start(bf16[2,2,64,800]{3,2,1,0:T(8,128)(2,1)S(1)} %constant_dynamic-slice_fusion.1), channel_id=1, source_target_pairs={{0,4},{1,5},{2,6},{3,7},{4,0},{5,1},{6,2},{7,3},{8,12},{9,13},{10,... | collective-permute-start | bytes 1228808 | tf_op jit(solution)/shard_map/ppermute | solution.py:584
  147.8 32.5 %collective-permute-start.28 = (bf16[13,128,128]{2,1,0:T(8,128)(2,1)S(1)}, bf16[13,128,128]{2,1,0:T(8,128)(2,1)S(1)}, u32[]{:S(2)}, u32[]{:S(2)}) collective-permute-start(bf16[13,128,128]{2,1,0:T(8,128)(2,1)S(1)} %constant_dynamic-slice_fusion.9), channel_id=1, source_target_pairs={{0,2},{1,3},{2,0},{3,1},{4,6},{5,7},{6,4},{7,5},{8,10},{9,11},{10,... | collective-permute-start | bytes 1277960 | tf_op jit(solution)/shard_map/ppermute | solution.py:584
  152.4 5.7 %collective-permute-start.19 = (bf16[12,64,128]{2,1,0:T(8,128)(2,1)S(1)}, bf16[12,64,128]{2,1,0:T(8,128)(2,1)S(1)}, u32[]{:S(2)}, u32[]{:S(2)}) collective-permute-start(bf16[12,64,128]{2,1,0:T(8,128)(2,1)S(1)} %constant_dynamic-slice_fusion.12), channel_id=1, source_target_pairs={{0,16},{8,24},{16,0},{24,8},{1,17},{9,25},{17,1},{25,9},{2,18},{10... | collective-permute-start | bytes 589832 | tf_op jit(solution)/shard_map/ppermute | solution.py:584
  154.1 18.3 %collective-permute-start.39 = (bf16[12,64,128]{2,1,0:T(8,128)(2,1)S(1)}, bf16[12,64,128]{2,1,0:T(8,128)(2,1)S(1)}, u32[]{:S(2)}, u32[]{:S(2)}) collective-permute-start(bf16[12,64,128]{2,1,0:T(8,128)(2,1)S(1)} %constant_dynamic-slice_fusion.4), channel_id=1, source_target_pairs={{0,2},{1,3},{2,0},{3,1},{4,6},{5,7},{6,4},{7,5},{8,10},{9,11},{10,... | collective-permute-start | bytes 589832 | tf_op jit(solution)/shard_map/ppermute | solution.py:584
  158.3 15.3 %collective-permute-start.20 = (bf16[12,32,128]{2,1,0:T(8,128)(2,1)S(1)}, bf16[12,32,128]{2,1,0:T(8,128)(2,1)S(1)}, u32[]{:S(2)}, u32[]{:S(2)}) collective-permute-start(bf16[12,32,128]{2,1,0:T(8,128)(2,1)S(1)} %constant_dynamic-slice_fusion.11), channel_id=1, source_target_pairs={{0,2},{1,3},{2,0},{3,1},{4,6},{5,7},{6,4},{7,5},{8,10},{9,11},{10,... | collective-permute-start | bytes 294920 | tf_op jit(solution)/shard_map/ppermute | solution.py:584
  172.5 4.7 %collective-permute-start.40 = (bf16[12,32,128]{2,1,0:T(8,128)(2,1)S(1)}, bf16[12,32,128]{2,1,0:T(8,128)(2,1)S(1)}, u32[]{:S(2)}, u32[]{:S(2)}) collective-permute-start(bf16[12,32,128]{2,1,0:T(8,128)(2,1)S(1)} %constant_dynamic-slice_fusion.3), channel_id=1, source_target_pairs={{0,8},{8,0},{16,24},{24,16},{1,9},{9,1},{17,25},{25,17},{2,10},{10... | collective-permute-start | bytes 294920 | tf_op jit(solution)/shard_map/ppermute | solution.py:584
  173.6 6.3 %collective-permute-start.21 = (bf16[12,16,128]{2,1,0:T(8,128)(2,1)S(1)}, bf16[12,16,128]{2,1,0:T(8,128)(2,1)S(1)}, u32[]{:S(2)}, u32[]{:S(2)}) collective-permute-start(bf16[12,16,128]{2,1,0:T(8,128)(2,1)S(1)} %constant_dynamic-slice_fusion.10), channel_id=1, source_target_pairs={{0,4},{1,5},{2,6},{3,7},{4,0},{5,1},{6,2},{7,3},{8,12},{9,13},{10,... | collective-permute-start | bytes 147464 | tf_op jit(solution)/shard_map/ppermute | solution.py:584
  177.2 5.1 %collective-permute-start.41 = (bf16[12,16,128]{2,1,0:T(8,128)(2,1)S(1)}, bf16[12,16,128]{2,1,0:T(8,128)(2,1)S(1)}, u32[]{:S(2)}, u32[]{:S(2)}) collective-permute-start(bf16[12,16,128]{2,1,0:T(8,128)(2,1)S(1)} %constant_dynamic-slice_fusion.2), channel_id=1, source_target_pairs={{0,4},{1,5},{2,6},{3,7},{4,0},{5,1},{6,2},{7,3},{8,12},{9,13},{10,... | collective-permute-start | bytes 147464 | tf_op jit(solution)/shard_map/ppermute | solution.py:584
  179.9 7.8 %collective-permute-start.22 = (bf16[12,16,128]{2,1,0:T(8,128)(2,1)S(1)}, bf16[12,16,128]{2,1,0:T(8,128)(2,1)S(1)}, u32[]{:S(2)}, u32[]{:S(2)}) collective-permute-start(bf16[12,16,128]{2,1,0:T(8,128)(2,1)S(1)} %add_convert_fusion.17), channel_id=1, source_target_pairs={{0,4},{1,5},{2,6},{3,7},{4,0},{5,1},{6,2},{7,3},{8,12},{9,13},{10,... | collective-permute-start | bytes 147464 | tf_op jit(solution)/shard_map/ppermute | solution.py:584
  180.5 5.9 %collective-permute-start.29 = (bf16[13,64,128]{2,1,0:T(8,128)(2,1)S(1)}, bf16[13,64,128]{2,1,0:T(8,128)(2,1)S(1)}, u32[]{:S(2)}, u32[]{:S(2)}) collective-permute-start(bf16[13,64,128]{2,1,0:T(8,128)(2,1)S(1)} %constant_dynamic-slice_fusion.8), channel_id=1, source_target_pairs={{0,8},{8,0},{16,24},{24,16},{1,9},{9,1},{17,25},{25,17},{2,10},{10... | collective-permute-start | bytes 638984 | tf_op jit(solution)/shard_map/ppermute | solution.py:584
  182.3 11.7 %collective-permute-start.42 = (bf16[12,16,128]{2,1,0:T(8,128)(2,1)S(1)}, bf16[12,16,128]{2,1,0:T(8,128)(2,1)S(1)}, u32[]{:S(2)}, u32[]{:S(2)}) collective-permute-start(bf16[12,16,128]{2,1,0:T(8,128)(2,1)S(1)} %add_convert_fusion.16), channel_id=1, source_target_pairs={{0,4},{1,5},{2,6},{3,7},{4,0},{5,1},{6,2},{7,3},{8,12},{9,13},{10,... | collective-permute-start | bytes 147464 | tf_op jit(solution)/shard_map/ppermute | solution.py:584
  186.5 4.8 %collective-permute-start.30 = (bf16[13,32,128]{2,1,0:T(8,128)(2,1)S(1)}, bf16[13,32,128]{2,1,0:T(8,128)(2,1)S(1)}, u32[]{:S(2)}, u32[]{:S(2)}) collective-permute-start(bf16[13,32,128]{2,1,0:T(8,128)(2,1)S(1)} %constant_dynamic-slice_fusion.7), channel_id=1, source_target_pairs={{0,16},{8,24},{16,0},{24,8},{1,17},{9,25},{17,1},{25,9},{2,18},{10... | collective-permute-start | bytes 319496 | tf_op jit(solution)/shard_map/ppermute | solution.py:584
  187.7 11.5 %collective-permute-start.23 = (bf16[12,32,128]{2,1,0:T(8,128)(2,1)S(1)}, bf16[12,32,128]{2,1,0:T(8,128)(2,1)S(1)}, u32[]{:S(2)}, u32[]{:S(2)}) collective-permute-start(bf16[12,32,128]{2,1,0:T(8,128)(2,1)S(1)} %maximum_select_fusion.10), channel_id=1, source_target_pairs={{0,2},{1,3},{2,0},{3,1},{4,6},{5,7},{6,4},{7,5},{8,10},{9,11},{10,... | collective-permute-start | bytes 294920 | tf_op jit(solution)/shard_map/ppermute | solution.py:584
  191.3 5.1 %collective-permute-start.31 = (bf16[13,16,128]{2,1,0:T(8,128)(2,1)S(1)}, bf16[13,16,128]{2,1,0:T(8,128)(2,1)S(1)}, u32[]{:S(2)}, u32[]{:S(2)}) collective-permute-start(bf16[13,16,128]{2,1,0:T(8,128)(2,1)S(1)} %constant_dynamic-slice_fusion.6), channel_id=1, source_target_pairs={{0,4},{1,5},{2,6},{3,7},{4,0},{5,1},{6,2},{7,3},{8,12},{9,13},{10,... | collective-permute-start | bytes 159752 | tf_op jit(solution)/shard_map/ppermute | solution.py:584
  194.0 9.0 %collective-permute-start.43 = (bf16[12,32,128]{2,1,0:T(8,128)(2,1)S(1)}, bf16[12,32,128]{2,1,0:T(8,128)(2,1)S(1)}, u32[]{:S(2)}, u32[]{:S(2)}) collective-permute-start(bf16[12,32,128]{2,1,0:T(8,128)(2,1)S(1)} %maximum_select_fusion.11), channel_id=1, source_target_pairs={{0,8},{8,0},{16,24},{24,16},{1,9},{9,1},{17,25},{25,17},{2,10},{10... | collective-permute-start | bytes 294920 | tf_op jit(solution)/shard_map/ppermute | solution.py:584
  196.5 5.1 %collective-permute-start.32 = (bf16[13,16,128]{2,1,0:T(8,128)(2,1)S(1)}, bf16[13,16,128]{2,1,0:T(8,128)(2,1)S(1)}, u32[]{:S(2)}, u32[]{:S(2)}) collective-permute-start(bf16[13,16,128]{2,1,0:T(8,128)(2,1)S(1)} %add_convert_fusion.15), channel_id=1, source_target_pairs={{0,4},{1,5},{2,6},{3,7},{4,0},{5,1},{6,2},{7,3},{8,12},{9,13},{10,... | collective-permute-start | bytes 159752 | tf_op jit(solution)/shard_map/ppermute | solution.py:584
  199.3 11.9 %collective-permute-start.24 = (bf16[12,64,128]{2,1,0:T(8,128)(2,1)S(1)}, bf16[12,64,128]{2,1,0:T(8,128)(2,1)S(1)}, u32[]{:S(2)}, u32[]{:S(2)}) collective-permute-start(bf16[12,64,128]{2,1,0:T(8,128)(2,1)S(1)} %maximum_select_fusion.7), channel_id=1, source_target_pairs={{0,16},{8,24},{16,0},{24,8},{1,17},{9,25},{17,1},{25,9},{2,18},{10... | collective-permute-start | bytes 589832 | tf_op jit(solution)/shard_map/ppermute | solution.py:584
  201.6 7.6 %collective-permute-start.33 = (bf16[13,32,128]{2,1,0:T(8,128)(2,1)S(1)}, bf16[13,32,128]{2,1,0:T(8,128)(2,1)S(1)}, u32[]{:S(2)}, u32[]{:S(2)}) collective-permute-start(bf16[13,32,128]{2,1,0:T(8,128)(2,1)S(1)} %maximum_select_fusion.9), channel_id=1, source_target_pairs={{0,16},{8,24},{16,0},{24,8},{1,17},{9,25},{17,1},{25,9},{2,18},{10... | collective-permute-start | bytes 319496 | tf_op jit(solution)/shard_map/ppermute | solution.py:584
  203.0 8.5 %collective-permute-start.44 = (bf16[12,64,128]{2,1,0:T(8,128)(2,1)S(1)}, bf16[12,64,128]{2,1,0:T(8,128)(2,1)S(1)}, u32[]{:S(2)}, u32[]{:S(2)}) collective-permute-start(bf16[12,64,128]{2,1,0:T(8,128)(2,1)S(1)} %maximum_select_fusion.8), channel_id=1, source_target_pairs={{0,2},{1,3},{2,0},{3,1},{4,6},{5,7},{6,4},{7,5},{8,10},{9,11},{10,... | collective-permute-start | bytes 589832 | tf_op jit(solution)/shard_map/ppermute | solution.py:584
  209.3 5.9 %collective-permute-start.34 = (bf16[13,64,128]{2,1,0:T(8,128)(2,1)S(1)}, bf16[13,64,128]{2,1,0:T(8,128)(2,1)S(1)}, u32[]{:S(2)}, u32[]{:S(2)}) collective-permute-start(bf16[13,64,128]{2,1,0:T(8,128)(2,1)S(1)} %maximum_select_fusion.6), channel_id=1, source_target_pairs={{0,8},{8,0},{16,24},{24,16},{1,9},{9,1},{17,25},{25,17},{2,10},{10... | collective-permute-start | bytes 638984 | tf_op jit(solution)/shard_map/ppermute | solution.py:584
  211.3 8.1 %collective-permute-start.25 = (bf16[12,128,128]{2,1,0:T(8,128)(2,1)S(1)}, bf16[12,128,128]{2,1,0:T(8,128)(2,1)S(1)}, u32[]{:S(2)}, u32[]{:S(2)}) collective-permute-start(bf16[12,128,128]{2,1,0:T(8,128)(2,1)S(1)} %maximum_select_fusion.4), channel_id=1, source_target_pairs={{0,8},{8,0},{16,24},{24,16},{1,9},{9,1},{17,25},{25,17},{2,10},{10... | collective-permute-start | bytes 1179656 | tf_op jit(solution)/shard_map/ppermute | solution.py:584
  211.7 8.1 %collective-permute-start.45 = (bf16[12,128,128]{2,1,0:T(8,128)(2,1)S(1)}, bf16[12,128,128]{2,1,0:T(8,128)(2,1)S(1)}, u32[]{:S(2)}, u32[]{:S(2)}) collective-permute-start(bf16[12,128,128]{2,1,0:T(8,128)(2,1)S(1)} %maximum_select_fusion.5), channel_id=1, source_target_pairs={{0,16},{8,24},{16,0},{24,8},{1,17},{9,25},{17,1},{25,9},{2,18},{10... | collective-permute-start | bytes 1179656 | tf_op jit(solution)/shard_map/ppermute | solution.py:584
  215.3 8.2 %collective-permute-start.35 = (bf16[13,128,128]{2,1,0:T(8,128)(2,1)S(1)}, bf16[13,128,128]{2,1,0:T(8,128)(2,1)S(1)}, u32[]{:S(2)}, u32[]{:S(2)}) collective-permute-start(bf16[13,128,128]{2,1,0:T(8,128)(2,1)S(1)} %maximum_select_fusion.3), channel_id=1, source_target_pairs={{0,2},{1,3},{2,0},{3,1},{4,6},{5,7},{6,4},{7,5},{8,10},{9,11},{10,... | collective-permute-start | bytes 1277960 | tf_op jit(solution)/shard_map/ppermute | solution.py:584
  219.6 4.1 %copy-start.4 = (bf16[12,256,128]{2,1,0:T(8,128)(2,1)}, bf16[12,256,128]{2,1,0:T(8,128)(2,1)S(1)}, u32[]{:S(2)}) copy-start(bf16[12,256,128]{2,1,0:T(8,128)(2,1)S(1)} %maximum_select_fusion.1.own1) | copy-start | bytes 2359300
  219.6 17.5 %collective-permute-start.26 = (bf16[12,256,128]{2,1,0:T(8,128)(2,1)S(1)}, bf16[12,256,128]{2,1,0:T(8,128)(2,1)}, u32[]{:S(2)}, u32[]{:S(2)}) collective-permute-start(bf16[12,256,128]{2,1,0:T(8,128)(2,1)S(1)} %maximum_select_fusion.1.own1), channel_id=1, source_target_pairs={{0,1},{1,0},{2,3},{3,2},{4,5},{5,4},{6,7},{7,6},{8,9},{9,8},{10,11... | collective-permute-start | bytes 2359304 | tf_op jit(solution)/shard_map/ppermute | solution.py:584
  220.0 5.6 %copy-start.3 = (bf16[12,256,128]{2,1,0:T(8,128)(2,1)}, bf16[12,256,128]{2,1,0:T(8,128)(2,1)S(1)}, u32[]{:S(2)}) copy-start(bf16[12,256,128]{2,1,0:T(8,128)(2,1)S(1)} %maximum_select_fusion.2.own) | copy-start | bytes 2359300
  220.0 12.8 %collective-permute-start.46 = (bf16[12,256,128]{2,1,0:T(8,128)(2,1)S(1)}, bf16[12,256,128]{2,1,0:T(8,128)(2,1)S(1)}, u32[]{:S(2)}, u32[]{:S(2)}) collective-permute-start(bf16[12,256,128]{2,1,0:T(8,128)(2,1)S(1)} %maximum_select_fusion.2.own), channel_id=1, source_target_pairs={{0,1},{1,0},{2,3},{3,2},{4,5},{5,4},{6,7},{7,6},{8,9},{9,8},{10,11... | collective-permute-start | bytes 2359304 | tf_op jit(solution)/shard_map/ppermute | solution.py:584
  223.8 13.4 %collective-permute-start.36 = (bf16[13,256,128]{2,1,0:T(8,128)(2,1)S(1)}, bf16[13,256,128]{2,1,0:T(8,128)(2,1)S(1)}, u32[]{:S(2)}, u32[]{:S(2)}) collective-permute-start(bf16[13,256,128]{2,1,0:T(8,128)(2,1)S(1)} %maximum_select_fusion.own3), channel_id=1, source_target_pairs={{0,1},{1,0},{2,3},{3,2},{4,5},{5,4},{6,7},{7,6},{8,9},{9,8},{10,11... | collective-permute-start | bytes 2555912 | tf_op jit(solution)/shard_map/ppermute | solution.py:584
  223.9 8.1 %collective-permute-start.49 = (bf16[2,1,64,800]{3,2,1,0:T(8,128)(2,1)S(1)}, bf16[2,1,64,800]{3,2,1,0:T(8,128)(2,1)S(1)}, u32[]{:S(2)}, u32[]{:S(2)}) collective-permute-start(bf16[2,1,64,800]{3,2,1,0:T(8,128)(2,1)S(1)} %constant_dynamic-slice_fusion), channel_id=1, source_target_pairs={{0,2},{1,3},{2,0},{3,1},{4,6},{5,7},{6,4},{7,5},{8,10},{9,11},{10,... | collective-permute-start | bytes 614408 | tf_op jit(solution)/shard_map/ppermute | solution.py:584
  (15 other events, 19.6 us)
where the time goes:
time: 251 us; the launch traced here: 250 us
  waiting for transfers between devices  90.7 us (36%)
  Pallas kernels  66 us (26%)
  starting transfers between devices  60.1 us (24%)
  local copies, waits for them, and re-layouts  25.9 us (10%)
  other arithmetic  5.87 us (2%)
    ppermute x50, waiting for transfers between devices, swap(): return lax.ppermute(value, axis, [(i, i ^ bit) for i in range(size)])  90.7 us
    pallas_call x8, Pallas kernels, call(): pl.pallas_call(kernel, out_shape=[jax.ShapeDtypeStruct(*o) for o in outs]...  66 us
    ppermute x50, starting transfers between devices, swap(): return lax.ppermute(value, axis, [(i, i ^ bit) for i in range(size)])  60.1 us
    unnamed x69, local copies, waits for them, and re-layouts  11.8 us
  transfers between devices with their start and end apart: 50, of which 22 were waited for; matrix products, arithmetic and copies ran while one was open for 7% of the time, Pallas kernels for 21%

commit v1 on v0

v1 whole, which is shorter than its diff:
```python
import functools

import jax
import jax.numpy as jnp
import numpy as np
from jax import lax
from jax.experimental import pallas as pl
from jax.experimental.pallas import tpu as pltpu
from jax.sharding import PartitionSpec as P

BF = jnp.bfloat16
F32 = jnp.float32
HEADS = 8
LANES = 128
GROUPS = 4
FAR = -1e30


def dims(left, right, a, b):
    return lax.dot_general(left, right, (((a,), (b,)), ((), ())), preferred_element_type=F32)


def nn(left, right):
    return dims(left, right, 1, 0)


def nt(left, right):
    return dims(left, right, 1, 1)


def tn(left, right):
    return dims(left, right, 0, 0)


def lane_masks(dtype=BF):
    lane = lax.broadcasted_iota(jnp.int32, (1, LANES), 1)
    low = (lane < LANES // 2).astype(F32)
    return low.astype(dtype), (1.0 - low).astype(dtype)


def pair(value, group):
    part = value[:, group * LANES : (group + 1) * LANES]
    low, high = lane_masks()
    return jnp.concatenate([part * low, part * high], axis=0)


def unpair(value):
    rows = value.shape[0] // 2
    lane = lax.broadcasted_iota(jnp.int32, (rows, LANES), 1)
    return jnp.where(lane < LANES // 2, value[:rows], value[rows:])


def eights(value, op):
    return op(value.reshape(value.shape[0] // 8, 8, value.shape[1]), axis=0)


def norm(value):
    center = value - jnp.mean(value, -1, keepdims=True)
    rstd = lax.rsqrt(jnp.mean(center * center, -1, keepdims=True) + 1e-05)
    return center * rstd, rstd


def norm_back(xhat, rstd, gain, grad):
    scaled = grad * gain
    inner = jnp.mean(scaled, -1, keepdims=True) + xhat * jnp.mean(
        scaled * xhat, -1, keepdims=True
    )
    return (
        rstd * (scaled - inner),
        jnp.sum(grad * xhat, 0, keepdims=True),
        jnp.sum(grad, 0, keepdims=True),
    )


def column_sum(value):
    return jnp.sum(value.astype(F32), 0, keepdims=True)


def row(ref, index):
    return ref[index : index + 1, :].astype(F32)


def cdf(value):
    return 0.5 * (1.0 + lax.erf(value * np.float32(0.7071067811865476)))


def density(value):
    return jnp.exp(-0.5 * value * value) * np.float32(0.3989422804014327)


def put_halves(core, value, index, keep_ref, send_ref, scratch):
    half = value.shape[0] // 2
    scratch[...] = value
    mine = pl.multiple_of(core * half, half)
    other = pl.multiple_of((1 - core) * half, half)
    for block in range(value.shape[1] // LANES):
        lanes = slice(block * LANES, (block + 1) * LANES)
        keep_ref[index + block] = scratch[pl.ds(mine, half), lanes].astype(BF)
        send_ref[index + block] = scratch[pl.ds(other, half), lanes].astype(BF)


def start_kernel(
    ids, up, down, tokens, cots, misc, send0, send1, send2, send3, first, second, turned, sems, *, rows_used
):
    pb, core = ids[0], ids[1]
    cut = first.shape[0]
    for side, ref in enumerate((up, down)):

        @pl.when(core == side)
        def _():
            one = pltpu.make_async_copy(ref.at[pl.ds(0, cut)], first, sems.at[0])
            two = pltpu.make_async_copy(ref.at[pl.ds(cut, cut)], second, sems.at[1])
            one.start()
            two.start()
            one.wait()
            two.wait()

    rows, width2 = turned.shape
    width = width2 // 2
    block = rows // GROUPS
    count = tokens.shape[0]
    place = lax.broadcasted_iota(jnp.int32, (rows, count), 0)
    query = lax.broadcasted_iota(jnp.int32, (rows, count), 1)
    hit = query == lax.rem(place, block) * GROUPS + lax.div(place, block)
    used = lax.rem(place, block) < rows_used
    chosen = jnp.where(jnp.logical_and(hit, used), 1.0, 0.0).astype(BF)
    turned[:, :width] = nn(chosen, tokens[...])
    turned[:, width:] = nn(chosen, cots[...])
    for b in range(GROUPS):
        at = b * block + rows_used
        turned[at : at + 2, :width] = misc[2:4, :].astype(F32)
    for k, ref in enumerate((send0, send1, send2, send3)):
        at = pl.multiple_of((pb ^ k) * block, block)
        ref[...] = turned[pl.ds(at, block), :].astype(BF)


def memory_kernel(
    ids, feats, sines, cosines, waves, in_proj, misc, cross_proj, cross_bias, featp, ki, vi, k, v, buf, sems
):
    blocks = GROUPS
    slots = buf.shape[0]
    part = slots // blocks
    padded = featp.shape[0] // blocks
    copy = pltpu.make_async_copy(feats.at[ids[0]], buf, sems)
    copy.start()
    for j in range(blocks):
        featp[(j + 1) * padded - 16 : (j + 1) * padded] = jnp.zeros((16, featp.shape[1]), BF)
    copy.wait()
    bias = row(misc, 0)
    for j in range(blocks):
        here = slice(j * padded, (j + 1) * padded)
        featp[j * padded : j * padded + part] = buf[j * part : (j + 1) * part]
        memory = nn(featp[here], in_proj[...]) + bias
        places = cosines[...] * row(waves, j) + sines[...] * row(waves, blocks + j)
        key_input = (memory + places).astype(BF)
        value_input = memory.astype(BF)
        ki[here] = key_input
        vi[here] = value_input
        k[here] = nn(key_input, cross_proj[1]).astype(BF)
        v[here] = (nn(value_input, cross_proj[2]) + row(cross_bias, 1)).astype(BF)


def forward_kernel(
    ids,
    own,
    got1,
    got2,
    got3,
    query_pos,
    self_proj,
    self_out,
    self_bias,
    cross_proj,
    cross_out,
    cross_bias,
    gains,
    shifts,
    k_ref,
    v_ref,
    up_,
    down_,
    x_out,
    cot_out,
    ai_out,
    sq_out,
    sk_out,
    sv_out,
    ps_out,
    sm_out,
    xhat1_out,
    rstd1_out,
    ci_out,
    cq_out,
    pc_out,
    cm_out,
    h2_out,
    xhat2_out,
    rstd2_out,
    bups_out,
    scores,
    pos_ref,
    *,
    rows_used,
    mask_at,
):
    pb = ids[0]
    width = pos_ref.shape[1]
    block = own.shape[0]
    for k, ref in enumerate((own, got1, got2, got3)):
        at = pl.multiple_of((pb ^ k) * block, block)
        x_out[pl.ds(at, block), :] = ref[:, :width]
        cot_out[pl.ds(at, block), :] = ref[:, width:]
        bups_out[2 * k : 2 * k + 2] = ref[rows_used : rows_used + 2, :width].astype(F32)
    rows = x_out.shape[0]
    pos_ref[...] = jnp.zeros(pos_ref.shape, F32)
    for b in range(GROUPS):
        pos_ref[b * block : b * block + rows_used] = query_pos[
            b * rows_used : (b + 1) * rows_used
        ].astype(F32)
    pos = pos_ref[...]
    x = x_out[...].astype(F32)
    ai = (x + pos).astype(BF)
    ai_out[...] = ai
    sq_out[...] = ((nn(ai, self_proj[0]) + row(self_bias, 0)) * 0.125).astype(BF)
    sk_out[...] = nn(ai, self_proj[1]).astype(BF)
    sv_out[...] = (nn(x_out[...], self_proj[2]) + row(self_bias, 1)).astype(BF)
    key_row = lax.broadcasted_iota(jnp.int32, (rows, 2 * rows), 0)
    spare = jnp.where(lax.rem(key_row, block) < rows_used, 0.0, FAR).astype(F32)
    for g in range(GROUPS):
        lanes = slice(g * LANES, (g + 1) * LANES)
        s = nt(sk_out[:, lanes], pair(sq_out[...], g)) + spare
        e = jnp.exp(s - jnp.max(s, 0, keepdims=True))
        p = (e * (1.0 / jnp.sum(e, 0, keepdims=True))).astype(BF)
        ps_out[g] = p
        sm_out[:, lanes] = unpair(tn(p, sv_out[:, lanes])).astype(BF)
    xhat, rstd = norm(x + nn(sm_out[...], self_out[...]) + row(self_bias, 2))
    xhat1_out[...] = xhat
    rstd1_out[...] = rstd
    h1 = xhat * row(gains, 0) + row(shifts, 0)
    ci = (h1 + pos).astype(BF)
    ci_out[...] = ci
    cq_out[...] = ((nn(ci, cross_proj[0]) + row(cross_bias, 0)) * 0.125).astype(BF)

    padded = k_ref.shape[0] // GROUPS
    used = rows_used * 12
    slot_row = lax.broadcasted_iota(jnp.int32, (padded, 2 * rows), 0)
    for g in range(GROUPS):
        lanes = slice(g * LANES, (g + 1) * LANES)
        queries = pair(cq_out[...], g)
        top = jnp.full((8, 2 * rows), FAR, F32)
        for j in range(GROUPS):
            here = slice(j * padded, (j + 1) * padded)
            live = jnp.where(ids[mask_at + pb * GROUPS + j] > 0, 0.0, -1000000000.0).astype(F32)
            s = nt(k_ref[here, lanes], queries) + jnp.where(slot_row < used, live, FAR)
            scores[here] = s
            top = jnp.maximum(top, eights(s, jnp.max))
        top = jnp.max(top, 0, keepdims=True)
        total = jnp.zeros((8, 2 * rows), F32)
        for j in range(GROUPS):
            here = slice(j * padded, (j + 1) * padded)
            e = jnp.exp(scores[here] - top)
            scores[here] = e
            total = total + eights(e, jnp.sum)
        inverse = 1.0 / jnp.sum(total, 0, keepdims=True)
        for j in range(GROUPS):
            here = slice(j * padded, (j + 1) * padded)
            pc_out[g, here] = (scores[here] * inverse).astype(BF)
        cm_out[:, lanes] = unpair(tn(pc_out[g], v_ref[:, lanes])).astype(BF)
    xhat, rstd = norm(h1 + nn(cm_out[...], cross_out[...]) + row(cross_bias, 2))
    xhat2_out[...] = xhat
    rstd2_out[...] = rstd
    h2_out[...] = xhat * row(gains, 1) + row(shifts, 1)


def ffn_kernel(
    ids,
    h2_ref,
    cot_ref,
    xhat2_ref,
    rstd2_ref,
    bups,
    up_own,
    down_own,
    misc,
    gains,
    shifts,
    fx0,
    fx1,
    fy0,
    fy1,
    fd0,
    fd1,
    sx0,
    sx1,
    sy0,
    sy1,
    sd0,
    sd1,
    res_out,
    ops_out,
    g2_out,
    small_out,
    bup_out,
    weights,
    pre_ref,
    sems,
):
    core = ids[1]
    width = h2_ref.shape[1]
    units = up_own.shape[0]
    cut = units // 2
    copies = []
    for side, refs in enumerate(((fx0, fx1, fy0, fy1, fd0, fd1), (sx0, sx1, sy0, sy1, sd0, sd1))):
        to = core if side == 0 else 1 - core
        copies.append(
            [
                pltpu.make_async_copy(
                    ref, weights.at[to, n // 2, pl.ds(n % 2 * cut, cut)], sems.at[side, n]
                )
                for n, ref in enumerate(refs)
            ]
        )
    for one in copies:
        for copy in one:
            copy.start()
    h2 = h2_ref[...]
    h2b = h2.astype(BF)
    ops_out[:, :width] = h2b
    down = jnp.zeros(h2.shape, F32)
    for p in range(4):
        if p > 0:
            for one in copies:
                one[2 * p - 2].wait()
                one[2 * p - 1].wait()
        up = up_own[...] if p == 0 else weights[0, p - 1]
        dn = down_own[...] if p == 0 else weights[1, p - 1]
        bias = jnp.concatenate(
            [bups[2 * p : 2 * p + 1], bups[2 * p + 1 : 2 * p + 2, : units - width]], axis=1
        )
        pre = nt(h2b, up) + bias
        pre_ref[p] = pre
        down = down + nn((pre * cdf(pre)).astype(BF), dn)
    xhat, rstd = norm(h2 + down + row(misc, 1))
    res_out[...] = (xhat * row(gains, 2) + row(shifts, 2)).astype(BF)
    g3, dgain3, dshift3 = norm_back(xhat, rstd, row(gains, 2), cot_ref[...].astype(F32))
    gb = g3.astype(BF)
    ops_out[:, width:] = gb
    gh = g3
    for p in range(4):
        up = up_own[...] if p == 0 else weights[0, p - 1]
        dn = down_own[...] if p == 0 else weights[1, p - 1]
        ga = nt(gb, dn).astype(BF).astype(F32)
        pre = pre_ref[p]
        gp = (ga * (cdf(pre) + pre * density(pre))).astype(BF)
        total = column_sum(gp)
        bup_out[p] = jnp.concatenate(
            [total, jnp.zeros((1, 2 * width - units), F32)], axis=1
        )
        gh = gh + nn(gp, up)
    g2, dgain2, dshift2 = norm_back(xhat2_ref[...], rstd2_ref[...], row(gains, 1), gh)
    g2_out[...] = g2
    small_out[0:1] = dgain3
    small_out[1:2] = dshift3
    small_out[2:3] = dgain2
    small_out[3:4] = dshift2
    small_out[4:5] = column_sum(gb)
    small_out[5:6] = column_sum(g2.astype(BF))
    small_out[6:8] = jnp.zeros((2, width), F32)


def backward_kernel(
    ids,
    g2_ref,
    pc_ref,
    k_ref,
    v_ref,
    cq_ref,
    ci_ref,
    cm_ref,
    xhat1_ref,
    rstd1_ref,
    x_ref,
    ai_ref,
    sq_ref,
    sk_ref,
    sv_ref,
    ps_ref,
    sm_ref,
    self_proj,
    self_out,
    cross_proj,
    cross_out,
    gains,
    ds_out,
    gcm_out,
    gx_out,
    gpos_out,
    small_out,
    keep,
    send,
    dp_ref,
    work,
    gq_ref,
    gk_ref,
    gv_ref,
):
    core = ids[1]
    width = x_ref.shape[1]
    rows = x_ref.shape[0]
    g2 = g2_ref[...]
    branch = g2.astype(BF)
    gcm_out[...] = nt(branch, cross_out[...]).astype(BF)
    padded = k_ref.shape[0] // GROUPS
    for g in range(GROUPS):
        lanes = slice(g * LANES, (g + 1) * LANES)
        grads = pair(gcm_out[...], g)
        total = jnp.zeros((8, 2 * rows), F32)
        for j in range(GROUPS):
            here = slice(j * padded, (j + 1) * padded)
            dp = nt(v_ref[here, lanes], grads).astype(BF)
            dp_ref[here] = dp
            total = total + eights(pc_ref[g, here].astype(F32) * dp.astype(F32), jnp.sum)
        total = jnp.sum(total, 0, keepdims=True)
        for j in range(GROUPS):
            here = slice(j * padded, (j + 1) * padded)
            ds_out[g, here] = (
                pc_ref[g, here].astype(F32) * (dp_ref[here].astype(F32) - total)
            ).astype(BF)
        gq_ref[:, lanes] = unpair(tn(ds_out[g], k_ref[:, lanes])).astype(BF) * 0.125
    gcq = gq_ref[...]
    gci = nt(gcq, cross_proj[0])
    small_out[0:1] = column_sum(gcq)
    put_halves(core, tn(ci_ref[...], gcq), 0, keep, send, work)
    put_halves(core, tn(cm_ref[...], branch), 8, keep, send, work)
    g1, dgain1, dshift1 = norm_back(xhat1_ref[...], rstd1_ref[...], row(gains, 0), g2 + gci)
    small_out[1:2] = dgain1
    small_out[2:3] = dshift1
    sbranch = g1.astype(BF)
    small_out[3:4] = column_sum(sbranch)
    put_halves(core, tn(sm_ref[...], sbranch), 4, keep, send, work)
    gsm = nt(sbranch, self_out[...]).astype(BF)
    for g in range(GROUPS):
        lanes = slice(g * LANES, (g + 1) * LANES)
        grads = pair(gsm, g)
        p = ps_ref[g]
        dp = nt(sv_ref[:, lanes], grads).astype(BF).astype(F32)
        pf = p.astype(F32)
        ds = (pf * (dp - jnp.sum(pf * dp, 0, keepdims=True))).astype(BF)
        gq_ref[:, lanes] = unpair(tn(ds, sk_ref[:, lanes])).astype(BF) * 0.125
        gk_ref[:, lanes] = nn(ds, pair(sq_ref[...], g)).astype(BF)
        gv_ref[:, lanes] = nn(p, grads).astype(BF)
    gq, gk, gv = gq_ref[...], gk_ref[...], gv_ref[...]
    gai = nt(gq, self_proj[0]) + nt(gk, self_proj[1])
    gx_out[...] = (g1 + gai + nt(gv, self_proj[2])).astype(BF)
    gpos_out[...] = gai + gci
    small_out[4:5] = column_sum(gq)
    small_out[5:6] = column_sum(gv)
    small_out[6:8] = jnp.zeros((2, width), F32)
    put_halves(core, tn(ai_ref[...], gq), 12, keep, send, work)
    put_halves(core, tn(ai_ref[...], gk), 16, keep, send, work)
    put_halves(core, tn(x_ref[...], gv), 20, keep, send, work)


def ffn_grad_kernel(ids, own, got1, got2, got3, up_own, misc, down_own, keep, send, work):
    core = ids[1]
    units, width = up_own.shape
    ops = jnp.concatenate([ref[...] for ref in (own, got1, got2, got3)], axis=0)
    inputs, branch = ops[:, :width], ops[:, width:]
    bias = jnp.concatenate([row(misc, 2), row(misc, 3)[:, : units - width]], axis=1)
    pre = nt(inputs, up_own[...]) + bias
    phi = cdf(pre)
    act = (pre * phi).astype(BF)
    gact = nt(branch, down_own[...]).astype(BF).astype(F32)
    gpre = (gact * (phi + pre * density(pre))).astype(BF)
    blocks, size = keep.shape[1], keep.shape[2]
    for side, grad in enumerate((tn(inputs, gpre), tn(branch, act))):
        work[...] = grad
        for block in range(blocks):
            mine = pl.multiple_of((2 * block + core) * size, size)
            other = pl.multiple_of((2 * block + 1 - core) * size, size)
            keep[side, block] = work[pl.ds(mine, size), :].astype(BF)
            send[side, block] = work[pl.ds(other, size), :].astype(BF)


def ffn_fold_kernel(ids, keep, got, stay, go, *, bit):
    for side in range(keep.shape[0]):
        for block in range(stay.shape[1]):
            for ref, at in ((stay, 2 * block + ids[bit]), (go, 2 * block + 1 - ids[bit])):
                ref[side, block] = plus(keep[side, at], got[side, at])


def ffn_finish_kernel(ids, keep, got, up_grad, down_grad):
    for side, ref in enumerate((up_grad, down_grad)):
        ref[...] = keep[side, 0].astype(F32) + got[side, 0].astype(F32)


def memory_back_kernel(
    ids,
    ds_ref,
    pc_ref,
    cq_ref,
    gcm_ref,
    featp,
    ki,
    vi,
    cross_proj,
    in_proj,
    res_ref,
    gx_ref,
    gpos_ref,
    small_a,
    small_b,
    bup,
    rows0,
    rows1,
    rows2,
    rows3,
    keep,
    send,
    gk_ref,
    gv_ref,
    gm_ref,
    gf_ref,
    work,
    small,
    *,
    rows_used,
):
    pb, core = ids[0], ids[1]
    width = featp.shape[1]
    rows = res_ref.shape[0]
    block = rows // GROUPS
    padded = featp.shape[0] // GROUPS
    pairs_q = [pair(cq_ref[...], g) for g in range(GROUPS)]
    pairs_g = [pair(gcm_ref[...], g) for g in range(GROUPS)]
    for j in range(GROUPS):
        here = slice(j * padded, (j + 1) * padded)
        for g in range(GROUPS):
            lanes = slice(g * LANES, (g + 1) * LANES)
            gk_ref[here, lanes] = nn(ds_ref[g, here], pairs_q[g]).astype(BF)
            gv_ref[here, lanes] = nn(pc_ref[g, here], pairs_g[g]).astype(BF)
        gm = (nt(gk_ref[here], cross_proj[1]) + nt(gv_ref[here], cross_proj[2])).astype(BF)
        gm_ref[here] = gm
        gf_ref[j] = nt(gm, in_proj[...]).astype(BF)
    for k, ref in enumerate((rows0, rows1, rows2, rows3)):
        at = pl.multiple_of((pb ^ k) * block, block)
        ref[0:padded] = gf_ref[pb ^ k]
        ref[padded : padded + block] = gx_ref[pl.ds(at, block), :]
        ref[padded + block : padded + 2 * block] = res_ref[pl.ds(at, block), :]
    put_halves(core, tn(ki[...], gk_ref[...]), 0, keep, send, work)
    put_halves(core, tn(vi[...], gv_ref[...]), 4, keep, send, work)
    put_halves(core, tn(featp[...], gm_ref[...]), 8, keep, send, work)

    small[...] = gpos_ref[...]
    extras = [
        row(small_b, 1),
        row(small_a, 2),
        row(small_a, 0),
        row(small_b, 2),
        row(small_a, 3),
        row(small_a, 1),
        row(small_b, 4),
        row(small_b, 5),
        row(small_b, 3),
        row(small_b, 0),
        column_sum(gv_ref[...]),
        row(small_a, 5),
        row(small_a, 4),
        column_sum(gm_ref[...]),
    ]
    for index, value in enumerate(extras):
        at = spare_row(index, block, rows_used)
        small[at : at + 1] = value
    for b in range(GROUPS):
        at = b * block + rows_used + 5
        total = bup[b ^ pb]
        small[at : at + 1] = total[:, :width]
        small[at + 1 : at + 2] = total[:, width:]
    for b in range(2):
        for side, ref in ((core, keep), (1 - core, send)):
            low = small[:, b * LANES : (b + 1) * LANES]
            high = small[:, (2 + b) * LANES : (3 + b) * LANES]
            ref[12, b * rows : (b + 1) * rows] = jnp.where(side == 0, low, high).astype(BF)


def spare_row(index, block, rows_used):
    return index // 5 * block + rows_used + index % 5


def put_whole(core, out, index, own, got):
    half = own.shape[1]
    mine = pl.multiple_of(core * half, half)
    other = pl.multiple_of((1 - core) * half, half)
    for b in range(4):
        lanes = slice(b * LANES, (b + 1) * LANES)
        out[pl.ds(mine, half), lanes] = own[index + b].astype(F32)
        out[pl.ds(other, half), lanes] = got[index + b].astype(F32)


def finish_chain_kernel(ids, own1, got1, own2, got2, cross_q, self_out, cross_out, self_proj):
    core = ids[1]
    put_whole(core, cross_q, 0, own1, got1)
    put_whole(core, self_out, 4, own1, got1)
    put_whole(core, cross_out, 8, own1, got1)
    for m in range(3):
        put_whole(core, self_proj.at[m], 4 * m, own2, got2)


def finish_memory_kernel(
    ids, own, got, cross_q, cross_, in_, pos_, self_bias_, cross_bias_, bup_, bdown_, gain_, shift_, inb_, small, *, rows_used
):
    core = ids[1]
    cross_[0] = cross_q[...]
    put_whole(core, cross_.at[1], 0, own, got)
    put_whole(core, cross_.at[2], 4, own, got)
    put_whole(core, in_, 8, own, got)
    rows, width = small.shape
    block = rows // GROUPS
    for b in range(2):
        here = slice(b * rows, (b + 1) * rows)
        first = own[12, here].astype(F32)
        second = got[12, here].astype(F32)
        small[:, b * LANES : (b + 1) * LANES] = jnp.where(core == 0, first, second)
        small[:, (2 + b) * LANES : (3 + b) * LANES] = jnp.where(core == 0, second, first)
    for b in range(GROUPS):
        pos_[b * rows_used : (b + 1) * rows_used] = small[b * block : b * block + rows_used]
        at = b * block + rows_used + 5
        bup_[b : b + 1, :width] = small[at : at + 1]
        bup_[b : b + 1, width:] = small[at + 1 : at + 2]

    def spare(index):
        at = spare_row(index, block, rows_used)
        return small[at : at + 1]

    for ref, index in ((gain_, 0), (shift_, 3), (self_bias_, 6), (cross_bias_, 9)):
        for i in range(3):
            ref[i : i + 1] = spare(index + i)
    bdown_[...] = spare(12)
    inb_[...] = spare(13)


def order_kernel(ids, own, got1, got2, got3, out, grad, feats):
    pb = ids[0]
    part, used = feats.shape[1], out.shape[1]
    block = out.shape[1] // 16 * 16 + 16
    padded = own.shape[0] - 2 * block
    for k, ref in enumerate((own, got1, got2, got3)):
        feats[pb ^ k] = ref[0:part]
        grad[pb ^ k] = ref[padded : padded + used]
        out[pb ^ k] = ref[padded + block : padded + block + used]


class Far:
    def __init__(self, value, parts=None, emit=False):
        self.value, self.parts, self.emit = value, parts, emit


class Raw:
    def __init__(self, value):
        self.value = value


class Late:
    def __init__(self, ref, buffers, sems, parts):
        self.shape = ref.shape
        self.parts = parts
        self.buffers = buffers
        sources = [ref] if parts is None else [ref.at[part] for part in parts]
        self.copies = [
            pltpu.make_async_copy(source, buffer, sems.at[n])
            for n, (source, buffer) in enumerate(zip(sources, buffers))
        ]
        for copy in self.copies:
            copy.start()
        self.waiting = set(range(len(sources)))

    def ready(self, n):
        if n in self.waiting:
            self.waiting.discard(n)
            self.copies[n].wait()

    def __getitem__(self, index):
        if self.parts is None:
            self.ready(0)
            return self.buffers[0][index]
        n = self.parts.index(index)
        self.ready(n)
        return self.buffers[n][...]


def call(kernel, args, outs, scratch=(), limit=16, near=True):
    specs = [pl.BlockSpec(memory_space=pltpu.SMEM)]
    values, extra, emitted, plans = [args[0]], [], [], [None]
    outs = list(outs)
    for arg in args[1:]:
        if isinstance(arg, (Far, Raw)):
            value = arg.value
            specs.append(pl.BlockSpec(memory_space=pl.ANY))
            values.append(pltpu.with_memory_space_constraint(value, pltpu.HBM))
            if isinstance(arg, Raw):
                plans.append(None)
                continue
            count = 1 if arg.parts is None else len(arg.parts)
            if arg.emit:
                plans.append((None, len(emitted), len(extra), count, arg.parts))
                emitted.append((value.shape, value.dtype))
            else:
                plans.append((len(extra), None, len(extra) + count, count, arg.parts))
                shape = value.shape if arg.parts is None else value.shape[1:]
                extra += [pltpu.VMEM(shape, value.dtype)] * count
            extra.append(pltpu.SemaphoreType.DMA((count,)))
        else:
            specs.append(pl.BlockSpec(memory_space=pltpu.VMEM))
            values.append(pltpu.with_memory_space_constraint(arg, pltpu.VMEM))
            plans.append(None)

    def body(*refs):
        given, rest = list(refs[: len(args)]), refs[len(args) :]
        first, rest = rest[: len(outs)], rest[len(outs) :]
        copies, rest = rest[: len(emitted)], rest[len(emitted) :]
        own, late = rest[: len(scratch)], rest[len(scratch) :]
        waits = []
        for index, plan in enumerate(plans):
            if plan is None:
                continue
            at, place, sem, count, parts = plan
            if place is None:
                buffers = late[at : at + count]
            elif parts is None:
                buffers = [copies[place]]
            else:
                buffers = [copies[place].at[part] for part in parts]
            given[index] = Late(given[index], buffers, late[sem], parts)
            waits.append(given[index])
        kernel(*given, *first, *own)
        for one in waits:
            for n in sorted(one.waiting):
                one.ready(n)

    whole = [(o, near) for o in outs] + [(o, True) for o in emitted]
    return pl.pallas_call(
        body,
        out_shape=[pltpu.VMEM(*o) if here else jax.ShapeDtypeStruct(*o) for o, here in whole],
        in_specs=specs,
        out_specs=[pl.BlockSpec(memory_space=pltpu.VMEM)] * len(whole),
        scratch_shapes=list(scratch) + extra,
        compiler_params=pltpu.CompilerParams(vmem_limit_bytes=limit * 1024 * 1024),
        cost_estimate=pl.CostEstimate(flops=1, bytes_accessed=1, transcendentals=0),
    )(*values)


def swap(value, axis, bit):
    size = lax.axis_size(axis)
    return lax.ppermute(value, axis, [(i, i ^ bit) for i in range(size)])


def bit_of(axis, bit):
    return (lax.axis_index(axis) // bit) % 2


def plus(left, right):
    return (left.astype(F32) + right.astype(F32)).astype(BF)


def halve(keep, got, bit):
    half = keep.shape[1] // 2
    total = plus(keep, got)
    mine = lax.dynamic_slice_in_dim(total, bit * half, half, 1)
    other = lax.dynamic_slice_in_dim(total, (1 - bit) * half, half, 1)
    return mine, other


def fold(ids, groups):
    rows = groups[0][0][0][0].shape[1] // 2
    if rows % 16:
        result = []
        for pieces, bit in groups:
            done = [halve(keep[a:b], got[a:b], ids[bit]) for keep, got, a, b in pieces]
            result += [jnp.concatenate(side) for side in zip(*done)]
        return result
    args, outs = [], []
    for pieces, bit in groups:
        count = sum(b - a for _, _, a, b in pieces)
        outs += [((count, rows, LANES), BF)] * 2
        for keep, got, _, _ in pieces:
            args += [keep, got]

    def kernel(ids, *refs):
        given, made = list(refs[: len(args)]), list(refs[len(args) :])
        for pieces, bit in groups:
            stay, go = made.pop(0), made.pop(0)
            mine = pl.multiple_of(ids[bit] * rows, rows)
            other = pl.multiple_of((1 - ids[bit]) * rows, rows)
            at = 0
            for _, _, a, b in pieces:
                keep, got = given.pop(0), given.pop(0)
                for block in range(a, b):
                    for ref, start in ((stay, mine), (go, other)):
                        here = pl.ds(start, rows)
                        ref[at] = plus(keep[block, here], got[block, here])
                    at += 1

    return call(kernel, [ids, *args], outs, limit=4)


def add_up(ids, keep, got):
    if keep.shape[1] % 16:
        return plus(keep, got)

    def kernel(ids, keep, got, out):
        out[...] = plus(keep[...], got[...])

    return call(kernel, [ids, keep, got], [(keep.shape, BF)], limit=4)[0]


def join(ids, value, got, bit, cuts=None):
    blocks, rows, lanes = value.shape
    cuts = cuts or [(0, blocks)]
    if rows % 16:
        full = jnp.where(
            ids[bit] == 0, jnp.concatenate([value, got], 1), jnp.concatenate([got, value], 1)
        )
        return [full[a:b] for a, b in cuts]

    def kernel(ids, value, got, *outs):
        mine = pl.multiple_of(ids[bit] * rows, rows)
        other = pl.multiple_of((1 - ids[bit]) * rows, rows)
        for out, (a, b) in zip(outs, cuts):
            for block in range(a, b):
                out[block - a, pl.ds(mine, rows)] = value[block]
                out[block - a, pl.ds(other, rows)] = got[block]

    outs = [((b - a, 2 * rows, lanes), BF) for a, b in cuts]
    return call(kernel, [ids, value, got], outs, limit=4)


def on_device(
    tokens,
    query_pos,
    features,
    camera_mask,
    out_grad,
    self_proj,
    self_out,
    self_bias,
    cross_proj,
    cross_out,
    cross_bias,
    w_up,
    b_up,
    w_down,
    b_down,
    norm_gain,
    norm_bias,
    in_proj,
    in_bias,
):
    pb = lax.axis_index("pb")
    pb_size = lax.axis_size("pb")
    dp_size = lax.axis_size("dp")
    ways = [("dp", 1 << i) for i in range(1, dp_size.bit_length() - 1)]
    core_way, x_way, y_way = ("dp", 1), ("pb", 1), ("pb", 2)
    bits = [core_way, x_way, y_way] + ways
    ids = jnp.concatenate(
        [jnp.stack([pb] + [bit_of(*way) for way in bits]).astype(jnp.int32), camera_mask.reshape(-1)]
    )
    at_of = {way: 1 + n for n, way in enumerate(bits)}
    mask_at = 1 + len(bits)
    width = tokens.shape[2]
    used = tokens.shape[1]
    block = -(-used // 16) * 16
    rows = block * pb_size
    mem = features.shape[1]
    part = mem // pb_size
    padded = -(-part // 16) * 16
    slots = padded * pb_size
    units = b_up.shape[0]

    misc = jnp.concatenate([in_bias, b_down, b_up, jnp.zeros((2 * width - units,), BF)])
    misc = misc.reshape(4, width)
    up, down = w_up.T, w_down.T
    cut = units // 2
    turn = lambda value: value.transpose(1, 0, 2).reshape(-1, width)
    *send, mine0, mine1 = call(
        functools.partial(start_kernel, rows_used=used),
        [ids, Raw(up), Raw(down), turn(tokens), turn(out_grad), misc],
        [((block, 2 * width), BF)] * 4 + [((cut, width), BF)] * 2,
        scratch=[pltpu.VMEM((rows, 2 * width), F32), pltpu.SemaphoreType.DMA((2,))],
    )
    fx1 = swap(mine1, *x_way)
    fy0 = swap(mine0, *y_way)
    got = [send[0]] + [swap(send[k], "pb", k) for k in range(1, pb_size)]

    column = np.arange(width)
    rate = 1.0 / 10000.0 ** ((column // 2 * 2) / width)
    angle = np.arange(padded)[:, None] * rate
    start = np.arange(pb_size)[:, None] * part * rate
    even = column % 2 == 0
    waves = np.concatenate(
        [
            np.where(even, np.sin(start), np.cos(start)),
            np.where(even, np.cos(start), -np.sin(start)),
        ]
    )
    sines, cosines, waves = [
        jnp.asarray(value.astype(np.float32)) for value in (np.sin(angle), np.cos(angle), waves)
    ]

    wide = (slots, width)
    featp, ki, vi, ck, cv, in_proj, cross_proj = call(
        memory_kernel,
        [
            ids,
            Raw(features),
            Far(sines),
            Far(cosines),
            Far(waves),
            Far(in_proj, emit=True),
            misc,
            Far(cross_proj, (1, 2, 0), emit=True),
            Far(cross_bias),
        ],
        [(wide, BF)] * 5,
        scratch=[pltpu.VMEM((mem, width), BF), pltpu.SemaphoreType.DMA],
    )
    ck, fx1, fy0, mine0, mine1, *got = lax.optimization_barrier(
        (ck, fx1, fy0, mine0, mine1, *got)
    )
    fd0 = swap(fy0, *x_way)
    fd1 = swap(fx1, *y_way)
    fx0 = swap(mine0, *x_way)
    fy1 = swap(mine1, *y_way)
    flat = (rows, width)
    scores = (GROUPS, slots, 2 * rows)
    (x, cot, ai, sq, sk, sv, ps, sm, xhat1, rstd1, ci, cq, pc, cm, h2, xhat2, rstd2, bups, self_proj, self_out, cross_out, norm_gain, norm_bias, up, down) = call(
        functools.partial(forward_kernel, rows_used=used, mask_at=mask_at),
        [
            ids,
            *got,
            Far(query_pos),
            Far(self_proj, (0, 1, 2), emit=True),
            Far(self_out, emit=True),
            Far(self_bias),
            cross_proj,
            Far(cross_out, emit=True),
            Far(cross_bias),
            Far(norm_gain, emit=True),
            Far(norm_bias, emit=True),
            ck,
            cv,
            Far(up, emit=True),
            Far(down, emit=True),
        ],
        [
            (flat, BF),
            (flat, BF),
            (flat, BF),
            (flat, BF),
            (flat, BF),
            (flat, BF),
            ((GROUPS, rows, 2 * rows), BF),
            (flat, BF),
            (flat, F32),
            ((rows, 1), F32),
            (flat, BF),
            (flat, BF),
            (scores, BF),
            (flat, BF),
            (flat, F32),
            (flat, F32),
            ((rows, 1), F32),
            ((2 * pb_size, width), F32),
        ],
        scratch=[pltpu.VMEM((slots, 2 * rows), F32), pltpu.VMEM(flat, F32)],
    )
    fetched = [fx0, fx1, fy0, fy1, fd0, fd1]
    h2, *fetched = lax.optimization_barrier((h2, *fetched))
    swapped = [swap(value, *core_way) for value in fetched]
    res, ops, g2, small_a, bup = call(
        ffn_kernel,
        [
            ids,
            h2,
            cot,
            xhat2,
            rstd2,
            bups,
            up,
            down,
            misc,
            norm_gain,
            norm_bias,
            *[Raw(value) for value in fetched],
            *[Raw(value) for value in swapped],
        ],
        [
            (flat, BF),
            ((rows, 2 * width), BF),
            (flat, F32),
            ((8, width), F32),
            ((pb_size, 1, 2 * width), F32),
        ],
        scratch=[
            pltpu.VMEM((2, 3, units, width), BF),
            pltpu.VMEM((4, rows, units), F32),
            pltpu.SemaphoreType.DMA((2, 6)),
        ],
    )
    others = [swap(ops, "pb", k) for k in range(1, pb_size)]
    halves = ((24, width // 2, LANES), BF)
    ds, gcm, gx, gpos, small_b, keep12, send12 = call(
        backward_kernel,
        [
            ids,
            g2,
            pc,
            ck,
            cv,
            cq,
            ci,
            cm,
            xhat1,
            rstd1,
            x,
            ai,
            sq,
            sk,
            sv,
            ps,
            sm,
            self_proj,
            self_out,
            cross_proj,
            cross_out,
            norm_gain,
        ],
        [
            (scores, BF),
            (flat, BF),
            (flat, BF),
            (flat, F32),
            ((8, width), F32),
            halves,
            halves,
        ],
        scratch=[
            pltpu.VMEM((slots, 2 * rows), BF),
            pltpu.VMEM((width, width), F32),
            pltpu.VMEM(flat, BF),
            pltpu.VMEM(flat, BF),
            pltpu.VMEM(flat, BF),
        ],
    )
    ops, *others, send12 = lax.optimization_barrier((ops, *others, send12))
    halves3 = ((13, width // 2, LANES), BF)
    *rows_out, keep3, send3 = call(
        functools.partial(memory_back_kernel, rows_used=used),
        [
            ids,
            ds,
            pc,
            cq,
            gcm,
            featp,
            ki,
            vi,
            cross_proj,
            in_proj,
            res,
            gx,
            gpos,
            small_a,
            small_b,
            bup,
        ],
        [((padded + 2 * block, width), BF)] * 4 + [halves3, halves3],
        scratch=[
            pltpu.VMEM(wide, BF),
            pltpu.VMEM(wide, BF),
            pltpu.VMEM(wide, BF),
            pltpu.VMEM((pb_size, padded, width), BF),
            pltpu.VMEM((width, width), F32),
            pltpu.VMEM(flat, F32),
        ],
    )

    got12 = swap(send12, *core_way)
    ka, sa, kb, sb = fold(
        ids, [([(keep12, got12, 0, 12)], at_of[x_way]), ([(keep12, got12, 12, 24)], at_of[y_way])]
    )
    ra, rb = swap(sa, *x_way), swap(sb, *y_way)
    ra, rb, keep3, send3 = lax.optimization_barrier((ra, rb, keep3, send3))
    got3 = swap(send3, *core_way)
    ka, sa, kb, sb = fold(
        ids, [([(ka, ra, 0, 12)], at_of[y_way]), ([(kb, rb, 0, 12)], at_of[x_way])]
    )
    ra, rb = swap(sa, *y_way), swap(sb, *x_way)
    order3 = [ways[0], x_way, y_way] + ways[1:]
    kc, sc = fold(ids, [([(keep3, got3, 0, 13)], at_of[order3[0]])])
    rc = swap(sc, *order3[0])
    piece = width // dp_size
    fkeep, fsend = call(
        ffn_grad_kernel,
        [ids, ops, *others, up, misc, down],
        [((2, dp_size // 2, piece, units), BF)] * 2,
        scratch=[pltpu.VMEM((width, units), F32)],
    )
    ra, rb, rc, fsend, *rows_out = lax.optimization_barrier((ra, rb, rc, fsend, *rows_out))
    fgot = swap(fsend, *core_way)
    arrived = [rows_out[0]] + [swap(rows_out[k], "pb", k) for k in range(1, pb_size)]
    kab, sab = fold(ids, [([(ka, ra, 0, 12), (kb, rb, 0, 12)], at_of[ways[0]])])
    rab = swap(sab, *ways[0])
    left = list(ways[1:])
    left3 = order3[1:]
    back, back3 = [], []
    vab = vc = None
    after = list(reversed(ways))
    after3 = list(reversed(order3))
    ab_done = False
    pair_out = None
    c_out = None
    while c_out is None:
        if left:
            way = left.pop(0)
            kab, sab = fold(ids, [([(kab, rab, 0, 24)], at_of[way])])
            rab = swap(sab, *way)
        elif vab is None:
            vab = add_up(ids, kab, rab)
            way = after.pop(0)
            rab = swap(vab, *way)
            last = way
        elif after:
            (vab,) = join(ids, vab, rab, at_of[last])
            last = after.pop(0)
            rab = swap(vab, *last)
        elif pair_out is None:
            va, vb = join(ids, vab, rab, at_of[last], [(0, 12), (12, 24)])
            ra, rb = swap(va, *y_way), swap(vb, *x_way)
            pair_out = 1
        elif pair_out == 1:
            (va,) = join(ids, va, ra, at_of[y_way])
            (vb,) = join(ids, vb, rb, at_of[x_way])
            ra, rb = swap(va, *x_way), swap(vb, *y_way)
            pair_out = 2
        elif pair_out == 2:
            (va,) = join(ids, va, ra, at_of[x_way])
            (vb,) = join(ids, vb, rb, at_of[y_way])
            ra, rb = swap(va, *core_way), swap(vb, *core_way)
            pair_out = 3
        if left3:
            way = left3.pop(0)
            kc, sc = fold(ids, [([(kc, rc, 0, 13)], at_of[way])])
            rc = swap(sc, *way)
        elif vc is None:
            vc = add_up(ids, kc, rc)
            last3 = after3.pop(0)
            rc = swap(vc, *last3)
        elif after3:
            (vc,) = join(ids, vc, rc, at_of[last3])
            last3 = after3.pop(0)
            rc = swap(vc, *last3)
        else:
            (c_out,) = join(ids, vc, rc, at_of[last3])
        if ways and fkeep.shape[1] > 1:
            way = ways[(dp_size // 2).bit_length() - fkeep.shape[1].bit_length()]
            fkeep, fsend = call(
                functools.partial(ffn_fold_kernel, bit=at_of[way]),
                [ids, fkeep, fgot],
                [((2, fkeep.shape[1] // 2, piece, units), BF)] * 2,
                limit=4,
            )
            fgot = swap(fsend, *way)
        if c_out is None:
            names = [rab, rc, fgot] if pair_out is None else [ra, rb, rc, fgot]
            if pair_out == 1:
                names += arrived[1:]
            names = lax.optimization_barrier(tuple(names))
            if pair_out is None:
                rab, rc, fgot = names
            else:
                ra, rb, rc, fgot = names[:4]
            if pair_out == 1:
                arrived[1:] = names[4:]
                layer_out, grad_tokens, grad_features = call(
                    order_kernel,
                    [ids, *arrived],
                    [(tokens.shape, BF), (tokens.shape, BF), ((pb_size, part, width), BF)],
                    near=False,
                )
    ffn_up, ffn_down = call(
        ffn_finish_kernel, [ids, fkeep, fgot], [((piece, units), F32)] * 2, near=False
    )
    c = c_out
    matrix = ((width, width), F32)
    three = ((3, width, width), F32)
    g_cross_q, g_self_out, g_cross_out, g_self_proj = call(
        finish_chain_kernel, [ids, va, ra, vb, rb], [matrix, matrix, matrix, three], near=False
    )
    c_other = swap(c, "dp", 1)
    bias3 = ((3, width), F32)
    bias1 = ((1, width), F32)
    (
        g_cross_proj,
        g_in_proj,
        g_pos,
        g_self_bias,
        g_cross_bias,
        g_bup,
        g_bdown,
        g_gain,
        g_shift,
        g_inb,
    ) = call(
        functools.partial(finish_memory_kernel, rows_used=used),
        [ids, c, c_other, g_cross_q],
        [
            three,
            matrix,
            (query_pos.shape, F32),
            bias3,
            bias3,
            ((pb_size, 2 * width), F32),
            bias1,
            bias3,
            bias3,
            bias1,
        ],
        scratch=[pltpu.VMEM(flat, F32)],
        near=False,
    )

    return (
        layer_out,
        grad_tokens,
        grad_features,
        g_pos,
        g_self_proj,
        g_self_out,
        g_self_bias,
        g_cross_proj,
        g_cross_out,
        g_cross_bias,
        ffn_up,
        g_bup[:, :units].reshape(-1),
        ffn_down,
        g_bdown[0],
        g_gain,
        g_shift,
        g_in_proj,
        g_inb[0],
    )


def solution(mesh):
    return jax.shard_map(
        on_device,
        mesh=mesh,
        in_specs=(
            P("dp", "pb", None),
            P(),
            P("dp", None, None),
            P("dp", None),
            P("dp", "pb", None),
            P(),
            P(),
            P(),
            P(),
            P(),
            P(),
            P(None, "pb"),
            P("pb"),
            P(None, "pb"),
            P(),
            P(),
            P(),
            P(),
            P(),
        ),
        out_specs=(
            P("dp", "pb", None),
            P("dp", "pb", None),
            P("dp", "pb", None),
            P(),
            P(),
            P(),
            P(),
            P(),
            P(),
            P(),
            P("dp", "pb"),
            P(),
            P("dp", "pb"),
            P(),
            P(),
            P(),
            P(),
            P(),
        ),
        check_vma=False,
    )
```

time: 251 us -> 217 us (0.86)
  local copies, waits for them, and re-layouts: 25.9 us -> 9.73 us
  starting transfers between devices: 60.1 us -> 50.9 us
  other arithmetic: 5.87 us -> 0 us
    ppermute x50 -> x49, starting transfers between devices: 60.1 us -> 50.9 us  [swap(): return lax.ppermute(value, axis, [(i, i ^ bit) for i in range(size)])]
    slice x6 -> x1, local copies, waits for them, and re-layouts: 8.61 us -> 0.01 us  [on_device(): g_bup[:, :units].reshape(-1)]
    unnamed x69 -> x27, local copies, waits for them, and re-layouts: 11.8 us -> 4.17 us
    convert_element_type x19 -> x0, other arithmetic: 2.64 us -> none  [the longest x18 1.84 us: plus(): return (left.astype(F32) + right.astype(F32)).astype(BF)]
    pallas_call x8 -> x33, Pallas kernels: 66 us -> 63.5 us  [call(): pl.pallas_call(body, out_shape=[pltpu.VMEM(*o) if here else jax.ShapeDtyp...]
    ppermute x50 -> x49, waiting for transfers between devices: 90.7 us -> 91 us  [swap(): return lax.ppermute(value, axis, [(i, i ^ bit) for i in range(size)])]
  transfers between devices with their start and end apart: 50 -> 49, of which waited for: 22 -> 28; matrix products, arithmetic and copies ran while one was open for 7% -> 2% of each run, Pallas kernels for 21% -> 21%
where the time goes in v1:
time: 217 us; the launch traced here: 216 us
  waiting for transfers between devices  91 us (42%)
  Pallas kernels  63.5 us (29%)
  starting transfers between devices  50.9 us (23%)
  local copies, waits for them, and re-layouts  9.73 us (4%)
    ppermute x49, waiting for transfers between devices, swap(): return lax.ppermute(value, axis, [(i, i ^ bit) for i in range(size)])  91 us
    pallas_call x33, Pallas kernels, call(): pl.pallas_call(body, out_shape=[pltpu.VMEM(*o) if here else jax.ShapeDtyp...  63.5 us
    ppermute x49, starting transfers between devices, swap(): return lax.ppermute(value, axis, [(i, i ^ bit) for i in range(size)])  50.9 us
  transfers between devices with their start and end apart: 49, of which 28 were waited for; matrix products, arithmetic and copies ran while one was open for 2% of the time, Pallas kernels for 21%

profile of v1, /device:TPU:0, one launch (start us, length us, event | category | flops | bytes accessed | tf_op | source)
XLA Modules:
  0.0 216.3 jit_solution(9559293425924778814)
XLA Ops:
  1.5 2.1 concatenate.7
  3.7 0.9 reshape.53.refs_3_
  4.6 0.9 reshape.54.refs_4_
  5.6 1.9 shard_map.350
  7.6 3.0 %collective-permute-start = (bf16[400,512]{1,0:T(8,128)(2,1)S(1)}, bf16[400,512]{1,0:T(8,128)(2,1)S(1)}, u32[]{:S(2)}, u32[]{:S(2)}) collective-permute-start(bf16[400,512]{1,0:T(8,128)(2,1)S(1)} %get-tuple-element.200), channel_id=1, source_target_pairs={{0,8},{8,0},{16,24},{24,16},{1,9},{9,1},{17,25},{25,17},{2,10},{10... | collective-permute-start | bytes 1228808 | tf_op jit(solution)/shard_map/ppermute | solution.py:754
  10.6 1.5 collective-permute-start.1
  12.7 2.9 %collective-permute-start.4 = (bf16[32,1024]{1,0:T(8,128)(2,1)S(1)}, bf16[32,1024]{1,0:T(8,128)(2,1)S(1)}, u32[]{:S(2)}, u32[]{:S(2)}) collective-permute-start(bf16[32,1024]{1,0:T(8,128)(2,1)S(1)} %get-tuple-element.188), channel_id=1, source_target_pairs={{0,24},{8,16},{16,8},{24,0},{1,25},{9,17},{17,9},{25,1},{2,26},{10... | collective-permute-start | bytes 196616 | tf_op jit(solution)/shard_map/ppermute | solution.py:754
  15.6 6.0 %shard_map.349 = (bf16[1216,512]{1,0:T(8,128)(2,1)S(1)}, bf16[1216,512]{1,0:T(8,128)(2,1)S(1)}, bf16[1216,512]{1,0:T(8,128)(2,1)S(1)}, bf16[1216,512]{1,0:T(8,12...) custom-call(s32[22]{0:T(128)S(1)} %concatenate.6.refs_0_, ...), custom_call_target="tpu_custom_call" | custom-call | flops 1 | bytes 1 | tf_op jit(solution)/shard_map/pallas_call | solution.py:741
  22.2 2.2 collective-permute-done.3.refs_3_
  24.4 1.3 collective-permute-start.5
  25.7 0.8 collective-permute-start.6
  26.5 1.2 collective-permute-start.8
  28.5 8.4 %shard_map.351 = (bf16[128,512]{1,0:T(8,128)(2,1)S(1)}, bf16[128,512]{1,0:T(8,128)(2,1)S(1)}, bf16[128,512]{1,0:T(8,128)(2,1)S(1)}, bf16[128,512]{1,0:T(8,128)(2...) custom-call(s32[22]{0:T(128)S(1)} %concatenate.6.refs_0_, ...), custom_call_target="tpu_custom_call" | custom-call | flops 1 | bytes 1 | tf_op jit(solution)/shard_map/pallas_call | solution.py:741
  36.9 1.2 collective-permute-done.6.refs_14_
  38.1 6.1 %collective-permute-done.8.refs_16_ = bf16[400,512]{1,0:T(8,128)(2,1)S(1)} collective-permute-done((bf16[400,512]{1,0:T(8,128)(2,1)S(1)}, bf16[400,512]{1,0:T(8,128)(2,1)S(1)}, u32[]{:S(2)}, u32[]{:S(2)}) %collective-permute-start.8) | collective-permute-done | bytes 409632 | tf_op jit(solution)/shard_map/ppermute | solution.py:754
  49.7 7.3 %shard_map.352 = (bf16[128,512]{1,0:T(8,128)(2,1)S(1)}, bf16[128,1024]{1,0:T(8,128)(2,1)S(1)}, f32[128,512]{1,0:T(8,128)S(1)}, f32[8,512]{1,0:T(8,128)S(1)}, f32[4,1,1024]{2,1,0:T(1,128)S(1)}) custom-call(s32[22]{0:T(128)S(1)} %concatenate.6.refs_0_, f32[128,512]{1,0:T(8,128)S(1)} %get-tuple-element.201.refs_1_, ...), custom_call_target="tpu_custom_call" | custom-call | flops 1 | bytes 1 | tf_op jit(solution)/shard_map/pallas_call | solution.py:741
  57.0 1.1 collective-permute-start.17
  58.1 1.0 collective-permute-start.16
  59.0 1.5 collective-permute-start.15
  60.5 7.7 %shard_map.353 = (bf16[4,1216,256]{2,1,0:T(8,128)(2,1)S(1)}, bf16[128,512]{1,0:T(8,128)(2,1)S(1)}, bf16[128,512]{1,0:T(8,128)(2,1)S(1)}, f32[128,512]{1,0:T(8,12...) custom-call(s32[22]{0:T(128)S(1)} %concatenate.6.refs_0_, ...), custom_call_target="tpu_custom_call" | custom-call | flops 1 | bytes 1 | tf_op jit(solution)/shard_map/pallas_call | solution.py:741
  68.3 3.5 %collective-permute-done.16.refs_3_ = bf16[128,1024]{1,0:T(8,128)(2,1)S(1)} collective-permute-done((bf16[128,1024]{1,0:T(8,128)(2,1)S(1)}, bf16[128,1024]{1,0:T(8,128)(2,1)S(1)}, u32[]{:S(2)}, u32[]{:S(2)}) %collective-permute-start.16) | collective-permute-done | bytes 262176 | tf_op jit(solution)/shard_map/ppermute | solution.py:754
  71.8 3.4 %collective-permute-done.18.refs_2_.refs_4_ = bf16[24,256,128]{2,1,0:T(8,128)(2,1)S(1)} collective-permute-done((bf16[24,256,128]{2,1,0:T(8,128)(2,1)S(1)}, bf16[24,256,128]{2,1,0:T(8,128)(2,1)S(1)}, u32[]{:S(2)}, u32[]{:S(2)}) %collective-permute-start.18) | collective-permute-done | bytes 1572896 | tf_op jit(solution)/shard_map/ppermute | solution.py:754
  75.2 0.9 shard_map.354
  76.8 1.1 collective-permute-start.20
  77.9 7.0 %shard_map.355 = (bf16[368,512]{1,0:T(8,128)(2,1)S(1)}, bf16[368,512]{1,0:T(8,128)(2,1)S(1)}, bf16[368,512]{1,0:T(8,128)(2,1)S(1)}, bf16[368,512]{1,0:T(8,128)(2...) custom-call(s32[22]{0:T(128)S(1)} %concatenate.6.refs_0_, ...), custom_call_target="tpu_custom_call" | custom-call | flops 1 | bytes 1 | tf_op jit(solution)/shard_map/pallas_call | solution.py:741
  84.9 2.4 %collective-permute-done.19.refs_2_ = bf16[12,128,128]{2,1,0:T(8,128)(2,1)S(1)} collective-permute-done((bf16[12,128,128]{2,1,0:T(8,128)(2,1)S(1)}, bf16[12,128,128]{2,1,0:T(8,128)(2,1)S(1)}, u32[]{:S(2)}, u32[]{:S(2)}) %collective-permute-start.19) | collective-permute-done | bytes 393248 | tf_op jit(solution)/shard_map/ppermute | solution.py:754
  87.7 2.4 %collective-permute-done.23.refs_2_ = bf16[13,256,128]{2,1,0:T(8,128)(2,1)S(1)} collective-permute-done((bf16[13,256,128]{2,1,0:T(8,128)(2,1)S(1)}, bf16[13,256,128]{2,1,0:T(8,128)(2,1)S(1)}, u32[]{:S(2)}, u32[]{:S(2)}) %collective-permute-start.23) | collective-permute-done | bytes 852000 | tf_op jit(solution)/shard_map/ppermute | solution.py:754
  90.8 1.6 collective-permute-start.24
  93.2 1.1 collective-permute-start.21
  94.3 1.0 collective-permute-start.22
  95.3 3.2 %shard_map.358 = (bf16[2,4,64,800]{3,2,1,0:T(8,128)(2,1)S(1)}, bf16[2,4,64,800]{3,2,1,0:T(8,128)(2,1)S(1)}) custom-call(s32[22]{0:T(128)S(1)} %concatenate.6.refs_0_, bf16[128,1024]{1,0:T(8,128)(2,1)S(1)} %get-tuple-element.262.refs_1_, bf16[128,1024]{1,0:T(8,128)(2,1)S(1)} %collective-permute-done.15.refs_2_, ...), custom_call_target="tpu_custom_call" | custom-call | flops 1 | bytes 1 | tf_op jit(solution)/shard_map/pallas_call | solution.py:741
  98.5 1.4 collective-permute-done.21.refs_2_
  100.7 2.0 collective-permute-done.24.refs_2_
  102.8 2.5 %collective-permute-done.28.refs_2_ = bf16[2,4,64,800]{3,2,1,0:T(8,128)(2,1)S(1)} collective-permute-done((bf16[2,4,64,800]{3,2,1,0:T(8,128)(2,1)S(1)}, bf16[2,4,64,800]{3,2,1,0:T(8,128)(2,1)S(1)}, u32[]{:S(2)}, u32[]{:S(2)}) %collective-permute-start.28) | collective-permute-done | bytes 819232 | tf_op jit(solution)/shard_map/ppermute | solution.py:754
  106.0 1.6 collective-permute-start.29
  109.4 1.4 collective-permute-start.27
  110.9 12.0 %collective-permute-done.25.refs_2_ = bf16[24,32,128]{2,1,0:T(8,128)(2,1)S(1)} collective-permute-done((bf16[24,32,128]{2,1,0:T(8,128)(2,1)S(1)}, bf16[24,32,128]{2,1,0:T(8,128)(2,1)S(1)}, u32[]{:S(2)}, u32[]{:S(2)}) %collective-permute-start.25) | collective-permute-done | bytes 196640 | tf_op jit(solution)/shard_map/ppermute | solution.py:754
  123.4 2.7 %collective-permute-start.26 = (bf16[24,16,128]{2,1,0:T(8,128)(2,1)S(1)}, bf16[24,16,128]{2,1,0:T(8,128)(2,1)S(1)}, u32[]{:S(2)}, u32[]{:S(2)}) collective-permute-start(bf16[24,16,128]{2,1,0:T(8,128)(2,1)S(1)} %get-tuple-element.279), channel_id=1, source_target_pairs={{0,4},{1,5},{2,6},{3,7},{4,0},{5,1},{6,2},{7,3},{8,12},{9,13},{10,... | collective-permute-start | bytes 294920 | tf_op jit(solution)/shard_map/ppermute | solution.py:754
  126.1 4.4 %collective-permute-done.26.refs_2_ = bf16[24,16,128]{2,1,0:T(8,128)(2,1)S(1)} collective-permute-done((bf16[24,16,128]{2,1,0:T(8,128)(2,1)S(1)}, bf16[24,16,128]{2,1,0:T(8,128)(2,1)S(1)}, u32[]{:S(2)}, u32[]{:S(2)}) %collective-permute-start.26) | collective-permute-done | bytes 98336 | tf_op jit(solution)/shard_map/ppermute | solution.py:754
  131.2 1.3 collective-permute-start.32
  133.0 1.1 collective-permute-start.31
  134.7 1.8 collective-permute-start.30
  136.5 1.0 collective-permute-start.38
  137.6 9.0 %collective-permute-done.30.refs_2_ = bf16[24,16,128]{2,1,0:T(8,128)(2,1)S(1)} collective-permute-done((bf16[24,16,128]{2,1,0:T(8,128)(2,1)S(1)}, bf16[24,16,128]{2,1,0:T(8,128)(2,1)S(1)}, u32[]{:S(2)}, u32[]{:S(2)}) %collective-permute-start.30) | collective-permute-done | bytes 98336 | tf_op jit(solution)/shard_map/ppermute | solution.py:754
  147.2 1.1 collective-permute-start.39
  148.3 1.7 collective-permute-start.40
  150.6 3.1 %collective-permute-start.34 = (bf16[13,16,128]{2,1,0:T(8,128)(2,1)S(1)}, bf16[13,16,128]{2,1,0:T(8,128)(2,1)S(1)}, u32[]{:S(2)}, u32[]{:S(2)}) collective-permute-start(bf16[13,16,128]{2,1,0:T(8,128)(2,1)S(1)} %get-tuple-element.296), channel_id=1, source_target_pairs={{0,4},{1,5},{2,6},{3,7},{4,0},{5,1},{6,2},{7,3},{8,12},{9,13},{10,... | collective-permute-start | bytes 159752 | tf_op jit(solution)/shard_map/ppermute | solution.py:754
  153.7 2.1 collective-permute-done.34.refs_2_
  156.4 1.0 collective-permute-start.35
  157.4 1.0 collective-permute-start.36
  159.0 2.8 %collective-permute-start.37 = (bf16[13,16,128]{2,1,0:T(8,128)(2,1)S(1)}, bf16[13,16,128]{2,1,0:T(8,128)(2,1)S(1)}, u32[]{:S(2)}, u32[]{:S(2)}) collective-permute-start(bf16[13,16,128]{2,1,0:T(8,128)(2,1)S(1)} %shard_map.369.refs_1_), channel_id=1, source_target_pairs={{0,4},{1,5},{2,6},{3,7},{4,0},{5,1},{6,2},{7,3},{8,12},{9,13},{10,... | collective-permute-start | bytes 159752 | tf_op jit(solution)/shard_map/ppermute | solution.py:754
  161.8 5.3 %collective-permute-done.39.refs_3_ = bf16[368,512]{1,0:T(8,128)(2,1)S(1)} collective-permute-done((bf16[368,512]{1,0:T(8,128)(2,1)S(1)}, bf16[368,512]{1,0:T(8,128)(2,1)S(1)}, u32[]{:S(2)}, u32[]{:S(2)}) %collective-permute-start.39) | collective-permute-done | bytes 376864 | tf_op jit(solution)/shard_map/ppermute | solution.py:754
  167.0 2.5 %collective-permute-done.35.refs_2_ = bf16[12,64,128]{2,1,0:T(8,128)(2,1)S(1)} collective-permute-done((bf16[12,64,128]{2,1,0:T(8,128)(2,1)S(1)}, bf16[12,64,128]{2,1,0:T(8,128)(2,1)S(1)}, u32[]{:S(2)}, u32[]{:S(2)}) %collective-permute-start.35) | collective-permute-done | bytes 196640 | tf_op jit(solution)/shard_map/ppermute | solution.py:754
  170.1 1.1 collective-permute-start.42
  171.8 1.1 collective-permute-start.41
  173.5 1.3 collective-permute-start.43
  174.8 7.1 %collective-permute-done.43.refs_2_ = bf16[13,32,128]{2,1,0:T(8,128)(2,1)S(1)} collective-permute-done((bf16[13,32,128]{2,1,0:T(8,128)(2,1)S(1)}, bf16[13,32,128]{2,1,0:T(8,128)(2,1)S(1)}, u32[]{:S(2)}, u32[]{:S(2)}) %collective-permute-start.43) | collective-permute-done | bytes 106528 | tf_op jit(solution)/shard_map/ppermute | solution.py:754
  184.4 1.6 collective-permute-start.46
  185.9 5.7 %collective-permute-done.46.refs_2_ = bf16[13,64,128]{2,1,0:T(8,128)(2,1)S(1)} collective-permute-done((bf16[13,64,128]{2,1,0:T(8,128)(2,1)S(1)}, bf16[13,64,128]{2,1,0:T(8,128)(2,1)S(1)}, u32[]{:S(2)}, u32[]{:S(2)}) %collective-permute-start.46) | collective-permute-done | bytes 213024 | tf_op jit(solution)/shard_map/ppermute | solution.py:754
  192.5 10.7 %collective-permute-done.47.refs_2_ = bf16[13,128,128]{2,1,0:T(8,128)(2,1)S(1)} collective-permute-done((bf16[13,128,128]{2,1,0:T(8,128)(2,1)S(1)}, bf16[13,128,128]{2,1,0:T(8,128)(2,1)S(1)}, u32[]{:S(2)}, u32[]{:S(2)}) %collective-permute-start.47) | collective-permute-done | bytes 426016 | tf_op jit(solution)/shard_map/ppermute | solution.py:754
  205.9 2.0 copy.42
  207.9 1.3 shard_map.381
  209.2 3.6 %shard_map.379 = (f32[512,512]{1,0:T(8,128)S(1)}, f32[512,512]{1,0:T(8,128)}, f32[512,512]{1,0:T(8,128)}, f32[3,512,512]{2,1,0:T(8,128)}) custom-call(s32[22]{0:T(128)S(1)} %concatenate.6.refs_0_, bf16[12,256,128]{2,1,0:T(8,128)(2,1)S(1)} %shard_map.375.refs_1_, bf16[12,256,128]{2,1,0:T(8,128)(2,1)S(1)} %collective-permute-done.44.refs_2_, ...), custom_call_target="tpu_custom_call" | custom-call | flops 1 | bytes 1 | tf_op jit(solution)/shard_map/pallas_call | solution.py:741
  212.9 2.8 %shard_map.380 = (f32[3,512,512]{2,1,0:T(8,128)}, f32[512,512]{1,0:T(8,128)}, f32[100,512]{1,0:T(8,128)}, f32[3,512]{1,0:T(4,128)}, f32[3,512]{1,0:T(4,128)}, /*...) custom-call(s32[22]{0:T(128)S(1)} %concatenate.6.refs_0_, ...), custom_call_target="tpu_custom_call" | custom-call | flops 1 | bytes 1 | tf_op jit(solution)/shard_map/pallas_call | solution.py:741
  (103 shorter events, 27.4 us)
Async XLA Ops:
  7.6 16.7 %collective-permute-start = (bf16[400,512]{1,0:T(8,128)(2,1)S(1)}, bf16[400,512]{1,0:T(8,128)(2,1)S(1)}, u32[]{:S(2)}, u32[]{:S(2)}) collective-permute-start(bf16[400,512]{1,0:T(8,128)(2,1)S(1)} %get-tuple-element.200), channel_id=1, source_target_pairs={{0,8},{8,0},{16,24},{24,16},{1,9},{9,1},{17,25},{25,17},{2,10},{10... | collective-permute-start | bytes 1228808 | tf_op jit(solution)/shard_map/ppermute | solution.py:754
  10.6 13.8 %collective-permute-start.1 = (bf16[400,512]{1,0:T(8,128)(2,1)S(1)}, bf16[400,512]{1,0:T(8,128)(2,1)S(1)}, u32[]{:S(2)}, u32[]{:S(2)}) collective-permute-start(bf16[400,512]{1,0:T(8,128)(2,1)S(1)} %get-tuple-element.197), channel_id=1, source_target_pairs={{0,16},{8,24},{16,0},{24,8},{1,17},{9,25},{17,1},{25,9},{2,18},{10... | collective-permute-start | bytes 1228808 | tf_op jit(solution)/shard_map/ppermute | solution.py:754
  12.1 10.1 %collective-permute-start.2 = (bf16[32,1024]{1,0:T(8,128)(2,1)S(1)}, bf16[32,1024]{1,0:T(8,128)(2,1)S(1)}, u32[]{:S(2)}, u32[]{:S(2)}) collective-permute-start(bf16[32,1024]{1,0:T(8,128)(2,1)S(1)} %get-tuple-element.186), channel_id=1, source_target_pairs={{0,8},{8,0},{16,24},{24,16},{1,9},{9,1},{17,25},{25,17},{2,10},{10... | collective-permute-start | bytes 196616 | tf_op jit(solution)/shard_map/ppermute | solution.py:754
  12.6 11.7 %collective-permute-start.3 = (bf16[32,1024]{1,0:T(8,128)(2,1)S(1)}, bf16[32,1024]{1,0:T(8,128)(2,1)S(1)}, u32[]{:S(2)}, u32[]{:S(2)}) collective-permute-start(bf16[32,1024]{1,0:T(8,128)(2,1)S(1)} %get-tuple-element.187), channel_id=1, source_target_pairs={{0,16},{8,24},{16,0},{24,8},{1,17},{9,25},{17,1},{25,9},{2,18},{10... | collective-permute-start | bytes 196616 | tf_op jit(solution)/shard_map/ppermute | solution.py:754
  12.7 11.6 %collective-permute-start.4 = (bf16[32,1024]{1,0:T(8,128)(2,1)S(1)}, bf16[32,1024]{1,0:T(8,128)(2,1)S(1)}, u32[]{:S(2)}, u32[]{:S(2)}) collective-permute-start(bf16[32,1024]{1,0:T(8,128)(2,1)S(1)} %get-tuple-element.188), channel_id=1, source_target_pairs={{0,24},{8,16},{16,8},{24,0},{1,25},{9,17},{17,9},{25,1},{2,26},{10... | collective-permute-start | bytes 196616 | tf_op jit(solution)/shard_map/ppermute | solution.py:754
  24.3 19.9 %copy-start = (bf16[400,512]{1,0:T(8,128)(2,1)}, bf16[400,512]{1,0:T(8,128)(2,1)S(1)}, u32[]{:S(2)}) copy-start(bf16[400,512]{1,0:T(8,128)(2,1)S(1)} %collective-permute-done.refs_12_) | copy-start | bytes 1228804
  24.3 20.4 %copy-start.1 = (bf16[400,512]{1,0:T(8,128)(2,1)}, bf16[400,512]{1,0:T(8,128)(2,1)S(1)}, u32[]{:S(2)}) copy-start(bf16[400,512]{1,0:T(8,128)(2,1)S(1)} %collective-permute-done.1.refs_13_) | copy-start | bytes 1228804
  24.4 12.5 %collective-permute-start.5 = (bf16[400,512]{1,0:T(8,128)(2,1)S(1)}, bf16[400,512]{1,0:T(8,128)(2,1)S(1)}, u32[]{:S(2)}, u32[]{:S(2)}) collective-permute-start(bf16[400,512]{1,0:T(8,128)(2,1)S(1)} %get-tuple-element.197), channel_id=1, source_target_pairs={{0,8},{8,0},{16,24},{24,16},{1,9},{9,1},{17,25},{25,17},{2,10},{10... | collective-permute-start | bytes 1228808 | tf_op jit(solution)/shard_map/ppermute | solution.py:754
  25.7 12.4 %collective-permute-start.6 = (bf16[400,512]{1,0:T(8,128)(2,1)S(1)}, bf16[400,512]{1,0:T(8,128)(2,1)S(1)}, u32[]{:S(2)}, u32[]{:S(2)}) collective-permute-start(bf16[400,512]{1,0:T(8,128)(2,1)S(1)} %get-tuple-element.200), channel_id=1, source_target_pairs={{0,16},{8,24},{16,0},{24,8},{1,17},{9,25},{17,1},{25,9},{2,18},{10... | collective-permute-start | bytes 1228808 | tf_op jit(solution)/shard_map/ppermute | solution.py:754
  26.5 17.7 %collective-permute-start.8 = (bf16[400,512]{1,0:T(8,128)(2,1)S(1)}, bf16[400,512]{1,0:T(8,128)(2,1)S(1)}, u32[]{:S(2)}, u32[]{:S(2)}) collective-permute-start(bf16[400,512]{1,0:T(8,128)(2,1)S(1)} %collective-permute-done.refs_12_), channel_id=1, source_target_pairs={{0,16},{8,24},{16,0},{24,8},{1,17},{9,25},{17,1},{25,9},{2,18},{10... | collective-permute-start | bytes 1228808 | tf_op jit(solution)/shard_map/ppermute | solution.py:754
  27.7 16.5 %collective-permute-start.7 = (bf16[400,512]{1,0:T(8,128)(2,1)S(1)}, bf16[400,512]{1,0:T(8,128)(2,1)S(1)}, u32[]{:S(2)}, u32[]{:S(2)}) collective-permute-start(bf16[400,512]{1,0:T(8,128)(2,1)S(1)} %collective-permute-done.1.refs_13_), channel_id=1, source_target_pairs={{0,8},{8,0},{16,24},{24,16},{1,9},{9,1},{17,25},{25,17},{2,10},{10... | collective-permute-start | bytes 1228808 | tf_op jit(solution)/shard_map/ppermute | solution.py:754
  36.9 12.0 %copy-start.2 = (bf16[400,512]{1,0:T(8,128)(2,1)}, bf16[400,512]{1,0:T(8,128)(2,1)S(1)}, u32[]{:S(2)}) copy-start(bf16[400,512]{1,0:T(8,128)(2,1)S(1)} %collective-permute-done.5.refs_11_) | copy-start | bytes 1228804
  38.1 10.9 %copy-start.3 = (bf16[400,512]{1,0:T(8,128)(2,1)}, bf16[400,512]{1,0:T(8,128)(2,1)S(1)}, u32[]{:S(2)}) copy-start(bf16[400,512]{1,0:T(8,128)(2,1)S(1)} %collective-permute-done.6.refs_14_) | copy-start | bytes 1228804
  44.2 4.8 %copy-start.4 = (bf16[400,512]{1,0:T(8,128)(2,1)}, bf16[400,512]{1,0:T(8,128)(2,1)S(1)}, u32[]{:S(2)}) copy-start(bf16[400,512]{1,0:T(8,128)(2,1)S(1)} %collective-permute-done.8.refs_16_) | copy-start | bytes 1228804
  44.2 4.8 %copy-start.5 = (bf16[400,512]{1,0:T(8,128)(2,1)}, bf16[400,512]{1,0:T(8,128)(2,1)S(1)}, u32[]{:S(2)}) copy-start(bf16[400,512]{1,0:T(8,128)(2,1)S(1)} %collective-permute-done.7.refs_15_) | copy-start | bytes 1228804
  44.2 1.8 collective-permute-start.9
  44.3 2.3 %collective-permute-start.10 = (bf16[400,512]{1,0:T(8,128)(2,1)S(1)}, bf16[400,512]{1,0:T(8,128)(2,1)S(1)}, u32[]{:S(2)}, u32[]{:S(2)}) collective-permute-start(bf16[400,512]{1,0:T(8,128)(2,1)S(1)} %collective-permute-done.refs_12_), channel_id=1, source_target_pairs={{0,1},{1,0},{2,3},{3,2},{4,5},{5,4},{6,7},{7,6},{8,9},{9,8},{10,11... | collective-permute-start | bytes 1228808 | tf_op jit(solution)/shard_map/ppermute | solution.py:754
  44.8 2.4 %collective-permute-start.11 = (bf16[400,512]{1,0:T(8,128)(2,1)S(1)}, bf16[400,512]{1,0:T(8,128)(2,1)S(1)}, u32[]{:S(2)}, u32[]{:S(2)}) collective-permute-start(bf16[400,512]{1,0:T(8,128)(2,1)S(1)} %collective-permute-done.1.refs_13_), channel_id=1, source_target_pairs={{0,1},{1,0},{2,3},{3,2},{4,5},{5,4},{6,7},{7,6},{8,9},{9,8},{10,11... | collective-permute-start | bytes 1228808 | tf_op jit(solution)/shard_map/ppermute | solution.py:754
  44.9 2.9 %collective-permute-start.12 = (bf16[400,512]{1,0:T(8,128)(2,1)S(1)}, bf16[400,512]{1,0:T(8,128)(2,1)S(1)}, u32[]{:S(2)}, u32[]{:S(2)}) collective-permute-start(bf16[400,512]{1,0:T(8,128)(2,1)S(1)} %collective-permute-done.6.refs_14_), channel_id=1, source_target_pairs={{0,1},{1,0},{2,3},{3,2},{4,5},{5,4},{6,7},{7,6},{8,9},{9,8},{10,11... | collective-permute-start | bytes 1228808 | tf_op jit(solution)/shard_map/ppermute | solution.py:754
  45.3 3.1 %collective-permute-start.13 = (bf16[400,512]{1,0:T(8,128)(2,1)S(1)}, bf16[400,512]{1,0:T(8,128)(2,1)S(1)}, u32[]{:S(2)}, u32[]{:S(2)}) collective-permute-start(bf16[400,512]{1,0:T(8,128)(2,1)S(1)} %collective-permute-done.7.refs_15_), channel_id=1, source_target_pairs={{0,1},{1,0},{2,3},{3,2},{4,5},{5,4},{6,7},{7,6},{8,9},{9,8},{10,11... | collective-permute-start | bytes 1228808 | tf_op jit(solution)/shard_map/ppermute | solution.py:754
  46.0 3.0 %copy-start.6 = (bf16[400,512]{1,0:T(8,128)(2,1)}, bf16[400,512]{1,0:T(8,128)(2,1)S(1)}, u32[]{:S(2)}) copy-start(bf16[400,512]{1,0:T(8,128)(2,1)S(1)} %collective-permute-done.9.refs_17_) | copy-start | bytes 1228804
  46.0 2.9 %collective-permute-start.14 = (bf16[400,512]{1,0:T(8,128)(2,1)S(1)}, bf16[400,512]{1,0:T(8,128)(2,1)S(1)}, u32[]{:S(2)}, u32[]{:S(2)}) collective-permute-start(bf16[400,512]{1,0:T(8,128)(2,1)S(1)} %collective-permute-done.8.refs_16_), channel_id=1, source_target_pairs={{0,1},{1,0},{2,3},{3,2},{4,5},{5,4},{6,7},{7,6},{8,9},{9,8},{10,11... | collective-permute-start | bytes 1228808 | tf_op jit(solution)/shard_map/ppermute | solution.py:754
  46.6 2.4 %copy-start.7 = (bf16[400,512]{1,0:T(8,128)(2,1)}, bf16[400,512]{1,0:T(8,128)(2,1)S(1)}, u32[]{:S(2)}) copy-start(bf16[400,512]{1,0:T(8,128)(2,1)S(1)} %collective-permute-done.10.refs_18_) | copy-start | bytes 1228804
  47.2 1.8 copy-start.8
  47.8 1.2 copy-start.9
  48.3 0.8 copy-start.10
  48.9 0.8 copy-start.11
  57.0 11.3 %collective-permute-start.17 = (bf16[128,1024]{1,0:T(8,128)(2,1)S(1)}, bf16[128,1024]{1,0:T(8,128)(2,1)S(1)}, u32[]{:S(2)}, u32[]{:S(2)}) collective-permute-start(bf16[128,1024]{1,0:T(8,128)(2,1)S(1)} %get-tuple-element.262.refs_1_), channel_id=1, source_target_pairs={{0,24},{8,16},{16,8},{24,0},{1,25},{9,17},{17,9},{25,1},{2,26},{10... | collective-permute-start | bytes 786440 | tf_op jit(solution)/shard_map/ppermute | solution.py:754
  58.1 13.7 %collective-permute-start.16 = (bf16[128,1024]{1,0:T(8,128)(2,1)S(1)}, bf16[128,1024]{1,0:T(8,128)(2,1)S(1)}, u32[]{:S(2)}, u32[]{:S(2)}) collective-permute-start(bf16[128,1024]{1,0:T(8,128)(2,1)S(1)} %get-tuple-element.262.refs_1_), channel_id=1, source_target_pairs={{0,16},{8,24},{16,0},{24,8},{1,17},{9,25},{17,1},{25,9},{2,18},{10... | collective-permute-start | bytes 786440 | tf_op jit(solution)/shard_map/ppermute | solution.py:754
  59.0 12.7 %collective-permute-start.15 = (bf16[128,1024]{1,0:T(8,128)(2,1)S(1)}, bf16[128,1024]{1,0:T(8,128)(2,1)S(1)}, u32[]{:S(2)}, u32[]{:S(2)}) collective-permute-start(bf16[128,1024]{1,0:T(8,128)(2,1)S(1)} %get-tuple-element.262.refs_1_), channel_id=1, source_target_pairs={{0,8},{8,0},{16,24},{24,16},{1,9},{9,1},{17,25},{25,17},{2,10},{10... | collective-permute-start | bytes 786440 | tf_op jit(solution)/shard_map/ppermute | solution.py:754
  71.8 3.4 %collective-permute-start.18 = (bf16[24,256,128]{2,1,0:T(8,128)(2,1)S(1)}, bf16[24,256,128]{2,1,0:T(8,128)(2,1)S(1)}, u32[]{:S(2)}, u32[]{:S(2)}) collective-permute-start(bf16[24,256,128]{2,1,0:T(8,128)(2,1)S(1)} %get-tuple-element.236), channel_id=1, source_target_pairs={{0,1},{1,0},{2,3},{3,2},{4,5},{5,4},{6,7},{7,6},{8,9},{9,8},{10,11... | collective-permute-start | bytes 4718600 | tf_op jit(solution)/shard_map/ppermute | solution.py:754
  76.1 11.2 %collective-permute-start.19 = (bf16[12,128,128]{2,1,0:T(8,128)(2,1)S(1)}, bf16[12,128,128]{2,1,0:T(8,128)(2,1)S(1)}, u32[]{:S(2)}, u32[]{:S(2)}) collective-permute-start(bf16[12,128,128]{2,1,0:T(8,128)(2,1)S(1)} %get-tuple-element.238), channel_id=1, source_target_pairs={{0,8},{8,0},{16,24},{24,16},{1,9},{9,1},{17,25},{25,17},{2,10},{10... | collective-permute-start | bytes 1179656 | tf_op jit(solution)/shard_map/ppermute | solution.py:754
  76.8 10.9 %collective-permute-start.20 = (bf16[12,128,128]{2,1,0:T(8,128)(2,1)S(1)}, bf16[12,128,128]{2,1,0:T(8,128)(2,1)S(1)}, u32[]{:S(2)}, u32[]{:S(2)}) collective-permute-start(bf16[12,128,128]{2,1,0:T(8,128)(2,1)S(1)} %get-tuple-element.239), channel_id=1, source_target_pairs={{0,16},{8,24},{16,0},{24,8},{1,17},{9,25},{17,1},{25,9},{2,18},{10... | collective-permute-start | bytes 1179656 | tf_op jit(solution)/shard_map/ppermute | solution.py:754
  87.7 2.4 %collective-permute-start.23 = (bf16[13,256,128]{2,1,0:T(8,128)(2,1)S(1)}, bf16[13,256,128]{2,1,0:T(8,128)(2,1)S(1)}, u32[]{:S(2)}, u32[]{:S(2)}) collective-permute-start(bf16[13,256,128]{2,1,0:T(8,128)(2,1)S(1)} %get-tuple-element.260), channel_id=1, source_target_pairs={{0,1},{1,0},{2,3},{3,2},{4,5},{5,4},{6,7},{7,6},{8,9},{9,8},{10,11... | collective-permute-start | bytes 2555912 | tf_op jit(solution)/shard_map/ppermute | solution.py:754
  90.8 11.9 %collective-permute-start.24 = (bf16[13,128,128]{2,1,0:T(8,128)(2,1)S(1)}, bf16[13,128,128]{2,1,0:T(8,128)(2,1)S(1)}, u32[]{:S(2)}, u32[]{:S(2)}) collective-permute-start(bf16[13,128,128]{2,1,0:T(8,128)(2,1)S(1)} %get-tuple-element.261), channel_id=1, source_target_pairs={{0,2},{1,3},{2,0},{3,1},{4,6},{5,7},{6,4},{7,5},{8,10},{9,11},{10,... | collective-permute-start | bytes 1277960 | tf_op jit(solution)/shard_map/ppermute | solution.py:754
  93.2 6.7 %collective-permute-start.21 = (bf16[12,64,128]{2,1,0:T(8,128)(2,1)S(1)}, bf16[12,64,128]{2,1,0:T(8,128)(2,1)S(1)}, u32[]{:S(2)}, u32[]{:S(2)}) collective-permute-start(bf16[12,64,128]{2,1,0:T(8,128)(2,1)S(1)} %get-tuple-element.257), channel_id=1, source_target_pairs={{0,16},{8,24},{16,0},{24,8},{1,17},{9,25},{17,1},{25,9},{2,18},{10... | collective-permute-start | bytes 589832 | tf_op jit(solution)/shard_map/ppermute | solution.py:754
  94.3 6.4 %collective-permute-start.22 = (bf16[12,64,128]{2,1,0:T(8,128)(2,1)S(1)}, bf16[12,64,128]{2,1,0:T(8,128)(2,1)S(1)}, u32[]{:S(2)}, u32[]{:S(2)}) collective-permute-start(bf16[12,64,128]{2,1,0:T(8,128)(2,1)S(1)} %get-tuple-element.258), channel_id=1, source_target_pairs={{0,8},{8,0},{16,24},{24,16},{1,9},{9,1},{17,25},{25,17},{2,10},{10... | collective-permute-start | bytes 589832 | tf_op jit(solution)/shard_map/ppermute | solution.py:754
  102.7 2.5 %collective-permute-start.28 = (bf16[2,4,64,800]{3,2,1,0:T(8,128)(2,1)S(1)}, bf16[2,4,64,800]{3,2,1,0:T(8,128)(2,1)S(1)}, u32[]{:S(2)}, u32[]{:S(2)}) collective-permute-start(bf16[2,4,64,800]{3,2,1,0:T(8,128)(2,1)S(1)} %get-tuple-element.284), channel_id=1, source_target_pairs={{0,1},{1,0},{2,3},{3,2},{4,5},{5,4},{6,7},{7,6},{8,9},{9,8},{10,11... | collective-permute-start | bytes 2457608 | tf_op jit(solution)/shard_map/ppermute | solution.py:754
  106.0 24.5 %collective-permute-start.29 = (bf16[2,2,64,800]{3,2,1,0:T(8,128)(2,1)S(1)}, bf16[2,2,64,800]{3,2,1,0:T(8,128)(2,1)S(1)}, u32[]{:S(2)}, u32[]{:S(2)}) collective-permute-start(bf16[2,2,64,800]{3,2,1,0:T(8,128)(2,1)S(1)} %get-tuple-element.285), channel_id=1, source_target_pairs={{0,2},{1,3},{2,0},{3,1},{4,6},{5,7},{6,4},{7,5},{8,10},{9,11},{10,... | collective-permute-start | bytes 1228808 | tf_op jit(solution)/shard_map/ppermute | solution.py:754
  108.3 14.6 %collective-permute-start.25 = (bf16[24,32,128]{2,1,0:T(8,128)(2,1)S(1)}, bf16[24,32,128]{2,1,0:T(8,128)(2,1)S(1)}, u32[]{:S(2)}, u32[]{:S(2)}) collective-permute-start(bf16[24,32,128]{2,1,0:T(8,128)(2,1)S(1)} %get-tuple-element.277), channel_id=1, source_target_pairs={{0,2},{1,3},{2,0},{3,1},{4,6},{5,7},{6,4},{7,5},{8,10},{9,11},{10,... | collective-permute-start | bytes 589832 | tf_op jit(solution)/shard_map/ppermute | solution.py:754
  109.4 16.6 %collective-permute-start.27 = (bf16[13,64,128]{2,1,0:T(8,128)(2,1)S(1)}, bf16[13,64,128]{2,1,0:T(8,128)(2,1)S(1)}, u32[]{:S(2)}, u32[]{:S(2)}) collective-permute-start(bf16[13,64,128]{2,1,0:T(8,128)(2,1)S(1)} %get-tuple-element.282), channel_id=1, source_target_pairs={{0,8},{8,0},{16,24},{24,16},{1,9},{9,1},{17,25},{25,17},{2,10},{10... | collective-permute-start | bytes 638984 | tf_op jit(solution)/shard_map/ppermute | solution.py:754
  123.4 7.1 %collective-permute-start.26 = (bf16[24,16,128]{2,1,0:T(8,128)(2,1)S(1)}, bf16[24,16,128]{2,1,0:T(8,128)(2,1)S(1)}, u32[]{:S(2)}, u32[]{:S(2)}) collective-permute-start(bf16[24,16,128]{2,1,0:T(8,128)(2,1)S(1)} %get-tuple-element.279), channel_id=1, source_target_pairs={{0,4},{1,5},{2,6},{3,7},{4,0},{5,1},{6,2},{7,3},{8,12},{9,13},{10,... | collective-permute-start | bytes 294920 | tf_op jit(solution)/shard_map/ppermute | solution.py:754
  131.2 15.3 %collective-permute-start.32 = (bf16[2,1,64,800]{3,2,1,0:T(8,128)(2,1)S(1)}, bf16[2,1,64,800]{3,2,1,0:T(8,128)(2,1)S(1)}, u32[]{:S(2)}, u32[]{:S(2)}) collective-permute-start(bf16[2,1,64,800]{3,2,1,0:T(8,128)(2,1)S(1)} %get-tuple-element.292), channel_id=1, source_target_pairs={{0,4},{1,5},{2,6},{3,7},{4,0},{5,1},{6,2},{7,3},{8,12},{9,13},{10,... | collective-permute-start | bytes 614408 | tf_op jit(solution)/shard_map/ppermute | solution.py:754
  133.0 13.5 %collective-permute-start.31 = (bf16[13,32,128]{2,1,0:T(8,128)(2,1)S(1)}, bf16[13,32,128]{2,1,0:T(8,128)(2,1)S(1)}, u32[]{:S(2)}, u32[]{:S(2)}) collective-permute-start(bf16[13,32,128]{2,1,0:T(8,128)(2,1)S(1)} %get-tuple-element.289), channel_id=1, source_target_pairs={{0,16},{8,24},{16,0},{24,8},{1,17},{9,25},{17,1},{25,9},{2,18},{10... | collective-permute-start | bytes 319496 | tf_op jit(solution)/shard_map/ppermute | solution.py:754
  134.7 11.8 %collective-permute-start.30 = (bf16[24,16,128]{2,1,0:T(8,128)(2,1)S(1)}, bf16[24,16,128]{2,1,0:T(8,128)(2,1)S(1)}, u32[]{:S(2)}, u32[]{:S(2)}) collective-permute-start(bf16[24,16,128]{2,1,0:T(8,128)(2,1)S(1)} %shard_map.363.refs_1_), channel_id=1, source_target_pairs={{0,4},{1,5},{2,6},{3,7},{4,0},{5,1},{6,2},{7,3},{8,12},{9,13},{10,... | collective-permute-start | bytes 294920 | tf_op jit(solution)/shard_map/ppermute | solution.py:754
  136.5 22.4 %collective-permute-start.38 = (bf16[368,512]{1,0:T(8,128)(2,1)S(1)}, bf16[368,512]{1,0:T(8,128)(2,1)S(1)}, u32[]{:S(2)}, u32[]{:S(2)}) collective-permute-start(bf16[368,512]{1,0:T(8,128)(2,1)S(1)} %get-tuple-element.304), channel_id=1, source_target_pairs={{0,8},{8,0},{16,24},{24,16},{1,9},{9,1},{17,25},{25,17},{2,10},{10... | collective-permute-start | bytes 1130504 | tf_op jit(solution)/shard_map/ppermute | solution.py:754
  147.1 8.7 %collective-permute-start.33 = (bf16[24,32,128]{2,1,0:T(8,128)(2,1)S(1)}, bf16[24,32,128]{2,1,0:T(8,128)(2,1)S(1)}, u32[]{:S(2)}, u32[]{:S(2)}) collective-permute-start(bf16[24,32,128]{2,1,0:T(8,128)(2,1)S(1)} %shard_map.366.refs_1_), channel_id=1, source_target_pairs={{0,2},{1,3},{2,0},{3,1},{4,6},{5,7},{6,4},{7,5},{8,10},{9,11},{10,... | collective-permute-start | bytes 589832 | tf_op jit(solution)/shard_map/ppermute | solution.py:754
  147.2 19.8 %collective-permute-start.39 = (bf16[368,512]{1,0:T(8,128)(2,1)S(1)}, bf16[368,512]{1,0:T(8,128)(2,1)S(1)}, u32[]{:S(2)}, u32[]{:S(2)}) collective-permute-start(bf16[368,512]{1,0:T(8,128)(2,1)S(1)} %get-tuple-element.305), channel_id=1, source_target_pairs={{0,16},{8,24},{16,0},{24,8},{1,17},{9,25},{17,1},{25,9},{2,18},{10... | collective-permute-start | bytes 1130504 | tf_op jit(solution)/shard_map/ppermute | solution.py:754
  148.3 18.7 %collective-permute-start.40 = (bf16[368,512]{1,0:T(8,128)(2,1)S(1)}, bf16[368,512]{1,0:T(8,128)(2,1)S(1)}, u32[]{:S(2)}, u32[]{:S(2)}) collective-permute-start(bf16[368,512]{1,0:T(8,128)(2,1)S(1)} %get-tuple-element.306), channel_id=1, source_target_pairs={{0,24},{8,16},{16,8},{24,0},{1,25},{9,17},{17,9},{25,1},{2,26},{10... | collective-permute-start | bytes 1130504 | tf_op jit(solution)/shard_map/ppermute | solution.py:754
  150.6 5.2 %collective-permute-start.34 = (bf16[13,16,128]{2,1,0:T(8,128)(2,1)S(1)}, bf16[13,16,128]{2,1,0:T(8,128)(2,1)S(1)}, u32[]{:S(2)}, u32[]{:S(2)}) collective-permute-start(bf16[13,16,128]{2,1,0:T(8,128)(2,1)S(1)} %get-tuple-element.296), channel_id=1, source_target_pairs={{0,4},{1,5},{2,6},{3,7},{4,0},{5,1},{6,2},{7,3},{8,12},{9,13},{10,... | collective-permute-start | bytes 159752 | tf_op jit(solution)/shard_map/ppermute | solution.py:754
  156.4 13.1 %collective-permute-start.35 = (bf16[12,64,128]{2,1,0:T(8,128)(2,1)S(1)}, bf16[12,64,128]{2,1,0:T(8,128)(2,1)S(1)}, u32[]{:S(2)}, u32[]{:S(2)}) collective-permute-start(bf16[12,64,128]{2,1,0:T(8,128)(2,1)S(1)} %get-tuple-element.299.refs_1_), channel_id=1, source_target_pairs={{0,16},{8,24},{16,0},{24,8},{1,17},{9,25},{17,1},{25,9},{2,18},{10... | collective-permute-start | bytes 589832 | tf_op jit(solution)/shard_map/ppermute | solution.py:754
  157.4 12.2 %collective-permute-start.36 = (bf16[12,64,128]{2,1,0:T(8,128)(2,1)S(1)}, bf16[12,64,128]{2,1,0:T(8,128)(2,1)S(1)}, u32[]{:S(2)}, u32[]{:S(2)}) collective-permute-start(bf16[12,64,128]{2,1,0:T(8,128)(2,1)S(1)} %get-tuple-element.300.refs_1_), channel_id=1, source_target_pairs={{0,8},{8,0},{16,24},{24,16},{1,9},{9,1},{17,25},{25,17},{2,10},{10... | collective-permute-start | bytes 589832 | tf_op jit(solution)/shard_map/ppermute | solution.py:754
  159.0 8.1 %collective-permute-start.37 = (bf16[13,16,128]{2,1,0:T(8,128)(2,1)S(1)}, bf16[13,16,128]{2,1,0:T(8,128)(2,1)S(1)}, u32[]{:S(2)}, u32[]{:S(2)}) collective-permute-start(bf16[13,16,128]{2,1,0:T(8,128)(2,1)S(1)} %shard_map.369.refs_1_), channel_id=1, source_target_pairs={{0,4},{1,5},{2,6},{3,7},{4,0},{5,1},{6,2},{7,3},{8,12},{9,13},{10,... | collective-permute-start | bytes 159752 | tf_op jit(solution)/shard_map/ppermute | solution.py:754
  170.1 11.8 %collective-permute-start.42 = (bf16[12,128,128]{2,1,0:T(8,128)(2,1)S(1)}, bf16[12,128,128]{2,1,0:T(8,128)(2,1)S(1)}, u32[]{:S(2)}, u32[]{:S(2)}) collective-permute-start(bf16[12,128,128]{2,1,0:T(8,128)(2,1)S(1)} %shard_map.373.refs_1_), channel_id=1, source_target_pairs={{0,16},{8,24},{16,0},{24,8},{1,17},{9,25},{17,1},{25,9},{2,18},{10... | collective-permute-start | bytes 1179656 | tf_op jit(solution)/shard_map/ppermute | solution.py:754
  171.8 10.1 %collective-permute-start.41 = (bf16[12,128,128]{2,1,0:T(8,128)(2,1)S(1)}, bf16[12,128,128]{2,1,0:T(8,128)(2,1)S(1)}, u32[]{:S(2)}, u32[]{:S(2)}) collective-permute-start(bf16[12,128,128]{2,1,0:T(8,128)(2,1)S(1)} %shard_map.372.refs_1_), channel_id=1, source_target_pairs={{0,8},{8,0},{16,24},{24,16},{1,9},{9,1},{17,25},{25,17},{2,10},{10... | collective-permute-start | bytes 1179656 | tf_op jit(solution)/shard_map/ppermute | solution.py:754
  173.5 8.4 %collective-permute-start.43 = (bf16[13,32,128]{2,1,0:T(8,128)(2,1)S(1)}, bf16[13,32,128]{2,1,0:T(8,128)(2,1)S(1)}, u32[]{:S(2)}, u32[]{:S(2)}) collective-permute-start(bf16[13,32,128]{2,1,0:T(8,128)(2,1)S(1)} %shard_map.371.refs_1_), channel_id=1, source_target_pairs={{0,16},{8,24},{16,0},{24,8},{1,17},{9,25},{17,1},{25,9},{2,18},{10... | collective-permute-start | bytes 319496 | tf_op jit(solution)/shard_map/ppermute | solution.py:754
  182.5 9.1 %collective-permute-start.45 = (bf16[12,256,128]{2,1,0:T(8,128)(2,1)S(1)}, bf16[12,256,128]{2,1,0:T(8,128)(2,1)S(1)}, u32[]{:S(2)}, u32[]{:S(2)}) collective-permute-start(bf16[12,256,128]{2,1,0:T(8,128)(2,1)S(1)} %shard_map.376.refs_3_), channel_id=1, source_target_pairs={{0,1},{1,0},{2,3},{3,2},{4,5},{5,4},{6,7},{7,6},{8,9},{9,8},{10,11... | collective-permute-start | bytes 2359304 | tf_op jit(solution)/shard_map/ppermute | solution.py:754
  183.2 8.4 %collective-permute-start.44 = (bf16[12,256,128]{2,1,0:T(8,128)(2,1)S(1)}, bf16[12,256,128]{2,1,0:T(8,128)(2,1)S(1)}, u32[]{:S(2)}, u32[]{:S(2)}) collective-permute-start(bf16[12,256,128]{2,1,0:T(8,128)(2,1)S(1)} %shard_map.375.refs_1_), channel_id=1, source_target_pairs={{0,1},{1,0},{2,3},{3,2},{4,5},{5,4},{6,7},{7,6},{8,9},{9,8},{10,11... | collective-permute-start | bytes 2359304 | tf_op jit(solution)/shard_map/ppermute | solution.py:754
  184.4 7.2 %collective-permute-start.46 = (bf16[13,64,128]{2,1,0:T(8,128)(2,1)S(1)}, bf16[13,64,128]{2,1,0:T(8,128)(2,1)S(1)}, u32[]{:S(2)}, u32[]{:S(2)}) collective-permute-start(bf16[13,64,128]{2,1,0:T(8,128)(2,1)S(1)} %shard_map.374.refs_1_), channel_id=1, source_target_pairs={{0,8},{8,0},{16,24},{24,16},{1,9},{9,1},{17,25},{25,17},{2,10},{10... | collective-permute-start | bytes 638984 | tf_op jit(solution)/shard_map/ppermute | solution.py:754
  192.2 11.0 %collective-permute-start.47 = (bf16[13,128,128]{2,1,0:T(8,128)(2,1)S(1)}, bf16[13,128,128]{2,1,0:T(8,128)(2,1)S(1)}, u32[]{:S(2)}, u32[]{:S(2)}) collective-permute-start(bf16[13,128,128]{2,1,0:T(8,128)(2,1)S(1)} %shard_map.377.refs_1_), channel_id=1, source_target_pairs={{0,2},{1,3},{2,0},{3,1},{4,6},{5,7},{6,4},{7,5},{8,10},{9,11},{10,... | collective-permute-start | bytes 1277960 | tf_op jit(solution)/shard_map/ppermute | solution.py:754
  203.8 9.1 %collective-permute-start.48 = (bf16[13,256,128]{2,1,0:T(8,128)(2,1)S(1)}, bf16[13,256,128]{2,1,0:T(8,128)(2,1)S(1)}, u32[]{:S(2)}, u32[]{:S(2)}) collective-permute-start(bf16[13,256,128]{2,1,0:T(8,128)(2,1)S(1)} %shard_map.378.refs_1_), channel_id=1, source_target_pairs={{0,1},{1,0},{2,3},{3,2},{4,5},{5,4},{6,7},{7,6},{8,9},{9,8},{10,11... | collective-permute-start | bytes 2555912 | tf_op jit(solution)/shard_map/ppermute | solution.py:754

commit v2 on v1

--- a/solution.py
+++ b/solution.py
@@ -14,6 +14,10 @@
 LANES = 128
 GROUPS = 4
 FAR = -1e30
+RATE = 1.15e9
+COST_P = 0.0
+COST_Q = 1.0
+COST_K = 2.6
 
 
 def dims(left, right, a, b):
@@ -86,6 +90,15 @@
 
 def density(value):
     return jnp.exp(-0.5 * value * value) * np.float32(0.3989422804014327)
+
+
+class Chain:
+    def __init__(self, refs):
+        self.refs = refs
+
+    def __setitem__(self, index, value):
+        size = self.refs[0].shape[0]
+        self.refs[index // size][index % size] = value
 
 
 def put_halves(core, value, index, keep_ref, send_ref, scratch):
@@ -99,33 +112,49 @@
         send_ref[index + block] = scratch[pl.ds(other, half), lanes].astype(BF)
 
 
-def start_kernel(
-    ids, up, down, tokens, cots, misc, send0, send1, send2, send3, first, second, turned, sems, *, rows_used
-):
-    pb, core = ids[0], ids[1]
-    cut = first.shape[0]
+def pick_kernel(ids, up, down, *refs):
+    outs, sems = refs[:4], refs[4]
+    core = ids[1]
+    units = up.shape[0]
+    starts = (0, units - outs[1].shape[0], units - outs[2].shape[0], 0)
     for side, ref in enumerate((up, down)):
 
         @pl.when(core == side)
         def _():
-            one = pltpu.make_async_copy(ref.at[pl.ds(0, cut)], first, sems.at[0])
-            two = pltpu.make_async_copy(ref.at[pl.ds(cut, cut)], second, sems.at[1])
-            one.start()
-            two.start()
-            one.wait()
-            two.wait()
-
+            copies = []
+            for n, (out, start) in enumerate(zip(outs, starts)):
+                half = out.shape[0] // 2
+                for m in range(2):
+                    copies.append(
+                        pltpu.make_async_copy(
+                            ref.at[pl.ds(start + m * half, half)],
+                            out.at[pl.ds(m * half, half)],
+                            sems.at[2 * n + m],
+                        )
+                    )
+            for copy in copies:
+                copy.start()
+            for copy in copies:
+                copy.wait()
+
+
+def start_kernel(
+    ids, tokens, cots, misc, send0, send1, send2, send3, flat, turned, *, rows_used
+):
+    pb = ids[0]
     rows, width2 = turned.shape
     width = width2 // 2
     block = rows // GROUPS
-    count = tokens.shape[0]
+    count = rows_used * GROUPS
+    for q in range(rows_used):
+        flat[q * GROUPS : (q + 1) * GROUPS, :width] = tokens[q].astype(F32)
+        flat[q * GROUPS : (q + 1) * GROUPS, width:] = cots[q].astype(F32)
     place = lax.broadcasted_iota(jnp.int32, (rows, count), 0)
     query = lax.broadcasted_iota(jnp.int32, (rows, count), 1)
     hit = query == lax.rem(place, block) * GROUPS + lax.div(place, block)
     used = lax.rem(place, block) < rows_used
     chosen = jnp.where(jnp.logical_and(hit, used), 1.0, 0.0).astype(BF)
-    turned[:, :width] = nn(chosen, tokens[...])
-    turned[:, width:] = nn(chosen, cots[...])
+    turned[...] = nn(chosen, flat[...].astype(BF))
     for b in range(GROUPS):
         at = b * block + rows_used
         turned[at : at + 2, :width] = misc[2:4, :].astype(F32)
@@ -162,6 +191,7 @@
 
 def forward_kernel(
     ids,
+    mask,
     own,
     got1,
     got2,
@@ -197,11 +227,11 @@
     xhat2_out,
     rstd2_out,
     bups_out,
+    h2b_out,
     scores,
     pos_ref,
     *,
     rows_used,
-    mask_at,
 ):
     pb = ids[0]
     width = pos_ref.shape[1]
@@ -250,7 +280,7 @@
         top = jnp.full((8, 2 * rows), FAR, F32)
         for j in range(GROUPS):
             here = slice(j * padded, (j + 1) * padded)
-            live = jnp.where(ids[mask_at + pb * GROUPS + j] > 0, 0.0, -1000000000.0).astype(F32)
+            live = jnp.where(mask[pb, j] > 0, 0.0, -1000000000.0).astype(F32)
             s = nt(k_ref[here, lanes], queries) + jnp.where(slot_row < used, live, FAR)
             scores[here] = s
             top = jnp.maximum(top, eights(s, jnp.max))
@@ -269,18 +299,71 @@
     xhat, rstd = norm(h1 + nn(cm_out[...], cross_out[...]) + row(cross_bias, 2))
     xhat2_out[...] = xhat
     rstd2_out[...] = rstd
-    h2_out[...] = xhat * row(gains, 1) + row(shifts, 1)
-
-
-def ffn_kernel(
+    h2 = xhat * row(gains, 1) + row(shifts, 1)
+    h2_out[...] = h2
+    h2b_out[...] = h2.astype(BF)
+
+
+def ffn_first_kernel(
+    ids, h2_ref, bups, up_own, down_own, fd0, fd1, sd0, sd1, down_out, pre_ref, weights, sems
+):
+    copies = gather_weights(ids[1], weights, sems, ((fd0, fd1), (sd0, sd1)))
+    h2 = h2_ref[...]
+    down = jnp.zeros(h2.shape, F32)
+    for p in range(2):
+        if p:
+            for copy in copies:
+                for one in copy:
+                    one.wait()
+        up = weights[0, 0] if p else up_own[...]
+        dn = weights[1, 0] if p else down_own[...]
+        pre = nt(h2, up) + bias_of(bups, 3 * p, up.shape[0])
+        pre_ref[p] = pre
+        down = down + nn((pre * cdf(pre)).astype(BF), dn)
+    down_out[...] = down
+
+
+def gather_weights(core, weights, sems, sides):
+    units = weights.shape[2]
+    copies = []
+    for n in range(len(sides[0])):
+        take = units // 2
+        source, start = (0, 0) if n % 2 == 0 else (sides[0][n].shape[0] - take, take)
+        copies.append(
+            [
+                pltpu.make_async_copy(
+                    refs[n].at[pl.ds(source, take)],
+                    weights.at[core if side == 0 else 1 - core, n // 2, pl.ds(start, take)],
+                    sems.at[side, n],
+                )
+                for side, refs in enumerate(sides)
+            ]
+        )
+        for one in copies[-1]:
+            one.start()
+    return copies
+
+
+def bias_of(bups, p, units):
+    width = bups.shape[1]
+    return jnp.concatenate(
+        [bups[2 * p : 2 * p + 1], bups[2 * p + 1 : 2 * p + 2, : units - width]], axis=1
+    )
+
+
+def ffn_second_kernel(
     ids,
     h2_ref,
+    h2b_ref,
     cot_ref,
     xhat2_ref,
     rstd2_ref,
     bups,
     up_own,
     down_own,
+    down_ref,
+    pre_ref,
+    far,
     misc,
     gains,
     shifts,
@@ -288,73 +371,53 @@
     fx1,
     fy0,
     fy1,
-    fd0,
-    fd1,
     sx0,
     sx1,
     sy0,
     sy1,
-    sd0,
-    sd1,
     res_out,
     ops_out,
     g2_out,
     small_out,
     bup_out,
-    weights,
-    pre_ref,
+    near,
     sems,
 ):
-    core = ids[1]
-    width = h2_ref.shape[1]
+    copies = gather_weights(ids[1], near, sems, ((fx0, fx1, fy0, fy1), (sx0, sx1, sy0, sy1)))
+    h2 = h2_ref[...]
+    width = h2.shape[1]
     units = up_own.shape[0]
-    cut = units // 2
-    copies = []
-    for side, refs in enumerate(((fx0, fx1, fy0, fy1, fd0, fd1), (sx0, sx1, sy0, sy1, sd0, sd1))):
-        to = core if side == 0 else 1 - core
-        copies.append(
-            [
-                pltpu.make_async_copy(
-                    ref, weights.at[to, n // 2, pl.ds(n % 2 * cut, cut)], sems.at[side, n]
-                )
-                for n, ref in enumerate(refs)
-            ]
-        )
-    for one in copies:
-        for copy in one:
-            copy.start()
-    h2 = h2_ref[...]
-    h2b = h2.astype(BF)
-    ops_out[:, :width] = h2b
-    down = jnp.zeros(h2.shape, F32)
-    for p in range(4):
-        if p > 0:
-            for one in copies:
-                one[2 * p - 2].wait()
-                one[2 * p - 1].wait()
-        up = up_own[...] if p == 0 else weights[0, p - 1]
-        dn = down_own[...] if p == 0 else weights[1, p - 1]
-        bias = jnp.concatenate(
-            [bups[2 * p : 2 * p + 1], bups[2 * p + 1 : 2 * p + 2, : units - width]], axis=1
-        )
-        pre = nt(h2b, up) + bias
-        pre_ref[p] = pre
-        down = down + nn((pre * cdf(pre)).astype(BF), dn)
+    h2b = h2b_ref[...]
+    down = down_ref[...]
+    pres = [pre_ref[0]]
+    for p in range(2):
+        for copy in copies[2 * p : 2 * p + 2]:
+            for one in copy:
+                one.wait()
+        pre = nt(h2b, near[0, p]) + bias_of(bups, p + 1, units)
+        pres.append(pre)
+        down = down + nn((pre * cdf(pre)).astype(BF), near[1, p])
+    pres.append(pre_ref[1])
     xhat, rstd = norm(h2 + down + row(misc, 1))
     res_out[...] = (xhat * row(gains, 2) + row(shifts, 2)).astype(BF)
     g3, dgain3, dshift3 = norm_back(xhat, rstd, row(gains, 2), cot_ref[...].astype(F32))
     gb = g3.astype(BF)
+    ops_out[:, :width] = h2b
     ops_out[:, width:] = gb
     gh = g3
-    for p in range(4):
-        up = up_own[...] if p == 0 else weights[0, p - 1]
-        dn = down_own[...] if p == 0 else weights[1, p - 1]
+    for p, (up, dn) in enumerate(
+        (
+            (up_own[...], down_own[...]),
+            (near[0, 0], near[1, 0]),
+            (near[0, 1], near[1, 1]),
+            (far[0, 0], far[1, 0]),
+        )
+    ):
+        pre = pres[p]
         ga = nt(gb, dn).astype(BF).astype(F32)
-        pre = pre_ref[p]
         gp = (ga * (cdf(pre) + pre * density(pre))).astype(BF)
-        total = column_sum(gp)
         bup_out[p] = jnp.concatenate(
-            [total, jnp.zeros((1, 2 * width - units), F32)], axis=1
+            [column_sum(gp), jnp.zeros((1, 2 * width - units), F32)], axis=1
         )
         gh = gh + nn(gp, up)
     g2, dgain2, dshift2 = norm_back(xhat2_ref[...], rstd2_ref[...], row(gains, 1), gh)
@@ -397,7 +460,10 @@
     gpos_out,
     small_out,
     keep,
-    send,
+    send0,
+    send1,
+    send2,
+    send3,
     dp_ref,
     work,
     gq_ref,
@@ -405,6 +471,7 @@
     gv_ref,
 ):
     core = ids[1]
+    send = Chain((send0, send1, send2, send3))
     width = x_ref.shape[1]
     rows = x_ref.shape[0]
     g2 = g2_ref[...]
@@ -461,10 +528,11 @@
     put_halves(core, tn(x_ref[...], gv), 20, keep, send, work)
 
 
-def ffn_grad_kernel(ids, own, got1, got2, got3, up_own, misc, down_own, keep, send, work):
+def ffn_grad_kernel(ids, *refs):
+    up_own, misc, down_own, keep, send0, send1, work = refs[4:]
     core = ids[1]
     units, width = up_own.shape
-    ops = jnp.concatenate([ref[...] for ref in (own, got1, got2, got3)], axis=0)
+    ops = jnp.concatenate([ref[...] for ref in refs[:4]], axis=0)
     inputs, branch = ops[:, :width], ops[:, width:]
     bias = jnp.concatenate([row(misc, 2), row(misc, 3)[:, : units - width]], axis=1)
     pre = nt(inputs, up_own[...]) + bias
@@ -479,19 +547,20 @@
             mine = pl.multiple_of((2 * block + core) * size, size)
             other = pl.multiple_of((2 * block + 1 - core) * size, size)
             keep[side, block] = work[pl.ds(mine, size), :].astype(BF)
-            send[side, block] = work[pl.ds(other, size), :].astype(BF)
-
-
-def ffn_fold_kernel(ids, keep, got, stay, go, *, bit):
-    for side in range(keep.shape[0]):
+            (send0, send1)[side][block] = work[pl.ds(other, size), :].astype(BF)
+
+
+def ffn_fold_kernel(ids, keep, got0, got1, stay, go0, go1, *, bit):
+    for side, (got, go) in enumerate(((got0, go0), (got1, go1))):
         for block in range(stay.shape[1]):
-            for ref, at in ((stay, 2 * block + ids[bit]), (go, 2 * block + 1 - ids[bit])):
-                ref[side, block] = plus(keep[side, at], got[side, at])
-
-
-def ffn_finish_kernel(ids, keep, got, up_grad, down_grad):
-    for side, ref in enumerate((up_grad, down_grad)):
-        ref[...] = keep[side, 0].astype(F32) + got[side, 0].astype(F32)
+            mine, other = 2 * block + ids[bit], 2 * block + 1 - ids[bit]
+            go[block] = plus(keep[side, other], got[other])
+            stay[side, block] = plus(keep[side, mine], got[mine])
+
+
+def ffn_finish_kernel(ids, keep, got0, got1, up_grad, down_grad):
+    up_grad[...] = keep[0, 0].astype(F32) + got0[0].astype(F32)
+    down_grad[...] = keep[1, 0].astype(F32) + got1[0].astype(F32)
 
 
 def memory_back_kernel(
@@ -511,6 +580,7 @@
     small_a,
     small_b,
     bup,
+    held,
     rows0,
     rows1,
     rows2,
@@ -592,9 +662,13 @@
     mine = pl.multiple_of(core * half, half)
     other = pl.multiple_of((1 - core) * half, half)
     for b in range(4):
-        lanes = slice(b * LANES, (b + 1) * LANES)
-        out[pl.ds(mine, half), lanes] = own[index + b].astype(F32)
-        out[pl.ds(other, half), lanes] = got[index + b].astype(F32)
+        put_block(mine, other, half, out, b, own, got, index + b)
+
+
+def put_block(mine, other, half, out, b, own, got, index):
+    lanes = slice(b * LANES, (b + 1) * LANES)
+    out[pl.ds(mine, half), lanes] = own[index].astype(F32)
+    out[pl.ds(other, half), lanes] = got[index].astype(F32)
 
 
 def finish_chain_kernel(ids, own1, got1, own2, got2, cross_q, self_out, cross_out, self_proj):
@@ -607,19 +681,22 @@
 
 
 def finish_memory_kernel(
-    ids, own, got, cross_q, cross_, in_, pos_, self_bias_, cross_bias_, bup_, bdown_, gain_, shift_, inb_, small, *, rows_used
+    ids, own1, got1, cross_q, cross_, in_, pos_, self_bias_, cross_bias_, bup_, bdown_, gain_, shift_, inb_, small, *, rows_used
 ):
     core = ids[1]
     cross_[0] = cross_q[...]
-    put_whole(core, cross_.at[1], 0, own, got)
-    put_whole(core, cross_.at[2], 4, own, got)
-    put_whole(core, in_, 8, own, got)
+    half = own1.shape[1]
+    mine = pl.multiple_of(core * half, half)
+    other = pl.multiple_of((1 - core) * half, half)
+    for index in range(12):
+        out = (cross_.at[1], cross_.at[2], in_)[index // 4]
+        put_block(mine, other, half, out, index % 4, own1, got1, index)
     rows, width = small.shape
     block = rows // GROUPS
     for b in range(2):
         here = slice(b * rows, (b + 1) * rows)
-        first = own[12, here].astype(F32)
-        second = got[12, here].astype(F32)
+        first = own1[12, here].astype(F32)
+        second = got1[12, here].astype(F32)
         small[:, b * LANES : (b + 1) * LANES] = jnp.where(core == 0, first, second)
         small[:, (2 + b) * LANES : (3 + b) * LANES] = jnp.where(core == 0, second, first)
     for b in range(GROUPS):
@@ -639,10 +716,13 @@
     inb_[...] = spare(13)
 
 
-def order_kernel(ids, own, got1, got2, got3, out, grad, feats):
+def hold_kernel(ids, got1, got2, got3, branch, out):
+    out[...] = got1[:16, :LANES] + got2[:16, :LANES] + got3[:16, :LANES] + branch[:16, :LANES]
+
+
+def order_kernel(ids, own, got1, got2, got3, out, grad, feats, *, block):
     pb = ids[0]
     part, used = feats.shape[1], out.shape[1]
-    block = out.shape[1] // 16 * 16 + 16
     padded = own.shape[0] - 2 * block
     for k, ref in enumerate((own, got1, got2, got3)):
         feats[pb ^ k] = ref[0:part]
@@ -688,11 +768,46 @@
         return self.buffers[n][...]
 
 
-def call(kernel, args, outs, scratch=(), limit=16, near=True):
-    specs = [pl.BlockSpec(memory_space=pltpu.SMEM)]
-    values, extra, emitted, plans = [args[0]], [], [], [None]
+class Places:
+    def __getitem__(self, index):
+        if index == 0:
+            return lax.axis_index("pb")
+        axis, bit = BITS[index - 1]
+        return lax.rem(lax.div(lax.axis_index(axis), bit), 2)
+
+
+CORE, X_WAY, Y_WAY = ("dp", 1), ("pb", 1), ("pb", 2)
+BITS = [CORE, X_WAY, Y_WAY] + [("dp", 2 << n) for n in range(16)]
+
+
+def place_of(way):
+    return 1 + BITS.index(way)
+
+
+class Order:
+    def __init__(self):
+        self.token = None
+
+    def after(self, values):
+        if self.token is None:
+            return list(values)
+        return list(lax.optimization_barrier((*values, self.token)))[:-1]
+
+
+def call(order, kernel, args, outs, scratch=(), limit=16, near=True, micros=0.6, through=()):
+    through = order.after(through)
+    bare = order.after([arg.value if isinstance(arg, (Far, Raw)) else arg for arg in args])
+    args = [
+        Far(value, arg.parts, arg.emit)
+        if isinstance(arg, Far)
+        else Raw(value)
+        if isinstance(arg, Raw)
+        else value
+        for value, arg in zip(bare, args)
+    ]
+    specs, values, extra, emitted, plans = [], [], [], [], []
     outs = list(outs)
-    for arg in args[1:]:
+    for arg in args:
         if isinstance(arg, (Far, Raw)):
             value = arg.value
             specs.append(pl.BlockSpec(memory_space=pl.ANY))
@@ -709,15 +824,19 @@
                 shape = value.shape if arg.parts is None else value.shape[1:]
                 extra += [pltpu.VMEM(shape, value.dtype)] * count
             extra.append(pltpu.SemaphoreType.DMA((count,)))
+        elif jnp.issubdtype(arg.dtype, jnp.integer):
+            specs.append(pl.BlockSpec(memory_space=pltpu.SMEM))
+            values.append(arg)
+            plans.append(None)
         else:
             specs.append(pl.BlockSpec(memory_space=pltpu.VMEM))
             values.append(pltpu.with_memory_space_constraint(arg, pltpu.VMEM))
             plans.append(None)
 
     def body(*refs):
-        given, rest = list(refs[: len(args)]), refs[len(args) :]
+        given, rest = list(refs[: len(args)]), refs[len(args) + len(through) :]
         first, rest = rest[: len(outs)], rest[len(outs) :]
-        copies, rest = rest[: len(emitted)], rest[len(emitted) :]
+        copies, rest = rest[: len(emitted)], rest[len(emitted) + len(through) :]
         own, late = rest[: len(scratch)], rest[len(scratch) :]
         waits = []
         for index, plan in enumerate(plans):
@@ -732,21 +851,28 @@
                 buffers = [copies[place].at[part] for part in parts]
             given[index] = Late(given[index], buffers, late[sem], parts)
             waits.append(given[index])
-        kernel(*given, *first, *own)
+        kernel(Places(), *given, *first, *own)
         for one in waits:
             for n in sorted(one.waiting):
                 one.ready(n)
 
     whole = [(o, near) for o in outs] + [(o, True) for o in emitted]
-    return pl.pallas_call(
+    result = pl.pallas_call(
         body,
-        out_shape=[pltpu.VMEM(*o) if here else jax.ShapeDtypeStruct(*o) for o, here in whole],
-        in_specs=specs,
-        out_specs=[pl.BlockSpec(memory_space=pltpu.VMEM)] * len(whole),
+        out_shape=[pltpu.VMEM(*o) if here else jax.ShapeDtypeStruct(*o) for o, here in whole]
+        + [jax.ShapeDtypeStruct(value.shape, value.dtype) for value in through],
+        in_specs=specs + [pl.BlockSpec(memory_space=pl.ANY)] * len(through),
+        out_specs=[pl.BlockSpec(memory_space=pltpu.VMEM)] * len(whole)
+        + [pl.BlockSpec(memory_space=pl.ANY)] * len(through),
+        input_output_aliases={len(args) + n: len(whole) + n for n in range(len(through))},
         scratch_shapes=list(scratch) + extra,
         compiler_params=pltpu.CompilerParams(vmem_limit_bytes=limit * 1024 * 1024),
-        cost_estimate=pl.CostEstimate(flops=1, bytes_accessed=1, transcendentals=0),
-    )(*values)
+        cost_estimate=pl.CostEstimate(
+            flops=int(micros * RATE) + 1, bytes_accessed=int(micros * 3.7e6) + 1, transcendentals=0
+        ),
+    )(*values, *through)
+    order.token = result[0]
+    return result
 
 
 def swap(value, axis, bit):
@@ -760,6 +886,11 @@
 
 def plus(left, right):
     return (left.astype(F32) + right.astype(F32)).astype(BF)
+
+
+def bit_of(way):
+    axis, bit = way
+    return (lax.axis_index(axis) // bit) % 2
 
 
 def halve(keep, got, bit):
@@ -770,68 +901,87 @@
     return mine, other
 
 
-def fold(ids, groups):
+def fold(order, groups, micros=0.6):
     rows = groups[0][0][0][0].shape[1] // 2
     if rows % 16:
         result = []
-        for pieces, bit in groups:
-            done = [halve(keep[a:b], got[a:b], ids[bit]) for keep, got, a, b in pieces]
+        for pieces, way in groups:
+            done = [
+                halve(keep[a:b], got[a - m : b - m], bit_of(way)) for keep, got, a, b, m in pieces
+            ]
             result += [jnp.concatenate(side) for side in zip(*done)]
         return result
     args, outs = [], []
-    for pieces, bit in groups:
-        count = sum(b - a for _, _, a, b in pieces)
+    for pieces, way in groups:
+        count = sum(b - a for _, _, a, b, _ in pieces)
         outs += [((count, rows, LANES), BF)] * 2
-        for keep, got, _, _ in pieces:
+        for keep, got, _, _, _ in pieces:
             args += [keep, got]
 
     def kernel(ids, *refs):
         given, made = list(refs[: len(args)]), list(refs[len(args) :])
-        for pieces, bit in groups:
+        for pieces, way in groups:
             stay, go = made.pop(0), made.pop(0)
-            mine = pl.multiple_of(ids[bit] * rows, rows)
-            other = pl.multiple_of((1 - ids[bit]) * rows, rows)
+            bit = ids[place_of(way)]
+            mine = pl.multiple_of(bit * rows, rows)
+            other = pl.multiple_of((1 - bit) * rows, rows)
             at = 0
-            for _, _, a, b in pieces:
+            for _, _, a, b, m in pieces:
                 keep, got = given.pop(0), given.pop(0)
                 for block in range(a, b):
-                    for ref, start in ((stay, mine), (go, other)):
+                    for ref, start in ((go, other), (stay, mine)):
                         here = pl.ds(start, rows)
-                        ref[at] = plus(keep[block, here], got[block, here])
+                        ref[at] = plus(keep[block, here], got[block - m, here])
                     at += 1
 
-    return call(kernel, [ids, *args], outs, limit=4)
-
-
-def add_up(ids, keep, got):
-    if keep.shape[1] % 16:
-        return plus(keep, got)
-
-    def kernel(ids, keep, got, out):
-        out[...] = plus(keep[...], got[...])
-
-    return call(kernel, [ids, keep, got], [(keep.shape, BF)], limit=4)[0]
-
-
-def join(ids, value, got, bit, cuts=None):
-    blocks, rows, lanes = value.shape
-    cuts = cuts or [(0, blocks)]
-    if rows % 16:
-        full = jnp.where(
-            ids[bit] == 0, jnp.concatenate([value, got], 1), jnp.concatenate([got, value], 1)
-        )
-        return [full[a:b] for a, b in cuts]
-
-    def kernel(ids, value, got, *outs):
-        mine = pl.multiple_of(ids[bit] * rows, rows)
-        other = pl.multiple_of((1 - ids[bit]) * rows, rows)
-        for out, (a, b) in zip(outs, cuts):
-            for block in range(a, b):
-                out[block - a, pl.ds(mine, rows)] = value[block]
-                out[block - a, pl.ds(other, rows)] = got[block]
-
-    outs = [((b - a, 2 * rows, lanes), BF) for a, b in cuts]
-    return call(kernel, [ids, value, got], outs, limit=4)
+    return call(order, kernel, args, outs, limit=4, micros=micros)
+
+
+def add_up(order, pieces, micros=0.6):
+    if pieces[0][0].shape[1] % 16:
+        return jnp.concatenate([plus(keep, got) for keep, got in pieces])
+
+    def kernel(ids, *refs):
+        at = 0
+        for keep, got in zip(refs[0:-1:2], refs[1:-1:2]):
+            refs[-1][at : at + keep.shape[0]] = plus(keep[...], got[...])
+            at += keep.shape[0]
+
+    count = sum(keep.shape[0] for keep, _ in pieces)
+    shape = (count,) + pieces[0][0].shape[1:]
+    args = [ref for piece in pieces for ref in piece]
+    return call(order, kernel, args, [(shape, BF)], limit=4, micros=micros)[0]
+
+
+def join(order, pieces, micros=0.6, through=()):
+    if pieces[0][0].shape[1] % 16:
+        result = []
+        for value, got, way, cuts in pieces:
+            full = jnp.where(
+                bit_of(way) == 0, jnp.concatenate([value, got], 1), jnp.concatenate([got, value], 1)
+            )
+            result += [full[a:b] for a, b in cuts]
+        return result + list(through)
+    outs = []
+    for value, _, _, cuts in pieces:
+        outs += [((b - a, 2 * value.shape[1], LANES), BF) for a, b in cuts]
+
+    def kernel(ids, *refs):
+        given, made = list(refs[: 2 * len(pieces)]), list(refs[2 * len(pieces) :])
+        for _, _, way, cuts in pieces:
+            value, got = given.pop(0), given.pop(0)
+            rows = value.shape[1]
+            bit = ids[place_of(way)]
+            mine = pl.multiple_of(bit * rows, rows)
+            other = pl.multiple_of((1 - bit) * rows, rows)
+            for a, b in cuts:
+                out = made.pop(0)
+                for block in range(a, b):
+                    out[block - a, pl.ds(mine, rows)] = value[block]
+                    out[block - a, pl.ds(other, rows)] = got[block]
+
+    args = [ref for value, got, _, _ in pieces for ref in (value, got)]
+    return call(order, kernel, args, outs, limit=4, micros=micros, through=through)
 
 
 def on_device(
@@ -855,17 +1005,10 @@
     in_proj,
     in_bias,
 ):
-    pb = lax.axis_index("pb")
+    order = Order()
     pb_size = lax.axis_size("pb")
     dp_size = lax.axis_size("dp")
     ways = [("dp", 1 << i) for i in range(1, dp_size.bit_length() - 1)]
-    core_way, x_way, y_way = ("dp", 1), ("pb", 1), ("pb", 2)
-    bits = [core_way, x_way, y_way] + ways
-    ids = jnp.concatenate(
-        [jnp.stack([pb] + [bit_of(*way) for way in bits]).astype(jnp.int32), camera_mask.reshape(-1)]
-    )
-    at_of = {way: 1 + n for n, way in enumerate(bits)}
-    mask_at = 1 + len(bits)
     width = tokens.shape[2]
     used = tokens.shape[1]
     block = -(-used // 16) * 16
@@ -876,21 +1019,36 @@
     slots = padded * pb_size
     units = b_up.shape[0]
 
-    misc = jnp.concatenate([in_bias, b_down, b_up, jnp.zeros((2 * width - units,), BF)])
-    misc = misc.reshape(4, width)
     up, down = w_up.T, w_down.T
     cut = units // 2
-    turn = lambda value: value.transpose(1, 0, 2).reshape(-1, width)
-    *send, mine0, mine1 = call(
+    low, high, after, before = call(
+        order,
+        pick_kernel,
+        [Raw(up), Raw(down)],
+        [((cut, width), BF)] * 2 + [((cut + 16, width), BF)] * 2,
+        micros=1.4,
+        scratch=[pltpu.SemaphoreType.DMA((8,))],
+        limit=4,
+    )
+    fy0 = swap(low, *Y_WAY)
+    fx1 = swap(high, *X_WAY)
+    misc = (
+        jnp.pad(in_bias[None], ((0, 3), (0, 0)))
+        + jnp.pad(b_down[None], ((1, 2), (0, 0)))
+        + jnp.pad(jnp.pad(b_up, (0, 2 * width - units)).reshape(2, width), ((2, 0), (0, 0)))
+    )
+    turn = lambda value: value.transpose(1, 0, 2)
+    send = call(
+        order,
         functools.partial(start_kernel, rows_used=used),
-        [ids, Raw(up), Raw(down), turn(tokens), turn(out_grad), misc],
-        [((block, 2 * width), BF)] * 4 + [((cut, width), BF)] * 2,
-        scratch=[pltpu.VMEM((rows, 2 * width), F32), pltpu.SemaphoreType.DMA((2,))],
-    )
-    fx1 = swap(mine1, *x_way)
-    fy0 = swap(mine0, *y_way)
+        [turn(tokens), turn(out_grad), misc],
+        [((block, 2 * width), BF)] * 4,
+        scratch=[
+            pltpu.VMEM((used * pb_size, 2 * width), F32),
+            pltpu.VMEM((rows, 2 * width), F32),
+        ],
+    )
     got = [send[0]] + [swap(send[k], "pb", k) for k in range(1, pb_size)]
-
     column = np.arange(width)
     rate = 1.0 / 10000.0 ** ((column // 2 * 2) / width)
     angle = np.arange(padded)[:, None] * rate
@@ -908,9 +1066,9 @@
 
     wide = (slots, width)
     featp, ki, vi, ck, cv, in_proj, cross_proj = call(
+        order,
         memory_kernel,
         [
-            ids,
             Raw(features),
             Far(sines),
             Far(cosines),
@@ -921,21 +1079,24 @@
             Far(cross_bias),
         ],
         [(wide, BF)] * 5,
+        micros=0.0,
         scratch=[pltpu.VMEM((mem, width), BF), pltpu.SemaphoreType.DMA],
     )
-    ck, fx1, fy0, mine0, mine1, *got = lax.optimization_barrier(
-        (ck, fx1, fy0, mine0, mine1, *got)
-    )
-    fd0 = swap(fy0, *x_way)
-    fd1 = swap(fx1, *y_way)
-    fx0 = swap(mine0, *x_way)
-    fy1 = swap(mine1, *y_way)
+    fx1, fy0, after, before = order.after((fx1, fy0, after, before))
+    fx0 = swap(before, *X_WAY)
+    fy1 = swap(after, *Y_WAY)
+    fx1, fy0, *got = order.after((fx1, fy0, *got))
+    fd0 = swap(fy0, *X_WAY)
+    fd1 = swap(fx1, *Y_WAY)
+    sx1, sy0 = swap(fx1, *CORE), swap(fy0, *CORE)
+    got[0], sx1, sy0 = lax.optimization_barrier((got[0], sx1, sy0))
     flat = (rows, width)
     scores = (GROUPS, slots, 2 * rows)
-    (x, cot, ai, sq, sk, sv, ps, sm, xhat1, rstd1, ci, cq, pc, cm, h2, xhat2, rstd2, bups, self_proj, self_out, cross_out, norm_gain, norm_bias, up, down) = call(
-        functools.partial(forward_kernel, rows_used=used, mask_at=mask_at),
+    (x, cot, ai, sq, sk, sv, ps, sm, xhat1, rstd1, ci, cq, pc, cm, h2, xhat2, rstd2, bups, h2b, self_proj, self_out, cross_out, norm_gain, norm_bias, up, down) = call(
+        order,
+        functools.partial(forward_kernel, rows_used=used),
         [
-            ids,
+            camera_mask,
             *got,
             Far(query_pos),
             Far(self_proj, (0, 1, 2), emit=True),
@@ -970,28 +1131,43 @@
             (flat, F32),
             ((rows, 1), F32),
             ((2 * pb_size, width), F32),
+            (flat, BF),
         ],
+        micros=8.0,
         scratch=[pltpu.VMEM((slots, 2 * rows), F32), pltpu.VMEM(flat, F32)],
     )
-    fetched = [fx0, fx1, fy0, fy1, fd0, fd1]
-    h2, *fetched = lax.optimization_barrier((h2, *fetched))
-    swapped = [swap(value, *core_way) for value in fetched]
+    fd0, fd1 = order.after((fd0, fd1))
+    sd0, sd1 = swap(fd0, *CORE), swap(fd1, *CORE)
+    down_part, pre, far_weights = call(
+        order,
+        ffn_first_kernel,
+        [h2b, bups, up, down, Raw(fd0), Raw(fd1), Raw(sd0), Raw(sd1)],
+        [(flat, F32), ((2, rows, units), F32), ((2, 1, units, width), BF)],
+        micros=0.0,
+        scratch=[pltpu.SemaphoreType.DMA((2, 2))],
+    )
+    fx0, fy1 = order.after((fx0, fy1))
+    sx0, sy1 = swap(fx0, *CORE), swap(fy1, *CORE)
+    near = [fx0, fx1, fy0, fy1, sx0, sx1, sy0, sy1]
     res, ops, g2, small_a, bup = call(
-        ffn_kernel,
+        order,
+        ffn_second_kernel,
         [
-            ids,
             h2,
+            h2b,
             cot,
             xhat2,
             rstd2,
             bups,
             up,
             down,
+            down_part,
+            pre,
+            far_weights,
             misc,
             norm_gain,
             norm_bias,
-            *[Raw(value) for value in fetched],
-            *[Raw(value) for value in swapped],
+            *[Raw(value) for value in near],
         ],
         [
             (flat, BF),
@@ -1000,18 +1176,15 @@
             ((8, width), F32),
             ((pb_size, 1, 2 * width), F32),
         ],
-        scratch=[
-            pltpu.VMEM((2, 3, units, width), BF),
-            pltpu.VMEM((4, rows, units), F32),
-            pltpu.SemaphoreType.DMA((2, 6)),
-        ],
+        micros=6.0,
+        scratch=[pltpu.VMEM((2, 2, units, width), BF), pltpu.SemaphoreType.DMA((2, 4))],
     )
     others = [swap(ops, "pb", k) for k in range(1, pb_size)]
     halves = ((24, width // 2, LANES), BF)
-    ds, gcm, gx, gpos, small_b, keep12, send12 = call(
+    ds, gcm, gx, gpos, small_b, keep12, *sends12 = call(
+        order,
         backward_kernel,
         [
-            ids,
             g2,
             pc,
             ck,
@@ -1041,8 +1214,9 @@
             (flat, F32),
             ((8, width), F32),
             halves,
-            halves,
-        ],
+        ]
+        + [((6, width // 2, LANES), BF)] * 4,
+        micros=7.8,
         scratch=[
             pltpu.VMEM((slots, 2 * rows), BF),
             pltpu.VMEM((width, width), F32),
@@ -1051,12 +1225,36 @@
             pltpu.VMEM(flat, BF),
         ],
     )
-    ops, *others, send12 = lax.optimization_barrier((ops, *others, send12))
+    got12 = [swap(send, *CORE) for send in sends12]
+    piece = width // dp_size
+    (held,) = call(order, hold_kernel, [*others, gcm], [((16, LANES), BF)], limit=2, micros=2.0)
+    ka, sa, kb, sb = fold(
+        order,
+        [
+            ([(keep12, got12[0], 0, 6, 0), (keep12, got12[1], 6, 12, 6)], X_WAY),
+            ([(keep12, got12[2], 12, 18, 12), (keep12, got12[3], 18, 24, 18)], Y_WAY),
+        ],
+    )
+    ra, rb = swap(sa, *X_WAY), swap(sb, *Y_WAY)
+
+    def ffn_fold(keep, gots, micros):
+        way = ways[(dp_size // 2).bit_length() - keep.shape[1].bit_length()]
+        half = keep.shape[1] // 2
+        keep, *sends = call(
+            order,
+            functools.partial(ffn_fold_kernel, bit=place_of(way)),
+            [keep, *gots],
+            [((2, half, piece, units), BF)] + [((half, piece, units), BF)] * 2,
+            limit=4,
+            micros=micros,
+        )
+        return keep, [swap(send, *way) for send in sends]
+
     halves3 = ((13, width // 2, LANES), BF)
     *rows_out, keep3, send3 = call(
+        order,
         functools.partial(memory_back_kernel, rows_used=used),
         [
-            ids,
             ds,
             pc,
             cq,
@@ -1072,8 +1270,10 @@
             small_a,
             small_b,
             bup,
+            held,
         ],
         [((padded + 2 * block, width), BF)] * 4 + [halves3, halves3],
+        micros=6.4,
         scratch=[
             pltpu.VMEM(wide, BF),
             pltpu.VMEM(wide, BF),
@@ -1084,119 +1284,85 @@
         ],
     )
 
-    got12 = swap(send12, *core_way)
+    fkeep, *fsends = call(
+        order,
+        ffn_grad_kernel,
+        [ops, *others, up, misc, down],
+        [((2, dp_size // 2, piece, units), BF)] + [((dp_size // 2, piece, units), BF)] * 2,
+        micros=2.8,
+        scratch=[pltpu.VMEM((width, units), F32)],
+    )
+    fgots = [swap(send, *CORE) for send in fsends]
+    ra, rb, send3 = lax.optimization_barrier((ra, rb, send3))
+    got3 = swap(send3, *CORE)
+    z_way, far_ways = ways[0], ways[1:]
     ka, sa, kb, sb = fold(
-        ids, [([(keep12, got12, 0, 12)], at_of[x_way]), ([(keep12, got12, 12, 24)], at_of[y_way])]
-    )
-    ra, rb = swap(sa, *x_way), swap(sb, *y_way)
-    ra, rb, keep3, send3 = lax.optimization_barrier((ra, rb, keep3, send3))
-    got3 = swap(send3, *core_way)
-    ka, sa, kb, sb = fold(
-        ids, [([(ka, ra, 0, 12)], at_of[y_way]), ([(kb, rb, 0, 12)], at_of[x_way])]
-    )
-    ra, rb = swap(sa, *y_way), swap(sb, *x_way)
-    order3 = [ways[0], x_way, y_way] + ways[1:]
-    kc, sc = fold(ids, [([(keep3, got3, 0, 13)], at_of[order3[0]])])
-    rc = swap(sc, *order3[0])
-    piece = width // dp_size
-    fkeep, fsend = call(
-        ffn_grad_kernel,
-        [ids, ops, *others, up, misc, down],
-        [((2, dp_size // 2, piece, units), BF)] * 2,
-        scratch=[pltpu.VMEM((width, units), F32)],
-    )
-    ra, rb, rc, fsend, *rows_out = lax.optimization_barrier((ra, rb, rc, fsend, *rows_out))
-    fgot = swap(fsend, *core_way)
+        order, [([(ka, ra, 0, 12, 0)], Y_WAY), ([(kb, rb, 0, 12, 0)], X_WAY)], 0.3
+    )
+    ra, rb = swap(sa, *Y_WAY), swap(sb, *X_WAY)
+    kc, sc = fold(order, [([(keep3, got3, 0, 13, 0)], z_way)], 0.3)
+    rc = swap(sc, *z_way)
+    kab, sab = fold(order, [([(ka, ra, 0, 12, 0), (kb, rb, 0, 12, 0)], z_way)], 2.7)
+    rab = swap(sab, *z_way)
+    fkeep, fgots = ffn_fold(fkeep, fgots, 0.0)
+    kc, sc = fold(order, [([(kc, rc, 0, 13, 0)], X_WAY)], 0.3)
+    rc = swap(sc, *X_WAY)
+    vab = add_up(order, [(kab, rab)], 0.6)
+    for way in far_ways[:-1]:
+        rab = swap(vab, *way)
+        vab = add_up(order, [(vab, rab)], 0.3)
+    rab = swap(vab, *far_ways[-1])
+    kc, sc = fold(order, [([(kc, rc, 0, 13, 0)], Y_WAY)], 0.3)
+    rc = swap(sc, *Y_WAY)
     arrived = [rows_out[0]] + [swap(rows_out[k], "pb", k) for k in range(1, pb_size)]
-    kab, sab = fold(ids, [([(ka, ra, 0, 12), (kb, rb, 0, 12)], at_of[ways[0]])])
-    rab = swap(sab, *ways[0])
-    left = list(ways[1:])
-    left3 = order3[1:]
-    back, back3 = [], []
-    vab = vc = None
-    after = list(reversed(ways))
-    after3 = list(reversed(order3))
-    ab_done = False
-    pair_out = None
-    c_out = None
-    while c_out is None:
-        if left:
-            way = left.pop(0)
-            kab, sab = fold(ids, [([(kab, rab, 0, 24)], at_of[way])])
-            rab = swap(sab, *way)
-        elif vab is None:
-            vab = add_up(ids, kab, rab)
-            way = after.pop(0)
-            rab = swap(vab, *way)
-            last = way
-        elif after:
-            (vab,) = join(ids, vab, rab, at_of[last])
-            last = after.pop(0)
-            rab = swap(vab, *last)
-        elif pair_out is None:
-            va, vb = join(ids, vab, rab, at_of[last], [(0, 12), (12, 24)])
-            ra, rb = swap(va, *y_way), swap(vb, *x_way)
-            pair_out = 1
-        elif pair_out == 1:
-            (va,) = join(ids, va, ra, at_of[y_way])
-            (vb,) = join(ids, vb, rb, at_of[x_way])
-            ra, rb = swap(va, *x_way), swap(vb, *y_way)
-            pair_out = 2
-        elif pair_out == 2:
-            (va,) = join(ids, va, ra, at_of[x_way])
-            (vb,) = join(ids, vb, rb, at_of[y_way])
-            ra, rb = swap(va, *core_way), swap(vb, *core_way)
-            pair_out = 3
-        if left3:
-            way = left3.pop(0)
-            kc, sc = fold(ids, [([(kc, rc, 0, 13)], at_of[way])])
-            rc = swap(sc, *way)
-        elif vc is None:
-            vc = add_up(ids, kc, rc)
-            last3 = after3.pop(0)
-            rc = swap(vc, *last3)
-        elif after3:
-            (vc,) = join(ids, vc, rc, at_of[last3])
-            last3 = after3.pop(0)
-            rc = swap(vc, *last3)
-        else:
-            (c_out,) = join(ids, vc, rc, at_of[last3])
-        if ways and fkeep.shape[1] > 1:
-            way = ways[(dp_size // 2).bit_length() - fkeep.shape[1].bit_length()]
-            fkeep, fsend = call(
-                functools.partial(ffn_fold_kernel, bit=at_of[way]),
-                [ids, fkeep, fgot],
-                [((2, fkeep.shape[1] // 2, piece, units), BF)] * 2,
-                limit=4,
-            )
-            fgot = swap(fsend, *way)
-        if c_out is None:
-            names = [rab, rc, fgot] if pair_out is None else [ra, rb, rc, fgot]
-            if pair_out == 1:
-                names += arrived[1:]
-            names = lax.optimization_barrier(tuple(names))
-            if pair_out is None:
-                rab, rc, fgot = names
-            else:
-                ra, rb, rc, fgot = names[:4]
-            if pair_out == 1:
-                arrived[1:] = names[4:]
-                layer_out, grad_tokens, grad_features = call(
-                    order_kernel,
-                    [ids, *arrived],
-                    [(tokens.shape, BF), (tokens.shape, BF), ((pb_size, part, width), BF)],
-                    near=False,
-                )
+    while fkeep.shape[1] > 1:
+        fkeep, fgots = ffn_fold(fkeep, fgots, 0.0)
+    vc = add_up(order, [(kc, rc)], 0.3)
+    for way in far_ways[:-1]:
+        rc = swap(vc, *way)
+        vc = add_up(order, [(vc, rc)], 0.3)
+    rc = swap(vc, *far_ways[-1])
+    vab = add_up(order, [(vab, rab)], 0.3)
+    rab = swap(vab, *z_way)
+    vc = add_up(order, [(vc, rc)], 1.2)
+    rc = swap(vc, *Y_WAY)
+    rab, *arrived[1:3] = lax.optimization_barrier((rab, *arrived[1:3]))
+    va, vb = join(order, [(vab, rab, z_way, [(0, 12), (12, 24)])], 0.3)
+    ra, rb = swap(va, *Y_WAY), swap(vb, *X_WAY)
+    (vc,) = join(order, [(vc, rc, Y_WAY, [(0, 13)])], 1.2)
+    rc = swap(vc, *X_WAY)
+    ra, arrived[3] = lax.optimization_barrier((ra, arrived[3]))
+    va, vb = join(order, [(va, ra, Y_WAY, [(0, 12)]), (vb, rb, X_WAY, [(0, 12)])], 0.5)
+    ra, rb = swap(va, *X_WAY), swap(vb, *Y_WAY)
+    (vc,) = join(order, [(vc, rc, X_WAY, [(0, 13)])], 2.4)
+    rc = swap(vc, *z_way)
+    exchanged = call(
+        order,
+        functools.partial(order_kernel, block=block),
+        arrived,
+        [(tokens.shape, BF), (tokens.shape, BF), ((pb_size, part, width), BF)],
+        micros=0.3,
+    )
+    exchanged = [turn(value) for value in exchanged]
     ffn_up, ffn_down = call(
-        ffn_finish_kernel, [ids, fkeep, fgot], [((piece, units), F32)] * 2, near=False
-    )
-    c = c_out
+        order, ffn_finish_kernel, [fkeep, *fgots], [((piece, units), F32)] * 2, near=False
+    )
+    va, vb, *exchanged = join(
+        order, [(va, ra, X_WAY, [(0, 12)]), (vb, rb, Y_WAY, [(0, 12)])], 0.6, exchanged
+    )
+    layer_out, grad_tokens, grad_features = [turn(value) for value in exchanged]
+    ra, rb = swap(va, *CORE), swap(vb, *CORE)
+    (vc,) = join(order, [(vc, rc, z_way, [(0, 13)])], 4.0)
+    rc = swap(vc, *CORE)
     matrix = ((width, width), F32)
     three = ((3, width, width), F32)
     g_cross_q, g_self_out, g_cross_out, g_self_proj = call(
-        finish_chain_kernel, [ids, va, ra, vb, rb], [matrix, matrix, matrix, three], near=False
-    )
-    c_other = swap(c, "dp", 1)
+        order,
+        finish_chain_kernel,
+        [va, ra, vb, rb],
+        [matrix, matrix, matrix, three],
+        near=False,
+    )
     bias3 = ((3, width), F32)
     bias1 = ((1, width), F32)
     (
@@ -1211,8 +1377,9 @@
         g_shift,
         g_inb,
     ) = call(
+        order,
         functools.partial(finish_memory_kernel, rows_used=used),
-        [ids, c, c_other, g_cross_q],
+        [vc, rc, g_cross_q],
         [
             three,
             matrix,

time: 217 us -> 161 us (0.74)
  waiting for transfers between devices: 91 us -> 57 us
  Pallas kernels: 63.5 us -> 48 us
  local copies, waits for them, and re-layouts: 9.73 us -> 5.09 us
    ppermute x49 -> x53, waiting for transfers between devices: 91 us -> 57 us  [swap(): return lax.ppermute(value, axis, [(i, i ^ bit) for i in range(size)])]
    pallas_call x33 -> x32, Pallas kernels: 63.5 us -> 48 us  [call(): pl.pallas_call(body, out_shape=[pltpu.VMEM(*o) if here else jax.ShapeDtyp...]
    unnamed x27 -> x36, local copies, waits for them, and re-layouts: 4.17 us -> 1.56 us
    reshape x4 -> x1, local copies, waits for them, and re-layouts: 2.63 us -> 0.01 us  [on_device(): jnp.pad(b_up, (0, 2 * width - units)).reshape(2, width)]
    concatenate x2 -> x0, local copies, waits for them, and re-layouts: 2.24 us -> none  [the longest x1 2.15 us: on_device(): jnp.concatenate([in_bias, b_down, b_up, jnp.zeros((2 * width - units,), B...]
    ppermute x49 -> x53, starting transfers between devices: 50.9 us -> 49.4 us  [swap(): return lax.ppermute(value, axis, [(i, i ^ bit) for i in range(size)])]
  transfers between devices with their start and end apart: 49 -> 53, of which waited for: 28 -> 32; matrix products, arithmetic and copies ran while one was open for 2% -> 2% of each run, Pallas kernels for 21% -> 24%
where the time goes in v2:
time: 161 us
  waiting for transfers between devices  57 us (35%)
  starting transfers between devices  49.4 us (31%)
  Pallas kernels  48 us (30%)
  local copies, waits for them, and re-layouts  5.09 us (3%)
    ppermute x53, waiting for transfers between devices, swap(): return lax.ppermute(value, axis, [(i, i ^ bit) for i in range(size)])  57 us
    ppermute x53, starting transfers between devices, swap(): return lax.ppermute(value, axis, [(i, i ^ bit) for i in range(size)])  49.4 us
    pallas_call x32, Pallas kernels, call(): pl.pallas_call(body, out_shape=[pltpu.VMEM(*o) if here else jax.ShapeDtyp...  48 us
  transfers between devices with their start and end apart: 53, of which 32 were waited for; matrix products, arithmetic and copies ran while one was open for 2% of the time, Pallas kernels for 24%

profile of v2, /device:TPU:0, one launch (start us, length us, event | category | flops | bytes accessed | tf_op | source)
XLA Modules:
  0.0 160.6 jit_solution(11699078279025509645)
XLA Ops:
  0.7 1.6 %shard_map.349 = (bf16[400,512]{1,0:T(8,128)(2,1)S(1)}, bf16[400,512]{1,0:T(8,128)(2,1)S(1)}, bf16[416,512]{1,0:T(8,128)(2,1)S(1)}, bf16[416,512]{1,0:T(8,128)(2,1)S(1)}) custom-call(bf16[800,512]{1,0:T(8,128)(2,1)} %bitcast.22, bf16[800,512]{1,0:T(8,128)(2,1)} %bitcast.24), custom_call_target="tpu_custom_call" | custom-call | flops 1610000000 | bytes 5180001 | tf_op jit(solution)/shard_map/pallas_call | solution.py:860
  2.3 3.0 %collective-permute-start = (bf16[400,512]{1,0:T(8,128)(2,1)S(1)}, bf16[400,512]{1,0:T(8,128)(2,1)S(1)}, u32[]{:S(2)}, u32[]{:S(2)}) collective-permute-start(bf16[400,512]{1,0:T(8,128)(2,1)S(1)} %get-tuple-element.337), channel_id=1, source_target_pairs={{0,8},{8,0},{16,24},{24,16},{1,9},{9,1},{17,25},{25,17},{2,10},{10... | collective-permute-start | bytes 1228808 | tf_op jit(solution)/shard_map/ppermute | solution.py:880
  5.3 1.5 collective-permute-start.1
  7.9 2.9 %collective-permute-start.4 = (bf16[32,1024]{1,0:T(8,128)(2,1)S(1)}, bf16[32,1024]{1,0:T(8,128)(2,1)S(1)}, u32[]{:S(2)}, u32[]{:S(2)}) collective-permute-start(bf16[32,1024]{1,0:T(8,128)(2,1)S(1)} %get-tuple-element.358), channel_id=1, source_target_pairs={{0,24},{8,16},{16,8},{24,0},{1,25},{9,17},{17,9},{25,1},{2,26},{10... | collective-permute-start | bytes 196616 | tf_op jit(solution)/shard_map/ppermute | solution.py:880
  10.8 5.4 %shard_map.351 = (bf16[1216,512]{1,0:T(8,128)(2,1)S(1)}, bf16[1216,512]{1,0:T(8,128)(2,1)S(1)}, bf16[1216,512]{1,0:T(8,128)(2,1)S(1)}, bf16[1216,512]{1,0:T(8,12...) custom-call(bf16[4,1200,512]{2,1,0:T(8,128)(2,1)} %refs_0_, ...), custom_call_target="tpu_custom_call" | custom-call | flops 1 | bytes 1 | tf_op jit(solution)/shard_map/pallas_call | solution.py:860
  16.3 1.4 collective-permute-done.1.refs_16_
  17.7 1.4 collective-permute-done.3.refs_3_
  19.6 1.5 collective-permute-start.8
  21.7 1.5 collective-permute-start.11
  23.7 8.1 %shard_map.352 = (bf16[128,512]{1,0:T(8,128)(2,1)S(1)}, bf16[128,512]{1,0:T(8,128)(2,1)S(1)}, bf16[128,512]{1,0:T(8,128)(2,1)S(1)}, bf16[128,512]{1,0:T(8,128)(2...) custom-call(s32[4,4]{1,0:T(4,128)S(1)} %copy-done.2, ...), custom_call_target="tpu_custom_call" | custom-call | flops 9200000000 | bytes 29600000 | tf_op jit(solution)/shard_map/pallas_call | solution.py:860
  32.0 1.6 collective-permute-done.7.refs_4_
  34.0 1.2 collective-permute-done.9.refs_6_
  36.6 2.5 %shard_map.353 = (f32[128,512]{1,0:T(8,128)S(1)}, f32[2,128,800]{2,1,0:T(8,128)S(1)}, bf16[2,1,800,512]{3,2,1,0:T(8,128)(2,1)S(1)}) custom-call(bf16[128,512]{1,0:T(8,128)(2,1)S(1)} %get-tuple-element.418.refs_0_.refs_1_, f32[8,512]{1,0:T(8,128)S(1)} %get-tuple-element.422.refs_1_.refs_5_, bf16[800,512]{1,0:T(8,128)(2,1)S(1)} %get-tuple-element.533.refs_2_.refs_6_.refs_4_, ...), custom_call_target="tpu_custom_call" | custom-call | flops 1 | bytes 1 | tf_op jit(solution)/shard_map/pallas_call | solution.py:860
  39.2 2.2 %collective-permute-done.11.refs_14_ = bf16[416,512]{1,0:T(8,128)(2,1)S(1)} collective-permute-done((bf16[416,512]{1,0:T(8,128)(2,1)S(1)}, bf16[416,512]{1,0:T(8,128)(2,1)S(1)}, u32[]{:S(2)}, u32[]{:S(2)}) %collective-permute-start.11) | collective-permute-done | bytes 426016 | tf_op jit(solution)/shard_map/ppermute | solution.py:880
  41.9 1.3 collective-permute-done.13.refs_18_
  44.6 5.4 %shard_map.354 = (bf16[128,512]{1,0:T(8,128)(2,1)S(1)}, bf16[128,1024]{1,0:T(8,128)(2,1)S(1)}, f32[128,512]{1,0:T(8,128)S(1)}, f32[8,512]{1,0:T(8,128)S(1)}, f32[4,1,1024]{2,1,0:T(1,128)S(1)}) custom-call(f32[128,512]{1,0:T(8,128)S(1)} %get-tuple-element.417.refs_0_, bf16[128,512]{1,0:T(8,128)(2,1)S(1)} %get-tuple-element.418.refs_0_.refs_1_, ...), custom_call_target="tpu_custom_call" | custom-call | flops 6900000256 | bytes 22200000 | tf_op jit(solution)/shard_map/pallas_call | solution.py:860
  49.9 1.2 collective-permute-start.21
  51.2 0.8 collective-permute-start.20
  52.0 1.5 collective-permute-start.19
  53.5 7.6 %shard_map.355 = (bf16[4,1216,256]{2,1,0:T(8,128)(2,1)S(1)}, bf16[128,512]{1,0:T(8,128)(2,1)S(1)}, bf16[128,512]{1,0:T(8,128)(2,1)S(1)}, f32[128,512]{1,0:T(8,12...) custom-call(f32[128,512]{1,0:T(8,128)S(1)} %get-tuple-element.456.re, ...), custom_call_target="tpu_custom_call" | custom-call | flops 8970000384 | bytes 28860000 | tf_op jit(solution)/shard_map/pallas_call | solution.py:860
  61.8 3.1 %collective-permute-done.20.refs_1_.refs_2_ = bf16[128,1024]{1,0:T(8,128)(2,1)S(1)} collective-permute-done((bf16[128,1024]{1,0:T(8,128)(2,1)S(1)}, bf16[128,1024]{1,0:T(8,128)(2,1)S(1)}, u32[]{:S(2)}, u32[]{:S(2)}) %collective-permute-start.20) | collective-permute-done | bytes 262176 | tf_op jit(solution)/shard_map/ppermute | solution.py:880
  64.9 1.7 %collective-permute-done.18.refs_7_ = bf16[6,256,128]{2,1,0:T(8,128)(2,1)S(1)} collective-permute-done((bf16[6,256,128]{2,1,0:T(8,128)(2,1)S(1)}, bf16[6,256,128]{2,1,0:T(8,128)(2,1)S(1)}, u32[]{:S(2)}, u32[]{:S(2)}) %collective-permute-start.18) | collective-permute-done | bytes 393248 | tf_op jit(solution)/shard_map/ppermute | solution.py:880
  67.5 1.2 collective-permute-start.23
  68.8 6.4 %shard_map.358 = (bf16[368,512]{1,0:T(8,128)(2,1)S(1)}, bf16[368,512]{1,0:T(8,128)(2,1)S(1)}, bf16[368,512]{1,0:T(8,128)(2,1)S(1)}, bf16[368,512]{1,0:T(8,128)(2...) custom-call(bf16[4,1216,256]{2,1,0:T(8,128)(2,1)S(1)} %get-tuple-element.508.refs_0_, ...), custom_call_target="tpu_custom_call" | custom-call | flops 7360000000 | bytes 23680000 | tf_op jit(solution)/shard_map/pallas_call | solution.py:860
  75.1 3.0 %collective-permute-done.22.refs_1_ = bf16[12,128,128]{2,1,0:T(8,128)(2,1)S(1)} collective-permute-done((bf16[12,128,128]{2,1,0:T(8,128)(2,1)S(1)}, bf16[12,128,128]{2,1,0:T(8,128)(2,1)S(1)}, u32[]{:S(2)}, u32[]{:S(2)}) %collective-permute-start.22) | collective-permute-done | bytes 393248 | tf_op jit(solution)/shard_map/ppermute | solution.py:880
  78.4 2.8 %shard_map.359 = (bf16[2,4,64,800]{3,2,1,0:T(8,128)(2,1)S(1)}, bf16[4,64,800]{2,1,0:T(8,128)(2,1)S(1)}, bf16[4,64,800]{2,1,0:T(8,128)(2,1)S(1)}) custom-call(bf16[128,1024]{1,0:T(8,128)(2,1)S(1)} %get-tuple-element.529.refs_0_, bf16[128,1024]{1,0:T(8,128)(2,1)S(1)} %collective-permute-done.19.refs_0_.refs_1_, ...), custom_call_target="tpu_custom_call" | custom-call | flops 3220000000 | bytes 10360001 | tf_op jit(solution)/shard_map/pallas_call | solution.py:860
  81.4 1.3 collective-permute-start.24
  82.7 0.8 collective-permute-start.25
  83.7 1.6 %collective-permute-start.28 = (bf16[13,128,128]{2,1,0:T(8,128)(2,1)S(1)}, bf16[13,128,128]{2,1,0:T(8,128)(2,1)S(1)}, u32[]{:S(2)}, u32[]{:S(2)}) collective-permute-start(bf16[13,128,128]{2,1,0:T(8,128)(2,1)S(1)} %get-tuple-element.556), channel_id=1, source_target_pairs={{0,2},{1,3},{2,0},{3,1},{4,6},{5,7},{6,4},{7,5},{8,10},{9,11},{10,... | collective-permute-start | bytes 1277960 | tf_op jit(solution)/shard_map/ppermute | solution.py:880
  85.8 3.0 %collective-permute-done.24.refs_1_ = bf16[12,64,128]{2,1,0:T(8,128)(2,1)S(1)} collective-permute-done((bf16[12,64,128]{2,1,0:T(8,128)(2,1)S(1)}, bf16[12,64,128]{2,1,0:T(8,128)(2,1)S(1)}, u32[]{:S(2)}, u32[]{:S(2)}) %collective-permute-start.24) | collective-permute-done | bytes 196640 | tf_op jit(solution)/shard_map/ppermute | solution.py:880
  88.8 0.9 collective-permute-done.25.refs_3_
  89.8 1.6 %collective-permute-start.27 = (bf16[24,32,128]{2,1,0:T(8,128)(2,1)S(1)}, bf16[24,32,128]{2,1,0:T(8,128)(2,1)S(1)}, u32[]{:S(2)}, u32[]{:S(2)}) collective-permute-start(bf16[24,32,128]{2,1,0:T(8,128)(2,1)S(1)} %get-tuple-element.555), channel_id=1, source_target_pairs={{0,2},{1,3},{2,0},{3,1},{4,6},{5,7},{6,4},{7,5},{8,10},{9,11},{10,... | collective-permute-start | bytes 589832 | tf_op jit(solution)/shard_map/ppermute | solution.py:880
  91.7 4.7 %collective-permute-done.28.refs_1_ = bf16[13,128,128]{2,1,0:T(8,128)(2,1)S(1)} collective-permute-done((bf16[13,128,128]{2,1,0:T(8,128)(2,1)S(1)}, bf16[13,128,128]{2,1,0:T(8,128)(2,1)S(1)}, u32[]{:S(2)}, u32[]{:S(2)}) %collective-permute-start.28) | collective-permute-done | bytes 426016 | tf_op jit(solution)/shard_map/ppermute | solution.py:880
  96.5 1.3 collective-permute-start.32
  97.9 1.6 collective-permute-start.34
  99.9 0.8 collective-permute-done.27.refs_1_
  100.7 1.8 %collective-permute-done.32.refs_1_ = bf16[13,64,128]{2,1,0:T(8,128)(2,1)S(1)} collective-permute-done((bf16[13,64,128]{2,1,0:T(8,128)(2,1)S(1)}, bf16[13,64,128]{2,1,0:T(8,128)(2,1)S(1)}, u32[]{:S(2)}, u32[]{:S(2)}) %collective-permute-start.32) | collective-permute-done | bytes 213024 | tf_op jit(solution)/shard_map/ppermute | solution.py:880
  102.5 1.6 collective-permute-start.33
  104.1 2.6 %collective-permute-start.31 = (bf16[24,32,128]{2,1,0:T(8,128)(2,1)S(1)}, bf16[24,32,128]{2,1,0:T(8,128)(2,1)S(1)}, u32[]{:S(2)}, u32[]{:S(2)}) collective-permute-start(bf16[24,32,128]{2,1,0:T(8,128)(2,1)S(1)} %shard_map.365.refs_0_), channel_id=1, source_target_pairs={{0,4},{1,5},{2,6},{3,7},{4,0},{5,1},{6,2},{7,3},{8,12},{9,13},{10,... | collective-permute-start | bytes 589832 | tf_op jit(solution)/shard_map/ppermute | solution.py:880
  107.2 1.3 collective-permute-done.34.refs_1_
  108.5 2.9 %collective-permute-start.38 = (bf16[368,512]{1,0:T(8,128)(2,1)S(1)}, bf16[368,512]{1,0:T(8,128)(2,1)S(1)}, u32[]{:S(2)}, u32[]{:S(2)}) collective-permute-start(bf16[368,512]{1,0:T(8,128)(2,1)S(1)} %get-tuple-element.584), channel_id=1, source_target_pairs={{0,16},{8,24},{16,0},{24,8},{1,17},{9,25},{17,1},{25,9},{2,18},{10... | collective-permute-start | bytes 1130504 | tf_op jit(solution)/shard_map/ppermute | solution.py:880
  111.4 2.3 %collective-permute-done.35.refs_2_ = bf16[2,64,800]{2,1,0:T(8,128)(2,1)S(1)} collective-permute-done((bf16[2,64,800]{2,1,0:T(8,128)(2,1)S(1)}, bf16[2,64,800]{2,1,0:T(8,128)(2,1)S(1)}, u32[]{:S(2)}, u32[]{:S(2)}) %collective-permute-start.35) | collective-permute-done | bytes 204832 | tf_op jit(solution)/shard_map/ppermute | solution.py:880
  113.9 1.0 collective-permute-start.39
  114.9 2.5 %collective-permute-start.36 = (bf16[24,32,128]{2,1,0:T(8,128)(2,1)S(1)}, bf16[24,32,128]{2,1,0:T(8,128)(2,1)S(1)}, u32[]{:S(2)}, u32[]{:S(2)}) collective-permute-start(bf16[24,32,128]{2,1,0:T(8,128)(2,1)S(1)} %shard_map.369.refs_0_), channel_id=1, source_target_pairs={{0,2},{1,3},{2,0},{3,1},{4,6},{5,7},{6,4},{7,5},{8,10},{9,11},{10,... | collective-permute-start | bytes 589832 | tf_op jit(solution)/shard_map/ppermute | solution.py:880
  117.5 3.2 %collective-permute-done.39.refs_1_ = bf16[13,32,128]{2,1,0:T(8,128)(2,1)S(1)} collective-permute-done((bf16[13,32,128]{2,1,0:T(8,128)(2,1)S(1)}, bf16[13,32,128]{2,1,0:T(8,128)(2,1)S(1)}, u32[]{:S(2)}, u32[]{:S(2)}) %collective-permute-start.39) | collective-permute-done | bytes 106528 | tf_op jit(solution)/shard_map/ppermute | solution.py:880
  120.7 1.7 %collective-permute-start.43 = (bf16[13,32,128]{2,1,0:T(8,128)(2,1)S(1)}, bf16[13,32,128]{2,1,0:T(8,128)(2,1)S(1)}, u32[]{:S(2)}, u32[]{:S(2)}) collective-permute-start(bf16[13,32,128]{2,1,0:T(8,128)(2,1)S(1)} %shard_map.370.refs_0_), channel_id=1, source_target_pairs={{0,16},{8,24},{16,0},{24,8},{1,17},{9,25},{17,1},{25,9},{2,18},{10... | collective-permute-start | bytes 319496 | tf_op jit(solution)/shard_map/ppermute | solution.py:880
  122.4 1.0 collective-permute-start.41
  123.5 0.9 collective-permute-start.42
  124.4 1.6 %collective-permute-start.40 = (bf16[12,64,128]{2,1,0:T(8,128)(2,1)S(1)}, bf16[12,64,128]{2,1,0:T(8,128)(2,1)S(1)}, u32[]{:S(2)}, u32[]{:S(2)}) collective-permute-start(bf16[12,64,128]{2,1,0:T(8,128)(2,1)S(1)} %get-tuple-element.596.refs_0_), channel_id=1, source_target_pairs={{0,16},{8,24},{16,0},{24,8},{1,17},{9,25},{17,1},{25,9},{2,18},{10... | collective-permute-start | bytes 589832 | tf_op jit(solution)/shard_map/ppermute | solution.py:880
  126.0 7.3 %collective-permute-done.43.refs_1_ = bf16[13,32,128]{2,1,0:T(8,128)(2,1)S(1)} collective-permute-done((bf16[13,32,128]{2,1,0:T(8,128)(2,1)S(1)}, bf16[13,32,128]{2,1,0:T(8,128)(2,1)S(1)}, u32[]{:S(2)}, u32[]{:S(2)}) %collective-permute-start.43) | collective-permute-done | bytes 106528 | tf_op jit(solution)/shard_map/ppermute | solution.py:880
  133.5 1.5 collective-permute-done.41.refs_3_
  135.0 1.4 collective-permute-start.47
  136.4 0.9 collective-permute-done.40.refs_1_
  137.5 1.7 %collective-permute-start.45 = (bf16[12,128,128]{2,1,0:T(8,128)(2,1)S(1)}, bf16[12,128,128]{2,1,0:T(8,128)(2,1)S(1)}, u32[]{:S(2)}, u32[]{:S(2)}) collective-permute-start(bf16[12,128,128]{2,1,0:T(8,128)(2,1)S(1)} %get-tuple-element.620.refs_2_), channel_id=1, source_target_pairs={{0,16},{8,24},{16,0},{24,8},{1,17},{9,25},{17,1},{25,9},{2,18},{10... | collective-permute-start | bytes 1179656 | tf_op jit(solution)/shard_map/ppermute | solution.py:880
  140.3 1.4 collective-permute-done.47.refs_2_
  141.7 2.0 %copy.49 = bf16[4,300,512]{2,0,1:T(4,128)(2,1)} copy(bf16[4,300,512]{2,1,0:T(8,128)(2,1)S(1)} %get-tuple-element.623) | data formatting | bytes 2457600 | tf_op jit(solution)/shard_map/pallas_call | solution.py:860
  143.6 0.8 shard_map.376
  144.4 0.8 copy_bitcast_fusion.1
  145.3 2.3 %collective-permute-done.45.refs_3_ = bf16[12,128,128]{2,1,0:T(8,128)(2,1)S(1)} collective-permute-done((bf16[12,128,128]{2,1,0:T(8,128)(2,1)S(1)}, bf16[12,128,128]{2,1,0:T(8,128)(2,1)S(1)}, u32[]{:S(2)}, u32[]{:S(2)}) %collective-permute-start.45) | collective-permute-done | bytes 393248 | tf_op jit(solution)/shard_map/ppermute | solution.py:880
  148.2 1.8 %collective-permute-done.49.refs_1_ = bf16[13,128,128]{2,1,0:T(8,128)(2,1)S(1)} collective-permute-done((bf16[13,128,128]{2,1,0:T(8,128)(2,1)S(1)}, bf16[13,128,128]{2,1,0:T(8,128)(2,1)S(1)}, u32[]{:S(2)}, u32[]{:S(2)}) %collective-permute-start.49) | collective-permute-done | bytes 426016 | tf_op jit(solution)/shard_map/ppermute | solution.py:880
  150.8 2.9 %collective-permute-done.52.refs_3_ = bf16[12,256,128]{2,1,0:T(8,128)(2,1)S(1)} collective-permute-done((bf16[12,256,128]{2,1,0:T(8,128)(2,1)S(1)}, bf16[12,256,128]{2,1,0:T(8,128)(2,1)S(1)}, u32[]{:S(2)}, u32[]{:S(2)}) %collective-permute-start.52) | collective-permute-done | bytes 786464 | tf_op jit(solution)/shard_map/ppermute | solution.py:880
  153.7 1.1 collective-permute-done.51.refs_1_
  154.8 2.8 %shard_map.379 = (f32[512,512]{1,0:T(8,128)S(1)}, f32[512,512]{1,0:T(8,128)}, f32[512,512]{1,0:T(8,128)}, f32[3,512,512]{2,1,0:T(8,128)}) custom-call(bf16[12,256,128]{2,1,0:T(8,128)(2,1)S(1)} %get-tuple-element.634.refs_0_, bf16[12,256,128]{2,1,0:T(8,128)(2,1)S(1)} %collective-permute-done.51.refs_1_, bf16[12,256,128]{2,1,0:T(8,128)(2,1)S(1)} %get-tuple-element.636.refs_2_, ...), custom_call_target="tpu_custom_call" | custom-call | flops 690000000 | bytes 2220001 | tf_op jit(solution)/shard_map/pallas_call | solution.py:860
  157.6 2.2 %shard_map.380 = (f32[3,512,512]{2,1,0:T(8,128)}, f32[512,512]{1,0:T(8,128)}, f32[100,512]{1,0:T(8,128)}, f32[3,512]{1,0:T(4,128)}, f32[3,512]{1,0:T(4,128)}, /*...) custom-call(bf16[13,256,128]{2,1,0:T(8,128)(2,1)S(1)} %shard_map.378.refs, ...), custom_call_target="tpu_custom_call" | custom-call | flops 690000000 | bytes 2220001 | tf_op jit(solution)/shard_map/pallas_call | solution.py:860
  (119 shorter events, 14.6 us)
Async XLA Ops:
  0.7 6.2 %copy-start.7 = (bf16[800]{0:T(1024)(128)(2,1)S(1)}, bf16[800]{0:T(1024)(128)(2,1)}, u32[]{:S(2)}) copy-start(bf16[800]{0:T(1024)(128)(2,1)} %param.34) | copy-start | bytes 4804
  0.7 6.2 %copy-start.8 = (bf16[512]{0:T(512)(128)(2,1)S(1)}, bf16[512]{0:T(512)(128)(2,1)}, u32[]{:S(2)}) copy-start(bf16[512]{0:T(512)(128)(2,1)} %param.36) | copy-start | bytes 3076
  0.7 6.2 %copy-start.9 = (bf16[512]{0:T(512)(128)(2,1)S(1)}, bf16[512]{0:T(512)(128)(2,1)}, u32[]{:S(2)}) copy-start(bf16[512]{0:T(512)(128)(2,1)} %param.40) | copy-start | bytes 3076
  0.7 6.3 %copy-start = (bf16[4,25,512]{2,0,1:T(4,128)(2,1)S(1)}, bf16[4,25,512]{2,0,1:T(4,128)(2,1)}, u32[]{:S(2)}) copy-start(bf16[4,25,512]{2,0,1:T(4,128)(2,1)} %param.22) | copy-start | bytes 307204
  0.7 6.3 %copy-start.1 = (bf16[4,25,512]{2,0,1:T(4,128)(2,1)S(1)}, bf16[4,25,512]{2,0,1:T(4,128)(2,1)}, u32[]{:S(2)}) copy-start(bf16[4,25,512]{2,0,1:T(4,128)(2,1)} %param.26) | copy-start | bytes 307204
  2.3 13.9 %collective-permute-start = (bf16[400,512]{1,0:T(8,128)(2,1)S(1)}, bf16[400,512]{1,0:T(8,128)(2,1)S(1)}, u32[]{:S(2)}, u32[]{:S(2)}) collective-permute-start(bf16[400,512]{1,0:T(8,128)(2,1)S(1)} %get-tuple-element.337), channel_id=1, source_target_pairs={{0,8},{8,0},{16,24},{24,16},{1,9},{9,1},{17,25},{25,17},{2,10},{10... | collective-permute-start | bytes 1228808 | tf_op jit(solution)/shard_map/ppermute | solution.py:880
  5.3 12.3 %collective-permute-start.1 = (bf16[400,512]{1,0:T(8,128)(2,1)S(1)}, bf16[400,512]{1,0:T(8,128)(2,1)S(1)}, u32[]{:S(2)}, u32[]{:S(2)}) collective-permute-start(bf16[400,512]{1,0:T(8,128)(2,1)S(1)} %get-tuple-element.338), channel_id=1, source_target_pairs={{0,16},{8,24},{16,0},{24,8},{1,17},{9,25},{17,1},{25,9},{2,18},{10... | collective-permute-start | bytes 1228808 | tf_op jit(solution)/shard_map/ppermute | solution.py:880
  7.3 10.4 %collective-permute-start.2 = (bf16[32,1024]{1,0:T(8,128)(2,1)S(1)}, bf16[32,1024]{1,0:T(8,128)(2,1)S(1)}, u32[]{:S(2)}, u32[]{:S(2)}) collective-permute-start(bf16[32,1024]{1,0:T(8,128)(2,1)S(1)} %get-tuple-element.356), channel_id=1, source_target_pairs={{0,8},{8,0},{16,24},{24,16},{1,9},{9,1},{17,25},{25,17},{2,10},{10... | collective-permute-start | bytes 196616 | tf_op jit(solution)/shard_map/ppermute | solution.py:880
  7.9 11.2 %collective-permute-start.3 = (bf16[32,1024]{1,0:T(8,128)(2,1)S(1)}, bf16[32,1024]{1,0:T(8,128)(2,1)S(1)}, u32[]{:S(2)}, u32[]{:S(2)}) collective-permute-start(bf16[32,1024]{1,0:T(8,128)(2,1)S(1)} %get-tuple-element.357), channel_id=1, source_target_pairs={{0,16},{8,24},{16,0},{24,8},{1,17},{9,25},{17,1},{25,9},{2,18},{10... | collective-permute-start | bytes 196616 | tf_op jit(solution)/shard_map/ppermute | solution.py:880
  7.9 11.2 %collective-permute-start.4 = (bf16[32,1024]{1,0:T(8,128)(2,1)S(1)}, bf16[32,1024]{1,0:T(8,128)(2,1)S(1)}, u32[]{:S(2)}, u32[]{:S(2)}) collective-permute-start(bf16[32,1024]{1,0:T(8,128)(2,1)S(1)} %get-tuple-element.358), channel_id=1, source_target_pairs={{0,24},{8,16},{16,8},{24,0},{1,25},{9,17},{17,9},{25,1},{2,26},{10... | collective-permute-start | bytes 196616 | tf_op jit(solution)/shard_map/ppermute | solution.py:880
  10.8 12.9 %copy-start.2 = (s32[4,4]{1,0:T(4,128)S(1)}, s32[4,4]{1,0:T(4,128)}, u32[]{:S(2)}) copy-start(s32[4,4]{1,0:T(4,128)} %refs_0_.1) | copy-start | bytes 196
  16.3 15.5 %copy-start.14 = (bf16[400,512]{1,0:T(8,128)(2,1)}, bf16[400,512]{1,0:T(8,128)(2,1)S(1)}, u32[]{:S(2)}) copy-start(bf16[400,512]{1,0:T(8,128)(2,1)S(1)} %collective-permute-done.refs_15_) | copy-start | bytes 1228804
  17.7 14.1 %copy-start.15 = (bf16[400,512]{1,0:T(8,128)(2,1)}, bf16[400,512]{1,0:T(8,128)(2,1)S(1)}, u32[]{:S(2)}) copy-start(bf16[400,512]{1,0:T(8,128)(2,1)S(1)} %collective-permute-done.1.refs_16_) | copy-start | bytes 1228804
  19.1 4.1 %collective-permute-start.5 = (bf16[400,512]{1,0:T(8,128)(2,1)S(1)}, bf16[400,512]{1,0:T(8,128)(2,1)S(1)}, u32[]{:S(2)}, u32[]{:S(2)}) collective-permute-start(bf16[400,512]{1,0:T(8,128)(2,1)S(1)} %collective-permute-done.refs_15_), channel_id=1, source_target_pairs={{0,1},{1,0},{2,3},{3,2},{4,5},{5,4},{6,7},{7,6},{8,9},{9,8},{10,11... | collective-permute-start | bytes 1228808 | tf_op jit(solution)/shard_map/ppermute | solution.py:880
  19.1 4.6 %collective-permute-start.6 = (bf16[400,512]{1,0:T(8,128)(2,1)S(1)}, bf16[400,512]{1,0:T(8,128)(2,1)S(1)}, u32[]{:S(2)}, u32[]{:S(2)}) collective-permute-start(bf16[400,512]{1,0:T(8,128)(2,1)S(1)} %collective-permute-done.1.refs_16_), channel_id=1, source_target_pairs={{0,1},{1,0},{2,3},{3,2},{4,5},{5,4},{6,7},{7,6},{8,9},{9,8},{10,11... | collective-permute-start | bytes 1228808 | tf_op jit(solution)/shard_map/ppermute | solution.py:880
  19.6 12.3 %collective-permute-start.8 = (bf16[400,512]{1,0:T(8,128)(2,1)S(1)}, bf16[400,512]{1,0:T(8,128)(2,1)S(1)}, u32[]{:S(2)}, u32[]{:S(2)}) collective-permute-start(bf16[400,512]{1,0:T(8,128)(2,1)S(1)} %collective-permute-done.refs_15_), channel_id=1, source_target_pairs={{0,16},{8,24},{16,0},{24,8},{1,17},{9,25},{17,1},{25,9},{2,18},{10... | collective-permute-start | bytes 1228808 | tf_op jit(solution)/shard_map/ppermute | solution.py:880
  21.1 12.4 %collective-permute-start.7 = (bf16[400,512]{1,0:T(8,128)(2,1)S(1)}, bf16[400,512]{1,0:T(8,128)(2,1)S(1)}, u32[]{:S(2)}, u32[]{:S(2)}) collective-permute-start(bf16[400,512]{1,0:T(8,128)(2,1)S(1)} %collective-permute-done.1.refs_16_), channel_id=1, source_target_pairs={{0,8},{8,0},{16,24},{24,16},{1,9},{9,1},{17,25},{25,17},{2,10},{10... | collective-permute-start | bytes 1228808 | tf_op jit(solution)/shard_map/ppermute | solution.py:880
  21.7 19.7 %collective-permute-start.11 = (bf16[416,512]{1,0:T(8,128)(2,1)S(1)}, bf16[416,512]{1,0:T(8,128)(2,1)S(1)}, u32[]{:S(2)}, u32[]{:S(2)}) collective-permute-start(bf16[416,512]{1,0:T(8,128)(2,1)S(1)} %get-tuple-element.411), channel_id=1, source_target_pairs={{0,8},{8,0},{16,24},{24,16},{1,9},{9,1},{17,25},{25,17},{2,10},{10... | collective-permute-start | bytes 1277960 | tf_op jit(solution)/shard_map/ppermute | solution.py:880
  23.2 8.6 %copy-start.16 = (bf16[400,512]{1,0:T(8,128)(2,1)}, bf16[400,512]{1,0:T(8,128)(2,1)S(1)}, u32[]{:S(2)}) copy-start(bf16[400,512]{1,0:T(8,128)(2,1)S(1)} %collective-permute-done.5.refs_19_) | copy-start | bytes 1228804
  23.2 18.2 %collective-permute-start.12 = (bf16[416,512]{1,0:T(8,128)(2,1)S(1)}, bf16[416,512]{1,0:T(8,128)(2,1)S(1)}, u32[]{:S(2)}, u32[]{:S(2)}) collective-permute-start(bf16[416,512]{1,0:T(8,128)(2,1)S(1)} %get-tuple-element.412), channel_id=1, source_target_pairs={{0,16},{8,24},{16,0},{24,8},{1,17},{9,25},{17,1},{25,9},{2,18},{10... | collective-permute-start | bytes 1277960 | tf_op jit(solution)/shard_map/ppermute | solution.py:880
  23.7 8.1 %copy-start.17 = (bf16[400,512]{1,0:T(8,128)(2,1)}, bf16[400,512]{1,0:T(8,128)(2,1)S(1)}, u32[]{:S(2)}) copy-start(bf16[400,512]{1,0:T(8,128)(2,1)S(1)} %collective-permute-done.6.refs_20_) | copy-start | bytes 1228804
  31.9 3.9 %copy-start.3 = (bf16[400,512]{1,0:T(8,128)(2,1)}, bf16[400,512]{1,0:T(8,128)(2,1)S(1)}, u32[]{:S(2)}) copy-start(bf16[400,512]{1,0:T(8,128)(2,1)S(1)} %collective-permute-done.8.refs_5_) | copy-start | bytes 1228804
  33.5 1.7 %collective-permute-start.9 = (bf16[400,512]{1,0:T(8,128)(2,1)S(1)}, bf16[400,512]{1,0:T(8,128)(2,1)S(1)}, u32[]{:S(2)}, u32[]{:S(2)}) collective-permute-start(bf16[400,512]{1,0:T(8,128)(2,1)S(1)} %collective-permute-done.7.refs_4_), channel_id=1, source_target_pairs={{0,1},{1,0},{2,3},{3,2},{4,5},{5,4},{6,7},{7,6},{8,9},{9,8},{10,11... | collective-permute-start | bytes 1228808 | tf_op jit(solution)/shard_map/ppermute | solution.py:880
  33.5 2.3 %collective-permute-start.10 = (bf16[400,512]{1,0:T(8,128)(2,1)S(1)}, bf16[400,512]{1,0:T(8,128)(2,1)S(1)}, u32[]{:S(2)}, u32[]{:S(2)}) collective-permute-start(bf16[400,512]{1,0:T(8,128)(2,1)S(1)} %collective-permute-done.8.refs_5_), channel_id=1, source_target_pairs={{0,1},{1,0},{2,3},{3,2},{4,5},{5,4},{6,7},{7,6},{8,9},{9,8},{10,11... | collective-permute-start | bytes 1228808 | tf_op jit(solution)/shard_map/ppermute | solution.py:880
  41.4 1.8 %collective-permute-start.13 = (bf16[416,512]{1,0:T(8,128)(2,1)S(1)}, bf16[416,512]{1,0:T(8,128)(2,1)S(1)}, u32[]{:S(2)}, u32[]{:S(2)}) collective-permute-start(bf16[416,512]{1,0:T(8,128)(2,1)S(1)} %collective-permute-done.11.refs_14_), channel_id=1, source_target_pairs={{0,1},{1,0},{2,3},{3,2},{4,5},{5,4},{6,7},{7,6},{8,9},{9,8},{10,11... | collective-permute-start | bytes 1277960 | tf_op jit(solution)/shard_map/ppermute | solution.py:880
  41.4 2.4 %collective-permute-start.14 = (bf16[416,512]{1,0:T(8,128)(2,1)S(1)}, bf16[416,512]{1,0:T(8,128)(2,1)S(1)}, u32[]{:S(2)}, u32[]{:S(2)}) collective-permute-start(bf16[416,512]{1,0:T(8,128)(2,1)S(1)} %collective-permute-done.12.refs_17_), channel_id=1, source_target_pairs={{0,1},{1,0},{2,3},{3,2},{4,5},{5,4},{6,7},{7,6},{8,9},{9,8},{10,11... | collective-permute-start | bytes 1277960 | tf_op jit(solution)/shard_map/ppermute | solution.py:880
  49.9 11.8 %collective-permute-start.21 = (bf16[128,1024]{1,0:T(8,128)(2,1)S(1)}, bf16[128,1024]{1,0:T(8,128)(2,1)S(1)}, u32[]{:S(2)}, u32[]{:S(2)}) collective-permute-start(bf16[128,1024]{1,0:T(8,128)(2,1)S(1)} %get-tuple-element.529.refs_0_), channel_id=1, source_target_pairs={{0,24},{8,16},{16,8},{24,0},{1,25},{9,17},{17,9},{25,1},{2,26},{10... | collective-permute-start | bytes 786440 | tf_op jit(solution)/shard_map/ppermute | solution.py:880
  51.2 13.7 %collective-permute-start.20 = (bf16[128,1024]{1,0:T(8,128)(2,1)S(1)}, bf16[128,1024]{1,0:T(8,128)(2,1)S(1)}, u32[]{:S(2)}, u32[]{:S(2)}) collective-permute-start(bf16[128,1024]{1,0:T(8,128)(2,1)S(1)} %get-tuple-element.529.refs_0_), channel_id=1, source_target_pairs={{0,16},{8,24},{16,0},{24,8},{1,17},{9,25},{17,1},{25,9},{2,18},{10... | collective-permute-start | bytes 786440 | tf_op jit(solution)/shard_map/ppermute | solution.py:880
  52.0 12.9 %collective-permute-start.19 = (bf16[128,1024]{1,0:T(8,128)(2,1)S(1)}, bf16[128,1024]{1,0:T(8,128)(2,1)S(1)}, u32[]{:S(2)}, u32[]{:S(2)}) collective-permute-start(bf16[128,1024]{1,0:T(8,128)(2,1)S(1)} %get-tuple-element.529.refs_0_), channel_id=1, source_target_pairs={{0,8},{8,0},{16,24},{24,16},{1,9},{9,1},{17,25},{25,17},{2,10},{10... | collective-permute-start | bytes 786440 | tf_op jit(solution)/shard_map/ppermute | solution.py:880
  61.1 3.8 %collective-permute-start.15 = (bf16[6,256,128]{2,1,0:T(8,128)(2,1)S(1)}, bf16[6,256,128]{2,1,0:T(8,128)(2,1)S(1)}, u32[]{:S(2)}, u32[]{:S(2)}) collective-permute-start(bf16[6,256,128]{2,1,0:T(8,128)(2,1)S(1)} %get-tuple-element.478), channel_id=1, source_target_pairs={{0,1},{1,0},{2,3},{3,2},{4,5},{5,4},{6,7},{7,6},{8,9},{9,8},{10,11... | collective-permute-start | bytes 1179656 | tf_op jit(solution)/shard_map/ppermute | solution.py:880
  61.2 3.7 %collective-permute-start.16 = (bf16[6,256,128]{2,1,0:T(8,128)(2,1)S(1)}, bf16[6,256,128]{2,1,0:T(8,128)(2,1)S(1)}, u32[]{:S(2)}, u32[]{:S(2)}) collective-permute-start(bf16[6,256,128]{2,1,0:T(8,128)(2,1)S(1)} %get-tuple-element.479), channel_id=1, source_target_pairs={{0,1},{1,0},{2,3},{3,2},{4,5},{5,4},{6,7},{7,6},{8,9},{9,8},{10,11... | collective-permute-start | bytes 1179656 | tf_op jit(solution)/shard_map/ppermute | solution.py:880
  61.7 3.2 %collective-permute-start.17 = (bf16[6,256,128]{2,1,0:T(8,128)(2,1)S(1)}, bf16[6,256,128]{2,1,0:T(8,128)(2,1)S(1)}, u32[]{:S(2)}, u32[]{:S(2)}) collective-permute-start(bf16[6,256,128]{2,1,0:T(8,128)(2,1)S(1)} %get-tuple-element.480), channel_id=1, source_target_pairs={{0,1},{1,0},{2,3},{3,2},{4,5},{5,4},{6,7},{7,6},{8,9},{9,8},{10,11... | collective-permute-start | bytes 1179656 | tf_op jit(solution)/shard_map/ppermute | solution.py:880
  64.9 1.7 %collective-permute-start.18 = (bf16[6,256,128]{2,1,0:T(8,128)(2,1)S(1)}, bf16[6,256,128]{2,1,0:T(8,128)(2,1)S(1)}, u32[]{:S(2)}, u32[]{:S(2)}) collective-permute-start(bf16[6,256,128]{2,1,0:T(8,128)(2,1)S(1)} %get-tuple-element.481), channel_id=1, source_target_pairs={{0,1},{1,0},{2,3},{3,2},{4,5},{5,4},{6,7},{7,6},{8,9},{9,8},{10,11... | collective-permute-start | bytes 1179656 | tf_op jit(solution)/shard_map/ppermute | solution.py:880
  66.9 11.2 %collective-permute-start.22 = (bf16[12,128,128]{2,1,0:T(8,128)(2,1)S(1)}, bf16[12,128,128]{2,1,0:T(8,128)(2,1)S(1)}, u32[]{:S(2)}, u32[]{:S(2)}) collective-permute-start(bf16[12,128,128]{2,1,0:T(8,128)(2,1)S(1)} %get-tuple-element.498), channel_id=1, source_target_pairs={{0,8},{8,0},{16,24},{24,16},{1,9},{9,1},{17,25},{25,17},{2,10},{10... | collective-permute-start | bytes 1179656 | tf_op jit(solution)/shard_map/ppermute | solution.py:880
  67.5 10.9 %collective-permute-start.23 = (bf16[12,128,128]{2,1,0:T(8,128)(2,1)S(1)}, bf16[12,128,128]{2,1,0:T(8,128)(2,1)S(1)}, u32[]{:S(2)}, u32[]{:S(2)}) collective-permute-start(bf16[12,128,128]{2,1,0:T(8,128)(2,1)S(1)} %get-tuple-element.499), channel_id=1, source_target_pairs={{0,16},{8,24},{16,0},{24,8},{1,17},{9,25},{17,1},{25,9},{2,18},{10... | collective-permute-start | bytes 1179656 | tf_op jit(solution)/shard_map/ppermute | solution.py:880
  78.4 5.1 %collective-permute-start.26 = (bf16[13,256,128]{2,1,0:T(8,128)(2,1)S(1)}, bf16[13,256,128]{2,1,0:T(8,128)(2,1)S(1)}, u32[]{:S(2)}, u32[]{:S(2)}) collective-permute-start(bf16[13,256,128]{2,1,0:T(8,128)(2,1)S(1)} %get-tuple-element.546), channel_id=1, source_target_pairs={{0,1},{1,0},{2,3},{3,2},{4,5},{5,4},{6,7},{7,6},{8,9},{9,8},{10,11... | collective-permute-start | bytes 2555912 | tf_op jit(solution)/shard_map/ppermute | solution.py:880
  81.4 7.4 %collective-permute-start.24 = (bf16[12,64,128]{2,1,0:T(8,128)(2,1)S(1)}, bf16[12,64,128]{2,1,0:T(8,128)(2,1)S(1)}, u32[]{:S(2)}, u32[]{:S(2)}) collective-permute-start(bf16[12,64,128]{2,1,0:T(8,128)(2,1)S(1)} %get-tuple-element.542), channel_id=1, source_target_pairs={{0,16},{8,24},{16,0},{24,8},{1,17},{9,25},{17,1},{25,9},{2,18},{10... | collective-permute-start | bytes 589832 | tf_op jit(solution)/shard_map/ppermute | solution.py:880
  82.7 7.0 %collective-permute-start.25 = (bf16[12,64,128]{2,1,0:T(8,128)(2,1)S(1)}, bf16[12,64,128]{2,1,0:T(8,128)(2,1)S(1)}, u32[]{:S(2)}, u32[]{:S(2)}) collective-permute-start(bf16[12,64,128]{2,1,0:T(8,128)(2,1)S(1)} %get-tuple-element.544), channel_id=1, source_target_pairs={{0,8},{8,0},{16,24},{24,16},{1,9},{9,1},{17,25},{25,17},{2,10},{10... | collective-permute-start | bytes 589832 | tf_op jit(solution)/shard_map/ppermute | solution.py:880
  83.7 12.8 %collective-permute-start.28 = (bf16[13,128,128]{2,1,0:T(8,128)(2,1)S(1)}, bf16[13,128,128]{2,1,0:T(8,128)(2,1)S(1)}, u32[]{:S(2)}, u32[]{:S(2)}) collective-permute-start(bf16[13,128,128]{2,1,0:T(8,128)(2,1)S(1)} %get-tuple-element.556), channel_id=1, source_target_pairs={{0,2},{1,3},{2,0},{3,1},{4,6},{5,7},{6,4},{7,5},{8,10},{9,11},{10,... | collective-permute-start | bytes 1277960 | tf_op jit(solution)/shard_map/ppermute | solution.py:880
  85.3 6.2 %collective-permute-start.29 = (bf16[4,64,800]{2,1,0:T(8,128)(2,1)S(1)}, bf16[4,64,800]{2,1,0:T(8,128)(2,1)S(1)}, u32[]{:S(2)}, u32[]{:S(2)}) collective-permute-start(bf16[4,64,800]{2,1,0:T(8,128)(2,1)S(1)} %get-tuple-element.557), channel_id=1, source_target_pairs={{0,1},{1,0},{2,3},{3,2},{4,5},{5,4},{6,7},{7,6},{8,9},{9,8},{10,11... | collective-permute-start | bytes 1228808 | tf_op jit(solution)/shard_map/ppermute | solution.py:880
  85.3 6.2 %collective-permute-start.30 = (bf16[4,64,800]{2,1,0:T(8,128)(2,1)S(1)}, bf16[4,64,800]{2,1,0:T(8,128)(2,1)S(1)}, u32[]{:S(2)}, u32[]{:S(2)}) collective-permute-start(bf16[4,64,800]{2,1,0:T(8,128)(2,1)S(1)} %get-tuple-element.558), channel_id=1, source_target_pairs={{0,1},{1,0},{2,3},{3,2},{4,5},{5,4},{6,7},{7,6},{8,9},{9,8},{10,11... | collective-permute-start | bytes 1228808 | tf_op jit(solution)/shard_map/ppermute | solution.py:880
  89.8 10.8 %collective-permute-start.27 = (bf16[24,32,128]{2,1,0:T(8,128)(2,1)S(1)}, bf16[24,32,128]{2,1,0:T(8,128)(2,1)S(1)}, u32[]{:S(2)}, u32[]{:S(2)}) collective-permute-start(bf16[24,32,128]{2,1,0:T(8,128)(2,1)S(1)} %get-tuple-element.555), channel_id=1, source_target_pairs={{0,2},{1,3},{2,0},{3,1},{4,6},{5,7},{6,4},{7,5},{8,10},{9,11},{10,... | collective-permute-start | bytes 589832 | tf_op jit(solution)/shard_map/ppermute | solution.py:880
  96.5 5.9 %collective-permute-start.32 = (bf16[13,64,128]{2,1,0:T(8,128)(2,1)S(1)}, bf16[13,64,128]{2,1,0:T(8,128)(2,1)S(1)}, u32[]{:S(2)}, u32[]{:S(2)}) collective-permute-start(bf16[13,64,128]{2,1,0:T(8,128)(2,1)S(1)} %get-tuple-element.568), channel_id=1, source_target_pairs={{0,8},{8,0},{16,24},{24,16},{1,9},{9,1},{17,25},{25,17},{2,10},{10... | collective-permute-start | bytes 638984 | tf_op jit(solution)/shard_map/ppermute | solution.py:880
  97.9 10.6 %collective-permute-start.34 = (bf16[2,64,800]{2,1,0:T(8,128)(2,1)S(1)}, bf16[2,64,800]{2,1,0:T(8,128)(2,1)S(1)}, u32[]{:S(2)}, u32[]{:S(2)}) collective-permute-start(bf16[2,64,800]{2,1,0:T(8,128)(2,1)S(1)} %get-tuple-element.573), channel_id=1, source_target_pairs={{0,2},{1,3},{2,0},{3,1},{4,6},{5,7},{6,4},{7,5},{8,10},{9,11},{10,... | collective-permute-start | bytes 614408 | tf_op jit(solution)/shard_map/ppermute | solution.py:880
  99.4 14.3 %collective-permute-start.35 = (bf16[2,64,800]{2,1,0:T(8,128)(2,1)S(1)}, bf16[2,64,800]{2,1,0:T(8,128)(2,1)S(1)}, u32[]{:S(2)}, u32[]{:S(2)}) collective-permute-start(bf16[2,64,800]{2,1,0:T(8,128)(2,1)S(1)} %get-tuple-element.574), channel_id=1, source_target_pairs={{0,2},{1,3},{2,0},{3,1},{4,6},{5,7},{6,4},{7,5},{8,10},{9,11},{10,... | collective-permute-start | bytes 614408 | tf_op jit(solution)/shard_map/ppermute | solution.py:880
  102.5 11.3 %collective-permute-start.33 = (bf16[13,32,128]{2,1,0:T(8,128)(2,1)S(1)}, bf16[13,32,128]{2,1,0:T(8,128)(2,1)S(1)}, u32[]{:S(2)}, u32[]{:S(2)}) collective-permute-start(bf16[13,32,128]{2,1,0:T(8,128)(2,1)S(1)} %get-tuple-element.572), channel_id=1, source_target_pairs={{0,16},{8,24},{16,0},{24,8},{1,17},{9,25},{17,1},{25,9},{2,18},{10... | collective-permute-start | bytes 319496 | tf_op jit(solution)/shard_map/ppermute | solution.py:880
  104.1 10.8 %collective-permute-start.31 = (bf16[24,32,128]{2,1,0:T(8,128)(2,1)S(1)}, bf16[24,32,128]{2,1,0:T(8,128)(2,1)S(1)}, u32[]{:S(2)}, u32[]{:S(2)}) collective-permute-start(bf16[24,32,128]{2,1,0:T(8,128)(2,1)S(1)} %shard_map.365.refs_0_), channel_id=1, source_target_pairs={{0,4},{1,5},{2,6},{3,7},{4,0},{5,1},{6,2},{7,3},{8,12},{9,13},{10,... | collective-permute-start | bytes 589832 | tf_op jit(solution)/shard_map/ppermute | solution.py:880
  106.7 16.8 %collective-permute-start.37 = (bf16[368,512]{1,0:T(8,128)(2,1)S(1)}, bf16[368,512]{1,0:T(8,128)(2,1)S(1)}, u32[]{:S(2)}, u32[]{:S(2)}) collective-permute-start(bf16[368,512]{1,0:T(8,128)(2,1)S(1)} %get-tuple-element.583), channel_id=1, source_target_pairs={{0,8},{8,0},{16,24},{24,16},{1,9},{9,1},{17,25},{25,17},{2,10},{10... | collective-permute-start | bytes 1130504 | tf_op jit(solution)/shard_map/ppermute | solution.py:880
  108.5 14.9 %collective-permute-start.38 = (bf16[368,512]{1,0:T(8,128)(2,1)S(1)}, bf16[368,512]{1,0:T(8,128)(2,1)S(1)}, u32[]{:S(2)}, u32[]{:S(2)}) collective-permute-start(bf16[368,512]{1,0:T(8,128)(2,1)S(1)} %get-tuple-element.584), channel_id=1, source_target_pairs={{0,16},{8,24},{16,0},{24,8},{1,17},{9,25},{17,1},{25,9},{2,18},{10... | collective-permute-start | bytes 1130504 | tf_op jit(solution)/shard_map/ppermute | solution.py:880
  113.9 6.8 %collective-permute-start.39 = (bf16[13,32,128]{2,1,0:T(8,128)(2,1)S(1)}, bf16[13,32,128]{2,1,0:T(8,128)(2,1)S(1)}, u32[]{:S(2)}, u32[]{:S(2)}) collective-permute-start(bf16[13,32,128]{2,1,0:T(8,128)(2,1)S(1)} %shard_map.368.refs_0_), channel_id=1, source_target_pairs={{0,4},{1,5},{2,6},{3,7},{4,0},{5,1},{6,2},{7,3},{8,12},{9,13},{10,... | collective-permute-start | bytes 319496 | tf_op jit(solution)/shard_map/ppermute | solution.py:880
  114.9 8.5 %collective-permute-start.36 = (bf16[24,32,128]{2,1,0:T(8,128)(2,1)S(1)}, bf16[24,32,128]{2,1,0:T(8,128)(2,1)S(1)}, u32[]{:S(2)}, u32[]{:S(2)}) collective-permute-start(bf16[24,32,128]{2,1,0:T(8,128)(2,1)S(1)} %shard_map.369.refs_0_), channel_id=1, source_target_pairs={{0,2},{1,3},{2,0},{3,1},{4,6},{5,7},{6,4},{7,5},{8,10},{9,11},{10,... | collective-permute-start | bytes 589832 | tf_op jit(solution)/shard_map/ppermute | solution.py:880
  120.7 12.5 %collective-permute-start.43 = (bf16[13,32,128]{2,1,0:T(8,128)(2,1)S(1)}, bf16[13,32,128]{2,1,0:T(8,128)(2,1)S(1)}, u32[]{:S(2)}, u32[]{:S(2)}) collective-permute-start(bf16[13,32,128]{2,1,0:T(8,128)(2,1)S(1)} %shard_map.370.refs_0_), channel_id=1, source_target_pairs={{0,16},{8,24},{16,0},{24,8},{1,17},{9,25},{17,1},{25,9},{2,18},{10... | collective-permute-start | bytes 319496 | tf_op jit(solution)/shard_map/ppermute | solution.py:880
  122.4 12.6 %collective-permute-start.41 = (bf16[368,512]{1,0:T(8,128)(2,1)S(1)}, bf16[368,512]{1,0:T(8,128)(2,1)S(1)}, u32[]{:S(2)}, u32[]{:S(2)}) collective-permute-start(bf16[368,512]{1,0:T(8,128)(2,1)S(1)} %get-tuple-element.591), channel_id=1, source_target_pairs={{0,24},{8,16},{16,8},{24,0},{1,25},{9,17},{17,9},{25,1},{2,26},{10... | collective-permute-start | bytes 1130504 | tf_op jit(solution)/shard_map/ppermute | solution.py:880
  123.5 13.9 %collective-permute-start.42 = (bf16[12,64,128]{2,1,0:T(8,128)(2,1)S(1)}, bf16[12,64,128]{2,1,0:T(8,128)(2,1)S(1)}, u32[]{:S(2)}, u32[]{:S(2)}) collective-permute-start(bf16[12,64,128]{2,1,0:T(8,128)(2,1)S(1)} %get-tuple-element.598.refs_2_), channel_id=1, source_target_pairs={{0,8},{8,0},{16,24},{24,16},{1,9},{9,1},{17,25},{25,17},{2,10},{10... | collective-permute-start | bytes 589832 | tf_op jit(solution)/shard_map/ppermute | solution.py:880
  124.4 12.9 %collective-permute-start.40 = (bf16[12,64,128]{2,1,0:T(8,128)(2,1)S(1)}, bf16[12,64,128]{2,1,0:T(8,128)(2,1)S(1)}, u32[]{:S(2)}, u32[]{:S(2)}) collective-permute-start(bf16[12,64,128]{2,1,0:T(8,128)(2,1)S(1)} %get-tuple-element.596.refs_0_), channel_id=1, source_target_pairs={{0,16},{8,24},{16,0},{24,8},{1,17},{9,25},{17,1},{25,9},{2,18},{10... | collective-permute-start | bytes 589832 | tf_op jit(solution)/shard_map/ppermute | solution.py:880
  133.3 6.7 %collective-permute-start.48 = (bf16[13,64,128]{2,1,0:T(8,128)(2,1)S(1)}, bf16[13,64,128]{2,1,0:T(8,128)(2,1)S(1)}, u32[]{:S(2)}, u32[]{:S(2)}) collective-permute-start(bf16[13,64,128]{2,1,0:T(8,128)(2,1)S(1)} %shard_map.372.refs_0_), channel_id=1, source_target_pairs={{0,8},{8,0},{16,24},{24,16},{1,9},{9,1},{17,25},{25,17},{2,10},{10... | collective-permute-start | bytes 638984 | tf_op jit(solution)/shard_map/ppermute | solution.py:880
  133.4 6.9 %collective-permute-start.46 = (bf16[1,64,800]{2,1,0:T(8,128)(2,1)S(1)}, bf16[1,64,800]{2,1,0:T(8,128)(2,1)S(1)}, u32[]{:S(2)}, u32[]{:S(2)}) collective-permute-start(bf16[1,64,800]{2,1,0:T(8,128)(2,1)S(1)} %get-tuple-element.602), channel_id=1, source_target_pairs={{0,4},{1,5},{2,6},{3,7},{4,0},{5,1},{6,2},{7,3},{8,12},{9,13},{10,... | collective-permute-start | bytes 307208 | tf_op jit(solution)/shard_map/ppermute | solution.py:880
  135.0 6.7 %collective-permute-start.47 = (bf16[1,64,800]{2,1,0:T(8,128)(2,1)S(1)}, bf16[1,64,800]{2,1,0:T(8,128)(2,1)S(1)}, u32[]{:S(2)}, u32[]{:S(2)}) collective-permute-start(bf16[1,64,800]{2,1,0:T(8,128)(2,1)S(1)} %get-tuple-element.603), channel_id=1, source_target_pairs={{0,4},{1,5},{2,6},{3,7},{4,0},{5,1},{6,2},{7,3},{8,12},{9,13},{10,... | collective-permute-start | bytes 307208 | tf_op jit(solution)/shard_map/ppermute | solution.py:880
  137.5 10.1 %collective-permute-start.45 = (bf16[12,128,128]{2,1,0:T(8,128)(2,1)S(1)}, bf16[12,128,128]{2,1,0:T(8,128)(2,1)S(1)}, u32[]{:S(2)}, u32[]{:S(2)}) collective-permute-start(bf16[12,128,128]{2,1,0:T(8,128)(2,1)S(1)} %get-tuple-element.620.refs_2_), channel_id=1, source_target_pairs={{0,16},{8,24},{16,0},{24,8},{1,17},{9,25},{17,1},{25,9},{2,18},{10... | collective-permute-start | bytes 1179656 | tf_op jit(solution)/shard_map/ppermute | solution.py:880
  139.2 8.9 %collective-permute-start.44 = (bf16[12,128,128]{2,1,0:T(8,128)(2,1)S(1)}, bf16[12,128,128]{2,1,0:T(8,128)(2,1)S(1)}, u32[]{:S(2)}, u32[]{:S(2)}) collective-permute-start(bf16[12,128,128]{2,1,0:T(8,128)(2,1)S(1)} %get-tuple-element.618.refs_0_), channel_id=1, source_target_pairs={{0,8},{8,0},{16,24},{24,16},{1,9},{9,1},{17,25},{25,17},{2,10},{10... | collective-permute-start | bytes 1179656 | tf_op jit(solution)/shard_map/ppermute | solution.py:880
  140.1 10.0 %collective-permute-start.49 = (bf16[13,128,128]{2,1,0:T(8,128)(2,1)S(1)}, bf16[13,128,128]{2,1,0:T(8,128)(2,1)S(1)}, u32[]{:S(2)}, u32[]{:S(2)}) collective-permute-start(bf16[13,128,128]{2,1,0:T(8,128)(2,1)S(1)} %shard_map.374.refs_0_), channel_id=1, source_target_pairs={{0,2},{1,3},{2,0},{3,1},{4,6},{5,7},{6,4},{7,5},{8,10},{9,11},{10,... | collective-permute-start | bytes 1277960 | tf_op jit(solution)/shard_map/ppermute | solution.py:880
  150.1 7.5 %collective-permute-start.50 = (bf16[13,256,128]{2,1,0:T(8,128)(2,1)S(1)}, bf16[13,256,128]{2,1,0:T(8,128)(2,1)S(1)}, u32[]{:S(2)}, u32[]{:S(2)}) collective-permute-start(bf16[13,256,128]{2,1,0:T(8,128)(2,1)S(1)} %shard_map.378.refs_0_), channel_id=1, source_target_pairs={{0,1},{1,0},{2,3},{3,2},{4,5},{5,4},{6,7},{7,6},{8,9},{9,8},{10,11... | collective-permute-start | bytes 2555912 | tf_op jit(solution)/shard_map/ppermute | solution.py:880
  150.2 3.5 %collective-permute-start.52 = (bf16[12,256,128]{2,1,0:T(8,128)(2,1)S(1)}, bf16[12,256,128]{2,1,0:T(8,128)(2,1)S(1)}, u32[]{:S(2)}, u32[]{:S(2)}) collective-permute-start(bf16[12,256,128]{2,1,0:T(8,128)(2,1)S(1)} %get-tuple-element.636.refs_2_), channel_id=1, source_target_pairs={{0,1},{1,0},{2,3},{3,2},{4,5},{5,4},{6,7},{7,6},{8,9},{9,8},{10,11... | collective-permute-start | bytes 2359304 | tf_op jit(solution)/shard_map/ppermute | solution.py:880
  150.7 4.1 %collective-permute-start.51 = (bf16[12,256,128]{2,1,0:T(8,128)(2,1)S(1)}, bf16[12,256,128]{2,1,0:T(8,128)(2,1)S(1)}, u32[]{:S(2)}, u32[]{:S(2)}) collective-permute-start(bf16[12,256,128]{2,1,0:T(8,128)(2,1)S(1)} %get-tuple-element.634.refs_0_), channel_id=1, source_target_pairs={{0,1},{1,0},{2,3},{3,2},{4,5},{5,4},{6,7},{7,6},{8,9},{9,8},{10,11... | collective-permute-start | bytes 2359304 | tf_op jit(solution)/shard_map/ppermute | solution.py:880
  (7 other events, 10.3 us)

commit v3 on v2

--- a/solution.py
+++ b/solution.py
@@ -14,10 +14,36 @@
 LANES = 128
 GROUPS = 4
 FAR = -1e30
+START_COSTS = (0.0, 8.0, 0.0, 6.0, 7.8, 2.0)
 RATE = 1.15e9
-COST_P = 0.0
-COST_Q = 1.0
-COST_K = 2.6
+STEPS = (
+    ("memory", 5.0),
+    ("ffn", 0.5),
+    ("features", 0.3),
+    ("ab2", 0.3),
+    ("c1", 0.3),
+    ("ab3", 2.7),
+    ("ffn1", 0.0),
+    ("c2", 0.3),
+    ("ab4", 0.6),
+    ("c3", 0.3),
+    ("ffn2", 0.0),
+    ("c4", 0.3),
+    ("ab5", 0.3),
+    ("c5", 1.2),
+    ("ab6", 0.3),
+    ("c6", 1.2),
+    ("ab7", 0.5),
+    ("c7", 2.4),
+    ("order", 0.3),
+    ("ffn3", 0.6),
+    ("ab8", 0.6),
+    ("own", 0.0),
+    ("c8", 4.0),
+    ("c_own", 0.0),
+    ("finish", 1.5),
+)
+NEAR_AT, FAR_AT = "ab5", "ab6"
 
 
 def dims(left, right, a, b):
@@ -52,6 +78,15 @@
     rows = value.shape[0] // 2
     lane = lax.broadcasted_iota(jnp.int32, (rows, LANES), 1)
     return jnp.where(lane < LANES // 2, value[:rows], value[rows:])
+
+
+def row_totals(mix, grad, group):
+    lanes = slice(group * LANES, (group + 1) * LANES)
+    product = (mix[:, lanes].astype(F32) * grad[:, lanes].astype(F32)).astype(BF)
+    low, high = lane_masks()
+    heads = jnp.concatenate([low, high, jnp.zeros((14, LANES), BF)], axis=0)
+    sums = nt(heads, product)
+    return jnp.concatenate([sums[0:1], sums[1:2]], axis=1)
 
 
 def eights(value, op):
@@ -112,30 +147,25 @@
         send_ref[index + block] = scratch[pl.ds(other, half), lanes].astype(BF)
 
 
-def pick_kernel(ids, up, down, *refs):
-    outs, sems = refs[:4], refs[4]
+def pick_kernel(ids, up, down, up_half, down_half, up_wide, down_wide, sems):
     core = ids[1]
-    units = up.shape[0]
-    starts = (0, units - outs[1].shape[0], units - outs[2].shape[0], 0)
-    for side, ref in enumerate((up, down)):
-
-        @pl.when(core == side)
-        def _():
-            copies = []
-            for n, (out, start) in enumerate(zip(outs, starts)):
-                half = out.shape[0] // 2
-                for m in range(2):
-                    copies.append(
-                        pltpu.make_async_copy(
-                            ref.at[pl.ds(start + m * half, half)],
-                            out.at[pl.ds(m * half, half)],
-                            sems.at[2 * n + m],
-                        )
+    copies = []
+    for ref, half, wide in ((up, up_half, up_wide), (down, down_half, down_wide)):
+        for out in (half, wide):
+            start = core * (ref.shape[0] - out.shape[0])
+            size = out.shape[0] // 2
+            for m in range(2):
+                copies.append(
+                    pltpu.make_async_copy(
+                        ref.at[pl.ds(pl.multiple_of(start + m * size, 16), size)],
+                        out.at[pl.ds(m * size, size)],
+                        sems.at[len(copies)],
                     )
-            for copy in copies:
-                copy.start()
-            for copy in copies:
-                copy.wait()
+                )
+    for copy in copies:
+        copy.start()
+    for copy in copies:
+        copy.wait()
 
 
 def start_kernel(
@@ -304,44 +334,9 @@
     h2b_out[...] = h2.astype(BF)
 
 
-def ffn_first_kernel(
-    ids, h2_ref, bups, up_own, down_own, fd0, fd1, sd0, sd1, down_out, pre_ref, weights, sems
-):
-    copies = gather_weights(ids[1], weights, sems, ((fd0, fd1), (sd0, sd1)))
-    h2 = h2_ref[...]
-    down = jnp.zeros(h2.shape, F32)
-    for p in range(2):
-        if p:
-            for copy in copies:
-                for one in copy:
-                    one.wait()
-        up = weights[0, 0] if p else up_own[...]
-        dn = weights[1, 0] if p else down_own[...]
-        pre = nt(h2, up) + bias_of(bups, 3 * p, up.shape[0])
-        pre_ref[p] = pre
-        down = down + nn((pre * cdf(pre)).astype(BF), dn)
-    down_out[...] = down
-
-
-def gather_weights(core, weights, sems, sides):
-    units = weights.shape[2]
-    copies = []
-    for n in range(len(sides[0])):
-        take = units // 2
-        source, start = (0, 0) if n % 2 == 0 else (sides[0][n].shape[0] - take, take)
-        copies.append(
-            [
-                pltpu.make_async_copy(
-                    refs[n].at[pl.ds(source, take)],
-                    weights.at[core if side == 0 else 1 - core, n // 2, pl.ds(start, take)],
-                    sems.at[side, n],
-                )
-                for side, refs in enumerate(sides)
-            ]
-        )
-        for one in copies[-1]:
-            one.start()
-    return copies
+def part_of(ref, cut, core):
+    spare = ref.shape[0] - cut
+    return ref[pl.ds(pl.multiple_of(core * spare, 16), cut), :]
 
 
 def bias_of(bups, p, units):
@@ -349,6 +344,29 @@
     return jnp.concatenate(
         [bups[2 * p : 2 * p + 1], bups[2 * p + 1 : 2 * p + 2, : units - width]], axis=1
     )
+
+
+def bias_halves(bups, p, units, core):
+    whole = bias_of(bups, p, units)
+    low, high = whole[:, : units // 2], whole[:, units // 2 :]
+    return jnp.where(core == 0, low, high), jnp.where(core == 0, high, low)
+
+
+def ffn_first_kernel(
+    ids, h2_ref, bups, up_own, down_own, up_f, down_f, up_s, down_s, down_out, pre_own, pre_far
+):
+    core = ids[1]
+    h2 = h2_ref[...]
+    units = up_own.shape[0]
+    pre = nt(h2, up_own[...]) + bias_of(bups, 0, units)
+    pre_own[...] = pre
+    down = nn((pre * cdf(pre)).astype(BF), down_own[...])
+    biases = bias_halves(bups, 3, units, core)
+    for n, (up, dn) in enumerate(((up_f, down_f), (up_s, down_s))):
+        pre = nt(h2, up[...]) + biases[n]
+        pre_far[n] = pre
+        down = down + nn((pre * cdf(pre)).astype(BF), dn[...])
+    down_out[...] = down
 
 
 def ffn_second_kernel(
@@ -362,64 +380,72 @@
     up_own,
     down_own,
     down_ref,
-    pre_ref,
-    far,
+    pre_own,
+    pre_far,
     misc,
     gains,
     shifts,
-    fx0,
-    fx1,
-    fy0,
-    fy1,
-    sx0,
-    sx1,
-    sy0,
-    sy1,
+    xu_f,
+    xd_f,
+    yu_f,
+    yd_f,
+    du_f,
+    dd_f,
+    xu_s,
+    xd_s,
+    yu_s,
+    yd_s,
+    du_s,
+    dd_s,
     res_out,
     ops_out,
     g2_out,
     small_out,
     bup_out,
-    near,
-    sems,
+    pre_near,
 ):
-    copies = gather_weights(ids[1], near, sems, ((fx0, fx1, fy0, fy1), (sx0, sx1, sy0, sy1)))
-    h2 = h2_ref[...]
-    width = h2.shape[1]
+    core = ids[1]
     units = up_own.shape[0]
+    cut = units // 2
+    width = h2_ref.shape[1]
+    near = (
+        (xu_f, xd_f, core),
+        (xu_s, xd_s, 1 - core),
+        (yu_f, yd_f, core),
+        (yu_s, yd_s, 1 - core),
+    )
     h2b = h2b_ref[...]
     down = down_ref[...]
-    pres = [pre_ref[0]]
-    for p in range(2):
-        for copy in copies[2 * p : 2 * p + 2]:
-            for one in copy:
-                one.wait()
-        pre = nt(h2b, near[0, p]) + bias_of(bups, p + 1, units)
-        pres.append(pre)
-        down = down + nn((pre * cdf(pre)).astype(BF), near[1, p])
-    pres.append(pre_ref[1])
-    xhat, rstd = norm(h2 + down + row(misc, 1))
+    for n, (up, dn, place) in enumerate(near):
+        pre = nt(h2b, part_of(up, cut, place)) + bias_halves(bups, n // 2 + 1, units, core)[n % 2]
+        pre_near[n] = pre
+        down = down + nn((pre * cdf(pre)).astype(BF), part_of(dn, cut, place))
+    xhat, rstd = norm(h2_ref[...] + down + row(misc, 1))
     res_out[...] = (xhat * row(gains, 2) + row(shifts, 2)).astype(BF)
     g3, dgain3, dshift3 = norm_back(xhat, rstd, row(gains, 2), cot_ref[...].astype(F32))
     gb = g3.astype(BF)
     ops_out[:, :width] = h2b
     ops_out[:, width:] = gb
-    gh = g3
-    for p, (up, dn) in enumerate(
-        (
-            (up_own[...], down_own[...]),
-            (near[0, 0], near[1, 0]),
-            (near[0, 1], near[1, 1]),
-            (far[0, 0], far[1, 0]),
-        )
-    ):
-        pre = pres[p]
+
+    def unit_grads(pre, dn):
         ga = nt(gb, dn).astype(BF).astype(F32)
-        gp = (ga * (cdf(pre) + pre * density(pre))).astype(BF)
-        bup_out[p] = jnp.concatenate(
-            [column_sum(gp), jnp.zeros((1, 2 * width - units), F32)], axis=1
-        )
-        gh = gh + nn(gp, up)
+        return (ga * (cdf(pre) + pre * density(pre))).astype(BF)
+
+    tail = jnp.zeros((1, 2 * width - units), F32)
+    gp = unit_grads(pre_own[...], down_own[...])
+    bup_out[0] = jnp.concatenate([column_sum(gp), tail], axis=1)
+    gh = g3 + nn(gp, up_own[...])
+    blocks = list(near) + [(du_f, dd_f, core), (du_s, dd_s, 1 - core)]
+    for p in range(3):
+        sums = []
+        for n in (2 * p, 2 * p + 1):
+            up, dn, place = blocks[n]
+            gp = unit_grads(pre_near[n] if n < 4 else pre_far[n - 4], part_of(dn, cut, place))
+            sums.append(column_sum(gp))
+            gh = gh + nn(gp, part_of(up, cut, place))
+        low = jnp.where(core == 0, sums[0], sums[1])
+        high = jnp.where(core == 0, sums[1], sums[0])
+        bup_out[p + 1] = jnp.concatenate([low, high, tail], axis=1)
     g2, dgain2, dshift2 = norm_back(xhat2_ref[...], rstd2_ref[...], row(gains, 1), gh)
     g2_out[...] = g2
     small_out[0:1] = dgain3
@@ -464,7 +490,6 @@
     send1,
     send2,
     send3,
-    dp_ref,
     work,
     gq_ref,
     gk_ref,
@@ -478,21 +503,15 @@
     branch = g2.astype(BF)
     gcm_out[...] = nt(branch, cross_out[...]).astype(BF)
     padded = k_ref.shape[0] // GROUPS
+    gcm = gcm_out[...]
     for g in range(GROUPS):
         lanes = slice(g * LANES, (g + 1) * LANES)
-        grads = pair(gcm_out[...], g)
-        total = jnp.zeros((8, 2 * rows), F32)
+        grads = pair(gcm, g)
+        total = row_totals(cm_ref[...], gcm, g)
         for j in range(GROUPS):
             here = slice(j * padded, (j + 1) * padded)
-            dp = nt(v_ref[here, lanes], grads).astype(BF)
-            dp_ref[here] = dp
-            total = total + eights(pc_ref[g, here].astype(F32) * dp.astype(F32), jnp.sum)
-        total = jnp.sum(total, 0, keepdims=True)
-        for j in range(GROUPS):
-            here = slice(j * padded, (j + 1) * padded)
-            ds_out[g, here] = (
-                pc_ref[g, here].astype(F32) * (dp_ref[here].astype(F32) - total)
-            ).astype(BF)
+            dp = nt(v_ref[here, lanes], grads)
+            ds_out[g, here] = (pc_ref[g, here].astype(F32) * (dp - total)).astype(BF)
         gq_ref[:, lanes] = unpair(tn(ds_out[g], k_ref[:, lanes])).astype(BF) * 0.125
     gcq = gq_ref[...]
     gci = nt(gcq, cross_proj[0])
@@ -510,9 +529,8 @@
         lanes = slice(g * LANES, (g + 1) * LANES)
         grads = pair(gsm, g)
         p = ps_ref[g]
-        dp = nt(sv_ref[:, lanes], grads).astype(BF).astype(F32)
-        pf = p.astype(F32)
-        ds = (pf * (dp - jnp.sum(pf * dp, 0, keepdims=True))).astype(BF)
+        dp = nt(sv_ref[:, lanes], grads)
+        ds = (p.astype(F32) * (dp - row_totals(sm_ref[...], gsm, g))).astype(BF)
         gq_ref[:, lanes] = unpair(tn(ds, sk_ref[:, lanes])).astype(BF) * 0.125
         gk_ref[:, lanes] = nn(ds, pair(sq_ref[...], g)).astype(BF)
         gv_ref[:, lanes] = nn(p, grads).astype(BF)
@@ -573,24 +591,16 @@
     ki,
     vi,
     cross_proj,
-    in_proj,
-    res_ref,
-    gx_ref,
     gpos_ref,
     small_a,
     small_b,
     bup,
     held,
-    rows0,
-    rows1,
-    rows2,
-    rows3,
+    gm_ref,
     keep,
     send,
     gk_ref,
     gv_ref,
-    gm_ref,
-    gf_ref,
     work,
     small,
     *,
@@ -598,7 +608,7 @@
 ):
     pb, core = ids[0], ids[1]
     width = featp.shape[1]
-    rows = res_ref.shape[0]
+    rows = gpos_ref.shape[0]
     block = rows // GROUPS
     padded = featp.shape[0] // GROUPS
     pairs_q = [pair(cq_ref[...], g) for g in range(GROUPS)]
@@ -611,12 +621,6 @@
             gv_ref[here, lanes] = nn(pc_ref[g, here], pairs_g[g]).astype(BF)
         gm = (nt(gk_ref[here], cross_proj[1]) + nt(gv_ref[here], cross_proj[2])).astype(BF)
         gm_ref[here] = gm
-        gf_ref[j] = nt(gm, in_proj[...]).astype(BF)
-    for k, ref in enumerate((rows0, rows1, rows2, rows3)):
-        at = pl.multiple_of((pb ^ k) * block, block)
-        ref[0:padded] = gf_ref[pb ^ k]
-        ref[padded : padded + block] = gx_ref[pl.ds(at, block), :]
-        ref[padded + block : padded + 2 * block] = res_ref[pl.ds(at, block), :]
     put_halves(core, tn(ki[...], gk_ref[...]), 0, keep, send, work)
     put_halves(core, tn(vi[...], gv_ref[...]), 4, keep, send, work)
     put_halves(core, tn(featp[...], gm_ref[...]), 8, keep, send, work)
@@ -653,57 +657,120 @@
             ref[12, b * rows : (b + 1) * rows] = jnp.where(side == 0, low, high).astype(BF)
 
 
+def feature_grad_kernel(ids, gm_ref, in_proj, res_ref, gx_ref, rows0, rows1, rows2, rows3, gf_ref):
+    pb = ids[0]
+    padded = gf_ref.shape[1]
+    block = res_ref.shape[0] // GROUPS
+    for j in range(GROUPS):
+        gf_ref[j] = nt(gm_ref[j * padded : (j + 1) * padded], in_proj[...]).astype(BF)
+    for k, ref in enumerate((rows0, rows1, rows2, rows3)):
+        at = pl.multiple_of((pb ^ k) * block, block)
+        ref[0:padded] = gf_ref[pb ^ k]
+        ref[padded : padded + block] = gx_ref[pl.ds(at, block), :]
+        ref[padded + block : padded + 2 * block] = res_ref[pl.ds(at, block), :]
+
+
 def spare_row(index, block, rows_used):
     return index // 5 * block + rows_used + index % 5
 
 
-def put_whole(core, out, index, own, got):
-    half = own.shape[1]
-    mine = pl.multiple_of(core * half, half)
-    other = pl.multiple_of((1 - core) * half, half)
-    for b in range(4):
-        put_block(mine, other, half, out, b, own, got, index + b)
-
-
-def put_block(mine, other, half, out, b, own, got, index):
-    lanes = slice(b * LANES, (b + 1) * LANES)
-    out[pl.ds(mine, half), lanes] = own[index].astype(F32)
-    out[pl.ds(other, half), lanes] = got[index].astype(F32)
-
-
-def finish_chain_kernel(ids, own1, got1, own2, got2, cross_q, self_out, cross_out, self_proj):
-    core = ids[1]
-    put_whole(core, cross_q, 0, own1, got1)
-    put_whole(core, self_out, 4, own1, got1)
-    put_whole(core, cross_out, 8, own1, got1)
-    for m in range(3):
-        put_whole(core, self_proj.at[m], 4 * m, own2, got2)
-
-
-def finish_memory_kernel(
-    ids, own1, got1, cross_q, cross_, in_, pos_, self_bias_, cross_bias_, bup_, bdown_, gain_, shift_, inb_, small, *, rows_used
+def write_rows(core, refs, places, work, sems):
+    half = work.shape[1]
+    rows = pl.ds(pl.multiple_of(core * half, half), half)
+    copies = []
+    for n, (ref, first, matrix) in enumerate(places):
+        for b in range(4):
+            work[n, :, b * LANES : (b + 1) * LANES] = refs[ref][first + b].astype(F32)
+        copies.append(pltpu.make_async_copy(work.at[n], matrix.at[rows], sems.at[n]))
+        copies[-1].start()
+    return copies
+
+
+def chain_places(cross, self_out, cross_out, self_proj):
+    return [
+        (0, 0, cross.at[0]),
+        (0, 4, self_out),
+        (0, 8, cross_out),
+        (1, 0, self_proj.at[0]),
+        (1, 4, self_proj.at[1]),
+        (1, 8, self_proj.at[2]),
+    ]
+
+
+def chain_own_kernel(ids, va, vb, cross, self_out, cross_out, self_proj, work, sems):
+    places = chain_places(cross, self_out, cross_out, self_proj)
+    for copy in write_rows(ids[1], (va, vb), places, work, sems):
+        copy.wait()
+
+
+def chain_other_kernel(
+    ids, ra, rb, in0, in1, in2, in3, cross, self_out, cross_out, self_proj, work, sems
+):
+    places = chain_places(cross, self_out, cross_out, self_proj)
+    for copy in write_rows(1 - ids[1], (ra, rb), places, work, sems):
+        copy.wait()
+
+
+def memory_places(cross, in_):
+    return [(0, 0, cross.at[1]), (0, 4, cross.at[2]), (0, 8, in_)]
+
+
+def memory_own_kernel(ids, vc, cross_in, cross, in_, work, sems):
+    for copy in write_rows(ids[1], (vc,), memory_places(cross, in_), work, sems):
+        copy.wait()
+
+
+def memory_other_kernel(
+    ids,
+    rc,
+    vc,
+    cross_in,
+    in_in,
+    pos_,
+    self_bias_,
+    cross_bias_,
+    bup_,
+    bdown_,
+    gain_,
+    shift_,
+    inb_,
+    cross,
+    in_,
+    work,
+    sems,
+    small,
+    tiles,
+    *,
+    rows_used,
+    units,
 ):
     core = ids[1]
-    cross_[0] = cross_q[...]
-    half = own1.shape[1]
-    mine = pl.multiple_of(core * half, half)
-    other = pl.multiple_of((1 - core) * half, half)
-    for index in range(12):
-        out = (cross_.at[1], cross_.at[2], in_)[index // 4]
-        put_block(mine, other, half, out, index % 4, own1, got1, index)
+    copies = write_rows(1 - core, (rc,), memory_places(cross, in_), work, sems)
     rows, width = small.shape
     block = rows // GROUPS
     for b in range(2):
         here = slice(b * rows, (b + 1) * rows)
-        first = own1[12, here].astype(F32)
-        second = got1[12, here].astype(F32)
+        first = vc[12, here].astype(F32)
+        second = rc[12, here].astype(F32)
         small[:, b * LANES : (b + 1) * LANES] = jnp.where(core == 0, first, second)
         small[:, (2 + b) * LANES : (3 + b) * LANES] = jnp.where(core == 0, second, first)
+    lane = lax.broadcasted_iota(jnp.int32, (8, LANES), 1)
+    tiles[...] = jnp.zeros(tiles.shape, F32)
     for b in range(GROUPS):
         pos_[b * rows_used : (b + 1) * rows_used] = small[b * block : b * block + rows_used]
         at = b * block + rows_used + 5
-        bup_[b : b + 1, :width] = small[at : at + 1]
-        bup_[b : b + 1, width:] = small[at + 1 : at + 2]
+        first, shift = b * units // LANES, b * units % LANES
+        both = [
+            small[at + n : at + n + 1, m * LANES : (m + 1) * LANES]
+            for n in range(2)
+            for m in range(4)
+        ]
+        part = jnp.concatenate(both, axis=0)
+        if shift:
+            part = pltpu.roll(part, shift, 1)
+        tiles[first : first + 8] += jnp.where(lane >= shift, part, 0.0)
+        tiles[first + 1 : first + 9] += jnp.where(lane < shift, part, 0.0)
+    bup_[...] = tiles[: bup_.shape[0]]
 
     def spare(index):
         at = spare_row(index, block, rows_used)
@@ -714,6 +781,8 @@
             ref[i : i + 1] = spare(index + i)
     bdown_[...] = spare(12)
     inb_[...] = spare(13)
+    for copy in copies:
+        copy.wait()
 
 
 def hold_kernel(ids, got1, got2, got3, branch, out):
@@ -794,7 +863,9 @@
         return list(lax.optimization_barrier((*values, self.token)))[:-1]
 
 
-def call(order, kernel, args, outs, scratch=(), limit=16, near=True, micros=0.6, through=()):
+def call(
+    order, kernel, args, outs, scratch=(), limit=16, near=True, micros=0.6, through=(), raw=(), alias=()
+):
     through = order.after(through)
     bare = order.after([arg.value if isinstance(arg, (Far, Raw)) else arg for arg in args])
     args = [
@@ -806,7 +877,7 @@
         for value, arg in zip(bare, args)
     ]
     specs, values, extra, emitted, plans = [], [], [], [], []
-    outs = list(outs)
+    outs, raw = list(outs), list(raw)
     for arg in args:
         if isinstance(arg, (Far, Raw)):
             value = arg.value
@@ -835,7 +906,7 @@
 
     def body(*refs):
         given, rest = list(refs[: len(args)]), refs[len(args) + len(through) :]
-        first, rest = rest[: len(outs)], rest[len(outs) :]
+        first, rest = rest[: len(outs) + len(raw)], rest[len(outs) + len(raw) :]
         copies, rest = rest[: len(emitted)], rest[len(emitted) + len(through) :]
         own, late = rest[: len(scratch)], rest[len(scratch) :]
         waits = []
@@ -856,15 +927,16 @@
             for n in sorted(one.waiting):
                 one.ready(n)
 
-    whole = [(o, near) for o in outs] + [(o, True) for o in emitted]
+    whole = [(o, near) for o in outs] + [(o, False) for o in raw] + [(o, True) for o in emitted]
+    spaces = [pltpu.VMEM] * len(outs) + [pl.ANY] * len(raw) + [pltpu.VMEM] * len(emitted)
     result = pl.pallas_call(
         body,
         out_shape=[pltpu.VMEM(*o) if here else jax.ShapeDtypeStruct(*o) for o, here in whole]
         + [jax.ShapeDtypeStruct(value.shape, value.dtype) for value in through],
         in_specs=specs + [pl.BlockSpec(memory_space=pl.ANY)] * len(through),
-        out_specs=[pl.BlockSpec(memory_space=pltpu.VMEM)] * len(whole)
+        out_specs=[pl.BlockSpec(memory_space=space) for space in spaces]
         + [pl.BlockSpec(memory_space=pl.ANY)] * len(through),
-        input_output_aliases={len(args) + n: len(whole) + n for n in range(len(through))},
+        input_output_aliases={len(args) + n: len(whole) + n for n in range(len(through))} | dict(alias),
         scratch_shapes=list(scratch) + extra,
         compiler_params=pltpu.CompilerParams(vmem_limit_bytes=limit * 1024 * 1024),
         cost_estimate=pl.CostEstimate(
@@ -1021,7 +1093,7 @@
 
     up, down = w_up.T, w_down.T
     cut = units // 2
-    low, high, after, before = call(
+    up_half, down_half, up_wide, down_wide = call(
         order,
         pick_kernel,
         [Raw(up), Raw(down)],
@@ -1030,8 +1102,8 @@
         scratch=[pltpu.SemaphoreType.DMA((8,))],
         limit=4,
     )
-    fy0 = swap(low, *Y_WAY)
-    fx1 = swap(high, *X_WAY)
+    fy0 = swap(up_half, *Y_WAY)
+    fx1 = swap(down_half, *X_WAY)
     misc = (
         jnp.pad(in_bias[None], ((0, 3), (0, 0)))
         + jnp.pad(b_down[None], ((1, 2), (0, 0)))
@@ -1079,12 +1151,12 @@
             Far(cross_bias),
         ],
         [(wide, BF)] * 5,
-        micros=0.0,
+        micros=START_COSTS[0],
         scratch=[pltpu.VMEM((mem, width), BF), pltpu.SemaphoreType.DMA],
     )
-    fx1, fy0, after, before = order.after((fx1, fy0, after, before))
-    fx0 = swap(before, *X_WAY)
-    fy1 = swap(after, *Y_WAY)
+    fx1, fy0, up_wide, down_wide = order.after((fx1, fy0, up_wide, down_wide))
+    fx0 = swap(up_wide, *X_WAY)
+    fy1 = swap(down_wide, *Y_WAY)
     fx1, fy0, *got = order.after((fx1, fy0, *got))
     fd0 = swap(fy0, *X_WAY)
     fd1 = swap(fx1, *Y_WAY)
@@ -1133,22 +1205,21 @@
             ((2 * pb_size, width), F32),
             (flat, BF),
         ],
-        micros=8.0,
+        micros=START_COSTS[1],
         scratch=[pltpu.VMEM((slots, 2 * rows), F32), pltpu.VMEM(flat, F32)],
     )
     fd0, fd1 = order.after((fd0, fd1))
     sd0, sd1 = swap(fd0, *CORE), swap(fd1, *CORE)
-    down_part, pre, far_weights = call(
+    down_part, pre_own, pre_far = call(
         order,
         ffn_first_kernel,
-        [h2b, bups, up, down, Raw(fd0), Raw(fd1), Raw(sd0), Raw(sd1)],
-        [(flat, F32), ((2, rows, units), F32), ((2, 1, units, width), BF)],
-        micros=0.0,
-        scratch=[pltpu.SemaphoreType.DMA((2, 2))],
+        [h2b, bups, up, down, fd0, fd1, sd0, sd1],
+        [(flat, F32), ((rows, units), F32), ((2, rows, cut), F32)],
+        micros=START_COSTS[2],
     )
     fx0, fy1 = order.after((fx0, fy1))
     sx0, sy1 = swap(fx0, *CORE), swap(fy1, *CORE)
-    near = [fx0, fx1, fy0, fy1, sx0, sx1, sy0, sy1]
+    pieces = [fx0, fx1, fy0, fy1, fd0, fd1, sx0, sx1, sy0, sy1, sd0, sd1]
     res, ops, g2, small_a, bup = call(
         order,
         ffn_second_kernel,
@@ -1162,12 +1233,12 @@
             up,
             down,
             down_part,
-            pre,
-            far_weights,
+            pre_own,
+            pre_far,
             misc,
             norm_gain,
             norm_bias,
-            *[Raw(value) for value in near],
+            *pieces,
         ],
         [
             (flat, BF),
@@ -1176,8 +1247,8 @@
             ((8, width), F32),
             ((pb_size, 1, 2 * width), F32),
         ],
-        micros=6.0,
-        scratch=[pltpu.VMEM((2, 2, units, width), BF), pltpu.SemaphoreType.DMA((2, 4))],
+        micros=START_COSTS[3],
+        scratch=[pltpu.VMEM((4, rows, cut), F32)],
     )
     others = [swap(ops, "pb", k) for k in range(1, pb_size)]
     halves = ((24, width // 2, LANES), BF)
@@ -1216,9 +1287,8 @@
             halves,
         ]
         + [((6, width // 2, LANES), BF)] * 4,
-        micros=7.8,
+        micros=START_COSTS[4],
         scratch=[
-            pltpu.VMEM((slots, 2 * rows), BF),
             pltpu.VMEM((width, width), F32),
             pltpu.VMEM(flat, BF),
             pltpu.VMEM(flat, BF),
@@ -1227,7 +1297,7 @@
     )
     got12 = [swap(send, *CORE) for send in sends12]
     piece = width // dp_size
-    (held,) = call(order, hold_kernel, [*others, gcm], [((16, LANES), BF)], limit=2, micros=2.0)
+    (held,) = call(order, hold_kernel, [*others, gcm], [((16, LANES), BF)], limit=2, micros=START_COSTS[5])
     ka, sa, kb, sb = fold(
         order,
         [
@@ -1251,123 +1321,237 @@
         return keep, [swap(send, *way) for send in sends]
 
     halves3 = ((13, width // 2, LANES), BF)
-    *rows_out, keep3, send3 = call(
-        order,
-        functools.partial(memory_back_kernel, rows_used=used),
-        [
-            ds,
-            pc,
-            cq,
-            gcm,
-            featp,
-            ki,
-            vi,
-            cross_proj,
-            in_proj,
-            res,
-            gx,
-            gpos,
-            small_a,
-            small_b,
-            bup,
-            held,
-        ],
-        [((padded + 2 * block, width), BF)] * 4 + [halves3, halves3],
-        micros=6.4,
-        scratch=[
-            pltpu.VMEM(wide, BF),
-            pltpu.VMEM(wide, BF),
-            pltpu.VMEM(wide, BF),
-            pltpu.VMEM((pb_size, padded, width), BF),
-            pltpu.VMEM((width, width), F32),
-            pltpu.VMEM(flat, F32),
-        ],
-    )
-
-    fkeep, *fsends = call(
-        order,
-        ffn_grad_kernel,
-        [ops, *others, up, misc, down],
-        [((2, dp_size // 2, piece, units), BF)] + [((dp_size // 2, piece, units), BF)] * 2,
-        micros=2.8,
-        scratch=[pltpu.VMEM((width, units), F32)],
-    )
-    fgots = [swap(send, *CORE) for send in fsends]
-    ra, rb, send3 = lax.optimization_barrier((ra, rb, send3))
-    got3 = swap(send3, *CORE)
     z_way, far_ways = ways[0], ways[1:]
-    ka, sa, kb, sb = fold(
-        order, [([(ka, ra, 0, 12, 0)], Y_WAY), ([(kb, rb, 0, 12, 0)], X_WAY)], 0.3
-    )
-    ra, rb = swap(sa, *Y_WAY), swap(sb, *X_WAY)
-    kc, sc = fold(order, [([(keep3, got3, 0, 13, 0)], z_way)], 0.3)
-    rc = swap(sc, *z_way)
-    kab, sab = fold(order, [([(ka, ra, 0, 12, 0), (kb, rb, 0, 12, 0)], z_way)], 2.7)
-    rab = swap(sab, *z_way)
-    fkeep, fgots = ffn_fold(fkeep, fgots, 0.0)
-    kc, sc = fold(order, [([(kc, rc, 0, 13, 0)], X_WAY)], 0.3)
-    rc = swap(sc, *X_WAY)
-    vab = add_up(order, [(kab, rab)], 0.6)
-    for way in far_ways[:-1]:
-        rab = swap(vab, *way)
-        vab = add_up(order, [(vab, rab)], 0.3)
-    rab = swap(vab, *far_ways[-1])
-    kc, sc = fold(order, [([(kc, rc, 0, 13, 0)], Y_WAY)], 0.3)
-    rc = swap(sc, *Y_WAY)
-    arrived = [rows_out[0]] + [swap(rows_out[k], "pb", k) for k in range(1, pb_size)]
-    while fkeep.shape[1] > 1:
-        fkeep, fgots = ffn_fold(fkeep, fgots, 0.0)
-    vc = add_up(order, [(kc, rc)], 0.3)
-    for way in far_ways[:-1]:
-        rc = swap(vc, *way)
-        vc = add_up(order, [(vc, rc)], 0.3)
-    rc = swap(vc, *far_ways[-1])
-    vab = add_up(order, [(vab, rab)], 0.3)
-    rab = swap(vab, *z_way)
-    vc = add_up(order, [(vc, rc)], 1.2)
-    rc = swap(vc, *Y_WAY)
-    rab, *arrived[1:3] = lax.optimization_barrier((rab, *arrived[1:3]))
-    va, vb = join(order, [(vab, rab, z_way, [(0, 12), (12, 24)])], 0.3)
-    ra, rb = swap(va, *Y_WAY), swap(vb, *X_WAY)
-    (vc,) = join(order, [(vc, rc, Y_WAY, [(0, 13)])], 1.2)
-    rc = swap(vc, *X_WAY)
-    ra, arrived[3] = lax.optimization_barrier((ra, arrived[3]))
-    va, vb = join(order, [(va, ra, Y_WAY, [(0, 12)]), (vb, rb, X_WAY, [(0, 12)])], 0.5)
-    ra, rb = swap(va, *X_WAY), swap(vb, *Y_WAY)
-    (vc,) = join(order, [(vc, rc, X_WAY, [(0, 13)])], 2.4)
-    rc = swap(vc, *z_way)
-    exchanged = call(
-        order,
-        functools.partial(order_kernel, block=block),
-        arrived,
-        [(tokens.shape, BF), (tokens.shape, BF), ((pb_size, part, width), BF)],
-        micros=0.3,
-    )
-    exchanged = [turn(value) for value in exchanged]
-    ffn_up, ffn_down = call(
-        order, ffn_finish_kernel, [fkeep, *fgots], [((piece, units), F32)] * 2, near=False
-    )
-    va, vb, *exchanged = join(
-        order, [(va, ra, X_WAY, [(0, 12)]), (vb, rb, Y_WAY, [(0, 12)])], 0.6, exchanged
-    )
-    layer_out, grad_tokens, grad_features = [turn(value) for value in exchanged]
-    ra, rb = swap(va, *CORE), swap(vb, *CORE)
-    (vc,) = join(order, [(vc, rc, z_way, [(0, 13)])], 4.0)
-    rc = swap(vc, *CORE)
     matrix = ((width, width), F32)
     three = ((3, width, width), F32)
-    g_cross_q, g_self_out, g_cross_out, g_self_proj = call(
-        order,
-        finish_chain_kernel,
-        [va, ra, vb, rb],
-        [matrix, matrix, matrix, three],
-        near=False,
-    )
+    st = {"ra": ra, "rb": rb}
+
+    def ffn_fold(micros):
+        keep = st["fkeep"]
+        way = ways[(dp_size // 2).bit_length() - keep.shape[1].bit_length()]
+        half = keep.shape[1] // 2
+        st["fkeep"], *sends = call(
+            order,
+            functools.partial(ffn_fold_kernel, bit=place_of(way)),
+            [keep, *st["fgots"]],
+            [((2, half, piece, units), BF)] + [((half, piece, units), BF)] * 2,
+            limit=4,
+            micros=micros,
+        )
+        st["fgots"] = [swap(send, *way) for send in sends]
+
+    def memory(micros):
+        st["gm"], st["keep3"], st["send3"] = call(
+            order,
+            functools.partial(memory_back_kernel, rows_used=used),
+            [ds, pc, cq, gcm, featp, ki, vi, cross_proj, gpos, small_a, small_b, bup, held],
+            [(wide, BF), halves3, halves3],
+            micros=micros,
+            scratch=[
+                pltpu.VMEM(wide, BF),
+                pltpu.VMEM(wide, BF),
+                pltpu.VMEM((width, width), F32),
+                pltpu.VMEM(flat, F32),
+            ],
+        )
+
+    def ffn(micros):
+        st["fkeep"], *sends = call(
+            order,
+            ffn_grad_kernel,
+            [ops, *others, up, misc, down],
+            [((2, dp_size // 2, piece, units), BF)] + [((dp_size // 2, piece, units), BF)] * 2,
+            micros=micros,
+            scratch=[pltpu.VMEM((width, units), F32)],
+        )
+        st["fgots"] = [swap(send, *CORE) for send in sends]
+
+    def ffn_last(micros):
+        st["ffn"] = call(
+            order,
+            ffn_finish_kernel,
+            [st["fkeep"], *st["fgots"]],
+            [((piece, units), F32)] * 2,
+            near=False,
+            micros=micros,
+        )
+
+    def features_step(micros):
+        rows_out = call(
+            order,
+            feature_grad_kernel,
+            [st["gm"], in_proj, res, gx],
+            [((padded + 2 * block, width), BF)] * 4,
+            micros=micros,
+            scratch=[pltpu.VMEM((pb_size, padded, width), BF)],
+        )
+        st["arrived"] = [rows_out[0]] + [swap(rows_out[k], "pb", k) for k in range(1, pb_size)]
+
+    def ab2(micros):
+        ra, rb, send3 = order.after([st["ra"], st["rb"], st["send3"]])
+        st["got3"] = swap(send3, *CORE)
+        st["ka"], sa, st["kb"], sb = fold(
+            order,
+            [([(ka, ra, 0, 12, 0)], Y_WAY), ([(kb, rb, 0, 12, 0)], X_WAY)],
+            micros,
+        )
+        st["ra"], st["rb"] = swap(sa, *Y_WAY), swap(sb, *X_WAY)
+
+    def ab3(micros):
+        st["kab"], send = fold(
+            order, [([(st["ka"], st["ra"], 0, 12, 0), (st["kb"], st["rb"], 0, 12, 0)], z_way)], micros
+        )
+        st["rab"] = swap(send, *z_way)
+
+    def exchange(name, keep, got, micros):
+        total = add_up(order, [(keep, got)], micros)
+        for way in far_ways[:-1]:
+            total = add_up(order, [(total, swap(total, *way))], micros)
+        st["v" + name] = total
+        st["r" + name] = swap(total, *far_ways[-1])
+
+    def ab4(micros):
+        exchange("ab", st["kab"], st["rab"], micros)
+
+    def ab5(micros):
+        st["vab"] = add_up(order, [(st["vab"], st["rab"])], micros)
+        st["rab"] = swap(st["vab"], *z_way)
+
+    def ab6(micros):
+        va, vb = join(order, [(st["vab"], st["rab"], z_way, [(0, 12), (12, 24)])], micros)
+        st["va"], st["vb"] = va, vb
+        st["ra"], st["rb"] = swap(va, *Y_WAY), swap(vb, *X_WAY)
+
+    def ab7(micros):
+        va, vb = join(
+            order,
+            [(st["va"], st["ra"], Y_WAY, [(0, 12)]), (st["vb"], st["rb"], X_WAY, [(0, 12)])],
+            micros,
+        )
+        st["va"], st["vb"] = va, vb
+        st["ra"], st["rb"] = swap(va, *X_WAY), swap(vb, *Y_WAY)
+
+    def ab8(micros):
+        va, vb, *st["exchanged"] = join(
+            order,
+            [(st["va"], st["ra"], X_WAY, [(0, 12)]), (st["vb"], st["rb"], Y_WAY, [(0, 12)])],
+            micros,
+            st["exchanged"],
+        )
+        st["va"], st["vb"] = va, vb
+        st["ra"], st["rb"] = swap(va, *CORE), swap(vb, *CORE)
+
+    def c_fold(way, first=False):
+        def run(micros):
+            keep, got = (st["keep3"], st["got3"]) if first else (st["kc"], st["rc"])
+            st["kc"], send = fold(order, [([(keep, got, 0, 13, 0)], way)], micros)
+            st["rc"] = swap(send, *way)
+
+        return run
+
+    def c4(micros):
+        exchange("c", st["kc"], st["rc"], micros)
+
+    def c5(micros):
+        st["vc"] = add_up(order, [(st["vc"], st["rc"])], micros)
+        st["rc"] = swap(st["vc"], *Y_WAY)
+
+    def c_join(way, onward):
+        def run(micros):
+            (st["vc"],) = join(order, [(st["vc"], st["rc"], way, [(0, 13)])], micros)
+            st["rc"] = swap(st["vc"], *onward)
+
+        return run
+
+    def order_rows(micros):
+        exchanged = call(
+            order,
+            functools.partial(order_kernel, block=block),
+            st["arrived"],
+            [(tokens.shape, BF), (tokens.shape, BF), ((pb_size, part, width), BF)],
+            micros=micros,
+        )
+        st["exchanged"] = [turn(value) for value in exchanged]
+
+    half = width // 2
+    six = [pltpu.VMEM((6, half, width), F32), pltpu.SemaphoreType.DMA((6,))]
+    chain = [three, matrix, matrix, three]
+
+    def own(micros):
+        st["chain"] = call(
+            order, chain_own_kernel, [st["va"], st["vb"]], [], raw=chain, scratch=six, micros=micros
+        )
+
+    def finish(micros):
+        st["chain"] = call(
+            order,
+            chain_other_kernel,
+            [st["ra"], st["rb"], *[Raw(value) for value in st["chain"]]],
+            [],
+            raw=chain,
+            alias=[(2 + n, n) for n in range(4)],
+            scratch=six,
+            micros=micros,
+        )
+
+    def c_own(micros):
+        cross, *rest = st["chain"]
+        cross, st["in_proj"] = call(
+            order,
+            memory_own_kernel,
+            [st["vc"], Raw(cross)],
+            [],
+            raw=[three, matrix],
+            alias=[(1, 0)],
+            scratch=[pltpu.VMEM((3, half, width), F32), pltpu.SemaphoreType.DMA((3,))],
+            micros=micros,
+        )
+        st["chain"] = [cross, *rest]
+
+    steps = {
+        "memory": memory,
+        "ffn": ffn,
+        "ffn1": ffn_fold,
+        "ffn2": lambda micros: [ffn_fold(micros) for _ in far_ways],
+        "ffn3": ffn_last,
+        "features": features_step,
+        "ab2": ab2,
+        "ab3": ab3,
+        "ab4": ab4,
+        "ab5": ab5,
+        "ab6": ab6,
+        "ab7": ab7,
+        "ab8": ab8,
+        "c1": c_fold(z_way, True),
+        "c2": c_fold(X_WAY),
+        "c3": c_fold(Y_WAY),
+        "c4": c4,
+        "c5": c5,
+        "c6": c_join(Y_WAY, X_WAY),
+        "c7": c_join(X_WAY, z_way),
+        "c8": c_join(z_way, CORE),
+        "order": order_rows,
+        "finish": finish,
+        "own": own,
+        "c_own": c_own,
+    }
+    waits = {"ab5": ("rab",), "ab6": ("rab",), "ab7": ("ra",), "c5": ("rc",), "c6": ("rc",), "ab8": ("ra",)}
+    for name, micros in STEPS:
+        for at, rows_from in ((NEAR_AT, (1, 2)), (FAR_AT, (3,))):
+            if name == at:
+                key = waits[name][0]
+                st[key], *rows_here = lax.optimization_barrier(
+                    (st[key], *[st["arrived"][k] for k in rows_from])
+                )
+                for k, value in zip(rows_from, rows_here):
+                    st["arrived"][k] = value
+        steps[name](micros)
+    ffn_up, ffn_down = st["ffn"]
+    cross_grad, g_self_out, g_cross_out, g_self_proj = st["chain"]
+    layer_out, grad_tokens, grad_features = [turn(value) for value in st["exchanged"]]
     bias3 = ((3, width), F32)
     bias1 = ((1, width), F32)
     (
-        g_cross_proj,
-        g_in_proj,
         g_pos,
         g_self_bias,
         g_cross_bias,
@@ -1376,23 +1560,30 @@
         g_gain,
         g_shift,
         g_inb,
+        g_cross_proj,
+        g_in_proj,
     ) = call(
         order,
-        functools.partial(finish_memory_kernel, rows_used=used),
-        [vc, rc, g_cross_q],
+        functools.partial(memory_other_kernel, rows_used=used, units=units),
+        [st["rc"], st["vc"], Raw(cross_grad), Raw(st["in_proj"])],
         [
-            three,
-            matrix,
             (query_pos.shape, F32),
             bias3,
             bias3,
-            ((pb_size, 2 * width), F32),
+            ((-(-pb_size * units // LANES), LANES), F32),
             bias1,
             bias3,
             bias3,
             bias1,
         ],
-        scratch=[pltpu.VMEM(flat, F32)],
+        raw=[three, matrix],
+        alias=[(2, 8), (3, 9)],
+        scratch=[
+            pltpu.VMEM((3, half, width), F32),
+            pltpu.SemaphoreType.DMA((3,)),
+            pltpu.VMEM(flat, F32),
+            pltpu.VMEM((40, LANES), F32),
+        ],
         near=False,
     )
 
@@ -1408,7 +1599,7 @@
         g_cross_out,
         g_cross_bias,
         ffn_up,
-        g_bup[:, :units].reshape(-1),
+        g_bup.reshape(-1)[: pb_size * units],
         ffn_down,
         g_bdown[0],
         g_gain,

time: 161 us -> 147 us (0.913)
  waiting for transfers between devices: 57 us -> 52.4 us
  starting transfers between devices: 49.4 us -> 45.1 us
  Pallas kernels: 48 us -> 45.5 us
  local copies, waits for them, and re-layouts: 5.09 us -> 2.87 us
    ppermute x53, waiting for transfers between devices: 57 us -> 52.4 us  [swap(): return lax.ppermute(value, axis, [(i, i ^ bit) for i in range(size)])]
    ppermute x53, starting transfers between devices: 49.4 us -> 45.1 us  [swap(): return lax.ppermute(value, axis, [(i, i ^ bit) for i in range(size)])]
    pallas_call x32 -> x35, Pallas kernels: 48 us -> 45.5 us  [call(): pl.pallas_call(body, out_shape=[pltpu.VMEM(*o) if here else jax.ShapeDtyp...]
  transfers between devices with their start and end apart: 53 -> 53, of which waited for: 32 -> 31; matrix products, arithmetic and copies ran while one was open for 2% -> 2% of each run, Pallas kernels for 24% -> 25%
where the time goes in v3:
time: 147 us
  waiting for transfers between devices  52.4 us (36%)
  Pallas kernels  45.5 us (31%)
  starting transfers between devices  45.1 us (31%)
  local copies, waits for them, and re-layouts  2.87 us (2%)
    ppermute x53, waiting for transfers between devices, swap(): return lax.ppermute(value, axis, [(i, i ^ bit) for i in range(size)])  52.4 us
    pallas_call x35, Pallas kernels, call(): pl.pallas_call(body, out_shape=[pltpu.VMEM(*o) if here else jax.ShapeDtyp...  45.5 us
    ppermute x53, starting transfers between devices, swap(): return lax.ppermute(value, axis, [(i, i ^ bit) for i in range(size)])  45.1 us
  transfers between devices with their start and end apart: 53, of which 31 were waited for; matrix products, arithmetic and copies ran while one was open for 2% of the time, Pallas kernels for 25%

profile of v3, /device:TPU:0, one launch (start us, length us, event | category | flops | bytes accessed | tf_op | source)
XLA Modules:
  0.0 147.3 jit_solution(5556392880045823757)
XLA Ops:
  0.7 1.6 %shard_map.349 = (bf16[400,512]{1,0:T(8,128)(2,1)S(1)}, bf16[400,512]{1,0:T(8,128)(2,1)S(1)}, bf16[416,512]{1,0:T(8,128)(2,1)S(1)}, bf16[416,512]{1,0:T(8,128)(2,1)S(1)}) custom-call(bf16[800,512]{1,0:T(8,128)(2,1)} %bitcast.23, bf16[800,512]{1,0:T(8,128)(2,1)} %bitcast.25), custom_call_target="tpu_custom_call" | custom-call | flops 1610000000 | bytes 5180001 | tf_op jit(solution)/shard_map/pallas_call | solution.py:932
  2.3 3.0 %collective-permute-start = (bf16[400,512]{1,0:T(8,128)(2,1)S(1)}, bf16[400,512]{1,0:T(8,128)(2,1)S(1)}, u32[]{:S(2)}, u32[]{:S(2)}) collective-permute-start(bf16[400,512]{1,0:T(8,128)(2,1)S(1)} %get-tuple-element.356), channel_id=1, source_target_pairs={{0,8},{8,0},{16,24},{24,16},{1,9},{9,1},{17,25},{25,17},{2,10},{10... | collective-permute-start | bytes 1228808 | tf_op jit(solution)/shard_map/ppermute | solution.py:952
  5.3 1.5 %collective-permute-start.1 = (bf16[400,512]{1,0:T(8,128)(2,1)S(1)}, bf16[400,512]{1,0:T(8,128)(2,1)S(1)}, u32[]{:S(2)}, u32[]{:S(2)}) collective-permute-start(bf16[400,512]{1,0:T(8,128)(2,1)S(1)} %get-tuple-element.357), channel_id=1, source_target_pairs={{0,16},{8,24},{16,0},{24,8},{1,17},{9,25},{17,1},{25,9},{2,18},{10... | collective-permute-start | bytes 1228808 | tf_op jit(solution)/shard_map/ppermute | solution.py:952
  7.9 2.9 %collective-permute-start.4 = (bf16[32,1024]{1,0:T(8,128)(2,1)S(1)}, bf16[32,1024]{1,0:T(8,128)(2,1)S(1)}, u32[]{:S(2)}, u32[]{:S(2)}) collective-permute-start(bf16[32,1024]{1,0:T(8,128)(2,1)S(1)} %get-tuple-element.377), channel_id=1, source_target_pairs={{0,24},{8,16},{16,8},{24,0},{1,25},{9,17},{17,9},{25,1},{2,26},{10... | collective-permute-start | bytes 196616 | tf_op jit(solution)/shard_map/ppermute | solution.py:952
  10.8 5.5 %shard_map.351 = (bf16[1216,512]{1,0:T(8,128)(2,1)S(1)}, bf16[1216,512]{1,0:T(8,128)(2,1)S(1)}, bf16[1216,512]{1,0:T(8,128)(2,1)S(1)}, bf16[1216,512]{1,0:T(8,12...) custom-call(bf16[4,1200,512]{2,1,0:T(8,128)(2,1)} %refs_0_, ...), custom_call_target="tpu_custom_call" | custom-call | flops 1 | bytes 1 | tf_op jit(solution)/shard_map/pallas_call | solution.py:932
  16.3 1.4 collective-permute-done.1.refs_16_
  17.7 1.4 collective-permute-done.3.refs_3_
  19.6 1.5 %collective-permute-start.8 = (bf16[400,512]{1,0:T(8,128)(2,1)S(1)}, bf16[400,512]{1,0:T(8,128)(2,1)S(1)}, u32[]{:S(2)}, u32[]{:S(2)}) collective-permute-start(bf16[400,512]{1,0:T(8,128)(2,1)S(1)} %collective-permute-done.refs_15_), channel_id=1, source_target_pairs={{0,16},{8,24},{16,0},{24,8},{1,17},{9,25},{17,1},{25,9},{2,18},{10... | collective-permute-start | bytes 1228808 | tf_op jit(solution)/shard_map/ppermute | solution.py:952
  21.7 1.5 %collective-permute-start.11 = (bf16[416,512]{1,0:T(8,128)(2,1)S(1)}, bf16[416,512]{1,0:T(8,128)(2,1)S(1)}, u32[]{:S(2)}, u32[]{:S(2)}) collective-permute-start(bf16[416,512]{1,0:T(8,128)(2,1)S(1)} %get-tuple-element.430), channel_id=1, source_target_pairs={{0,8},{8,0},{16,24},{24,16},{1,9},{9,1},{17,25},{25,17},{2,10},{10... | collective-permute-start | bytes 1277960 | tf_op jit(solution)/shard_map/ppermute | solution.py:952
  23.7 8.0 %shard_map.352 = (bf16[128,512]{1,0:T(8,128)(2,1)S(1)}, bf16[128,512]{1,0:T(8,128)(2,1)S(1)}, bf16[128,512]{1,0:T(8,128)(2,1)S(1)}, bf16[128,512]{1,0:T(8,128)(2...) custom-call(s32[4,4]{1,0:T(4,128)S(1)} %copy-done.2, ...), custom_call_target="tpu_custom_call" | custom-call | flops 9200000000 | bytes 29600000 | tf_op jit(solution)/shard_map/pallas_call | solution.py:932
  31.9 1.6 %collective-permute-done.7.refs_4_.refs_18_ = bf16[400,512]{1,0:T(8,128)(2,1)S(1)} collective-permute-done((bf16[400,512]{1,0:T(8,128)(2,1)S(1)}, bf16[400,512]{1,0:T(8,128)(2,1)S(1)}, u32[]{:S(2)}, u32[]{:S(2)}) %collective-permute-start.7) | collective-permute-done | bytes 409632 | tf_op jit(solution)/shard_map/ppermute | solution.py:952
  34.0 1.2 collective-permute-done.9.refs_6_.refs_24_
  35.8 1.2 shard_map.353
  37.0 4.3 %collective-permute-done.11.refs_14_ = bf16[416,512]{1,0:T(8,128)(2,1)S(1)} collective-permute-done((bf16[416,512]{1,0:T(8,128)(2,1)S(1)}, bf16[416,512]{1,0:T(8,128)(2,1)S(1)}, u32[]{:S(2)}, u32[]{:S(2)}) %collective-permute-start.11) | collective-permute-done | bytes 426016 | tf_op jit(solution)/shard_map/ppermute | solution.py:952
  41.9 1.3 collective-permute-done.13.refs_20_
  43.1 0.6 collective-permute-done.14.refs_23_
  43.7 4.6 %shard_map.354 = (bf16[128,512]{1,0:T(8,128)(2,1)S(1)}, bf16[128,1024]{1,0:T(8,128)(2,1)S(1)}, f32[128,512]{1,0:T(8,128)S(1)}, f32[8,512]{1,0:T(8,128)S(1)}, f32[4,1,1024]{2,1,0:T(1,128)S(1)}) custom-call(f32[128,512]{1,0:T(8,128)S(1)} %get-tuple-element.436.refs_0_, bf16[128,512]{1,0:T(8,128)(2,1)S(1)} %get-tuple-element.437.refs_0_.refs_1_, ...), custom_call_target="tpu_custom_call" | custom-call | flops 6900000256 | bytes 22200000 | tf_op jit(solution)/shard_map/pallas_call | solution.py:932
  48.3 1.2 collective-permute-start.21
  49.6 0.8 collective-permute-start.20
  50.4 1.5 %collective-permute-start.19 = (bf16[128,1024]{1,0:T(8,128)(2,1)S(1)}, bf16[128,1024]{1,0:T(8,128)(2,1)S(1)}, u32[]{:S(2)}, u32[]{:S(2)}) collective-permute-start(bf16[128,1024]{1,0:T(8,128)(2,1)S(1)} %get-tuple-element.546.refs_0_), channel_id=1, source_target_pairs={{0,8},{8,0},{16,24},{24,16},{1,9},{9,1},{17,25},{25,17},{2,10},{10... | collective-permute-start | bytes 786440 | tf_op jit(solution)/shard_map/ppermute | solution.py:952
  51.9 5.9 %shard_map.355 = (bf16[4,1216,256]{2,1,0:T(8,128)(2,1)S(1)}, bf16[128,512]{1,0:T(8,128)(2,1)S(1)}, bf16[128,512]{1,0:T(8,128)(2,1)S(1)}, f32[128,512]{1,0:T(8,12...) custom-call(f32[128,512]{1,0:T(8,128)S(1)} %get-tuple-element.479.re, ...), custom_call_target="tpu_custom_call" | custom-call | flops 8970000384 | bytes 28860000 | tf_op jit(solution)/shard_map/pallas_call | solution.py:932
  58.5 4.8 %collective-permute-done.20.refs_1_.refs_2_ = bf16[128,1024]{1,0:T(8,128)(2,1)S(1)} collective-permute-done((bf16[128,1024]{1,0:T(8,128)(2,1)S(1)}, bf16[128,1024]{1,0:T(8,128)(2,1)S(1)}, u32[]{:S(2)}, u32[]{:S(2)}) %collective-permute-start.20) | collective-permute-done | bytes 262176 | tf_op jit(solution)/shard_map/ppermute | solution.py:952
  63.3 1.7 %collective-permute-done.18.refs_7_ = bf16[6,256,128]{2,1,0:T(8,128)(2,1)S(1)} collective-permute-done((bf16[6,256,128]{2,1,0:T(8,128)(2,1)S(1)}, bf16[6,256,128]{2,1,0:T(8,128)(2,1)S(1)}, u32[]{:S(2)}, u32[]{:S(2)}) %collective-permute-start.18) | collective-permute-done | bytes 393248 | tf_op jit(solution)/shard_map/ppermute | solution.py:952
  65.3 0.6 collective-permute-start.22
  65.9 1.2 collective-permute-start.23
  67.1 5.1 %shard_map.358 = (bf16[1216,512]{1,0:T(8,128)(2,1)S(1)}, bf16[13,256,128]{2,1,0:T(8,128)(2,1)S(1)}, bf16[13,256,128]{2,1,0:T(8,128)(2,1)S(1)}) custom-call(bf16[4,1216,256]{2,1,0:T(8,128)(2,1)S(1)} %get-tuple-element.529.refs_0_, bf16[4,1216,256]{2,1,0:T(8,128)(2,1)S(1)} %get-tuple-element.530.refs_1_, ...), custom_call_target="tpu_custom_call" | custom-call | flops 5750000128 | bytes 18500000 | tf_op jit(solution)/shard_map/pallas_call | solution.py:932
  72.2 3.0 %shard_map.359 = (bf16[2,4,64,800]{3,2,1,0:T(8,128)(2,1)S(1)}, bf16[4,64,800]{2,1,0:T(8,128)(2,1)S(1)}, bf16[4,64,800]{2,1,0:T(8,128)(2,1)S(1)}) custom-call(bf16[128,1024]{1,0:T(8,128)(2,1)S(1)} %get-tuple-element.546.refs_0_, bf16[128,1024]{1,0:T(8,128)(2,1)S(1)} %collective-permute-done.19.refs_0_.refs_1_, ...), custom_call_target="tpu_custom_call" | custom-call | flops 575000000 | bytes 1850001 | tf_op jit(solution)/shard_map/pallas_call | solution.py:932
  75.3 0.9 shard_map.360
  77.0 1.3 collective-permute-start.24
  78.3 0.8 collective-permute-start.25
  79.4 1.6 %collective-permute-start.28 = (bf16[13,128,128]{2,1,0:T(8,128)(2,1)S(1)}, bf16[13,128,128]{2,1,0:T(8,128)(2,1)S(1)}, u32[]{:S(2)}, u32[]{:S(2)}) collective-permute-start(bf16[13,128,128]{2,1,0:T(8,128)(2,1)S(1)} %get-tuple-element.581), channel_id=1, source_target_pairs={{0,2},{1,3},{2,0},{3,1},{4,6},{5,7},{6,4},{7,5},{8,10},{9,11},{10,... | collective-permute-start | bytes 1277960 | tf_op jit(solution)/shard_map/ppermute | solution.py:952
  81.5 2.8 %collective-permute-done.24.refs_1_ = bf16[12,64,128]{2,1,0:T(8,128)(2,1)S(1)} collective-permute-done((bf16[12,64,128]{2,1,0:T(8,128)(2,1)S(1)}, bf16[12,64,128]{2,1,0:T(8,128)(2,1)S(1)}, u32[]{:S(2)}, u32[]{:S(2)}) %collective-permute-start.24) | collective-permute-done | bytes 196640 | tf_op jit(solution)/shard_map/ppermute | solution.py:952
  84.4 0.9 collective-permute-done.25.refs_3_
  85.4 1.6 %collective-permute-start.27 = (bf16[24,32,128]{2,1,0:T(8,128)(2,1)S(1)}, bf16[24,32,128]{2,1,0:T(8,128)(2,1)S(1)}, u32[]{:S(2)}, u32[]{:S(2)}) collective-permute-start(bf16[24,32,128]{2,1,0:T(8,128)(2,1)S(1)} %get-tuple-element.580), channel_id=1, source_target_pairs={{0,2},{1,3},{2,0},{3,1},{4,6},{5,7},{6,4},{7,5},{8,10},{9,11},{10,... | collective-permute-start | bytes 589832 | tf_op jit(solution)/shard_map/ppermute | solution.py:952
  87.3 4.8 %collective-permute-done.28.refs_1_ = bf16[13,128,128]{2,1,0:T(8,128)(2,1)S(1)} collective-permute-done((bf16[13,128,128]{2,1,0:T(8,128)(2,1)S(1)}, bf16[13,128,128]{2,1,0:T(8,128)(2,1)S(1)}, u32[]{:S(2)}, u32[]{:S(2)}) %collective-permute-start.28) | collective-permute-done | bytes 426016 | tf_op jit(solution)/shard_map/ppermute | solution.py:952
  92.2 1.5 %collective-permute-start.34 = (bf16[13,64,128]{2,1,0:T(8,128)(2,1)S(1)}, bf16[13,64,128]{2,1,0:T(8,128)(2,1)S(1)}, u32[]{:S(2)}, u32[]{:S(2)}) collective-permute-start(bf16[13,64,128]{2,1,0:T(8,128)(2,1)S(1)} %get-tuple-element.596), channel_id=1, source_target_pairs={{0,8},{8,0},{16,24},{24,16},{1,9},{9,1},{17,25},{25,17},{2,10},{10... | collective-permute-start | bytes 638984 | tf_op jit(solution)/shard_map/ppermute | solution.py:952
  93.8 1.6 %collective-permute-start.36 = (bf16[2,64,800]{2,1,0:T(8,128)(2,1)S(1)}, bf16[2,64,800]{2,1,0:T(8,128)(2,1)S(1)}, u32[]{:S(2)}, u32[]{:S(2)}) collective-permute-start(bf16[2,64,800]{2,1,0:T(8,128)(2,1)S(1)} %get-tuple-element.601), channel_id=1, source_target_pairs={{0,2},{1,3},{2,0},{3,1},{4,6},{5,7},{6,4},{7,5},{8,10},{9,11},{10,... | collective-permute-start | bytes 614408 | tf_op jit(solution)/shard_map/ppermute | solution.py:952
  95.9 1.4 collective-permute-start.33
  97.9 2.4 %collective-permute-done.34.refs_1_ = bf16[13,64,128]{2,1,0:T(8,128)(2,1)S(1)} collective-permute-done((bf16[13,64,128]{2,1,0:T(8,128)(2,1)S(1)}, bf16[13,64,128]{2,1,0:T(8,128)(2,1)S(1)}, u32[]{:S(2)}, u32[]{:S(2)}) %collective-permute-start.34) | collective-permute-done | bytes 213024 | tf_op jit(solution)/shard_map/ppermute | solution.py:952
  100.4 1.6 %collective-permute-start.35 = (bf16[13,32,128]{2,1,0:T(8,128)(2,1)S(1)}, bf16[13,32,128]{2,1,0:T(8,128)(2,1)S(1)}, u32[]{:S(2)}, u32[]{:S(2)}) collective-permute-start(bf16[13,32,128]{2,1,0:T(8,128)(2,1)S(1)} %get-tuple-element.600), channel_id=1, source_target_pairs={{0,16},{8,24},{16,0},{24,8},{1,17},{9,25},{17,1},{25,9},{2,18},{10... | collective-permute-start | bytes 319496 | tf_op jit(solution)/shard_map/ppermute | solution.py:952
  102.0 2.4 %collective-permute-done.36.refs_1_ = bf16[2,64,800]{2,1,0:T(8,128)(2,1)S(1)} collective-permute-done((bf16[2,64,800]{2,1,0:T(8,128)(2,1)S(1)}, bf16[2,64,800]{2,1,0:T(8,128)(2,1)S(1)}, u32[]{:S(2)}, u32[]{:S(2)}) %collective-permute-start.36) | collective-permute-done | bytes 204832 | tf_op jit(solution)/shard_map/ppermute | solution.py:952
  104.9 2.6 %collective-permute-done.37.refs_2_ = bf16[2,64,800]{2,1,0:T(8,128)(2,1)S(1)} collective-permute-done((bf16[2,64,800]{2,1,0:T(8,128)(2,1)S(1)}, bf16[2,64,800]{2,1,0:T(8,128)(2,1)S(1)}, u32[]{:S(2)}, u32[]{:S(2)}) %collective-permute-start.37) | collective-permute-done | bytes 204832 | tf_op jit(solution)/shard_map/ppermute | solution.py:952
  107.5 2.1 %collective-permute-start.39 = (bf16[368,512]{1,0:T(8,128)(2,1)S(1)}, bf16[368,512]{1,0:T(8,128)(2,1)S(1)}, u32[]{:S(2)}, u32[]{:S(2)}) collective-permute-start(bf16[368,512]{1,0:T(8,128)(2,1)S(1)} %get-tuple-element.611), channel_id=1, source_target_pairs={{0,24},{8,16},{16,8},{24,0},{1,25},{9,17},{17,9},{25,1},{2,26},{10... | collective-permute-start | bytes 1130504 | tf_op jit(solution)/shard_map/ppermute | solution.py:952
  109.8 1.7 %collective-permute-start.40 = (bf16[13,32,128]{2,1,0:T(8,128)(2,1)S(1)}, bf16[13,32,128]{2,1,0:T(8,128)(2,1)S(1)}, u32[]{:S(2)}, u32[]{:S(2)}) collective-permute-start(bf16[13,32,128]{2,1,0:T(8,128)(2,1)S(1)} %shard_map.369.refs_0_), channel_id=1, source_target_pairs={{0,4},{1,5},{2,6},{3,7},{4,0},{5,1},{6,2},{7,3},{8,12},{9,13},{10,... | collective-permute-start | bytes 319496 | tf_op jit(solution)/shard_map/ppermute | solution.py:952
  111.4 5.6 %collective-permute-done.31.refs_1_ = bf16[24,32,128]{2,1,0:T(8,128)(2,1)S(1)} collective-permute-done((bf16[24,32,128]{2,1,0:T(8,128)(2,1)S(1)}, bf16[24,32,128]{2,1,0:T(8,128)(2,1)S(1)}, u32[]{:S(2)}, u32[]{:S(2)}) %collective-permute-start.31) | collective-permute-done | bytes 196640 | tf_op jit(solution)/shard_map/ppermute | solution.py:952
  117.2 1.0 collective-permute-done.40.refs_1_
  118.7 4.2 %collective-permute-done.38.refs_1_ = bf16[24,32,128]{2,1,0:T(8,128)(2,1)S(1)} collective-permute-done((bf16[24,32,128]{2,1,0:T(8,128)(2,1)S(1)}, bf16[24,32,128]{2,1,0:T(8,128)(2,1)S(1)}, u32[]{:S(2)}, u32[]{:S(2)}) %collective-permute-start.38) | collective-permute-done | bytes 196640 | tf_op jit(solution)/shard_map/ppermute | solution.py:952
  123.0 1.0 collective-permute-done.43.refs_1_
  124.1 1.0 collective-permute-start.48
  125.1 1.5 collective-permute-start.46
  126.5 1.5 collective-permute-start.47
  128.0 1.1 collective-permute-done.42.refs_3_
  129.2 0.9 collective-permute-done.41.refs_1_
  130.2 2.7 %collective-permute-start.44 = (bf16[12,128,128]{2,1,0:T(8,128)(2,1)S(1)}, bf16[12,128,128]{2,1,0:T(8,128)(2,1)S(1)}, u32[]{:S(2)}, u32[]{:S(2)}) collective-permute-start(bf16[12,128,128]{2,1,0:T(8,128)(2,1)S(1)} %get-tuple-element.643.refs_0_), channel_id=1, source_target_pairs={{0,8},{8,0},{16,24},{24,16},{1,9},{9,1},{17,25},{25,17},{2,10},{10... | collective-permute-start | bytes 1179656 | tf_op jit(solution)/shard_map/ppermute | solution.py:952
  132.9 0.8 collective-permute-done.48.refs_1_
  134.0 1.1 collective-permute-done.47.refs_2_
  135.1 2.0 %copy.56 = bf16[4,300,512]{2,0,1:T(4,128)(2,1)} copy(bf16[4,300,512]{2,1,0:T(8,128)(2,1)S(1)} %get-tuple-element.648) | data formatting | bytes 2457600 | tf_op jit(solution)/shard_map/pallas_call | solution.py:932
  137.1 0.8 shard_map.377
  137.8 0.8 copy_bitcast_fusion.1
  138.7 0.6 collective-permute-done.44.refs_1_
  140.0 1.8 %shard_map.379 = (f32[3,512,512]{2,1,0:T(8,128)}, f32[512,512]{1,0:T(8,128)}, f32[512,512]{1,0:T(8,128)}, f32[3,512,512]{2,1,0:T(8,128)}) custom-call(bf16[12,256,128]{2,1,0:T(8,128)(2,1)S(1)} %get-tuple-element.657.refs_0_, bf16[12,256,128]{2,1,0:T(8,128)(2,1)S(1)} %get-tuple-element.658.refs_1_), custom_call_target="tpu_custom_call" | custom-call | flops 1 | bytes 1 | tf_op jit(solution)/shard_map/pallas_call | solution.py:932
  142.1 1.2 shard_map.381
  143.4 1.8 %shard_map.382 = (f32[3,512,512]{2,1,0:T(8,128)}, f32[512,512]{1,0:T(8,128)}, f32[512,512]{1,0:T(8,128)}, f32[3,512,512]{2,1,0:T(8,128)}) custom-call(bf16[12,256,128]{2,1,0:T(8,128)(2,1)S(1)} %collective-permute-done.51.refs_0_, ...), custom_call_target="tpu_custom_call", output_to_operand_aliasing={{0}: (2, {}), {1}: (3, {}), {2}: (4, {}), {3}: (5, {})} | custom-call | flops 1725000064 | bytes 5550001 | tf_op jit(solution)/shard_map/pallas_call | solution.py:932
  145.2 2.0 %shard_map.383 = (f32[100,512]{1,0:T(8,128)}, f32[3,512]{1,0:T(4,128)}, f32[3,512]{1,0:T(4,128)}, f32[25,128]{1,0:T(8,128)}, f32[1,512]{1,0:T(1,128)}, /*index=5...) custom-call(bf16[13,256,128]{2,1,0:T(8,128)(2,1)S(1)} %collective-pe, ...), custom_call_target="tpu_custom_call", output_to_operand_aliasing={{8}: (2, {}), {9}: (3, {})} | custom-call | flops 690000000 | bytes 2220001 | tf_op jit(solution)/shard_map/pallas_call | solution.py:932
  (96 shorter events, 11.7 us)
Async XLA Ops:
  0.7 6.2 %copy-start.3 = (bf16[800]{0:T(1024)(128)(2,1)S(1)}, bf16[800]{0:T(1024)(128)(2,1)}, u32[]{:S(2)}) copy-start(bf16[800]{0:T(1024)(128)(2,1)} %param.34) | copy-start | bytes 4804
  0.7 6.2 %copy-start.4 = (bf16[512]{0:T(512)(128)(2,1)S(1)}, bf16[512]{0:T(512)(128)(2,1)}, u32[]{:S(2)}) copy-start(bf16[512]{0:T(512)(128)(2,1)} %param.36) | copy-start | bytes 3076
  0.7 6.2 %copy-start.5 = (bf16[512]{0:T(512)(128)(2,1)S(1)}, bf16[512]{0:T(512)(128)(2,1)}, u32[]{:S(2)}) copy-start(bf16[512]{0:T(512)(128)(2,1)} %param.40) | copy-start | bytes 3076
  0.7 6.3 %copy-start = (bf16[4,25,512]{2,0,1:T(4,128)(2,1)S(1)}, bf16[4,25,512]{2,0,1:T(4,128)(2,1)}, u32[]{:S(2)}) copy-start(bf16[4,25,512]{2,0,1:T(4,128)(2,1)} %param.22) | copy-start | bytes 307204
  0.7 6.3 %copy-start.1 = (bf16[4,25,512]{2,0,1:T(4,128)(2,1)S(1)}, bf16[4,25,512]{2,0,1:T(4,128)(2,1)}, u32[]{:S(2)}) copy-start(bf16[4,25,512]{2,0,1:T(4,128)(2,1)} %param.26) | copy-start | bytes 307204
  2.3 13.9 %collective-permute-start = (bf16[400,512]{1,0:T(8,128)(2,1)S(1)}, bf16[400,512]{1,0:T(8,128)(2,1)S(1)}, u32[]{:S(2)}, u32[]{:S(2)}) collective-permute-start(bf16[400,512]{1,0:T(8,128)(2,1)S(1)} %get-tuple-element.356), channel_id=1, source_target_pairs={{0,8},{8,0},{16,24},{24,16},{1,9},{9,1},{17,25},{25,17},{2,10},{10... | collective-permute-start | bytes 1228808 | tf_op jit(solution)/shard_map/ppermute | solution.py:952
  5.3 12.3 %collective-permute-start.1 = (bf16[400,512]{1,0:T(8,128)(2,1)S(1)}, bf16[400,512]{1,0:T(8,128)(2,1)S(1)}, u32[]{:S(2)}, u32[]{:S(2)}) collective-permute-start(bf16[400,512]{1,0:T(8,128)(2,1)S(1)} %get-tuple-element.357), channel_id=1, source_target_pairs={{0,16},{8,24},{16,0},{24,8},{1,17},{9,25},{17,1},{25,9},{2,18},{10... | collective-permute-start | bytes 1228808 | tf_op jit(solution)/shard_map/ppermute | solution.py:952
  7.3 10.4 %collective-permute-start.2 = (bf16[32,1024]{1,0:T(8,128)(2,1)S(1)}, bf16[32,1024]{1,0:T(8,128)(2,1)S(1)}, u32[]{:S(2)}, u32[]{:S(2)}) collective-permute-start(bf16[32,1024]{1,0:T(8,128)(2,1)S(1)} %get-tuple-element.375), channel_id=1, source_target_pairs={{0,8},{8,0},{16,24},{24,16},{1,9},{9,1},{17,25},{25,17},{2,10},{10... | collective-permute-start | bytes 196616 | tf_op jit(solution)/shard_map/ppermute | solution.py:952
  7.9 11.2 %collective-permute-start.3 = (bf16[32,1024]{1,0:T(8,128)(2,1)S(1)}, bf16[32,1024]{1,0:T(8,128)(2,1)S(1)}, u32[]{:S(2)}, u32[]{:S(2)}) collective-permute-start(bf16[32,1024]{1,0:T(8,128)(2,1)S(1)} %get-tuple-element.376), channel_id=1, source_target_pairs={{0,16},{8,24},{16,0},{24,8},{1,17},{9,25},{17,1},{25,9},{2,18},{10... | collective-permute-start | bytes 196616 | tf_op jit(solution)/shard_map/ppermute | solution.py:952
  7.9 11.2 %collective-permute-start.4 = (bf16[32,1024]{1,0:T(8,128)(2,1)S(1)}, bf16[32,1024]{1,0:T(8,128)(2,1)S(1)}, u32[]{:S(2)}, u32[]{:S(2)}) collective-permute-start(bf16[32,1024]{1,0:T(8,128)(2,1)S(1)} %get-tuple-element.377), channel_id=1, source_target_pairs={{0,24},{8,16},{16,8},{24,0},{1,25},{9,17},{17,9},{25,1},{2,26},{10... | collective-permute-start | bytes 196616 | tf_op jit(solution)/shard_map/ppermute | solution.py:952
  10.8 12.8 %copy-start.2 = (s32[4,4]{1,0:T(4,128)S(1)}, s32[4,4]{1,0:T(4,128)}, u32[]{:S(2)}) copy-start(s32[4,4]{1,0:T(4,128)} %refs_0_.1) | copy-start | bytes 196
  19.1 4.1 %collective-permute-start.5 = (bf16[400,512]{1,0:T(8,128)(2,1)S(1)}, bf16[400,512]{1,0:T(8,128)(2,1)S(1)}, u32[]{:S(2)}, u32[]{:S(2)}) collective-permute-start(bf16[400,512]{1,0:T(8,128)(2,1)S(1)} %collective-permute-done.refs_15_), channel_id=1, source_target_pairs={{0,1},{1,0},{2,3},{3,2},{4,5},{5,4},{6,7},{7,6},{8,9},{9,8},{10,11... | collective-permute-start | bytes 1228808 | tf_op jit(solution)/shard_map/ppermute | solution.py:952
  19.1 4.6 %collective-permute-start.6 = (bf16[400,512]{1,0:T(8,128)(2,1)S(1)}, bf16[400,512]{1,0:T(8,128)(2,1)S(1)}, u32[]{:S(2)}, u32[]{:S(2)}) collective-permute-start(bf16[400,512]{1,0:T(8,128)(2,1)S(1)} %collective-permute-done.1.refs_16_), channel_id=1, source_target_pairs={{0,1},{1,0},{2,3},{3,2},{4,5},{5,4},{6,7},{7,6},{8,9},{9,8},{10,11... | collective-permute-start | bytes 1228808 | tf_op jit(solution)/shard_map/ppermute | solution.py:952
  19.6 12.3 %collective-permute-start.8 = (bf16[400,512]{1,0:T(8,128)(2,1)S(1)}, bf16[400,512]{1,0:T(8,128)(2,1)S(1)}, u32[]{:S(2)}, u32[]{:S(2)}) collective-permute-start(bf16[400,512]{1,0:T(8,128)(2,1)S(1)} %collective-permute-done.refs_15_), channel_id=1, source_target_pairs={{0,16},{8,24},{16,0},{24,8},{1,17},{9,25},{17,1},{25,9},{2,18},{10... | collective-permute-start | bytes 1228808 | tf_op jit(solution)/shard_map/ppermute | solution.py:952
  21.1 12.4 %collective-permute-start.7 = (bf16[400,512]{1,0:T(8,128)(2,1)S(1)}, bf16[400,512]{1,0:T(8,128)(2,1)S(1)}, u32[]{:S(2)}, u32[]{:S(2)}) collective-permute-start(bf16[400,512]{1,0:T(8,128)(2,1)S(1)} %collective-permute-done.1.refs_16_), channel_id=1, source_target_pairs={{0,8},{8,0},{16,24},{24,16},{1,9},{9,1},{17,25},{25,17},{2,10},{10... | collective-permute-start | bytes 1228808 | tf_op jit(solution)/shard_map/ppermute | solution.py:952
  21.7 19.7 %collective-permute-start.11 = (bf16[416,512]{1,0:T(8,128)(2,1)S(1)}, bf16[416,512]{1,0:T(8,128)(2,1)S(1)}, u32[]{:S(2)}, u32[]{:S(2)}) collective-permute-start(bf16[416,512]{1,0:T(8,128)(2,1)S(1)} %get-tuple-element.430), channel_id=1, source_target_pairs={{0,8},{8,0},{16,24},{24,16},{1,9},{9,1},{17,25},{25,17},{2,10},{10... | collective-permute-start | bytes 1277960 | tf_op jit(solution)/shard_map/ppermute | solution.py:952
  23.1 18.2 %collective-permute-start.12 = (bf16[416,512]{1,0:T(8,128)(2,1)S(1)}, bf16[416,512]{1,0:T(8,128)(2,1)S(1)}, u32[]{:S(2)}, u32[]{:S(2)}) collective-permute-start(bf16[416,512]{1,0:T(8,128)(2,1)S(1)} %get-tuple-element.431), channel_id=1, source_target_pairs={{0,16},{8,24},{16,0},{24,8},{1,17},{9,25},{17,1},{25,9},{2,18},{10... | collective-permute-start | bytes 1277960 | tf_op jit(solution)/shard_map/ppermute | solution.py:952
  33.5 1.7 %collective-permute-start.9 = (bf16[400,512]{1,0:T(8,128)(2,1)S(1)}, bf16[400,512]{1,0:T(8,128)(2,1)S(1)}, u32[]{:S(2)}, u32[]{:S(2)}) collective-permute-start(bf16[400,512]{1,0:T(8,128)(2,1)S(1)} %collective-permute-done.7.refs_4_.refs_18_), channel_id=1, source_target_pairs={{0,1},{1,0},{2,3},{3,2},{4,5},{5,4},{6,7},{7,6},{8,9},{9,8},{10,11... | collective-permute-start | bytes 1228808 | tf_op jit(solution)/shard_map/ppermute | solution.py:952
  33.5 2.3 %collective-permute-start.10 = (bf16[400,512]{1,0:T(8,128)(2,1)S(1)}, bf16[400,512]{1,0:T(8,128)(2,1)S(1)}, u32[]{:S(2)}, u32[]{:S(2)}) collective-permute-start(bf16[400,512]{1,0:T(8,128)(2,1)S(1)} %collective-permute-done.8.refs_5_.refs_19_), channel_id=1, source_target_pairs={{0,1},{1,0},{2,3},{3,2},{4,5},{5,4},{6,7},{7,6},{8,9},{9,8},{10,11... | collective-permute-start | bytes 1228808 | tf_op jit(solution)/shard_map/ppermute | solution.py:952
  41.3 1.8 %collective-permute-start.13 = (bf16[416,512]{1,0:T(8,128)(2,1)S(1)}, bf16[416,512]{1,0:T(8,128)(2,1)S(1)}, u32[]{:S(2)}, u32[]{:S(2)}) collective-permute-start(bf16[416,512]{1,0:T(8,128)(2,1)S(1)} %collective-permute-done.11.refs_14_), channel_id=1, source_target_pairs={{0,1},{1,0},{2,3},{3,2},{4,5},{5,4},{6,7},{7,6},{8,9},{9,8},{10,11... | collective-permute-start | bytes 1277960 | tf_op jit(solution)/shard_map/ppermute | solution.py:952
  41.3 2.4 %collective-permute-start.14 = (bf16[416,512]{1,0:T(8,128)(2,1)S(1)}, bf16[416,512]{1,0:T(8,128)(2,1)S(1)}, u32[]{:S(2)}, u32[]{:S(2)}) collective-permute-start(bf16[416,512]{1,0:T(8,128)(2,1)S(1)} %collective-permute-done.12.refs_17_), channel_id=1, source_target_pairs={{0,1},{1,0},{2,3},{3,2},{4,5},{5,4},{6,7},{7,6},{8,9},{9,8},{10,11... | collective-permute-start | bytes 1277960 | tf_op jit(solution)/shard_map/ppermute | solution.py:952
  48.3 10.2 %collective-permute-start.21 = (bf16[128,1024]{1,0:T(8,128)(2,1)S(1)}, bf16[128,1024]{1,0:T(8,128)(2,1)S(1)}, u32[]{:S(2)}, u32[]{:S(2)}) collective-permute-start(bf16[128,1024]{1,0:T(8,128)(2,1)S(1)} %get-tuple-element.546.refs_0_), channel_id=1, source_target_pairs={{0,24},{8,16},{16,8},{24,0},{1,25},{9,17},{17,9},{25,1},{2,26},{10... | collective-permute-start | bytes 786440 | tf_op jit(solution)/shard_map/ppermute | solution.py:952
  49.6 13.7 %collective-permute-start.20 = (bf16[128,1024]{1,0:T(8,128)(2,1)S(1)}, bf16[128,1024]{1,0:T(8,128)(2,1)S(1)}, u32[]{:S(2)}, u32[]{:S(2)}) collective-permute-start(bf16[128,1024]{1,0:T(8,128)(2,1)S(1)} %get-tuple-element.546.refs_0_), channel_id=1, source_target_pairs={{0,16},{8,24},{16,0},{24,8},{1,17},{9,25},{17,1},{25,9},{2,18},{10... | collective-permute-start | bytes 786440 | tf_op jit(solution)/shard_map/ppermute | solution.py:952
  50.4 12.9 %collective-permute-start.19 = (bf16[128,1024]{1,0:T(8,128)(2,1)S(1)}, bf16[128,1024]{1,0:T(8,128)(2,1)S(1)}, u32[]{:S(2)}, u32[]{:S(2)}) collective-permute-start(bf16[128,1024]{1,0:T(8,128)(2,1)S(1)} %get-tuple-element.546.refs_0_), channel_id=1, source_target_pairs={{0,8},{8,0},{16,24},{24,16},{1,9},{9,1},{17,25},{25,17},{2,10},{10... | collective-permute-start | bytes 786440 | tf_op jit(solution)/shard_map/ppermute | solution.py:952
  57.8 5.5 %collective-permute-start.15 = (bf16[6,256,128]{2,1,0:T(8,128)(2,1)S(1)}, bf16[6,256,128]{2,1,0:T(8,128)(2,1)S(1)}, u32[]{:S(2)}, u32[]{:S(2)}) collective-permute-start(bf16[6,256,128]{2,1,0:T(8,128)(2,1)S(1)} %get-tuple-element.501), channel_id=1, source_target_pairs={{0,1},{1,0},{2,3},{3,2},{4,5},{5,4},{6,7},{7,6},{8,9},{9,8},{10,11... | collective-permute-start | bytes 1179656 | tf_op jit(solution)/shard_map/ppermute | solution.py:952
  57.8 5.4 %collective-permute-start.16 = (bf16[6,256,128]{2,1,0:T(8,128)(2,1)S(1)}, bf16[6,256,128]{2,1,0:T(8,128)(2,1)S(1)}, u32[]{:S(2)}, u32[]{:S(2)}) collective-permute-start(bf16[6,256,128]{2,1,0:T(8,128)(2,1)S(1)} %get-tuple-element.502), channel_id=1, source_target_pairs={{0,1},{1,0},{2,3},{3,2},{4,5},{5,4},{6,7},{7,6},{8,9},{9,8},{10,11... | collective-permute-start | bytes 1179656 | tf_op jit(solution)/shard_map/ppermute | solution.py:952
  58.5 4.8 %collective-permute-start.17 = (bf16[6,256,128]{2,1,0:T(8,128)(2,1)S(1)}, bf16[6,256,128]{2,1,0:T(8,128)(2,1)S(1)}, u32[]{:S(2)}, u32[]{:S(2)}) collective-permute-start(bf16[6,256,128]{2,1,0:T(8,128)(2,1)S(1)} %get-tuple-element.503), channel_id=1, source_target_pairs={{0,1},{1,0},{2,3},{3,2},{4,5},{5,4},{6,7},{7,6},{8,9},{9,8},{10,11... | collective-permute-start | bytes 1179656 | tf_op jit(solution)/shard_map/ppermute | solution.py:952
  63.2 1.7 %collective-permute-start.18 = (bf16[6,256,128]{2,1,0:T(8,128)(2,1)S(1)}, bf16[6,256,128]{2,1,0:T(8,128)(2,1)S(1)}, u32[]{:S(2)}, u32[]{:S(2)}) collective-permute-start(bf16[6,256,128]{2,1,0:T(8,128)(2,1)S(1)} %get-tuple-element.504), channel_id=1, source_target_pairs={{0,1},{1,0},{2,3},{3,2},{4,5},{5,4},{6,7},{7,6},{8,9},{9,8},{10,11... | collective-permute-start | bytes 1179656 | tf_op jit(solution)/shard_map/ppermute | solution.py:952
  65.3 11.2 %collective-permute-start.22 = (bf16[12,128,128]{2,1,0:T(8,128)(2,1)S(1)}, bf16[12,128,128]{2,1,0:T(8,128)(2,1)S(1)}, u32[]{:S(2)}, u32[]{:S(2)}) collective-permute-start(bf16[12,128,128]{2,1,0:T(8,128)(2,1)S(1)} %get-tuple-element.521), channel_id=1, source_target_pairs={{0,8},{8,0},{16,24},{24,16},{1,9},{9,1},{17,25},{25,17},{2,10},{10... | collective-permute-start | bytes 1179656 | tf_op jit(solution)/shard_map/ppermute | solution.py:952
  65.9 10.9 %collective-permute-start.23 = (bf16[12,128,128]{2,1,0:T(8,128)(2,1)S(1)}, bf16[12,128,128]{2,1,0:T(8,128)(2,1)S(1)}, u32[]{:S(2)}, u32[]{:S(2)}) collective-permute-start(bf16[12,128,128]{2,1,0:T(8,128)(2,1)S(1)} %get-tuple-element.522), channel_id=1, source_target_pairs={{0,16},{8,24},{16,0},{24,8},{1,17},{9,25},{17,1},{25,9},{2,18},{10... | collective-permute-start | bytes 1179656 | tf_op jit(solution)/shard_map/ppermute | solution.py:952
  76.8 2.4 %collective-permute-start.26 = (bf16[13,256,128]{2,1,0:T(8,128)(2,1)S(1)}, bf16[13,256,128]{2,1,0:T(8,128)(2,1)S(1)}, u32[]{:S(2)}, u32[]{:S(2)}) collective-permute-start(bf16[13,256,128]{2,1,0:T(8,128)(2,1)S(1)} %get-tuple-element.571), channel_id=1, source_target_pairs={{0,1},{1,0},{2,3},{3,2},{4,5},{5,4},{6,7},{7,6},{8,9},{9,8},{10,11... | collective-permute-start | bytes 2555912 | tf_op jit(solution)/shard_map/ppermute | solution.py:952
  77.0 7.4 %collective-permute-start.24 = (bf16[12,64,128]{2,1,0:T(8,128)(2,1)S(1)}, bf16[12,64,128]{2,1,0:T(8,128)(2,1)S(1)}, u32[]{:S(2)}, u32[]{:S(2)}) collective-permute-start(bf16[12,64,128]{2,1,0:T(8,128)(2,1)S(1)} %get-tuple-element.567), channel_id=1, source_target_pairs={{0,16},{8,24},{16,0},{24,8},{1,17},{9,25},{17,1},{25,9},{2,18},{10... | collective-permute-start | bytes 589832 | tf_op jit(solution)/shard_map/ppermute | solution.py:952
  78.3 7.0 %collective-permute-start.25 = (bf16[12,64,128]{2,1,0:T(8,128)(2,1)S(1)}, bf16[12,64,128]{2,1,0:T(8,128)(2,1)S(1)}, u32[]{:S(2)}, u32[]{:S(2)}) collective-permute-start(bf16[12,64,128]{2,1,0:T(8,128)(2,1)S(1)} %get-tuple-element.569), channel_id=1, source_target_pairs={{0,8},{8,0},{16,24},{24,16},{1,9},{9,1},{17,25},{25,17},{2,10},{10... | collective-permute-start | bytes 589832 | tf_op jit(solution)/shard_map/ppermute | solution.py:952
  79.4 12.7 %collective-permute-start.28 = (bf16[13,128,128]{2,1,0:T(8,128)(2,1)S(1)}, bf16[13,128,128]{2,1,0:T(8,128)(2,1)S(1)}, u32[]{:S(2)}, u32[]{:S(2)}) collective-permute-start(bf16[13,128,128]{2,1,0:T(8,128)(2,1)S(1)} %get-tuple-element.581), channel_id=1, source_target_pairs={{0,2},{1,3},{2,0},{3,1},{4,6},{5,7},{6,4},{7,5},{8,10},{9,11},{10,... | collective-permute-start | bytes 1277960 | tf_op jit(solution)/shard_map/ppermute | solution.py:952
  81.0 6.0 %collective-permute-start.29 = (bf16[4,64,800]{2,1,0:T(8,128)(2,1)S(1)}, bf16[4,64,800]{2,1,0:T(8,128)(2,1)S(1)}, u32[]{:S(2)}, u32[]{:S(2)}) collective-permute-start(bf16[4,64,800]{2,1,0:T(8,128)(2,1)S(1)} %get-tuple-element.582), channel_id=1, source_target_pairs={{0,1},{1,0},{2,3},{3,2},{4,5},{5,4},{6,7},{7,6},{8,9},{9,8},{10,11... | collective-permute-start | bytes 1228808 | tf_op jit(solution)/shard_map/ppermute | solution.py:952
  81.0 6.0 %collective-permute-start.30 = (bf16[4,64,800]{2,1,0:T(8,128)(2,1)S(1)}, bf16[4,64,800]{2,1,0:T(8,128)(2,1)S(1)}, u32[]{:S(2)}, u32[]{:S(2)}) collective-permute-start(bf16[4,64,800]{2,1,0:T(8,128)(2,1)S(1)} %get-tuple-element.583), channel_id=1, source_target_pairs={{0,1},{1,0},{2,3},{3,2},{4,5},{5,4},{6,7},{7,6},{8,9},{9,8},{10,11... | collective-permute-start | bytes 1228808 | tf_op jit(solution)/shard_map/ppermute | solution.py:952
  85.4 11.9 %collective-permute-start.27 = (bf16[24,32,128]{2,1,0:T(8,128)(2,1)S(1)}, bf16[24,32,128]{2,1,0:T(8,128)(2,1)S(1)}, u32[]{:S(2)}, u32[]{:S(2)}) collective-permute-start(bf16[24,32,128]{2,1,0:T(8,128)(2,1)S(1)} %get-tuple-element.580), channel_id=1, source_target_pairs={{0,2},{1,3},{2,0},{3,1},{4,6},{5,7},{6,4},{7,5},{8,10},{9,11},{10,... | collective-permute-start | bytes 589832 | tf_op jit(solution)/shard_map/ppermute | solution.py:952
  92.2 8.1 %collective-permute-start.34 = (bf16[13,64,128]{2,1,0:T(8,128)(2,1)S(1)}, bf16[13,64,128]{2,1,0:T(8,128)(2,1)S(1)}, u32[]{:S(2)}, u32[]{:S(2)}) collective-permute-start(bf16[13,64,128]{2,1,0:T(8,128)(2,1)S(1)} %get-tuple-element.596), channel_id=1, source_target_pairs={{0,8},{8,0},{16,24},{24,16},{1,9},{9,1},{17,25},{25,17},{2,10},{10... | collective-permute-start | bytes 638984 | tf_op jit(solution)/shard_map/ppermute | solution.py:952
  93.8 10.6 %collective-permute-start.36 = (bf16[2,64,800]{2,1,0:T(8,128)(2,1)S(1)}, bf16[2,64,800]{2,1,0:T(8,128)(2,1)S(1)}, u32[]{:S(2)}, u32[]{:S(2)}) collective-permute-start(bf16[2,64,800]{2,1,0:T(8,128)(2,1)S(1)} %get-tuple-element.601), channel_id=1, source_target_pairs={{0,2},{1,3},{2,0},{3,1},{4,6},{5,7},{6,4},{7,5},{8,10},{9,11},{10,... | collective-permute-start | bytes 614408 | tf_op jit(solution)/shard_map/ppermute | solution.py:952
  95.3 16.1 %collective-permute-start.32 = (bf16[368,512]{1,0:T(8,128)(2,1)S(1)}, bf16[368,512]{1,0:T(8,128)(2,1)S(1)}, u32[]{:S(2)}, u32[]{:S(2)}) collective-permute-start(bf16[368,512]{1,0:T(8,128)(2,1)S(1)} %get-tuple-element.593), channel_id=1, source_target_pairs={{0,8},{8,0},{16,24},{24,16},{1,9},{9,1},{17,25},{25,17},{2,10},{10... | collective-permute-start | bytes 1130504 | tf_op jit(solution)/shard_map/ppermute | solution.py:952
  95.9 15.6 %collective-permute-start.33 = (bf16[368,512]{1,0:T(8,128)(2,1)S(1)}, bf16[368,512]{1,0:T(8,128)(2,1)S(1)}, u32[]{:S(2)}, u32[]{:S(2)}) collective-permute-start(bf16[368,512]{1,0:T(8,128)(2,1)S(1)} %get-tuple-element.594), channel_id=1, source_target_pairs={{0,16},{8,24},{16,0},{24,8},{1,17},{9,25},{17,1},{25,9},{2,18},{10... | collective-permute-start | bytes 1130504 | tf_op jit(solution)/shard_map/ppermute | solution.py:952
  97.3 10.2 %collective-permute-start.37 = (bf16[2,64,800]{2,1,0:T(8,128)(2,1)S(1)}, bf16[2,64,800]{2,1,0:T(8,128)(2,1)S(1)}, u32[]{:S(2)}, u32[]{:S(2)}) collective-permute-start(bf16[2,64,800]{2,1,0:T(8,128)(2,1)S(1)} %get-tuple-element.602), channel_id=1, source_target_pairs={{0,2},{1,3},{2,0},{3,1},{4,6},{5,7},{6,4},{7,5},{8,10},{9,11},{10,... | collective-permute-start | bytes 614408 | tf_op jit(solution)/shard_map/ppermute | solution.py:952
  100.4 9.3 %collective-permute-start.35 = (bf16[13,32,128]{2,1,0:T(8,128)(2,1)S(1)}, bf16[13,32,128]{2,1,0:T(8,128)(2,1)S(1)}, u32[]{:S(2)}, u32[]{:S(2)}) collective-permute-start(bf16[13,32,128]{2,1,0:T(8,128)(2,1)S(1)} %get-tuple-element.600), channel_id=1, source_target_pairs={{0,16},{8,24},{16,0},{24,8},{1,17},{9,25},{17,1},{25,9},{2,18},{10... | collective-permute-start | bytes 319496 | tf_op jit(solution)/shard_map/ppermute | solution.py:952
  104.4 12.6 %collective-permute-start.31 = (bf16[24,32,128]{2,1,0:T(8,128)(2,1)S(1)}, bf16[24,32,128]{2,1,0:T(8,128)(2,1)S(1)}, u32[]{:S(2)}, u32[]{:S(2)}) collective-permute-start(bf16[24,32,128]{2,1,0:T(8,128)(2,1)S(1)} %shard_map.366.refs_0_), channel_id=1, source_target_pairs={{0,4},{1,5},{2,6},{3,7},{4,0},{5,1},{6,2},{7,3},{8,12},{9,13},{10,... | collective-permute-start | bytes 589832 | tf_op jit(solution)/shard_map/ppermute | solution.py:952
  107.5 11.2 %collective-permute-start.39 = (bf16[368,512]{1,0:T(8,128)(2,1)S(1)}, bf16[368,512]{1,0:T(8,128)(2,1)S(1)}, u32[]{:S(2)}, u32[]{:S(2)}) collective-permute-start(bf16[368,512]{1,0:T(8,128)(2,1)S(1)} %get-tuple-element.611), channel_id=1, source_target_pairs={{0,24},{8,16},{16,8},{24,0},{1,25},{9,17},{17,9},{25,1},{2,26},{10... | collective-permute-start | bytes 1130504 | tf_op jit(solution)/shard_map/ppermute | solution.py:952
  109.8 8.4 %collective-permute-start.40 = (bf16[13,32,128]{2,1,0:T(8,128)(2,1)S(1)}, bf16[13,32,128]{2,1,0:T(8,128)(2,1)S(1)}, u32[]{:S(2)}, u32[]{:S(2)}) collective-permute-start(bf16[13,32,128]{2,1,0:T(8,128)(2,1)S(1)} %shard_map.369.refs_0_), channel_id=1, source_target_pairs={{0,4},{1,5},{2,6},{3,7},{4,0},{5,1},{6,2},{7,3},{8,12},{9,13},{10,... | collective-permute-start | bytes 319496 | tf_op jit(solution)/shard_map/ppermute | solution.py:952
  117.1 5.7 %collective-permute-start.38 = (bf16[24,32,128]{2,1,0:T(8,128)(2,1)S(1)}, bf16[24,32,128]{2,1,0:T(8,128)(2,1)S(1)}, u32[]{:S(2)}, u32[]{:S(2)}) collective-permute-start(bf16[24,32,128]{2,1,0:T(8,128)(2,1)S(1)} %shard_map.370.refs_0_), channel_id=1, source_target_pairs={{0,2},{1,3},{2,0},{3,1},{4,6},{5,7},{6,4},{7,5},{8,10},{9,11},{10,... | collective-permute-start | bytes 589832 | tf_op jit(solution)/shard_map/ppermute | solution.py:952
  118.2 5.8 %collective-permute-start.43 = (bf16[13,32,128]{2,1,0:T(8,128)(2,1)S(1)}, bf16[13,32,128]{2,1,0:T(8,128)(2,1)S(1)}, u32[]{:S(2)}, u32[]{:S(2)}) collective-permute-start(bf16[13,32,128]{2,1,0:T(8,128)(2,1)S(1)} %shard_map.371.refs_0_), channel_id=1, source_target_pairs={{0,16},{8,24},{16,0},{24,8},{1,17},{9,25},{17,1},{25,9},{2,18},{10... | collective-permute-start | bytes 319496 | tf_op jit(solution)/shard_map/ppermute | solution.py:952
  122.9 6.3 %collective-permute-start.42 = (bf16[12,64,128]{2,1,0:T(8,128)(2,1)S(1)}, bf16[12,64,128]{2,1,0:T(8,128)(2,1)S(1)}, u32[]{:S(2)}, u32[]{:S(2)}) collective-permute-start(bf16[12,64,128]{2,1,0:T(8,128)(2,1)S(1)} %get-tuple-element.623.refs_2_), channel_id=1, source_target_pairs={{0,8},{8,0},{16,24},{24,16},{1,9},{9,1},{17,25},{25,17},{2,10},{10... | collective-permute-start | bytes 589832 | tf_op jit(solution)/shard_map/ppermute | solution.py:952
  123.0 7.1 %collective-permute-start.41 = (bf16[12,64,128]{2,1,0:T(8,128)(2,1)S(1)}, bf16[12,64,128]{2,1,0:T(8,128)(2,1)S(1)}, u32[]{:S(2)}, u32[]{:S(2)}) collective-permute-start(bf16[12,64,128]{2,1,0:T(8,128)(2,1)S(1)} %get-tuple-element.621.refs_0_), channel_id=1, source_target_pairs={{0,16},{8,24},{16,0},{24,8},{1,17},{9,25},{17,1},{25,9},{2,18},{10... | collective-permute-start | bytes 589832 | tf_op jit(solution)/shard_map/ppermute | solution.py:952
  124.1 9.6 %collective-permute-start.48 = (bf16[13,64,128]{2,1,0:T(8,128)(2,1)S(1)}, bf16[13,64,128]{2,1,0:T(8,128)(2,1)S(1)}, u32[]{:S(2)}, u32[]{:S(2)}) collective-permute-start(bf16[13,64,128]{2,1,0:T(8,128)(2,1)S(1)} %shard_map.373.refs_0_), channel_id=1, source_target_pairs={{0,8},{8,0},{16,24},{24,16},{1,9},{9,1},{17,25},{25,17},{2,10},{10... | collective-permute-start | bytes 638984 | tf_op jit(solution)/shard_map/ppermute | solution.py:952
  125.1 8.9 %collective-permute-start.46 = (bf16[1,64,800]{2,1,0:T(8,128)(2,1)S(1)}, bf16[1,64,800]{2,1,0:T(8,128)(2,1)S(1)}, u32[]{:S(2)}, u32[]{:S(2)}) collective-permute-start(bf16[1,64,800]{2,1,0:T(8,128)(2,1)S(1)} %get-tuple-element.627), channel_id=1, source_target_pairs={{0,4},{1,5},{2,6},{3,7},{4,0},{5,1},{6,2},{7,3},{8,12},{9,13},{10,... | collective-permute-start | bytes 307208 | tf_op jit(solution)/shard_map/ppermute | solution.py:952
  126.5 8.5 %collective-permute-start.47 = (bf16[1,64,800]{2,1,0:T(8,128)(2,1)S(1)}, bf16[1,64,800]{2,1,0:T(8,128)(2,1)S(1)}, u32[]{:S(2)}, u32[]{:S(2)}) collective-permute-start(bf16[1,64,800]{2,1,0:T(8,128)(2,1)S(1)} %get-tuple-element.628), channel_id=1, source_target_pairs={{0,4},{1,5},{2,6},{3,7},{4,0},{5,1},{6,2},{7,3},{8,12},{9,13},{10,... | collective-permute-start | bytes 307208 | tf_op jit(solution)/shard_map/ppermute | solution.py:952
  130.1 8.6 %collective-permute-start.45 = (bf16[12,128,128]{2,1,0:T(8,128)(2,1)S(1)}, bf16[12,128,128]{2,1,0:T(8,128)(2,1)S(1)}, u32[]{:S(2)}, u32[]{:S(2)}) collective-permute-start(bf16[12,128,128]{2,1,0:T(8,128)(2,1)S(1)} %get-tuple-element.645.refs_2_), channel_id=1, source_target_pairs={{0,16},{8,24},{16,0},{24,8},{1,17},{9,25},{17,1},{25,9},{2,18},{10... | collective-permute-start | bytes 1179656 | tf_op jit(solution)/shard_map/ppermute | solution.py:952
  130.2 9.1 %collective-permute-start.44 = (bf16[12,128,128]{2,1,0:T(8,128)(2,1)S(1)}, bf16[12,128,128]{2,1,0:T(8,128)(2,1)S(1)}, u32[]{:S(2)}, u32[]{:S(2)}) collective-permute-start(bf16[12,128,128]{2,1,0:T(8,128)(2,1)S(1)} %get-tuple-element.643.refs_0_), channel_id=1, source_target_pairs={{0,8},{8,0},{16,24},{24,16},{1,9},{9,1},{17,25},{25,17},{2,10},{10... | collective-permute-start | bytes 1179656 | tf_op jit(solution)/shard_map/ppermute | solution.py:952
  133.8 8.2 %collective-permute-start.49 = (bf16[13,128,128]{2,1,0:T(8,128)(2,1)S(1)}, bf16[13,128,128]{2,1,0:T(8,128)(2,1)S(1)}, u32[]{:S(2)}, u32[]{:S(2)}) collective-permute-start(bf16[13,128,128]{2,1,0:T(8,128)(2,1)S(1)} %shard_map.375.refs_0_), channel_id=1, source_target_pairs={{0,2},{1,3},{2,0},{3,1},{4,6},{5,7},{6,4},{7,5},{8,10},{9,11},{10,... | collective-permute-start | bytes 1277960 | tf_op jit(solution)/shard_map/ppermute | solution.py:952
  139.4 3.9 %collective-permute-start.51 = (bf16[12,256,128]{2,1,0:T(8,128)(2,1)S(1)}, bf16[12,256,128]{2,1,0:T(8,128)(2,1)S(1)}, u32[]{:S(2)}, u32[]{:S(2)}) collective-permute-start(bf16[12,256,128]{2,1,0:T(8,128)(2,1)S(1)} %get-tuple-element.657.refs_0_), channel_id=1, source_target_pairs={{0,1},{1,0},{2,3},{3,2},{4,5},{5,4},{6,7},{7,6},{8,9},{9,8},{10,11... | collective-permute-start | bytes 2359304 | tf_op jit(solution)/shard_map/ppermute | solution.py:952
  139.5 3.8 %collective-permute-start.52 = (bf16[12,256,128]{2,1,0:T(8,128)(2,1)S(1)}, bf16[12,256,128]{2,1,0:T(8,128)(2,1)S(1)}, u32[]{:S(2)}, u32[]{:S(2)}) collective-permute-start(bf16[12,256,128]{2,1,0:T(8,128)(2,1)S(1)} %get-tuple-element.658.refs_1_), channel_id=1, source_target_pairs={{0,1},{1,0},{2,3},{3,2},{4,5},{5,4},{6,7},{7,6},{8,9},{9,8},{10,11... | collective-permute-start | bytes 2359304 | tf_op jit(solution)/shard_map/ppermute | solution.py:952
  142.0 3.1 %collective-permute-start.50 = (bf16[13,256,128]{2,1,0:T(8,128)(2,1)S(1)}, bf16[13,256,128]{2,1,0:T(8,128)(2,1)S(1)}, u32[]{:S(2)}, u32[]{:S(2)}) collective-permute-start(bf16[13,256,128]{2,1,0:T(8,128)(2,1)S(1)} %shard_map.380.refs_0_.refs_1_), channel_id=1, source_target_pairs={{0,1},{1,0},{2,3},{3,2},{4,5},{5,4},{6,7},{7,6},{8,9},{9,8},{10,11... | collective-permute-start | bytes 2555912 | tf_op jit(solution)/shard_map/ppermute | solution.py:952

commit v4 on v3

--- a/solution.py
+++ b/solution.py
@@ -14,7 +14,7 @@
 LANES = 128
 GROUPS = 4
 FAR = -1e30
-START_COSTS = (0.0, 8.0, 0.0, 6.0, 7.8, 2.0)
+START_COSTS = (0.0, 8.0, 0.0, 6.0, 7.8, 6.2)
 RATE = 1.15e9
 STEPS = (
     ("memory", 5.0),
@@ -136,32 +136,29 @@
         self.refs[index // size][index % size] = value
 
 
-def put_halves(core, value, index, keep_ref, send_ref, scratch):
-    half = value.shape[0] // 2
-    scratch[...] = value
-    mine = pl.multiple_of(core * half, half)
-    other = pl.multiple_of((1 - core) * half, half)
-    for block in range(value.shape[1] // LANES):
-        lanes = slice(block * LANES, (block + 1) * LANES)
-        keep_ref[index + block] = scratch[pl.ds(mine, half), lanes].astype(BF)
-        send_ref[index + block] = scratch[pl.ds(other, half), lanes].astype(BF)
-
-
-def pick_kernel(ids, up, down, up_half, down_half, up_wide, down_wide, sems):
+def put_halves(core, left_ref, grad, index, keep_ref, send_ref):
+    half = left_ref.shape[1] // 2
+    for ref, place in ((send_ref, 1 - core), (keep_ref, core)):
+        columns = pl.ds(pl.multiple_of(place * half, LANES), half)
+        value = tn(left_ref[:, columns], grad).astype(BF)
+        for block in range(value.shape[1] // LANES):
+            ref[index + block] = value[:, block * LANES : (block + 1) * LANES]
+
+
+def pick_kernel(ids, up, down, up_part, down_part, sems):
     core = ids[1]
     copies = []
-    for ref, half, wide in ((up, up_half, up_wide), (down, down_half, down_wide)):
-        for out in (half, wide):
-            start = core * (ref.shape[0] - out.shape[0])
-            size = out.shape[0] // 2
-            for m in range(2):
-                copies.append(
-                    pltpu.make_async_copy(
-                        ref.at[pl.ds(pl.multiple_of(start + m * size, 16), size)],
-                        out.at[pl.ds(m * size, size)],
-                        sems.at[len(copies)],
-                    )
+    for ref, out in ((up, up_part), (down, down_part)):
+        start = core * (ref.shape[0] - out.shape[0])
+        size = out.shape[0] // 2
+        for m in range(2):
+            copies.append(
+                pltpu.make_async_copy(
+                    ref.at[pl.ds(pl.multiple_of(start + m * size, 16), size)],
+                    out.at[pl.ds(m * size, size)],
+                    sems.at[len(copies)],
                 )
+            )
     for copy in copies:
         copy.start()
     for copy in copies:
@@ -403,6 +400,9 @@
     small_out,
     bup_out,
     pre_near,
+    dense,
+    *,
+    rows_used,
 ):
     core = ids[1]
     units = up_own.shape[0]
@@ -424,8 +424,14 @@
     res_out[...] = (xhat * row(gains, 2) + row(shifts, 2)).astype(BF)
     g3, dgain3, dshift3 = norm_back(xhat, rstd, row(gains, 2), cot_ref[...].astype(F32))
     gb = g3.astype(BF)
-    ops_out[:, :width] = h2b
-    ops_out[:, width:] = gb
+    block = h2b.shape[0] // GROUPS
+    dense[...] = jnp.zeros(dense.shape, F32)
+    for b in range(GROUPS):
+        here = slice(b * block, b * block + rows_used)
+        there = slice(b * rows_used, (b + 1) * rows_used)
+        dense[there, :width] = h2b[here].astype(F32)
+        dense[there, width:] = gb[here].astype(F32)
+    ops_out[...] = dense[...].astype(BF)
 
     def unit_grads(pre, dn):
         ga = nt(gb, dn).astype(BF).astype(F32)
@@ -488,15 +494,13 @@
     keep,
     send0,
     send1,
-    send2,
-    send3,
     work,
     gq_ref,
     gk_ref,
     gv_ref,
 ):
     core = ids[1]
-    send = Chain((send0, send1, send2, send3))
+    send = Chain((send0, send1))
     width = x_ref.shape[1]
     rows = x_ref.shape[0]
     g2 = g2_ref[...]
@@ -516,14 +520,14 @@
     gcq = gq_ref[...]
     gci = nt(gcq, cross_proj[0])
     small_out[0:1] = column_sum(gcq)
-    put_halves(core, tn(ci_ref[...], gcq), 0, keep, send, work)
-    put_halves(core, tn(cm_ref[...], branch), 8, keep, send, work)
+    put_halves(core, ci_ref, gcq, 0, keep, send)
+    put_halves(core, cm_ref, branch, 8, keep, send)
     g1, dgain1, dshift1 = norm_back(xhat1_ref[...], rstd1_ref[...], row(gains, 0), g2 + gci)
     small_out[1:2] = dgain1
     small_out[2:3] = dshift1
     sbranch = g1.astype(BF)
     small_out[3:4] = column_sum(sbranch)
-    put_halves(core, tn(sm_ref[...], sbranch), 4, keep, send, work)
+    put_halves(core, sm_ref, sbranch, 4, keep, send)
     gsm = nt(sbranch, self_out[...]).astype(BF)
     for g in range(GROUPS):
         lanes = slice(g * LANES, (g + 1) * LANES)
@@ -541,9 +545,9 @@
     small_out[4:5] = column_sum(gq)
     small_out[5:6] = column_sum(gv)
     small_out[6:8] = jnp.zeros((2, width), F32)
-    put_halves(core, tn(ai_ref[...], gq), 12, keep, send, work)
-    put_halves(core, tn(ai_ref[...], gk), 16, keep, send, work)
-    put_halves(core, tn(x_ref[...], gv), 20, keep, send, work)
+    put_halves(core, ai_ref, gq, 12, keep, send)
+    put_halves(core, ai_ref, gk, 16, keep, send)
+    put_halves(core, x_ref, gv, 20, keep, send)
 
 
 def ffn_grad_kernel(ids, *refs):
@@ -621,9 +625,9 @@
             gv_ref[here, lanes] = nn(pc_ref[g, here], pairs_g[g]).astype(BF)
         gm = (nt(gk_ref[here], cross_proj[1]) + nt(gv_ref[here], cross_proj[2])).astype(BF)
         gm_ref[here] = gm
-    put_halves(core, tn(ki[...], gk_ref[...]), 0, keep, send, work)
-    put_halves(core, tn(vi[...], gv_ref[...]), 4, keep, send, work)
-    put_halves(core, tn(featp[...], gm_ref[...]), 8, keep, send, work)
+    put_halves(core, ki, gk_ref[...], 0, keep, send)
+    put_halves(core, vi, gv_ref[...], 4, keep, send)
+    put_halves(core, featp, gm_ref[...], 8, keep, send)
 
     small[...] = gpos_ref[...]
     extras = [
@@ -1093,17 +1097,21 @@
 
     up, down = w_up.T, w_down.T
     cut = units // 2
-    up_half, down_half, up_wide, down_wide = call(
-        order,
-        pick_kernel,
-        [Raw(up), Raw(down)],
-        [((cut, width), BF)] * 2 + [((cut + 16, width), BF)] * 2,
-        micros=1.4,
-        scratch=[pltpu.SemaphoreType.DMA((8,))],
-        limit=4,
-    )
+    def pick(count):
+        return call(
+            order,
+            pick_kernel,
+            [Raw(up), Raw(down)],
+            [((count, width), BF)] * 2,
+            scratch=[pltpu.SemaphoreType.DMA((4,))],
+            limit=4,
+            micros=0.0,
+        )
+
+    up_half, down_half = pick(cut)
     fy0 = swap(up_half, *Y_WAY)
     fx1 = swap(down_half, *X_WAY)
+    up_wide, down_wide = pick(cut + 16)
     misc = (
         jnp.pad(in_bias[None], ((0, 3), (0, 0)))
         + jnp.pad(b_down[None], ((1, 2), (0, 0)))
@@ -1160,8 +1168,6 @@
     fx1, fy0, *got = order.after((fx1, fy0, *got))
     fd0 = swap(fy0, *X_WAY)
     fd1 = swap(fx1, *Y_WAY)
-    sx1, sy0 = swap(fx1, *CORE), swap(fy0, *CORE)
-    got[0], sx1, sy0 = lax.optimization_barrier((got[0], sx1, sy0))
     flat = (rows, width)
     scores = (GROUPS, slots, 2 * rows)
     (x, cot, ai, sq, sk, sv, ps, sm, xhat1, rstd1, ci, cq, pc, cm, h2, xhat2, rstd2, bups, h2b, self_proj, self_out, cross_out, norm_gain, norm_bias, up, down) = call(
@@ -1208,7 +1214,8 @@
         micros=START_COSTS[1],
         scratch=[pltpu.VMEM((slots, 2 * rows), F32), pltpu.VMEM(flat, F32)],
     )
-    fd0, fd1 = order.after((fd0, fd1))
+    fx1, fy0, fd0, fd1 = order.after((fx1, fy0, fd0, fd1))
+    sx1, sy0 = swap(fx1, *CORE), swap(fy0, *CORE)
     sd0, sd1 = swap(fd0, *CORE), swap(fd1, *CORE)
     down_part, pre_own, pre_far = call(
         order,
@@ -1220,9 +1227,10 @@
     fx0, fy1 = order.after((fx0, fy1))
     sx0, sy1 = swap(fx0, *CORE), swap(fy1, *CORE)
     pieces = [fx0, fx1, fy0, fy1, fd0, fd1, sx0, sx1, sy0, sy1, sd0, sd1]
+    dense = (-(-used * pb_size // 8) * 8, 2 * width)
     res, ops, g2, small_a, bup = call(
         order,
-        ffn_second_kernel,
+        functools.partial(ffn_second_kernel, rows_used=used),
         [
             h2,
             h2b,
@@ -1242,13 +1250,13 @@
         ],
         [
             (flat, BF),
-            ((rows, 2 * width), BF),
+            (dense, BF),
             (flat, F32),
             ((8, width), F32),
             ((pb_size, 1, 2 * width), F32),
         ],
         micros=START_COSTS[3],
-        scratch=[pltpu.VMEM((4, rows, cut), F32)],
+        scratch=[pltpu.VMEM((4, rows, cut), F32), pltpu.VMEM(dense, F32)],
     )
     others = [swap(ops, "pb", k) for k in range(1, pb_size)]
     halves = ((24, width // 2, LANES), BF)
@@ -1286,7 +1294,7 @@
             ((8, width), F32),
             halves,
         ]
-        + [((6, width // 2, LANES), BF)] * 4,
+        + [((12, width // 2, LANES), BF)] * 2,
         micros=START_COSTS[4],
         scratch=[
             pltpu.VMEM((width, width), F32),
@@ -1301,8 +1309,8 @@
     ka, sa, kb, sb = fold(
         order,
         [
-            ([(keep12, got12[0], 0, 6, 0), (keep12, got12[1], 6, 12, 6)], X_WAY),
-            ([(keep12, got12[2], 12, 18, 12), (keep12, got12[3], 18, 24, 18)], Y_WAY),
+            ([(keep12, got12[0], 0, 12, 0)], X_WAY),
+            ([(keep12, got12[1], 12, 24, 12)], Y_WAY),
         ],
     )
     ra, rb = swap(sa, *X_WAY), swap(sb, *Y_WAY)

time: 147 us -> 141 us (0.959)
  waiting for transfers between devices: 52.4 us -> 41 us
  starting transfers between devices: 45.1 us -> 49.8 us
    ppermute x53 -> x51, waiting for transfers between devices: 52.4 us -> 41 us  [swap(): return lax.ppermute(value, axis, [(i, i ^ bit) for i in range(size)])]
    ppermute x53 -> x51, starting transfers between devices: 45.1 us -> 49.8 us  [swap(): return lax.ppermute(value, axis, [(i, i ^ bit) for i in range(size)])]
    pallas_call x35 -> x36, Pallas kernels: 45.5 us -> 45.3 us  [call(): pl.pallas_call(body, out_shape=[pltpu.VMEM(*o) if here else jax.ShapeDtyp...]
  transfers between devices with their start and end apart: 53 -> 51, of which waited for: 31 -> 26; matrix products, arithmetic and copies ran while one was open for 2% -> 2% of each run, Pallas kernels for 25% -> 26%
where the time goes in v4:
time: 141 us; the launch traced here: 140 us
  starting transfers between devices  49.8 us (35%)
  Pallas kernels  45.3 us (32%)
  waiting for transfers between devices  41 us (29%)
  local copies, waits for them, and re-layouts  2.87 us (2%)
    ppermute x51, starting transfers between devices, swap(): return lax.ppermute(value, axis, [(i, i ^ bit) for i in range(size)])  49.8 us
    pallas_call x36, Pallas kernels, call(): pl.pallas_call(body, out_shape=[pltpu.VMEM(*o) if here else jax.ShapeDtyp...  45.3 us
    ppermute x51, waiting for transfers between devices, swap(): return lax.ppermute(value, axis, [(i, i ^ bit) for i in range(size)])  41 us
  transfers between devices with their start and end apart: 51, of which 26 were waited for; matrix products, arithmetic and copies ran while one was open for 2% of the time, Pallas kernels for 26%

profile of v4, /device:TPU:0, one launch (start us, length us, event | category | flops | bytes accessed | tf_op | source)
XLA Modules:
  0.0 140.3 jit_solution(14496371458164552388)
XLA Ops:
  0.7 1.3 shard_map.349
  2.0 3.0 %collective-permute-start = (bf16[400,512]{1,0:T(8,128)(2,1)S(1)}, bf16[400,512]{1,0:T(8,128)(2,1)S(1)}, u32[]{:S(2)}, u32[]{:S(2)}) collective-permute-start(bf16[400,512]{1,0:T(8,128)(2,1)S(1)} %get-tuple-element.351), channel_id=1, source_target_pairs={{0,8},{8,0},{16,24},{24,16},{1,9},{9,1},{17,25},{25,17},{2,10},{10... | collective-permute-start | bytes 1228808 | tf_op jit(solution)/shard_map/ppermute | solution.py:956
  5.1 1.5 %collective-permute-start.1 = (bf16[400,512]{1,0:T(8,128)(2,1)S(1)}, bf16[400,512]{1,0:T(8,128)(2,1)S(1)}, u32[]{:S(2)}, u32[]{:S(2)}) collective-permute-start(bf16[400,512]{1,0:T(8,128)(2,1)S(1)} %get-tuple-element.352), channel_id=1, source_target_pairs={{0,16},{8,24},{16,0},{24,8},{1,17},{9,25},{17,1},{25,9},{2,18},{10... | collective-permute-start | bytes 1228808 | tf_op jit(solution)/shard_map/ppermute | solution.py:956
  6.6 1.3 shard_map.350
  8.9 2.9 %collective-permute-start.4 = (bf16[32,1024]{1,0:T(8,128)(2,1)S(1)}, bf16[32,1024]{1,0:T(8,128)(2,1)S(1)}, u32[]{:S(2)}, u32[]{:S(2)}) collective-permute-start(bf16[32,1024]{1,0:T(8,128)(2,1)S(1)} %get-tuple-element.374), channel_id=1, source_target_pairs={{0,24},{8,16},{16,8},{24,0},{1,25},{9,17},{17,9},{25,1},{2,26},{10... | collective-permute-start | bytes 196616 | tf_op jit(solution)/shard_map/ppermute | solution.py:956
  11.8 5.4 %shard_map.352 = (bf16[1216,512]{1,0:T(8,128)(2,1)S(1)}, bf16[1216,512]{1,0:T(8,128)(2,1)S(1)}, bf16[1216,512]{1,0:T(8,128)(2,1)S(1)}, bf16[1216,512]{1,0:T(8,12...) custom-call(bf16[4,1200,512]{2,1,0:T(8,128)(2,1)} %refs_0_, ...), custom_call_target="tpu_custom_call" | custom-call | flops 1 | bytes 1 | tf_op jit(solution)/shard_map/pallas_call | solution.py:936
  17.4 1.4 %collective-permute-done.3.refs_3_ = bf16[32,1024]{1,0:T(8,128)(2,1)S(1)} collective-permute-done((bf16[32,1024]{1,0:T(8,128)(2,1)S(1)}, bf16[32,1024]{1,0:T(8,128)(2,1)S(1)}, u32[]{:S(2)}, u32[]{:S(2)}) %collective-permute-start.3) | collective-permute-done | bytes 65568 | tf_op jit(solution)/shard_map/ppermute | solution.py:956
  18.8 1.5 %collective-permute-start.6 = (bf16[400,512]{1,0:T(8,128)(2,1)S(1)}, bf16[400,512]{1,0:T(8,128)(2,1)S(1)}, u32[]{:S(2)}, u32[]{:S(2)}) collective-permute-start(bf16[400,512]{1,0:T(8,128)(2,1)S(1)} %collective-permute-done.refs_15_), channel_id=1, source_target_pairs={{0,16},{8,24},{16,0},{24,8},{1,17},{9,25},{17,1},{25,9},{2,18},{10... | collective-permute-start | bytes 1228808 | tf_op jit(solution)/shard_map/ppermute | solution.py:956
  20.8 1.5 %collective-permute-start.9 = (bf16[416,512]{1,0:T(8,128)(2,1)S(1)}, bf16[416,512]{1,0:T(8,128)(2,1)S(1)}, u32[]{:S(2)}, u32[]{:S(2)}) collective-permute-start(bf16[416,512]{1,0:T(8,128)(2,1)S(1)} %get-tuple-element.426), channel_id=1, source_target_pairs={{0,8},{8,0},{16,24},{24,16},{1,9},{9,1},{17,25},{25,17},{2,10},{10... | collective-permute-start | bytes 1277960 | tf_op jit(solution)/shard_map/ppermute | solution.py:956
  22.8 8.0 %shard_map.353 = (bf16[128,512]{1,0:T(8,128)(2,1)S(1)}, bf16[128,512]{1,0:T(8,128)(2,1)S(1)}, bf16[128,512]{1,0:T(8,128)(2,1)S(1)}, bf16[128,512]{1,0:T(8,128)(2...) custom-call(s32[4,4]{1,0:T(4,128)S(1)} %copy-done.2, ...), custom_call_target="tpu_custom_call" | custom-call | flops 9200000000 | bytes 29600000 | tf_op jit(solution)/shard_map/pallas_call | solution.py:936
  31.2 1.5 %collective-permute-done.5.refs_4_.refs_18_ = bf16[400,512]{1,0:T(8,128)(2,1)S(1)} collective-permute-done((bf16[400,512]{1,0:T(8,128)(2,1)S(1)}, bf16[400,512]{1,0:T(8,128)(2,1)S(1)}, u32[]{:S(2)}, u32[]{:S(2)}) %collective-permute-start.5) | collective-permute-done | bytes 409632 | tf_op jit(solution)/shard_map/ppermute | solution.py:956
  33.2 1.2 collective-permute-done.7.refs_6_.refs_24_
  35.0 1.2 shard_map.354
  36.3 2.2 %collective-permute-done.9.refs_14_ = bf16[416,512]{1,0:T(8,128)(2,1)S(1)} collective-permute-done((bf16[416,512]{1,0:T(8,128)(2,1)S(1)}, bf16[416,512]{1,0:T(8,128)(2,1)S(1)}, u32[]{:S(2)}, u32[]{:S(2)}) %collective-permute-start.9) | collective-permute-done | bytes 426016 | tf_op jit(solution)/shard_map/ppermute | solution.py:956
  39.5 1.9 %collective-permute-done.12.refs_21_ = bf16[400,512]{1,0:T(8,128)(2,1)S(1)} collective-permute-done((bf16[400,512]{1,0:T(8,128)(2,1)S(1)}, bf16[400,512]{1,0:T(8,128)(2,1)S(1)}, u32[]{:S(2)}, u32[]{:S(2)}) %collective-permute-start.12) | collective-permute-done | bytes 409632 | tf_op jit(solution)/shard_map/ppermute | solution.py:956
  42.0 4.6 %shard_map.355 = (bf16[128,512]{1,0:T(8,128)(2,1)S(1)}, bf16[104,1024]{1,0:T(8,128)(2,1)S(1)}, f32[128,512]{1,0:T(8,128)S(1)}, f32[8,512]{1,0:T(8,128)S(1)}, f32[4,1,1024]{2,1,0:T(1,128)S(1)}) custom-call(f32[128,512]{1,0:T(8,128)S(1)} %get-tuple-element.432.refs_0_, bf16[128,512]{1,0:T(8,128)(2,1)S(1)} %get-tuple-element.433.refs_0_.refs_1_, ...), custom_call_target="tpu_custom_call" | custom-call | flops 6900000256 | bytes 22200000 | tf_op jit(solution)/shard_map/pallas_call | solution.py:936
  46.6 2.0 %collective-permute-start.19 = (bf16[104,1024]{1,0:T(8,128)(2,1)S(1)}, bf16[104,1024]{1,0:T(8,128)(2,1)S(1)}, u32[]{:S(2)}, u32[]{:S(2)}) collective-permute-start(bf16[104,1024]{1,0:T(8,128)(2,1)S(1)} %get-tuple-element.536.refs_0_), channel_id=1, source_target_pairs={{0,24},{8,16},{16,8},{24,0},{1,25},{9,17},{17,9},{25,1},{2,26},{10... | collective-permute-start | bytes 638984 | tf_op jit(solution)/shard_map/ppermute | solution.py:956
  49.1 1.1 collective-permute-start.17
  50.2 5.0 %shard_map.356 = (bf16[4,1216,256]{2,1,0:T(8,128)(2,1)S(1)}, bf16[128,512]{1,0:T(8,128)(2,1)S(1)}, bf16[128,512]{1,0:T(8,128)(2,1)S(1)}, f32[128,512]{1,0:T(8,12...) custom-call(f32[128,512]{1,0:T(8,128)S(1)} %get-tuple-element.475.re, ...), custom_call_target="tpu_custom_call" | custom-call | flops 8970000384 | bytes 28860000 | tf_op jit(solution)/shard_map/pallas_call | solution.py:936
  55.8 3.6 %collective-permute-done.18.refs_1_.refs_2_ = bf16[104,1024]{1,0:T(8,128)(2,1)S(1)} collective-permute-done((bf16[104,1024]{1,0:T(8,128)(2,1)S(1)}, bf16[104,1024]{1,0:T(8,128)(2,1)S(1)}, u32[]{:S(2)}, u32[]{:S(2)}) %collective-permute-start.18) | collective-permute-done | bytes 213024 | tf_op jit(solution)/shard_map/ppermute | solution.py:956
  59.9 1.1 collective-permute-start.20
  61.0 1.3 collective-permute-start.21
  62.2 5.0 %shard_map.359 = (bf16[1216,512]{1,0:T(8,128)(2,1)S(1)}, bf16[13,256,128]{2,1,0:T(8,128)(2,1)S(1)}, bf16[13,256,128]{2,1,0:T(8,128)(2,1)S(1)}) custom-call(bf16[4,1216,256]{2,1,0:T(8,128)(2,1)S(1)} %get-tuple-element.519.refs_0_, bf16[4,1216,256]{2,1,0:T(8,128)(2,1)S(1)} %get-tuple-element.520.refs_1_, ...), custom_call_target="tpu_custom_call" | custom-call | flops 5750000128 | bytes 18500000 | tf_op jit(solution)/shard_map/pallas_call | solution.py:936
  67.2 2.8 %shard_map.360 = (bf16[2,4,64,800]{3,2,1,0:T(8,128)(2,1)S(1)}, bf16[4,64,800]{2,1,0:T(8,128)(2,1)S(1)}, bf16[4,64,800]{2,1,0:T(8,128)(2,1)S(1)}) custom-call(bf16[104,1024]{1,0:T(8,128)(2,1)S(1)} %get-tuple-element.536.refs_0_, bf16[104,1024]{1,0:T(8,128)(2,1)S(1)} %collective-permute-done.17.refs_0_.refs_1_, ...), custom_call_target="tpu_custom_call" | custom-call | flops 575000000 | bytes 1850001 | tf_op jit(solution)/shard_map/pallas_call | solution.py:936
  70.0 0.9 shard_map.361
  71.8 1.3 collective-permute-start.22
  73.1 0.8 collective-permute-start.23
  74.2 1.6 %collective-permute-start.26 = (bf16[13,128,128]{2,1,0:T(8,128)(2,1)S(1)}, bf16[13,128,128]{2,1,0:T(8,128)(2,1)S(1)}, u32[]{:S(2)}, u32[]{:S(2)}) collective-permute-start(bf16[13,128,128]{2,1,0:T(8,128)(2,1)S(1)} %get-tuple-element.571), channel_id=1, source_target_pairs={{0,2},{1,3},{2,0},{3,1},{4,6},{5,7},{6,4},{7,5},{8,10},{9,11},{10,... | collective-permute-start | bytes 1277960 | tf_op jit(solution)/shard_map/ppermute | solution.py:956
  76.4 2.8 %collective-permute-done.22.refs_1_ = bf16[12,64,128]{2,1,0:T(8,128)(2,1)S(1)} collective-permute-done((bf16[12,64,128]{2,1,0:T(8,128)(2,1)S(1)}, bf16[12,64,128]{2,1,0:T(8,128)(2,1)S(1)}, u32[]{:S(2)}, u32[]{:S(2)}) %collective-permute-start.22) | collective-permute-done | bytes 196640 | tf_op jit(solution)/shard_map/ppermute | solution.py:956
  79.2 0.9 collective-permute-done.23.refs_3_
  80.2 1.6 %collective-permute-start.25 = (bf16[24,32,128]{2,1,0:T(8,128)(2,1)S(1)}, bf16[24,32,128]{2,1,0:T(8,128)(2,1)S(1)}, u32[]{:S(2)}, u32[]{:S(2)}) collective-permute-start(bf16[24,32,128]{2,1,0:T(8,128)(2,1)S(1)} %get-tuple-element.570), channel_id=1, source_target_pairs={{0,2},{1,3},{2,0},{3,1},{4,6},{5,7},{6,4},{7,5},{8,10},{9,11},{10,... | collective-permute-start | bytes 589832 | tf_op jit(solution)/shard_map/ppermute | solution.py:956
  82.1 4.8 %collective-permute-done.26.refs_1_ = bf16[13,128,128]{2,1,0:T(8,128)(2,1)S(1)} collective-permute-done((bf16[13,128,128]{2,1,0:T(8,128)(2,1)S(1)}, bf16[13,128,128]{2,1,0:T(8,128)(2,1)S(1)}, u32[]{:S(2)}, u32[]{:S(2)}) %collective-permute-start.26) | collective-permute-done | bytes 426016 | tf_op jit(solution)/shard_map/ppermute | solution.py:956
  87.0 1.2 collective-permute-start.32
  88.2 1.6 %collective-permute-start.34 = (bf16[2,64,800]{2,1,0:T(8,128)(2,1)S(1)}, bf16[2,64,800]{2,1,0:T(8,128)(2,1)S(1)}, u32[]{:S(2)}, u32[]{:S(2)}) collective-permute-start(bf16[2,64,800]{2,1,0:T(8,128)(2,1)S(1)} %get-tuple-element.591), channel_id=1, source_target_pairs={{0,2},{1,3},{2,0},{3,1},{4,6},{5,7},{6,4},{7,5},{8,10},{9,11},{10,... | collective-permute-start | bytes 614408 | tf_op jit(solution)/shard_map/ppermute | solution.py:956
  89.8 0.9 collective-permute-start.30
  90.7 1.2 collective-permute-start.31
  91.9 0.8 collective-permute-start.35
  92.8 2.5 %collective-permute-done.32.refs_1_ = bf16[13,64,128]{2,1,0:T(8,128)(2,1)S(1)} collective-permute-done((bf16[13,64,128]{2,1,0:T(8,128)(2,1)S(1)}, bf16[13,64,128]{2,1,0:T(8,128)(2,1)S(1)}, u32[]{:S(2)}, u32[]{:S(2)}) %collective-permute-start.32) | collective-permute-done | bytes 213024 | tf_op jit(solution)/shard_map/ppermute | solution.py:956
  95.3 1.3 collective-permute-start.33
  96.8 2.6 %collective-permute-start.29 = (bf16[24,32,128]{2,1,0:T(8,128)(2,1)S(1)}, bf16[24,32,128]{2,1,0:T(8,128)(2,1)S(1)}, u32[]{:S(2)}, u32[]{:S(2)}) collective-permute-start(bf16[24,32,128]{2,1,0:T(8,128)(2,1)S(1)} %shard_map.367.refs_0_), channel_id=1, source_target_pairs={{0,4},{1,5},{2,6},{3,7},{4,0},{5,1},{6,2},{7,3},{8,12},{9,13},{10,... | collective-permute-start | bytes 589832 | tf_op jit(solution)/shard_map/ppermute | solution.py:956
  99.3 4.0 %collective-permute-done.35.refs_2_ = bf16[2,64,800]{2,1,0:T(8,128)(2,1)S(1)} collective-permute-done((bf16[2,64,800]{2,1,0:T(8,128)(2,1)S(1)}, bf16[2,64,800]{2,1,0:T(8,128)(2,1)S(1)}, u32[]{:S(2)}, u32[]{:S(2)}) %collective-permute-start.35) | collective-permute-done | bytes 204832 | tf_op jit(solution)/shard_map/ppermute | solution.py:956
  103.3 1.4 %collective-permute-start.37 = (bf16[368,512]{1,0:T(8,128)(2,1)S(1)}, bf16[368,512]{1,0:T(8,128)(2,1)S(1)}, u32[]{:S(2)}, u32[]{:S(2)}) collective-permute-start(bf16[368,512]{1,0:T(8,128)(2,1)S(1)} %get-tuple-element.601), channel_id=1, source_target_pairs={{0,24},{8,16},{16,8},{24,0},{1,25},{9,17},{17,9},{25,1},{2,26},{10... | collective-permute-start | bytes 1130504 | tf_op jit(solution)/shard_map/ppermute | solution.py:956
  104.9 1.2 collective-permute-start.38
  106.1 3.2 %collective-permute-done.29.refs_1_ = bf16[24,32,128]{2,1,0:T(8,128)(2,1)S(1)} collective-permute-done((bf16[24,32,128]{2,1,0:T(8,128)(2,1)S(1)}, bf16[24,32,128]{2,1,0:T(8,128)(2,1)S(1)}, u32[]{:S(2)}, u32[]{:S(2)}) %collective-permute-start.29) | collective-permute-done | bytes 196640 | tf_op jit(solution)/shard_map/ppermute | solution.py:956
  109.9 2.1 %collective-permute-done.38.refs_1_ = bf16[13,32,128]{2,1,0:T(8,128)(2,1)S(1)} collective-permute-done((bf16[13,32,128]{2,1,0:T(8,128)(2,1)S(1)}, bf16[13,32,128]{2,1,0:T(8,128)(2,1)S(1)}, u32[]{:S(2)}, u32[]{:S(2)}) %collective-permute-start.38) | collective-permute-done | bytes 106528 | tf_op jit(solution)/shard_map/ppermute | solution.py:956
  112.0 1.2 collective-permute-start.41
  113.2 1.8 %collective-permute-done.36.refs_1_ = bf16[24,32,128]{2,1,0:T(8,128)(2,1)S(1)} collective-permute-done((bf16[24,32,128]{2,1,0:T(8,128)(2,1)S(1)}, bf16[24,32,128]{2,1,0:T(8,128)(2,1)S(1)}, u32[]{:S(2)}, u32[]{:S(2)}) %collective-permute-start.36) | collective-permute-done | bytes 196640 | tf_op jit(solution)/shard_map/ppermute | solution.py:956
  115.1 1.1 collective-permute-start.40
  116.2 1.0 collective-permute-start.39
  118.0 1.1 collective-permute-start.46
  119.1 1.9 %collective-permute-start.44 = (bf16[1,64,800]{2,1,0:T(8,128)(2,1)S(1)}, bf16[1,64,800]{2,1,0:T(8,128)(2,1)S(1)}, u32[]{:S(2)}, u32[]{:S(2)}) collective-permute-start(bf16[1,64,800]{2,1,0:T(8,128)(2,1)S(1)} %get-tuple-element.617), channel_id=1, source_target_pairs={{0,4},{1,5},{2,6},{3,7},{4,0},{5,1},{6,2},{7,3},{8,12},{9,13},{10,... | collective-permute-start | bytes 307208 | tf_op jit(solution)/shard_map/ppermute | solution.py:956
  121.0 1.1 collective-permute-start.45
  122.1 1.2 collective-permute-start.43
  123.3 1.0 collective-permute-start.42
  124.3 1.3 collective-permute-done.46.refs_1_
  125.7 0.9 collective-permute-start.47
  126.7 0.9 collective-permute-done.45.refs_2_
  127.5 2.0 %copy.56 = bf16[4,300,512]{2,0,1:T(4,128)(2,1)} copy(bf16[4,300,512]{2,1,0:T(8,128)(2,1)S(1)} %get-tuple-element.638) | data formatting | bytes 2457600 | tf_op jit(solution)/shard_map/pallas_call | solution.py:936
  130.3 0.8 copy_bitcast_fusion.1
  131.2 1.2 collective-permute-done.42.refs_1_
  133.0 1.8 %shard_map.380 = (f32[3,512,512]{2,1,0:T(8,128)}, f32[512,512]{1,0:T(8,128)}, f32[512,512]{1,0:T(8,128)}, f32[3,512,512]{2,1,0:T(8,128)}) custom-call(bf16[12,256,128]{2,1,0:T(8,128)(2,1)S(1)} %get-tuple-element.647.refs_0_, bf16[12,256,128]{2,1,0:T(8,128)(2,1)S(1)} %get-tuple-element.648.refs_1_), custom_call_target="tpu_custom_call" | custom-call | flops 1 | bytes 1 | tf_op jit(solution)/shard_map/pallas_call | solution.py:936
  135.1 1.2 shard_map.382
  136.4 1.8 %shard_map.383 = (f32[3,512,512]{2,1,0:T(8,128)}, f32[512,512]{1,0:T(8,128)}, f32[512,512]{1,0:T(8,128)}, f32[3,512,512]{2,1,0:T(8,128)}) custom-call(bf16[12,256,128]{2,1,0:T(8,128)(2,1)S(1)} %collective-permute-done.49.refs_0_, ...), custom_call_target="tpu_custom_call", output_to_operand_aliasing={{0}: (2, {}), {1}: (3, {}), {2}: (4, {}), {3}: (5, {})} | custom-call | flops 1725000064 | bytes 5550001 | tf_op jit(solution)/shard_map/pallas_call | solution.py:936
  138.2 2.0 %shard_map.384 = (f32[100,512]{1,0:T(8,128)}, f32[3,512]{1,0:T(4,128)}, f32[3,512]{1,0:T(4,128)}, f32[25,128]{1,0:T(8,128)}, f32[1,512]{1,0:T(1,128)}, /*index=5...) custom-call(bf16[13,256,128]{2,1,0:T(8,128)(2,1)S(1)} %collective-pe, ...), custom_call_target="tpu_custom_call", output_to_operand_aliasing={{8}: (2, {}), {9}: (3, {})} | custom-call | flops 690000000 | bytes 2220001 | tf_op jit(solution)/shard_map/pallas_call | solution.py:936
  (93 shorter events, 12.7 us)
Async XLA Ops:
  0.7 7.2 %copy-start.3 = (bf16[800]{0:T(1024)(128)(2,1)S(1)}, bf16[800]{0:T(1024)(128)(2,1)}, u32[]{:S(2)}) copy-start(bf16[800]{0:T(1024)(128)(2,1)} %param.34) | copy-start | bytes 4804
  0.7 7.2 %copy-start.4 = (bf16[512]{0:T(512)(128)(2,1)S(1)}, bf16[512]{0:T(512)(128)(2,1)}, u32[]{:S(2)}) copy-start(bf16[512]{0:T(512)(128)(2,1)} %param.36) | copy-start | bytes 3076
  0.7 7.2 %copy-start.5 = (bf16[512]{0:T(512)(128)(2,1)S(1)}, bf16[512]{0:T(512)(128)(2,1)}, u32[]{:S(2)}) copy-start(bf16[512]{0:T(512)(128)(2,1)} %param.40) | copy-start | bytes 3076
  0.7 7.3 %copy-start = (bf16[4,25,512]{2,0,1:T(4,128)(2,1)S(1)}, bf16[4,25,512]{2,0,1:T(4,128)(2,1)}, u32[]{:S(2)}) copy-start(bf16[4,25,512]{2,0,1:T(4,128)(2,1)} %param.22) | copy-start | bytes 307204
  0.7 7.3 %copy-start.1 = (bf16[4,25,512]{2,0,1:T(4,128)(2,1)S(1)}, bf16[4,25,512]{2,0,1:T(4,128)(2,1)}, u32[]{:S(2)}) copy-start(bf16[4,25,512]{2,0,1:T(4,128)(2,1)} %param.26) | copy-start | bytes 307204
  2.0 15.2 %collective-permute-start = (bf16[400,512]{1,0:T(8,128)(2,1)S(1)}, bf16[400,512]{1,0:T(8,128)(2,1)S(1)}, u32[]{:S(2)}, u32[]{:S(2)}) collective-permute-start(bf16[400,512]{1,0:T(8,128)(2,1)S(1)} %get-tuple-element.351), channel_id=1, source_target_pairs={{0,8},{8,0},{16,24},{24,16},{1,9},{9,1},{17,25},{25,17},{2,10},{10... | collective-permute-start | bytes 1228808 | tf_op jit(solution)/shard_map/ppermute | solution.py:956
  5.1 12.3 %collective-permute-start.1 = (bf16[400,512]{1,0:T(8,128)(2,1)S(1)}, bf16[400,512]{1,0:T(8,128)(2,1)S(1)}, u32[]{:S(2)}, u32[]{:S(2)}) collective-permute-start(bf16[400,512]{1,0:T(8,128)(2,1)S(1)} %get-tuple-element.352), channel_id=1, source_target_pairs={{0,16},{8,24},{16,0},{24,8},{1,17},{9,25},{17,1},{25,9},{2,18},{10... | collective-permute-start | bytes 1228808 | tf_op jit(solution)/shard_map/ppermute | solution.py:956
  8.3 9.1 %collective-permute-start.2 = (bf16[32,1024]{1,0:T(8,128)(2,1)S(1)}, bf16[32,1024]{1,0:T(8,128)(2,1)S(1)}, u32[]{:S(2)}, u32[]{:S(2)}) collective-permute-start(bf16[32,1024]{1,0:T(8,128)(2,1)S(1)} %get-tuple-element.372), channel_id=1, source_target_pairs={{0,8},{8,0},{16,24},{24,16},{1,9},{9,1},{17,25},{25,17},{2,10},{10... | collective-permute-start | bytes 196616 | tf_op jit(solution)/shard_map/ppermute | solution.py:956
  8.9 9.9 %collective-permute-start.3 = (bf16[32,1024]{1,0:T(8,128)(2,1)S(1)}, bf16[32,1024]{1,0:T(8,128)(2,1)S(1)}, u32[]{:S(2)}, u32[]{:S(2)}) collective-permute-start(bf16[32,1024]{1,0:T(8,128)(2,1)S(1)} %get-tuple-element.373), channel_id=1, source_target_pairs={{0,16},{8,24},{16,0},{24,8},{1,17},{9,25},{17,1},{25,9},{2,18},{10... | collective-permute-start | bytes 196616 | tf_op jit(solution)/shard_map/ppermute | solution.py:956
  8.9 9.9 %collective-permute-start.4 = (bf16[32,1024]{1,0:T(8,128)(2,1)S(1)}, bf16[32,1024]{1,0:T(8,128)(2,1)S(1)}, u32[]{:S(2)}, u32[]{:S(2)}) collective-permute-start(bf16[32,1024]{1,0:T(8,128)(2,1)S(1)} %get-tuple-element.374), channel_id=1, source_target_pairs={{0,24},{8,16},{16,8},{24,0},{1,25},{9,17},{17,9},{25,1},{2,26},{10... | collective-permute-start | bytes 196616 | tf_op jit(solution)/shard_map/ppermute | solution.py:956
  11.8 11.0 %copy-start.2 = (s32[4,4]{1,0:T(4,128)S(1)}, s32[4,4]{1,0:T(4,128)}, u32[]{:S(2)}) copy-start(s32[4,4]{1,0:T(4,128)} %refs_0_.1) | copy-start | bytes 196
  18.8 12.4 %collective-permute-start.6 = (bf16[400,512]{1,0:T(8,128)(2,1)S(1)}, bf16[400,512]{1,0:T(8,128)(2,1)S(1)}, u32[]{:S(2)}, u32[]{:S(2)}) collective-permute-start(bf16[400,512]{1,0:T(8,128)(2,1)S(1)} %collective-permute-done.refs_15_), channel_id=1, source_target_pairs={{0,16},{8,24},{16,0},{24,8},{1,17},{9,25},{17,1},{25,9},{2,18},{10... | collective-permute-start | bytes 1228808 | tf_op jit(solution)/shard_map/ppermute | solution.py:956
  20.3 12.4 %collective-permute-start.5 = (bf16[400,512]{1,0:T(8,128)(2,1)S(1)}, bf16[400,512]{1,0:T(8,128)(2,1)S(1)}, u32[]{:S(2)}, u32[]{:S(2)}) collective-permute-start(bf16[400,512]{1,0:T(8,128)(2,1)S(1)} %collective-permute-done.1.refs_16_), channel_id=1, source_target_pairs={{0,8},{8,0},{16,24},{24,16},{1,9},{9,1},{17,25},{25,17},{2,10},{10... | collective-permute-start | bytes 1228808 | tf_op jit(solution)/shard_map/ppermute | solution.py:956
  20.8 17.6 %collective-permute-start.9 = (bf16[416,512]{1,0:T(8,128)(2,1)S(1)}, bf16[416,512]{1,0:T(8,128)(2,1)S(1)}, u32[]{:S(2)}, u32[]{:S(2)}) collective-permute-start(bf16[416,512]{1,0:T(8,128)(2,1)S(1)} %get-tuple-element.426), channel_id=1, source_target_pairs={{0,8},{8,0},{16,24},{24,16},{1,9},{9,1},{17,25},{25,17},{2,10},{10... | collective-permute-start | bytes 1277960 | tf_op jit(solution)/shard_map/ppermute | solution.py:956
  22.3 16.1 %collective-permute-start.10 = (bf16[416,512]{1,0:T(8,128)(2,1)S(1)}, bf16[416,512]{1,0:T(8,128)(2,1)S(1)}, u32[]{:S(2)}, u32[]{:S(2)}) collective-permute-start(bf16[416,512]{1,0:T(8,128)(2,1)S(1)} %get-tuple-element.427), channel_id=1, source_target_pairs={{0,16},{8,24},{16,0},{24,8},{1,17},{9,25},{17,1},{25,9},{2,18},{10... | collective-permute-start | bytes 1277960 | tf_op jit(solution)/shard_map/ppermute | solution.py:956
  32.7 1.7 %collective-permute-start.7 = (bf16[400,512]{1,0:T(8,128)(2,1)S(1)}, bf16[400,512]{1,0:T(8,128)(2,1)S(1)}, u32[]{:S(2)}, u32[]{:S(2)}) collective-permute-start(bf16[400,512]{1,0:T(8,128)(2,1)S(1)} %collective-permute-done.5.refs_4_.refs_18_), channel_id=1, source_target_pairs={{0,1},{1,0},{2,3},{3,2},{4,5},{5,4},{6,7},{7,6},{8,9},{9,8},{10,11... | collective-permute-start | bytes 1228808 | tf_op jit(solution)/shard_map/ppermute | solution.py:956
  32.7 2.3 %collective-permute-start.8 = (bf16[400,512]{1,0:T(8,128)(2,1)S(1)}, bf16[400,512]{1,0:T(8,128)(2,1)S(1)}, u32[]{:S(2)}, u32[]{:S(2)}) collective-permute-start(bf16[400,512]{1,0:T(8,128)(2,1)S(1)} %collective-permute-done.6.refs_5_.refs_19_), channel_id=1, source_target_pairs={{0,1},{1,0},{2,3},{3,2},{4,5},{5,4},{6,7},{7,6},{8,9},{9,8},{10,11... | collective-permute-start | bytes 1228808 | tf_op jit(solution)/shard_map/ppermute | solution.py:956
  38.5 3.6 %collective-permute-start.11 = (bf16[416,512]{1,0:T(8,128)(2,1)S(1)}, bf16[416,512]{1,0:T(8,128)(2,1)S(1)}, u32[]{:S(2)}, u32[]{:S(2)}) collective-permute-start(bf16[416,512]{1,0:T(8,128)(2,1)S(1)} %collective-permute-done.9.refs_14_), channel_id=1, source_target_pairs={{0,1},{1,0},{2,3},{3,2},{4,5},{5,4},{6,7},{7,6},{8,9},{9,8},{10,11... | collective-permute-start | bytes 1277960 | tf_op jit(solution)/shard_map/ppermute | solution.py:956
  38.5 3.6 %collective-permute-start.14 = (bf16[416,512]{1,0:T(8,128)(2,1)S(1)}, bf16[416,512]{1,0:T(8,128)(2,1)S(1)}, u32[]{:S(2)}, u32[]{:S(2)}) collective-permute-start(bf16[416,512]{1,0:T(8,128)(2,1)S(1)} %collective-permute-done.10.refs_17_), channel_id=1, source_target_pairs={{0,1},{1,0},{2,3},{3,2},{4,5},{5,4},{6,7},{7,6},{8,9},{9,8},{10,11... | collective-permute-start | bytes 1277960 | tf_op jit(solution)/shard_map/ppermute | solution.py:956
  39.0 2.5 %collective-permute-start.12 = (bf16[400,512]{1,0:T(8,128)(2,1)S(1)}, bf16[400,512]{1,0:T(8,128)(2,1)S(1)}, u32[]{:S(2)}, u32[]{:S(2)}) collective-permute-start(bf16[400,512]{1,0:T(8,128)(2,1)S(1)} %collective-permute-done.refs_15_), channel_id=1, source_target_pairs={{0,1},{1,0},{2,3},{3,2},{4,5},{5,4},{6,7},{7,6},{8,9},{9,8},{10,11... | collective-permute-start | bytes 1228808 | tf_op jit(solution)/shard_map/ppermute | solution.py:956
  39.0 3.0 %collective-permute-start.13 = (bf16[400,512]{1,0:T(8,128)(2,1)S(1)}, bf16[400,512]{1,0:T(8,128)(2,1)S(1)}, u32[]{:S(2)}, u32[]{:S(2)}) collective-permute-start(bf16[400,512]{1,0:T(8,128)(2,1)S(1)} %collective-permute-done.1.refs_16_), channel_id=1, source_target_pairs={{0,1},{1,0},{2,3},{3,2},{4,5},{5,4},{6,7},{7,6},{8,9},{9,8},{10,11... | collective-permute-start | bytes 1228808 | tf_op jit(solution)/shard_map/ppermute | solution.py:956
  46.6 9.2 %collective-permute-start.19 = (bf16[104,1024]{1,0:T(8,128)(2,1)S(1)}, bf16[104,1024]{1,0:T(8,128)(2,1)S(1)}, u32[]{:S(2)}, u32[]{:S(2)}) collective-permute-start(bf16[104,1024]{1,0:T(8,128)(2,1)S(1)} %get-tuple-element.536.refs_0_), channel_id=1, source_target_pairs={{0,24},{8,16},{16,8},{24,0},{1,25},{9,17},{17,9},{25,1},{2,26},{10... | collective-permute-start | bytes 638984 | tf_op jit(solution)/shard_map/ppermute | solution.py:956
  48.6 10.9 %collective-permute-start.18 = (bf16[104,1024]{1,0:T(8,128)(2,1)S(1)}, bf16[104,1024]{1,0:T(8,128)(2,1)S(1)}, u32[]{:S(2)}, u32[]{:S(2)}) collective-permute-start(bf16[104,1024]{1,0:T(8,128)(2,1)S(1)} %get-tuple-element.536.refs_0_), channel_id=1, source_target_pairs={{0,16},{8,24},{16,0},{24,8},{1,17},{9,25},{17,1},{25,9},{2,18},{10... | collective-permute-start | bytes 638984 | tf_op jit(solution)/shard_map/ppermute | solution.py:956
  49.1 10.4 %collective-permute-start.17 = (bf16[104,1024]{1,0:T(8,128)(2,1)S(1)}, bf16[104,1024]{1,0:T(8,128)(2,1)S(1)}, u32[]{:S(2)}, u32[]{:S(2)}) collective-permute-start(bf16[104,1024]{1,0:T(8,128)(2,1)S(1)} %get-tuple-element.536.refs_0_), channel_id=1, source_target_pairs={{0,8},{8,0},{16,24},{24,16},{1,9},{9,1},{17,25},{25,17},{2,10},{10... | collective-permute-start | bytes 638984 | tf_op jit(solution)/shard_map/ppermute | solution.py:956
  55.2 4.2 %collective-permute-start.15 = (bf16[12,256,128]{2,1,0:T(8,128)(2,1)S(1)}, bf16[12,256,128]{2,1,0:T(8,128)(2,1)S(1)}, u32[]{:S(2)}, u32[]{:S(2)}) collective-permute-start(bf16[12,256,128]{2,1,0:T(8,128)(2,1)S(1)} %get-tuple-element.497), channel_id=1, source_target_pairs={{0,1},{1,0},{2,3},{3,2},{4,5},{5,4},{6,7},{7,6},{8,9},{9,8},{10,11... | collective-permute-start | bytes 2359304 | tf_op jit(solution)/shard_map/ppermute | solution.py:956
  55.3 4.2 %collective-permute-start.16 = (bf16[12,256,128]{2,1,0:T(8,128)(2,1)S(1)}, bf16[12,256,128]{2,1,0:T(8,128)(2,1)S(1)}, u32[]{:S(2)}, u32[]{:S(2)}) collective-permute-start(bf16[12,256,128]{2,1,0:T(8,128)(2,1)S(1)} %get-tuple-element.498), channel_id=1, source_target_pairs={{0,1},{1,0},{2,3},{3,2},{4,5},{5,4},{6,7},{7,6},{8,9},{9,8},{10,11... | collective-permute-start | bytes 2359304 | tf_op jit(solution)/shard_map/ppermute | solution.py:956
  59.9 11.1 %collective-permute-start.20 = (bf16[12,128,128]{2,1,0:T(8,128)(2,1)S(1)}, bf16[12,128,128]{2,1,0:T(8,128)(2,1)S(1)}, u32[]{:S(2)}, u32[]{:S(2)}) collective-permute-start(bf16[12,128,128]{2,1,0:T(8,128)(2,1)S(1)} %get-tuple-element.511), channel_id=1, source_target_pairs={{0,8},{8,0},{16,24},{24,16},{1,9},{9,1},{17,25},{25,17},{2,10},{10... | collective-permute-start | bytes 1179656 | tf_op jit(solution)/shard_map/ppermute | solution.py:956
  61.0 10.7 %collective-permute-start.21 = (bf16[12,128,128]{2,1,0:T(8,128)(2,1)S(1)}, bf16[12,128,128]{2,1,0:T(8,128)(2,1)S(1)}, u32[]{:S(2)}, u32[]{:S(2)}) collective-permute-start(bf16[12,128,128]{2,1,0:T(8,128)(2,1)S(1)} %get-tuple-element.512), channel_id=1, source_target_pairs={{0,16},{8,24},{16,0},{24,8},{1,17},{9,25},{17,1},{25,9},{2,18},{10... | collective-permute-start | bytes 1179656 | tf_op jit(solution)/shard_map/ppermute | solution.py:956
  71.6 2.4 %collective-permute-start.24 = (bf16[13,256,128]{2,1,0:T(8,128)(2,1)S(1)}, bf16[13,256,128]{2,1,0:T(8,128)(2,1)S(1)}, u32[]{:S(2)}, u32[]{:S(2)}) collective-permute-start(bf16[13,256,128]{2,1,0:T(8,128)(2,1)S(1)} %get-tuple-element.561), channel_id=1, source_target_pairs={{0,1},{1,0},{2,3},{3,2},{4,5},{5,4},{6,7},{7,6},{8,9},{9,8},{10,11... | collective-permute-start | bytes 2555912 | tf_op jit(solution)/shard_map/ppermute | solution.py:956
  71.8 7.4 %collective-permute-start.22 = (bf16[12,64,128]{2,1,0:T(8,128)(2,1)S(1)}, bf16[12,64,128]{2,1,0:T(8,128)(2,1)S(1)}, u32[]{:S(2)}, u32[]{:S(2)}) collective-permute-start(bf16[12,64,128]{2,1,0:T(8,128)(2,1)S(1)} %get-tuple-element.557), channel_id=1, source_target_pairs={{0,16},{8,24},{16,0},{24,8},{1,17},{9,25},{17,1},{25,9},{2,18},{10... | collective-permute-start | bytes 589832 | tf_op jit(solution)/shard_map/ppermute | solution.py:956
  73.1 7.0 %collective-permute-start.23 = (bf16[12,64,128]{2,1,0:T(8,128)(2,1)S(1)}, bf16[12,64,128]{2,1,0:T(8,128)(2,1)S(1)}, u32[]{:S(2)}, u32[]{:S(2)}) collective-permute-start(bf16[12,64,128]{2,1,0:T(8,128)(2,1)S(1)} %get-tuple-element.559), channel_id=1, source_target_pairs={{0,8},{8,0},{16,24},{24,16},{1,9},{9,1},{17,25},{25,17},{2,10},{10... | collective-permute-start | bytes 589832 | tf_op jit(solution)/shard_map/ppermute | solution.py:956
  74.2 12.7 %collective-permute-start.26 = (bf16[13,128,128]{2,1,0:T(8,128)(2,1)S(1)}, bf16[13,128,128]{2,1,0:T(8,128)(2,1)S(1)}, u32[]{:S(2)}, u32[]{:S(2)}) collective-permute-start(bf16[13,128,128]{2,1,0:T(8,128)(2,1)S(1)} %get-tuple-element.571), channel_id=1, source_target_pairs={{0,2},{1,3},{2,0},{3,1},{4,6},{5,7},{6,4},{7,5},{8,10},{9,11},{10,... | collective-permute-start | bytes 1277960 | tf_op jit(solution)/shard_map/ppermute | solution.py:956
  75.8 6.0 %collective-permute-start.27 = (bf16[4,64,800]{2,1,0:T(8,128)(2,1)S(1)}, bf16[4,64,800]{2,1,0:T(8,128)(2,1)S(1)}, u32[]{:S(2)}, u32[]{:S(2)}) collective-permute-start(bf16[4,64,800]{2,1,0:T(8,128)(2,1)S(1)} %get-tuple-element.572), channel_id=1, source_target_pairs={{0,1},{1,0},{2,3},{3,2},{4,5},{5,4},{6,7},{7,6},{8,9},{9,8},{10,11... | collective-permute-start | bytes 1228808 | tf_op jit(solution)/shard_map/ppermute | solution.py:956
  75.8 6.0 %collective-permute-start.28 = (bf16[4,64,800]{2,1,0:T(8,128)(2,1)S(1)}, bf16[4,64,800]{2,1,0:T(8,128)(2,1)S(1)}, u32[]{:S(2)}, u32[]{:S(2)}) collective-permute-start(bf16[4,64,800]{2,1,0:T(8,128)(2,1)S(1)} %get-tuple-element.573), channel_id=1, source_target_pairs={{0,1},{1,0},{2,3},{3,2},{4,5},{5,4},{6,7},{7,6},{8,9},{9,8},{10,11... | collective-permute-start | bytes 1228808 | tf_op jit(solution)/shard_map/ppermute | solution.py:956
  80.2 11.7 %collective-permute-start.25 = (bf16[24,32,128]{2,1,0:T(8,128)(2,1)S(1)}, bf16[24,32,128]{2,1,0:T(8,128)(2,1)S(1)}, u32[]{:S(2)}, u32[]{:S(2)}) collective-permute-start(bf16[24,32,128]{2,1,0:T(8,128)(2,1)S(1)} %get-tuple-element.570), channel_id=1, source_target_pairs={{0,2},{1,3},{2,0},{3,1},{4,6},{5,7},{6,4},{7,5},{8,10},{9,11},{10,... | collective-permute-start | bytes 589832 | tf_op jit(solution)/shard_map/ppermute | solution.py:956
  87.0 8.3 %collective-permute-start.32 = (bf16[13,64,128]{2,1,0:T(8,128)(2,1)S(1)}, bf16[13,64,128]{2,1,0:T(8,128)(2,1)S(1)}, u32[]{:S(2)}, u32[]{:S(2)}) collective-permute-start(bf16[13,64,128]{2,1,0:T(8,128)(2,1)S(1)} %get-tuple-element.586), channel_id=1, source_target_pairs={{0,8},{8,0},{16,24},{24,16},{1,9},{9,1},{17,25},{25,17},{2,10},{10... | collective-permute-start | bytes 638984 | tf_op jit(solution)/shard_map/ppermute | solution.py:956
  88.2 8.5 %collective-permute-start.34 = (bf16[2,64,800]{2,1,0:T(8,128)(2,1)S(1)}, bf16[2,64,800]{2,1,0:T(8,128)(2,1)S(1)}, u32[]{:S(2)}, u32[]{:S(2)}) collective-permute-start(bf16[2,64,800]{2,1,0:T(8,128)(2,1)S(1)} %get-tuple-element.591), channel_id=1, source_target_pairs={{0,2},{1,3},{2,0},{3,1},{4,6},{5,7},{6,4},{7,5},{8,10},{9,11},{10,... | collective-permute-start | bytes 614408 | tf_op jit(solution)/shard_map/ppermute | solution.py:956
  89.8 16.3 %collective-permute-start.30 = (bf16[368,512]{1,0:T(8,128)(2,1)S(1)}, bf16[368,512]{1,0:T(8,128)(2,1)S(1)}, u32[]{:S(2)}, u32[]{:S(2)}) collective-permute-start(bf16[368,512]{1,0:T(8,128)(2,1)S(1)} %get-tuple-element.583), channel_id=1, source_target_pairs={{0,8},{8,0},{16,24},{24,16},{1,9},{9,1},{17,25},{25,17},{2,10},{10... | collective-permute-start | bytes 1130504 | tf_op jit(solution)/shard_map/ppermute | solution.py:956
  90.7 15.4 %collective-permute-start.31 = (bf16[368,512]{1,0:T(8,128)(2,1)S(1)}, bf16[368,512]{1,0:T(8,128)(2,1)S(1)}, u32[]{:S(2)}, u32[]{:S(2)}) collective-permute-start(bf16[368,512]{1,0:T(8,128)(2,1)S(1)} %get-tuple-element.584), channel_id=1, source_target_pairs={{0,16},{8,24},{16,0},{24,8},{1,17},{9,25},{17,1},{25,9},{2,18},{10... | collective-permute-start | bytes 1130504 | tf_op jit(solution)/shard_map/ppermute | solution.py:956
  91.9 11.4 %collective-permute-start.35 = (bf16[2,64,800]{2,1,0:T(8,128)(2,1)S(1)}, bf16[2,64,800]{2,1,0:T(8,128)(2,1)S(1)}, u32[]{:S(2)}, u32[]{:S(2)}) collective-permute-start(bf16[2,64,800]{2,1,0:T(8,128)(2,1)S(1)} %get-tuple-element.592), channel_id=1, source_target_pairs={{0,2},{1,3},{2,0},{3,1},{4,6},{5,7},{6,4},{7,5},{8,10},{9,11},{10,... | collective-permute-start | bytes 614408 | tf_op jit(solution)/shard_map/ppermute | solution.py:956
  95.3 9.5 %collective-permute-start.33 = (bf16[13,32,128]{2,1,0:T(8,128)(2,1)S(1)}, bf16[13,32,128]{2,1,0:T(8,128)(2,1)S(1)}, u32[]{:S(2)}, u32[]{:S(2)}) collective-permute-start(bf16[13,32,128]{2,1,0:T(8,128)(2,1)S(1)} %get-tuple-element.590), channel_id=1, source_target_pairs={{0,16},{8,24},{16,0},{24,8},{1,17},{9,25},{17,1},{25,9},{2,18},{10... | collective-permute-start | bytes 319496 | tf_op jit(solution)/shard_map/ppermute | solution.py:956
  96.8 12.5 %collective-permute-start.29 = (bf16[24,32,128]{2,1,0:T(8,128)(2,1)S(1)}, bf16[24,32,128]{2,1,0:T(8,128)(2,1)S(1)}, u32[]{:S(2)}, u32[]{:S(2)}) collective-permute-start(bf16[24,32,128]{2,1,0:T(8,128)(2,1)S(1)} %shard_map.367.refs_0_), channel_id=1, source_target_pairs={{0,4},{1,5},{2,6},{3,7},{4,0},{5,1},{6,2},{7,3},{8,12},{9,13},{10,... | collective-permute-start | bytes 589832 | tf_op jit(solution)/shard_map/ppermute | solution.py:956
  103.3 9.9 %collective-permute-start.37 = (bf16[368,512]{1,0:T(8,128)(2,1)S(1)}, bf16[368,512]{1,0:T(8,128)(2,1)S(1)}, u32[]{:S(2)}, u32[]{:S(2)}) collective-permute-start(bf16[368,512]{1,0:T(8,128)(2,1)S(1)} %get-tuple-element.601), channel_id=1, source_target_pairs={{0,24},{8,16},{16,8},{24,0},{1,25},{9,17},{17,9},{25,1},{2,26},{10... | collective-permute-start | bytes 1130504 | tf_op jit(solution)/shard_map/ppermute | solution.py:956
  104.9 7.1 %collective-permute-start.38 = (bf16[13,32,128]{2,1,0:T(8,128)(2,1)S(1)}, bf16[13,32,128]{2,1,0:T(8,128)(2,1)S(1)}, u32[]{:S(2)}, u32[]{:S(2)}) collective-permute-start(bf16[13,32,128]{2,1,0:T(8,128)(2,1)S(1)} %shard_map.370.refs_0_), channel_id=1, source_target_pairs={{0,4},{1,5},{2,6},{3,7},{4,0},{5,1},{6,2},{7,3},{8,12},{9,13},{10,... | collective-permute-start | bytes 319496 | tf_op jit(solution)/shard_map/ppermute | solution.py:956
  109.3 5.7 %collective-permute-start.36 = (bf16[24,32,128]{2,1,0:T(8,128)(2,1)S(1)}, bf16[24,32,128]{2,1,0:T(8,128)(2,1)S(1)}, u32[]{:S(2)}, u32[]{:S(2)}) collective-permute-start(bf16[24,32,128]{2,1,0:T(8,128)(2,1)S(1)} %shard_map.371.refs_0_), channel_id=1, source_target_pairs={{0,2},{1,3},{2,0},{3,1},{4,6},{5,7},{6,4},{7,5},{8,10},{9,11},{10,... | collective-permute-start | bytes 589832 | tf_op jit(solution)/shard_map/ppermute | solution.py:956
  112.0 5.9 %collective-permute-start.41 = (bf16[13,32,128]{2,1,0:T(8,128)(2,1)S(1)}, bf16[13,32,128]{2,1,0:T(8,128)(2,1)S(1)}, u32[]{:S(2)}, u32[]{:S(2)}) collective-permute-start(bf16[13,32,128]{2,1,0:T(8,128)(2,1)S(1)} %shard_map.372.refs_0_), channel_id=1, source_target_pairs={{0,16},{8,24},{16,0},{24,8},{1,17},{9,25},{17,1},{25,9},{2,18},{10... | collective-permute-start | bytes 319496 | tf_op jit(solution)/shard_map/ppermute | solution.py:956
  115.1 6.9 %collective-permute-start.40 = (bf16[12,64,128]{2,1,0:T(8,128)(2,1)S(1)}, bf16[12,64,128]{2,1,0:T(8,128)(2,1)S(1)}, u32[]{:S(2)}, u32[]{:S(2)}) collective-permute-start(bf16[12,64,128]{2,1,0:T(8,128)(2,1)S(1)} %get-tuple-element.613.refs_2_), channel_id=1, source_target_pairs={{0,8},{8,0},{16,24},{24,16},{1,9},{9,1},{17,25},{25,17},{2,10},{10... | collective-permute-start | bytes 589832 | tf_op jit(solution)/shard_map/ppermute | solution.py:956
  116.2 5.8 %collective-permute-start.39 = (bf16[12,64,128]{2,1,0:T(8,128)(2,1)S(1)}, bf16[12,64,128]{2,1,0:T(8,128)(2,1)S(1)}, u32[]{:S(2)}, u32[]{:S(2)}) collective-permute-start(bf16[12,64,128]{2,1,0:T(8,128)(2,1)S(1)} %get-tuple-element.611.refs_0_), channel_id=1, source_target_pairs={{0,16},{8,24},{16,0},{24,8},{1,17},{9,25},{17,1},{25,9},{2,18},{10... | collective-permute-start | bytes 589832 | tf_op jit(solution)/shard_map/ppermute | solution.py:956
  118.0 7.7 %collective-permute-start.46 = (bf16[13,64,128]{2,1,0:T(8,128)(2,1)S(1)}, bf16[13,64,128]{2,1,0:T(8,128)(2,1)S(1)}, u32[]{:S(2)}, u32[]{:S(2)}) collective-permute-start(bf16[13,64,128]{2,1,0:T(8,128)(2,1)S(1)} %shard_map.374.refs_0_), channel_id=1, source_target_pairs={{0,8},{8,0},{16,24},{24,16},{1,9},{9,1},{17,25},{25,17},{2,10},{10... | collective-permute-start | bytes 638984 | tf_op jit(solution)/shard_map/ppermute | solution.py:956
  119.1 7.6 %collective-permute-start.44 = (bf16[1,64,800]{2,1,0:T(8,128)(2,1)S(1)}, bf16[1,64,800]{2,1,0:T(8,128)(2,1)S(1)}, u32[]{:S(2)}, u32[]{:S(2)}) collective-permute-start(bf16[1,64,800]{2,1,0:T(8,128)(2,1)S(1)} %get-tuple-element.617), channel_id=1, source_target_pairs={{0,4},{1,5},{2,6},{3,7},{4,0},{5,1},{6,2},{7,3},{8,12},{9,13},{10,... | collective-permute-start | bytes 307208 | tf_op jit(solution)/shard_map/ppermute | solution.py:956
  121.0 6.6 %collective-permute-start.45 = (bf16[1,64,800]{2,1,0:T(8,128)(2,1)S(1)}, bf16[1,64,800]{2,1,0:T(8,128)(2,1)S(1)}, u32[]{:S(2)}, u32[]{:S(2)}) collective-permute-start(bf16[1,64,800]{2,1,0:T(8,128)(2,1)S(1)} %get-tuple-element.618), channel_id=1, source_target_pairs={{0,4},{1,5},{2,6},{3,7},{4,0},{5,1},{6,2},{7,3},{8,12},{9,13},{10,... | collective-permute-start | bytes 307208 | tf_op jit(solution)/shard_map/ppermute | solution.py:956
  122.1 9.1 %collective-permute-start.43 = (bf16[12,128,128]{2,1,0:T(8,128)(2,1)S(1)}, bf16[12,128,128]{2,1,0:T(8,128)(2,1)S(1)}, u32[]{:S(2)}, u32[]{:S(2)}) collective-permute-start(bf16[12,128,128]{2,1,0:T(8,128)(2,1)S(1)} %get-tuple-element.635.refs_2_), channel_id=1, source_target_pairs={{0,16},{8,24},{16,0},{24,8},{1,17},{9,25},{17,1},{25,9},{2,18},{10... | collective-permute-start | bytes 1179656 | tf_op jit(solution)/shard_map/ppermute | solution.py:956
  123.3 9.0 %collective-permute-start.42 = (bf16[12,128,128]{2,1,0:T(8,128)(2,1)S(1)}, bf16[12,128,128]{2,1,0:T(8,128)(2,1)S(1)}, u32[]{:S(2)}, u32[]{:S(2)}) collective-permute-start(bf16[12,128,128]{2,1,0:T(8,128)(2,1)S(1)} %get-tuple-element.633.refs_0_), channel_id=1, source_target_pairs={{0,8},{8,0},{16,24},{24,16},{1,9},{9,1},{17,25},{25,17},{2,10},{10... | collective-permute-start | bytes 1179656 | tf_op jit(solution)/shard_map/ppermute | solution.py:956
  125.7 9.3 %collective-permute-start.47 = (bf16[13,128,128]{2,1,0:T(8,128)(2,1)S(1)}, bf16[13,128,128]{2,1,0:T(8,128)(2,1)S(1)}, u32[]{:S(2)}, u32[]{:S(2)}) collective-permute-start(bf16[13,128,128]{2,1,0:T(8,128)(2,1)S(1)} %shard_map.376.refs_0_), channel_id=1, source_target_pairs={{0,2},{1,3},{2,0},{3,1},{4,6},{5,7},{6,4},{7,5},{8,10},{9,11},{10,... | collective-permute-start | bytes 1277960 | tf_op jit(solution)/shard_map/ppermute | solution.py:956
  132.4 3.9 %collective-permute-start.49 = (bf16[12,256,128]{2,1,0:T(8,128)(2,1)S(1)}, bf16[12,256,128]{2,1,0:T(8,128)(2,1)S(1)}, u32[]{:S(2)}, u32[]{:S(2)}) collective-permute-start(bf16[12,256,128]{2,1,0:T(8,128)(2,1)S(1)} %get-tuple-element.647.refs_0_), channel_id=1, source_target_pairs={{0,1},{1,0},{2,3},{3,2},{4,5},{5,4},{6,7},{7,6},{8,9},{9,8},{10,11... | collective-permute-start | bytes 2359304 | tf_op jit(solution)/shard_map/ppermute | solution.py:956
  132.5 3.8 %collective-permute-start.50 = (bf16[12,256,128]{2,1,0:T(8,128)(2,1)S(1)}, bf16[12,256,128]{2,1,0:T(8,128)(2,1)S(1)}, u32[]{:S(2)}, u32[]{:S(2)}) collective-permute-start(bf16[12,256,128]{2,1,0:T(8,128)(2,1)S(1)} %get-tuple-element.648.refs_1_), channel_id=1, source_target_pairs={{0,1},{1,0},{2,3},{3,2},{4,5},{5,4},{6,7},{7,6},{8,9},{9,8},{10,11... | collective-permute-start | bytes 2359304 | tf_op jit(solution)/shard_map/ppermute | solution.py:956
  135.0 3.1 %collective-permute-start.48 = (bf16[13,256,128]{2,1,0:T(8,128)(2,1)S(1)}, bf16[13,256,128]{2,1,0:T(8,128)(2,1)S(1)}, u32[]{:S(2)}, u32[]{:S(2)}) collective-permute-start(bf16[13,256,128]{2,1,0:T(8,128)(2,1)S(1)} %shard_map.381.refs_0_.refs_1_), channel_id=1, source_target_pairs={{0,1},{1,0},{2,3},{3,2},{4,5},{5,4},{6,7},{7,6},{8,9},{9,8},{10,11... | collective-permute-start | bytes 2555912 | tf_op jit(solution)/shard_map/ppermute | solution.py:956

commit v5 on v4

--- a/solution.py
+++ b/solution.py
@@ -150,12 +150,12 @@
     copies = []
     for ref, out in ((up, up_part), (down, down_part)):
         start = core * (ref.shape[0] - out.shape[0])
-        size = out.shape[0] // 2
-        for m in range(2):
+        middle = -(-out.shape[0] // 32) * 16
+        for at, size in ((0, middle), (middle, out.shape[0] - middle)):
             copies.append(
                 pltpu.make_async_copy(
-                    ref.at[pl.ds(pl.multiple_of(start + m * size, 16), size)],
-                    out.at[pl.ds(m * size, size)],
+                    ref.at[pl.ds(pl.multiple_of(start + at, 16), size)],
+                    out.at[pl.ds(at, size)],
                     sems.at[len(copies)],
                 )
             )

time: 141 us -> 141 us (level)
  no operation moved by 1% of the time
where the time goes in v5:
time: 141 us; the launch traced here: 140 us
  starting transfers between devices  49.8 us (35%)
  Pallas kernels  45.3 us (32%)
  waiting for transfers between devices  41 us (29%)
  local copies, waits for them, and re-layouts  2.87 us (2%)
    ppermute x51, starting transfers between devices, swap(): return lax.ppermute(value, axis, [(i, i ^ bit) for i in range(size)])  49.8 us
    pallas_call x36, Pallas kernels, call(): pl.pallas_call(body, out_shape=[pltpu.VMEM(*o) if here else jax.ShapeDtyp...  45.3 us
    ppermute x51, waiting for transfers between devices, swap(): return lax.ppermute(value, axis, [(i, i ^ bit) for i in range(size)])  41 us
  transfers between devices with their start and end apart: 51, of which 26 were waited for; matrix products, arithmetic and copies ran while one was open for 2% of the time, Pallas kernels for 26%

profile of v5, /device:TPU:0, one launch (start us, length us, event | category | flops | bytes accessed | tf_op | source)
XLA Modules:
  0.0 140.3 jit_solution(17563447467265285177)
XLA Ops:
  0.7 1.3 shard_map.349
  2.0 3.0 %collective-permute-start = (bf16[400,512]{1,0:T(8,128)(2,1)S(1)}, bf16[400,512]{1,0:T(8,128)(2,1)S(1)}, u32[]{:S(2)}, u32[]{:S(2)}) collective-permute-start(bf16[400,512]{1,0:T(8,128)(2,1)S(1)} %get-tuple-element.351), channel_id=1, source_target_pairs={{0,8},{8,0},{16,24},{24,16},{1,9},{9,1},{17,25},{25,17},{2,10},{10... | collective-permute-start | bytes 1228808 | tf_op jit(solution)/shard_map/ppermute | solution.py:956
  5.1 1.5 %collective-permute-start.1 = (bf16[400,512]{1,0:T(8,128)(2,1)S(1)}, bf16[400,512]{1,0:T(8,128)(2,1)S(1)}, u32[]{:S(2)}, u32[]{:S(2)}) collective-permute-start(bf16[400,512]{1,0:T(8,128)(2,1)S(1)} %get-tuple-element.352), channel_id=1, source_target_pairs={{0,16},{8,24},{16,0},{24,8},{1,17},{9,25},{17,1},{25,9},{2,18},{10... | collective-permute-start | bytes 1228808 | tf_op jit(solution)/shard_map/ppermute | solution.py:956
  6.6 1.3 shard_map.350
  8.9 2.9 %collective-permute-start.4 = (bf16[32,1024]{1,0:T(8,128)(2,1)S(1)}, bf16[32,1024]{1,0:T(8,128)(2,1)S(1)}, u32[]{:S(2)}, u32[]{:S(2)}) collective-permute-start(bf16[32,1024]{1,0:T(8,128)(2,1)S(1)} %get-tuple-element.374), channel_id=1, source_target_pairs={{0,24},{8,16},{16,8},{24,0},{1,25},{9,17},{17,9},{25,1},{2,26},{10... | collective-permute-start | bytes 196616 | tf_op jit(solution)/shard_map/ppermute | solution.py:956
  11.8 5.4 %shard_map.352 = (bf16[1216,512]{1,0:T(8,128)(2,1)S(1)}, bf16[1216,512]{1,0:T(8,128)(2,1)S(1)}, bf16[1216,512]{1,0:T(8,128)(2,1)S(1)}, bf16[1216,512]{1,0:T(8,12...) custom-call(bf16[4,1200,512]{2,1,0:T(8,128)(2,1)} %refs_0_, ...), custom_call_target="tpu_custom_call" | custom-call | flops 1 | bytes 1 | tf_op jit(solution)/shard_map/pallas_call | solution.py:936
  17.4 1.4 %collective-permute-done.3.refs_3_ = bf16[32,1024]{1,0:T(8,128)(2,1)S(1)} collective-permute-done((bf16[32,1024]{1,0:T(8,128)(2,1)S(1)}, bf16[32,1024]{1,0:T(8,128)(2,1)S(1)}, u32[]{:S(2)}, u32[]{:S(2)}) %collective-permute-start.3) | collective-permute-done | bytes 65568 | tf_op jit(solution)/shard_map/ppermute | solution.py:956
  18.8 1.5 %collective-permute-start.6 = (bf16[400,512]{1,0:T(8,128)(2,1)S(1)}, bf16[400,512]{1,0:T(8,128)(2,1)S(1)}, u32[]{:S(2)}, u32[]{:S(2)}) collective-permute-start(bf16[400,512]{1,0:T(8,128)(2,1)S(1)} %collective-permute-done.refs_15_), channel_id=1, source_target_pairs={{0,16},{8,24},{16,0},{24,8},{1,17},{9,25},{17,1},{25,9},{2,18},{10... | collective-permute-start | bytes 1228808 | tf_op jit(solution)/shard_map/ppermute | solution.py:956
  20.8 1.5 %collective-permute-start.9 = (bf16[416,512]{1,0:T(8,128)(2,1)S(1)}, bf16[416,512]{1,0:T(8,128)(2,1)S(1)}, u32[]{:S(2)}, u32[]{:S(2)}) collective-permute-start(bf16[416,512]{1,0:T(8,128)(2,1)S(1)} %get-tuple-element.426), channel_id=1, source_target_pairs={{0,8},{8,0},{16,24},{24,16},{1,9},{9,1},{17,25},{25,17},{2,10},{10... | collective-permute-start | bytes 1277960 | tf_op jit(solution)/shard_map/ppermute | solution.py:956
  22.8 8.0 %shard_map.353 = (bf16[128,512]{1,0:T(8,128)(2,1)S(1)}, bf16[128,512]{1,0:T(8,128)(2,1)S(1)}, bf16[128,512]{1,0:T(8,128)(2,1)S(1)}, bf16[128,512]{1,0:T(8,128)(2...) custom-call(s32[4,4]{1,0:T(4,128)S(1)} %copy-done.2, ...), custom_call_target="tpu_custom_call" | custom-call | flops 9200000000 | bytes 29600000 | tf_op jit(solution)/shard_map/pallas_call | solution.py:936
  31.2 1.5 %collective-permute-done.5.refs_4_.refs_18_ = bf16[400,512]{1,0:T(8,128)(2,1)S(1)} collective-permute-done((bf16[400,512]{1,0:T(8,128)(2,1)S(1)}, bf16[400,512]{1,0:T(8,128)(2,1)S(1)}, u32[]{:S(2)}, u32[]{:S(2)}) %collective-permute-start.5) | collective-permute-done | bytes 409632 | tf_op jit(solution)/shard_map/ppermute | solution.py:956
  33.2 1.2 collective-permute-done.7.refs_6_.refs_24_
  35.0 1.2 shard_map.354
  36.3 2.2 %collective-permute-done.9.refs_14_ = bf16[416,512]{1,0:T(8,128)(2,1)S(1)} collective-permute-done((bf16[416,512]{1,0:T(8,128)(2,1)S(1)}, bf16[416,512]{1,0:T(8,128)(2,1)S(1)}, u32[]{:S(2)}, u32[]{:S(2)}) %collective-permute-start.9) | collective-permute-done | bytes 426016 | tf_op jit(solution)/shard_map/ppermute | solution.py:956
  39.5 1.9 %collective-permute-done.12.refs_21_ = bf16[400,512]{1,0:T(8,128)(2,1)S(1)} collective-permute-done((bf16[400,512]{1,0:T(8,128)(2,1)S(1)}, bf16[400,512]{1,0:T(8,128)(2,1)S(1)}, u32[]{:S(2)}, u32[]{:S(2)}) %collective-permute-start.12) | collective-permute-done | bytes 409632 | tf_op jit(solution)/shard_map/ppermute | solution.py:956
  42.0 4.6 %shard_map.355 = (bf16[128,512]{1,0:T(8,128)(2,1)S(1)}, bf16[104,1024]{1,0:T(8,128)(2,1)S(1)}, f32[128,512]{1,0:T(8,128)S(1)}, f32[8,512]{1,0:T(8,128)S(1)}, f32[4,1,1024]{2,1,0:T(1,128)S(1)}) custom-call(f32[128,512]{1,0:T(8,128)S(1)} %get-tuple-element.432.refs_0_, bf16[128,512]{1,0:T(8,128)(2,1)S(1)} %get-tuple-element.433.refs_0_.refs_1_, ...), custom_call_target="tpu_custom_call" | custom-call | flops 6900000256 | bytes 22200000 | tf_op jit(solution)/shard_map/pallas_call | solution.py:936
  46.6 2.0 %collective-permute-start.19 = (bf16[104,1024]{1,0:T(8,128)(2,1)S(1)}, bf16[104,1024]{1,0:T(8,128)(2,1)S(1)}, u32[]{:S(2)}, u32[]{:S(2)}) collective-permute-start(bf16[104,1024]{1,0:T(8,128)(2,1)S(1)} %get-tuple-element.536.refs_0_), channel_id=1, source_target_pairs={{0,24},{8,16},{16,8},{24,0},{1,25},{9,17},{17,9},{25,1},{2,26},{10... | collective-permute-start | bytes 638984 | tf_op jit(solution)/shard_map/ppermute | solution.py:956
  49.1 1.1 collective-permute-start.17
  50.2 5.0 %shard_map.356 = (bf16[4,1216,256]{2,1,0:T(8,128)(2,1)S(1)}, bf16[128,512]{1,0:T(8,128)(2,1)S(1)}, bf16[128,512]{1,0:T(8,128)(2,1)S(1)}, f32[128,512]{1,0:T(8,12...) custom-call(f32[128,512]{1,0:T(8,128)S(1)} %get-tuple-element.475.re, ...), custom_call_target="tpu_custom_call" | custom-call | flops 8970000384 | bytes 28860000 | tf_op jit(solution)/shard_map/pallas_call | solution.py:936
  55.8 3.6 %collective-permute-done.18.refs_1_.refs_2_ = bf16[104,1024]{1,0:T(8,128)(2,1)S(1)} collective-permute-done((bf16[104,1024]{1,0:T(8,128)(2,1)S(1)}, bf16[104,1024]{1,0:T(8,128)(2,1)S(1)}, u32[]{:S(2)}, u32[]{:S(2)}) %collective-permute-start.18) | collective-permute-done | bytes 213024 | tf_op jit(solution)/shard_map/ppermute | solution.py:956
  59.9 1.1 collective-permute-start.20
  61.0 1.3 collective-permute-start.21
  62.2 5.0 %shard_map.359 = (bf16[1216,512]{1,0:T(8,128)(2,1)S(1)}, bf16[13,256,128]{2,1,0:T(8,128)(2,1)S(1)}, bf16[13,256,128]{2,1,0:T(8,128)(2,1)S(1)}) custom-call(bf16[4,1216,256]{2,1,0:T(8,128)(2,1)S(1)} %get-tuple-element.519.refs_0_, bf16[4,1216,256]{2,1,0:T(8,128)(2,1)S(1)} %get-tuple-element.520.refs_1_, ...), custom_call_target="tpu_custom_call" | custom-call | flops 5750000128 | bytes 18500000 | tf_op jit(solution)/shard_map/pallas_call | solution.py:936
  67.2 2.8 %shard_map.360 = (bf16[2,4,64,800]{3,2,1,0:T(8,128)(2,1)S(1)}, bf16[4,64,800]{2,1,0:T(8,128)(2,1)S(1)}, bf16[4,64,800]{2,1,0:T(8,128)(2,1)S(1)}) custom-call(bf16[104,1024]{1,0:T(8,128)(2,1)S(1)} %get-tuple-element.536.refs_0_, bf16[104,1024]{1,0:T(8,128)(2,1)S(1)} %collective-permute-done.17.refs_0_.refs_1_, ...), custom_call_target="tpu_custom_call" | custom-call | flops 575000000 | bytes 1850001 | tf_op jit(solution)/shard_map/pallas_call | solution.py:936
  70.0 0.9 shard_map.361
  71.8 1.3 collective-permute-start.22
  73.1 0.8 collective-permute-start.23
  74.2 1.6 %collective-permute-start.26 = (bf16[13,128,128]{2,1,0:T(8,128)(2,1)S(1)}, bf16[13,128,128]{2,1,0:T(8,128)(2,1)S(1)}, u32[]{:S(2)}, u32[]{:S(2)}) collective-permute-start(bf16[13,128,128]{2,1,0:T(8,128)(2,1)S(1)} %get-tuple-element.571), channel_id=1, source_target_pairs={{0,2},{1,3},{2,0},{3,1},{4,6},{5,7},{6,4},{7,5},{8,10},{9,11},{10,... | collective-permute-start | bytes 1277960 | tf_op jit(solution)/shard_map/ppermute | solution.py:956
  76.4 2.8 %collective-permute-done.22.refs_1_ = bf16[12,64,128]{2,1,0:T(8,128)(2,1)S(1)} collective-permute-done((bf16[12,64,128]{2,1,0:T(8,128)(2,1)S(1)}, bf16[12,64,128]{2,1,0:T(8,128)(2,1)S(1)}, u32[]{:S(2)}, u32[]{:S(2)}) %collective-permute-start.22) | collective-permute-done | bytes 196640 | tf_op jit(solution)/shard_map/ppermute | solution.py:956
  79.2 0.9 collective-permute-done.23.refs_3_
  80.2 1.6 %collective-permute-start.25 = (bf16[24,32,128]{2,1,0:T(8,128)(2,1)S(1)}, bf16[24,32,128]{2,1,0:T(8,128)(2,1)S(1)}, u32[]{:S(2)}, u32[]{:S(2)}) collective-permute-start(bf16[24,32,128]{2,1,0:T(8,128)(2,1)S(1)} %get-tuple-element.570), channel_id=1, source_target_pairs={{0,2},{1,3},{2,0},{3,1},{4,6},{5,7},{6,4},{7,5},{8,10},{9,11},{10,... | collective-permute-start | bytes 589832 | tf_op jit(solution)/shard_map/ppermute | solution.py:956
  82.1 4.8 %collective-permute-done.26.refs_1_ = bf16[13,128,128]{2,1,0:T(8,128)(2,1)S(1)} collective-permute-done((bf16[13,128,128]{2,1,0:T(8,128)(2,1)S(1)}, bf16[13,128,128]{2,1,0:T(8,128)(2,1)S(1)}, u32[]{:S(2)}, u32[]{:S(2)}) %collective-permute-start.26) | collective-permute-done | bytes 426016 | tf_op jit(solution)/shard_map/ppermute | solution.py:956
  87.0 1.2 collective-permute-start.32
  88.2 1.6 %collective-permute-start.34 = (bf16[2,64,800]{2,1,0:T(8,128)(2,1)S(1)}, bf16[2,64,800]{2,1,0:T(8,128)(2,1)S(1)}, u32[]{:S(2)}, u32[]{:S(2)}) collective-permute-start(bf16[2,64,800]{2,1,0:T(8,128)(2,1)S(1)} %get-tuple-element.591), channel_id=1, source_target_pairs={{0,2},{1,3},{2,0},{3,1},{4,6},{5,7},{6,4},{7,5},{8,10},{9,11},{10,... | collective-permute-start | bytes 614408 | tf_op jit(solution)/shard_map/ppermute | solution.py:956
  89.8 0.9 collective-permute-start.30
  90.7 1.2 collective-permute-start.31
  91.9 0.8 collective-permute-start.35
  92.8 2.5 %collective-permute-done.32.refs_1_ = bf16[13,64,128]{2,1,0:T(8,128)(2,1)S(1)} collective-permute-done((bf16[13,64,128]{2,1,0:T(8,128)(2,1)S(1)}, bf16[13,64,128]{2,1,0:T(8,128)(2,1)S(1)}, u32[]{:S(2)}, u32[]{:S(2)}) %collective-permute-start.32) | collective-permute-done | bytes 213024 | tf_op jit(solution)/shard_map/ppermute | solution.py:956
  95.3 1.3 collective-permute-start.33
  96.8 2.6 %collective-permute-start.29 = (bf16[24,32,128]{2,1,0:T(8,128)(2,1)S(1)}, bf16[24,32,128]{2,1,0:T(8,128)(2,1)S(1)}, u32[]{:S(2)}, u32[]{:S(2)}) collective-permute-start(bf16[24,32,128]{2,1,0:T(8,128)(2,1)S(1)} %shard_map.367.refs_0_), channel_id=1, source_target_pairs={{0,4},{1,5},{2,6},{3,7},{4,0},{5,1},{6,2},{7,3},{8,12},{9,13},{10,... | collective-permute-start | bytes 589832 | tf_op jit(solution)/shard_map/ppermute | solution.py:956
  99.3 4.0 %collective-permute-done.35.refs_2_ = bf16[2,64,800]{2,1,0:T(8,128)(2,1)S(1)} collective-permute-done((bf16[2,64,800]{2,1,0:T(8,128)(2,1)S(1)}, bf16[2,64,800]{2,1,0:T(8,128)(2,1)S(1)}, u32[]{:S(2)}, u32[]{:S(2)}) %collective-permute-start.35) | collective-permute-done | bytes 204832 | tf_op jit(solution)/shard_map/ppermute | solution.py:956
  103.3 1.4 %collective-permute-start.37 = (bf16[368,512]{1,0:T(8,128)(2,1)S(1)}, bf16[368,512]{1,0:T(8,128)(2,1)S(1)}, u32[]{:S(2)}, u32[]{:S(2)}) collective-permute-start(bf16[368,512]{1,0:T(8,128)(2,1)S(1)} %get-tuple-element.601), channel_id=1, source_target_pairs={{0,24},{8,16},{16,8},{24,0},{1,25},{9,17},{17,9},{25,1},{2,26},{10... | collective-permute-start | bytes 1130504 | tf_op jit(solution)/shard_map/ppermute | solution.py:956
  104.9 1.2 collective-permute-start.38
  106.1 3.2 %collective-permute-done.29.refs_1_ = bf16[24,32,128]{2,1,0:T(8,128)(2,1)S(1)} collective-permute-done((bf16[24,32,128]{2,1,0:T(8,128)(2,1)S(1)}, bf16[24,32,128]{2,1,0:T(8,128)(2,1)S(1)}, u32[]{:S(2)}, u32[]{:S(2)}) %collective-permute-start.29) | collective-permute-done | bytes 196640 | tf_op jit(solution)/shard_map/ppermute | solution.py:956
  109.9 2.1 %collective-permute-done.38.refs_1_ = bf16[13,32,128]{2,1,0:T(8,128)(2,1)S(1)} collective-permute-done((bf16[13,32,128]{2,1,0:T(8,128)(2,1)S(1)}, bf16[13,32,128]{2,1,0:T(8,128)(2,1)S(1)}, u32[]{:S(2)}, u32[]{:S(2)}) %collective-permute-start.38) | collective-permute-done | bytes 106528 | tf_op jit(solution)/shard_map/ppermute | solution.py:956
  112.0 1.2 collective-permute-start.41
  113.2 1.8 %collective-permute-done.36.refs_1_ = bf16[24,32,128]{2,1,0:T(8,128)(2,1)S(1)} collective-permute-done((bf16[24,32,128]{2,1,0:T(8,128)(2,1)S(1)}, bf16[24,32,128]{2,1,0:T(8,128)(2,1)S(1)}, u32[]{:S(2)}, u32[]{:S(2)}) %collective-permute-start.36) | collective-permute-done | bytes 196640 | tf_op jit(solution)/shard_map/ppermute | solution.py:956
  115.1 1.1 collective-permute-start.40
  116.2 1.0 collective-permute-start.39
  118.0 1.1 collective-permute-start.46
  119.1 1.9 %collective-permute-start.44 = (bf16[1,64,800]{2,1,0:T(8,128)(2,1)S(1)}, bf16[1,64,800]{2,1,0:T(8,128)(2,1)S(1)}, u32[]{:S(2)}, u32[]{:S(2)}) collective-permute-start(bf16[1,64,800]{2,1,0:T(8,128)(2,1)S(1)} %get-tuple-element.617), channel_id=1, source_target_pairs={{0,4},{1,5},{2,6},{3,7},{4,0},{5,1},{6,2},{7,3},{8,12},{9,13},{10,... | collective-permute-start | bytes 307208 | tf_op jit(solution)/shard_map/ppermute | solution.py:956
  121.0 1.1 collective-permute-start.45
  122.1 1.2 collective-permute-start.43
  123.3 1.0 collective-permute-start.42
  124.3 1.3 collective-permute-done.46.refs_1_
  125.7 0.9 collective-permute-start.47
  126.7 0.9 collective-permute-done.45.refs_2_
  127.5 2.0 %copy.56 = bf16[4,300,512]{2,0,1:T(4,128)(2,1)} copy(bf16[4,300,512]{2,1,0:T(8,128)(2,1)S(1)} %get-tuple-element.638) | data formatting | bytes 2457600 | tf_op jit(solution)/shard_map/pallas_call | solution.py:936
  130.3 0.8 copy_bitcast_fusion.1
  131.2 1.2 collective-permute-done.42.refs_1_
  133.0 1.8 %shard_map.380 = (f32[3,512,512]{2,1,0:T(8,128)}, f32[512,512]{1,0:T(8,128)}, f32[512,512]{1,0:T(8,128)}, f32[3,512,512]{2,1,0:T(8,128)}) custom-call(bf16[12,256,128]{2,1,0:T(8,128)(2,1)S(1)} %get-tuple-element.647.refs_0_, bf16[12,256,128]{2,1,0:T(8,128)(2,1)S(1)} %get-tuple-element.648.refs_1_), custom_call_target="tpu_custom_call" | custom-call | flops 1 | bytes 1 | tf_op jit(solution)/shard_map/pallas_call | solution.py:936
  135.1 1.2 shard_map.382
  136.4 1.8 %shard_map.383 = (f32[3,512,512]{2,1,0:T(8,128)}, f32[512,512]{1,0:T(8,128)}, f32[512,512]{1,0:T(8,128)}, f32[3,512,512]{2,1,0:T(8,128)}) custom-call(bf16[12,256,128]{2,1,0:T(8,128)(2,1)S(1)} %collective-permute-done.49.refs_0_, ...), custom_call_target="tpu_custom_call", output_to_operand_aliasing={{0}: (2, {}), {1}: (3, {}), {2}: (4, {}), {3}: (5, {})} | custom-call | flops 1725000064 | bytes 5550001 | tf_op jit(solution)/shard_map/pallas_call | solution.py:936
  138.2 2.0 %shard_map.384 = (f32[100,512]{1,0:T(8,128)}, f32[3,512]{1,0:T(4,128)}, f32[3,512]{1,0:T(4,128)}, f32[25,128]{1,0:T(8,128)}, f32[1,512]{1,0:T(1,128)}, /*index=5...) custom-call(bf16[13,256,128]{2,1,0:T(8,128)(2,1)S(1)} %collective-pe, ...), custom_call_target="tpu_custom_call", output_to_operand_aliasing={{8}: (2, {}), {9}: (3, {})} | custom-call | flops 690000000 | bytes 2220001 | tf_op jit(solution)/shard_map/pallas_call | solution.py:936
  (93 shorter events, 12.7 us)
Async XLA Ops:
  0.7 7.2 %copy-start.3 = (bf16[800]{0:T(1024)(128)(2,1)S(1)}, bf16[800]{0:T(1024)(128)(2,1)}, u32[]{:S(2)}) copy-start(bf16[800]{0:T(1024)(128)(2,1)} %param.34) | copy-start | bytes 4804
  0.7 7.2 %copy-start.4 = (bf16[512]{0:T(512)(128)(2,1)S(1)}, bf16[512]{0:T(512)(128)(2,1)}, u32[]{:S(2)}) copy-start(bf16[512]{0:T(512)(128)(2,1)} %param.36) | copy-start | bytes 3076
  0.7 7.2 %copy-start.5 = (bf16[512]{0:T(512)(128)(2,1)S(1)}, bf16[512]{0:T(512)(128)(2,1)}, u32[]{:S(2)}) copy-start(bf16[512]{0:T(512)(128)(2,1)} %param.40) | copy-start | bytes 3076
  0.7 7.3 %copy-start = (bf16[4,25,512]{2,0,1:T(4,128)(2,1)S(1)}, bf16[4,25,512]{2,0,1:T(4,128)(2,1)}, u32[]{:S(2)}) copy-start(bf16[4,25,512]{2,0,1:T(4,128)(2,1)} %param.22) | copy-start | bytes 307204
  0.7 7.3 %copy-start.1 = (bf16[4,25,512]{2,0,1:T(4,128)(2,1)S(1)}, bf16[4,25,512]{2,0,1:T(4,128)(2,1)}, u32[]{:S(2)}) copy-start(bf16[4,25,512]{2,0,1:T(4,128)(2,1)} %param.26) | copy-start | bytes 307204
  2.0 15.2 %collective-permute-start = (bf16[400,512]{1,0:T(8,128)(2,1)S(1)}, bf16[400,512]{1,0:T(8,128)(2,1)S(1)}, u32[]{:S(2)}, u32[]{:S(2)}) collective-permute-start(bf16[400,512]{1,0:T(8,128)(2,1)S(1)} %get-tuple-element.351), channel_id=1, source_target_pairs={{0,8},{8,0},{16,24},{24,16},{1,9},{9,1},{17,25},{25,17},{2,10},{10... | collective-permute-start | bytes 1228808 | tf_op jit(solution)/shard_map/ppermute | solution.py:956
  5.1 12.3 %collective-permute-start.1 = (bf16[400,512]{1,0:T(8,128)(2,1)S(1)}, bf16[400,512]{1,0:T(8,128)(2,1)S(1)}, u32[]{:S(2)}, u32[]{:S(2)}) collective-permute-start(bf16[400,512]{1,0:T(8,128)(2,1)S(1)} %get-tuple-element.352), channel_id=1, source_target_pairs={{0,16},{8,24},{16,0},{24,8},{1,17},{9,25},{17,1},{25,9},{2,18},{10... | collective-permute-start | bytes 1228808 | tf_op jit(solution)/shard_map/ppermute | solution.py:956
  8.3 9.1 %collective-permute-start.2 = (bf16[32,1024]{1,0:T(8,128)(2,1)S(1)}, bf16[32,1024]{1,0:T(8,128)(2,1)S(1)}, u32[]{:S(2)}, u32[]{:S(2)}) collective-permute-start(bf16[32,1024]{1,0:T(8,128)(2,1)S(1)} %get-tuple-element.372), channel_id=1, source_target_pairs={{0,8},{8,0},{16,24},{24,16},{1,9},{9,1},{17,25},{25,17},{2,10},{10... | collective-permute-start | bytes 196616 | tf_op jit(solution)/shard_map/ppermute | solution.py:956
  8.9 9.9 %collective-permute-start.3 = (bf16[32,1024]{1,0:T(8,128)(2,1)S(1)}, bf16[32,1024]{1,0:T(8,128)(2,1)S(1)}, u32[]{:S(2)}, u32[]{:S(2)}) collective-permute-start(bf16[32,1024]{1,0:T(8,128)(2,1)S(1)} %get-tuple-element.373), channel_id=1, source_target_pairs={{0,16},{8,24},{16,0},{24,8},{1,17},{9,25},{17,1},{25,9},{2,18},{10... | collective-permute-start | bytes 196616 | tf_op jit(solution)/shard_map/ppermute | solution.py:956
  8.9 9.9 %collective-permute-start.4 = (bf16[32,1024]{1,0:T(8,128)(2,1)S(1)}, bf16[32,1024]{1,0:T(8,128)(2,1)S(1)}, u32[]{:S(2)}, u32[]{:S(2)}) collective-permute-start(bf16[32,1024]{1,0:T(8,128)(2,1)S(1)} %get-tuple-element.374), channel_id=1, source_target_pairs={{0,24},{8,16},{16,8},{24,0},{1,25},{9,17},{17,9},{25,1},{2,26},{10... | collective-permute-start | bytes 196616 | tf_op jit(solution)/shard_map/ppermute | solution.py:956
  11.8 11.0 %copy-start.2 = (s32[4,4]{1,0:T(4,128)S(1)}, s32[4,4]{1,0:T(4,128)}, u32[]{:S(2)}) copy-start(s32[4,4]{1,0:T(4,128)} %refs_0_.1) | copy-start | bytes 196
  18.8 12.4 %collective-permute-start.6 = (bf16[400,512]{1,0:T(8,128)(2,1)S(1)}, bf16[400,512]{1,0:T(8,128)(2,1)S(1)}, u32[]{:S(2)}, u32[]{:S(2)}) collective-permute-start(bf16[400,512]{1,0:T(8,128)(2,1)S(1)} %collective-permute-done.refs_15_), channel_id=1, source_target_pairs={{0,16},{8,24},{16,0},{24,8},{1,17},{9,25},{17,1},{25,9},{2,18},{10... | collective-permute-start | bytes 1228808 | tf_op jit(solution)/shard_map/ppermute | solution.py:956
  20.3 12.4 %collective-permute-start.5 = (bf16[400,512]{1,0:T(8,128)(2,1)S(1)}, bf16[400,512]{1,0:T(8,128)(2,1)S(1)}, u32[]{:S(2)}, u32[]{:S(2)}) collective-permute-start(bf16[400,512]{1,0:T(8,128)(2,1)S(1)} %collective-permute-done.1.refs_16_), channel_id=1, source_target_pairs={{0,8},{8,0},{16,24},{24,16},{1,9},{9,1},{17,25},{25,17},{2,10},{10... | collective-permute-start | bytes 1228808 | tf_op jit(solution)/shard_map/ppermute | solution.py:956
  20.8 17.6 %collective-permute-start.9 = (bf16[416,512]{1,0:T(8,128)(2,1)S(1)}, bf16[416,512]{1,0:T(8,128)(2,1)S(1)}, u32[]{:S(2)}, u32[]{:S(2)}) collective-permute-start(bf16[416,512]{1,0:T(8,128)(2,1)S(1)} %get-tuple-element.426), channel_id=1, source_target_pairs={{0,8},{8,0},{16,24},{24,16},{1,9},{9,1},{17,25},{25,17},{2,10},{10... | collective-permute-start | bytes 1277960 | tf_op jit(solution)/shard_map/ppermute | solution.py:956
  22.3 16.1 %collective-permute-start.10 = (bf16[416,512]{1,0:T(8,128)(2,1)S(1)}, bf16[416,512]{1,0:T(8,128)(2,1)S(1)}, u32[]{:S(2)}, u32[]{:S(2)}) collective-permute-start(bf16[416,512]{1,0:T(8,128)(2,1)S(1)} %get-tuple-element.427), channel_id=1, source_target_pairs={{0,16},{8,24},{16,0},{24,8},{1,17},{9,25},{17,1},{25,9},{2,18},{10... | collective-permute-start | bytes 1277960 | tf_op jit(solution)/shard_map/ppermute | solution.py:956
  32.7 1.7 %collective-permute-start.7 = (bf16[400,512]{1,0:T(8,128)(2,1)S(1)}, bf16[400,512]{1,0:T(8,128)(2,1)S(1)}, u32[]{:S(2)}, u32[]{:S(2)}) collective-permute-start(bf16[400,512]{1,0:T(8,128)(2,1)S(1)} %collective-permute-done.5.refs_4_.refs_18_), channel_id=1, source_target_pairs={{0,1},{1,0},{2,3},{3,2},{4,5},{5,4},{6,7},{7,6},{8,9},{9,8},{10,11... | collective-permute-start | bytes 1228808 | tf_op jit(solution)/shard_map/ppermute | solution.py:956
  32.7 2.3 %collective-permute-start.8 = (bf16[400,512]{1,0:T(8,128)(2,1)S(1)}, bf16[400,512]{1,0:T(8,128)(2,1)S(1)}, u32[]{:S(2)}, u32[]{:S(2)}) collective-permute-start(bf16[400,512]{1,0:T(8,128)(2,1)S(1)} %collective-permute-done.6.refs_5_.refs_19_), channel_id=1, source_target_pairs={{0,1},{1,0},{2,3},{3,2},{4,5},{5,4},{6,7},{7,6},{8,9},{9,8},{10,11... | collective-permute-start | bytes 1228808 | tf_op jit(solution)/shard_map/ppermute | solution.py:956
  38.5 3.6 %collective-permute-start.11 = (bf16[416,512]{1,0:T(8,128)(2,1)S(1)}, bf16[416,512]{1,0:T(8,128)(2,1)S(1)}, u32[]{:S(2)}, u32[]{:S(2)}) collective-permute-start(bf16[416,512]{1,0:T(8,128)(2,1)S(1)} %collective-permute-done.9.refs_14_), channel_id=1, source_target_pairs={{0,1},{1,0},{2,3},{3,2},{4,5},{5,4},{6,7},{7,6},{8,9},{9,8},{10,11... | collective-permute-start | bytes 1277960 | tf_op jit(solution)/shard_map/ppermute | solution.py:956
  38.5 3.6 %collective-permute-start.14 = (bf16[416,512]{1,0:T(8,128)(2,1)S(1)}, bf16[416,512]{1,0:T(8,128)(2,1)S(1)}, u32[]{:S(2)}, u32[]{:S(2)}) collective-permute-start(bf16[416,512]{1,0:T(8,128)(2,1)S(1)} %collective-permute-done.10.refs_17_), channel_id=1, source_target_pairs={{0,1},{1,0},{2,3},{3,2},{4,5},{5,4},{6,7},{7,6},{8,9},{9,8},{10,11... | collective-permute-start | bytes 1277960 | tf_op jit(solution)/shard_map/ppermute | solution.py:956
  39.0 2.5 %collective-permute-start.12 = (bf16[400,512]{1,0:T(8,128)(2,1)S(1)}, bf16[400,512]{1,0:T(8,128)(2,1)S(1)}, u32[]{:S(2)}, u32[]{:S(2)}) collective-permute-start(bf16[400,512]{1,0:T(8,128)(2,1)S(1)} %collective-permute-done.refs_15_), channel_id=1, source_target_pairs={{0,1},{1,0},{2,3},{3,2},{4,5},{5,4},{6,7},{7,6},{8,9},{9,8},{10,11... | collective-permute-start | bytes 1228808 | tf_op jit(solution)/shard_map/ppermute | solution.py:956
  39.0 3.0 %collective-permute-start.13 = (bf16[400,512]{1,0:T(8,128)(2,1)S(1)}, bf16[400,512]{1,0:T(8,128)(2,1)S(1)}, u32[]{:S(2)}, u32[]{:S(2)}) collective-permute-start(bf16[400,512]{1,0:T(8,128)(2,1)S(1)} %collective-permute-done.1.refs_16_), channel_id=1, source_target_pairs={{0,1},{1,0},{2,3},{3,2},{4,5},{5,4},{6,7},{7,6},{8,9},{9,8},{10,11... | collective-permute-start | bytes 1228808 | tf_op jit(solution)/shard_map/ppermute | solution.py:956
  46.6 9.2 %collective-permute-start.19 = (bf16[104,1024]{1,0:T(8,128)(2,1)S(1)}, bf16[104,1024]{1,0:T(8,128)(2,1)S(1)}, u32[]{:S(2)}, u32[]{:S(2)}) collective-permute-start(bf16[104,1024]{1,0:T(8,128)(2,1)S(1)} %get-tuple-element.536.refs_0_), channel_id=1, source_target_pairs={{0,24},{8,16},{16,8},{24,0},{1,25},{9,17},{17,9},{25,1},{2,26},{10... | collective-permute-start | bytes 638984 | tf_op jit(solution)/shard_map/ppermute | solution.py:956
  48.6 10.9 %collective-permute-start.18 = (bf16[104,1024]{1,0:T(8,128)(2,1)S(1)}, bf16[104,1024]{1,0:T(8,128)(2,1)S(1)}, u32[]{:S(2)}, u32[]{:S(2)}) collective-permute-start(bf16[104,1024]{1,0:T(8,128)(2,1)S(1)} %get-tuple-element.536.refs_0_), channel_id=1, source_target_pairs={{0,16},{8,24},{16,0},{24,8},{1,17},{9,25},{17,1},{25,9},{2,18},{10... | collective-permute-start | bytes 638984 | tf_op jit(solution)/shard_map/ppermute | solution.py:956
  49.1 10.4 %collective-permute-start.17 = (bf16[104,1024]{1,0:T(8,128)(2,1)S(1)}, bf16[104,1024]{1,0:T(8,128)(2,1)S(1)}, u32[]{:S(2)}, u32[]{:S(2)}) collective-permute-start(bf16[104,1024]{1,0:T(8,128)(2,1)S(1)} %get-tuple-element.536.refs_0_), channel_id=1, source_target_pairs={{0,8},{8,0},{16,24},{24,16},{1,9},{9,1},{17,25},{25,17},{2,10},{10... | collective-permute-start | bytes 638984 | tf_op jit(solution)/shard_map/ppermute | solution.py:956
  55.2 4.2 %collective-permute-start.15 = (bf16[12,256,128]{2,1,0:T(8,128)(2,1)S(1)}, bf16[12,256,128]{2,1,0:T(8,128)(2,1)S(1)}, u32[]{:S(2)}, u32[]{:S(2)}) collective-permute-start(bf16[12,256,128]{2,1,0:T(8,128)(2,1)S(1)} %get-tuple-element.497), channel_id=1, source_target_pairs={{0,1},{1,0},{2,3},{3,2},{4,5},{5,4},{6,7},{7,6},{8,9},{9,8},{10,11... | collective-permute-start | bytes 2359304 | tf_op jit(solution)/shard_map/ppermute | solution.py:956
  55.3 4.2 %collective-permute-start.16 = (bf16[12,256,128]{2,1,0:T(8,128)(2,1)S(1)}, bf16[12,256,128]{2,1,0:T(8,128)(2,1)S(1)}, u32[]{:S(2)}, u32[]{:S(2)}) collective-permute-start(bf16[12,256,128]{2,1,0:T(8,128)(2,1)S(1)} %get-tuple-element.498), channel_id=1, source_target_pairs={{0,1},{1,0},{2,3},{3,2},{4,5},{5,4},{6,7},{7,6},{8,9},{9,8},{10,11... | collective-permute-start | bytes 2359304 | tf_op jit(solution)/shard_map/ppermute | solution.py:956
  59.9 11.1 %collective-permute-start.20 = (bf16[12,128,128]{2,1,0:T(8,128)(2,1)S(1)}, bf16[12,128,128]{2,1,0:T(8,128)(2,1)S(1)}, u32[]{:S(2)}, u32[]{:S(2)}) collective-permute-start(bf16[12,128,128]{2,1,0:T(8,128)(2,1)S(1)} %get-tuple-element.511), channel_id=1, source_target_pairs={{0,8},{8,0},{16,24},{24,16},{1,9},{9,1},{17,25},{25,17},{2,10},{10... | collective-permute-start | bytes 1179656 | tf_op jit(solution)/shard_map/ppermute | solution.py:956
  61.0 10.7 %collective-permute-start.21 = (bf16[12,128,128]{2,1,0:T(8,128)(2,1)S(1)}, bf16[12,128,128]{2,1,0:T(8,128)(2,1)S(1)}, u32[]{:S(2)}, u32[]{:S(2)}) collective-permute-start(bf16[12,128,128]{2,1,0:T(8,128)(2,1)S(1)} %get-tuple-element.512), channel_id=1, source_target_pairs={{0,16},{8,24},{16,0},{24,8},{1,17},{9,25},{17,1},{25,9},{2,18},{10... | collective-permute-start | bytes 1179656 | tf_op jit(solution)/shard_map/ppermute | solution.py:956
  71.6 2.4 %collective-permute-start.24 = (bf16[13,256,128]{2,1,0:T(8,128)(2,1)S(1)}, bf16[13,256,128]{2,1,0:T(8,128)(2,1)S(1)}, u32[]{:S(2)}, u32[]{:S(2)}) collective-permute-start(bf16[13,256,128]{2,1,0:T(8,128)(2,1)S(1)} %get-tuple-element.561), channel_id=1, source_target_pairs={{0,1},{1,0},{2,3},{3,2},{4,5},{5,4},{6,7},{7,6},{8,9},{9,8},{10,11... | collective-permute-start | bytes 2555912 | tf_op jit(solution)/shard_map/ppermute | solution.py:956
  71.8 7.4 %collective-permute-start.22 = (bf16[12,64,128]{2,1,0:T(8,128)(2,1)S(1)}, bf16[12,64,128]{2,1,0:T(8,128)(2,1)S(1)}, u32[]{:S(2)}, u32[]{:S(2)}) collective-permute-start(bf16[12,64,128]{2,1,0:T(8,128)(2,1)S(1)} %get-tuple-element.557), channel_id=1, source_target_pairs={{0,16},{8,24},{16,0},{24,8},{1,17},{9,25},{17,1},{25,9},{2,18},{10... | collective-permute-start | bytes 589832 | tf_op jit(solution)/shard_map/ppermute | solution.py:956
  73.1 7.0 %collective-permute-start.23 = (bf16[12,64,128]{2,1,0:T(8,128)(2,1)S(1)}, bf16[12,64,128]{2,1,0:T(8,128)(2,1)S(1)}, u32[]{:S(2)}, u32[]{:S(2)}) collective-permute-start(bf16[12,64,128]{2,1,0:T(8,128)(2,1)S(1)} %get-tuple-element.559), channel_id=1, source_target_pairs={{0,8},{8,0},{16,24},{24,16},{1,9},{9,1},{17,25},{25,17},{2,10},{10... | collective-permute-start | bytes 589832 | tf_op jit(solution)/shard_map/ppermute | solution.py:956
  74.2 12.7 %collective-permute-start.26 = (bf16[13,128,128]{2,1,0:T(8,128)(2,1)S(1)}, bf16[13,128,128]{2,1,0:T(8,128)(2,1)S(1)}, u32[]{:S(2)}, u32[]{:S(2)}) collective-permute-start(bf16[13,128,128]{2,1,0:T(8,128)(2,1)S(1)} %get-tuple-element.571), channel_id=1, source_target_pairs={{0,2},{1,3},{2,0},{3,1},{4,6},{5,7},{6,4},{7,5},{8,10},{9,11},{10,... | collective-permute-start | bytes 1277960 | tf_op jit(solution)/shard_map/ppermute | solution.py:956
  75.8 6.0 %collective-permute-start.27 = (bf16[4,64,800]{2,1,0:T(8,128)(2,1)S(1)}, bf16[4,64,800]{2,1,0:T(8,128)(2,1)S(1)}, u32[]{:S(2)}, u32[]{:S(2)}) collective-permute-start(bf16[4,64,800]{2,1,0:T(8,128)(2,1)S(1)} %get-tuple-element.572), channel_id=1, source_target_pairs={{0,1},{1,0},{2,3},{3,2},{4,5},{5,4},{6,7},{7,6},{8,9},{9,8},{10,11... | collective-permute-start | bytes 1228808 | tf_op jit(solution)/shard_map/ppermute | solution.py:956
  75.8 6.0 %collective-permute-start.28 = (bf16[4,64,800]{2,1,0:T(8,128)(2,1)S(1)}, bf16[4,64,800]{2,1,0:T(8,128)(2,1)S(1)}, u32[]{:S(2)}, u32[]{:S(2)}) collective-permute-start(bf16[4,64,800]{2,1,0:T(8,128)(2,1)S(1)} %get-tuple-element.573), channel_id=1, source_target_pairs={{0,1},{1,0},{2,3},{3,2},{4,5},{5,4},{6,7},{7,6},{8,9},{9,8},{10,11... | collective-permute-start | bytes 1228808 | tf_op jit(solution)/shard_map/ppermute | solution.py:956
  80.2 11.7 %collective-permute-start.25 = (bf16[24,32,128]{2,1,0:T(8,128)(2,1)S(1)}, bf16[24,32,128]{2,1,0:T(8,128)(2,1)S(1)}, u32[]{:S(2)}, u32[]{:S(2)}) collective-permute-start(bf16[24,32,128]{2,1,0:T(8,128)(2,1)S(1)} %get-tuple-element.570), channel_id=1, source_target_pairs={{0,2},{1,3},{2,0},{3,1},{4,6},{5,7},{6,4},{7,5},{8,10},{9,11},{10,... | collective-permute-start | bytes 589832 | tf_op jit(solution)/shard_map/ppermute | solution.py:956
  87.0 8.3 %collective-permute-start.32 = (bf16[13,64,128]{2,1,0:T(8,128)(2,1)S(1)}, bf16[13,64,128]{2,1,0:T(8,128)(2,1)S(1)}, u32[]{:S(2)}, u32[]{:S(2)}) collective-permute-start(bf16[13,64,128]{2,1,0:T(8,128)(2,1)S(1)} %get-tuple-element.586), channel_id=1, source_target_pairs={{0,8},{8,0},{16,24},{24,16},{1,9},{9,1},{17,25},{25,17},{2,10},{10... | collective-permute-start | bytes 638984 | tf_op jit(solution)/shard_map/ppermute | solution.py:956
  88.2 8.5 %collective-permute-start.34 = (bf16[2,64,800]{2,1,0:T(8,128)(2,1)S(1)}, bf16[2,64,800]{2,1,0:T(8,128)(2,1)S(1)}, u32[]{:S(2)}, u32[]{:S(2)}) collective-permute-start(bf16[2,64,800]{2,1,0:T(8,128)(2,1)S(1)} %get-tuple-element.591), channel_id=1, source_target_pairs={{0,2},{1,3},{2,0},{3,1},{4,6},{5,7},{6,4},{7,5},{8,10},{9,11},{10,... | collective-permute-start | bytes 614408 | tf_op jit(solution)/shard_map/ppermute | solution.py:956
  89.8 16.3 %collective-permute-start.30 = (bf16[368,512]{1,0:T(8,128)(2,1)S(1)}, bf16[368,512]{1,0:T(8,128)(2,1)S(1)}, u32[]{:S(2)}, u32[]{:S(2)}) collective-permute-start(bf16[368,512]{1,0:T(8,128)(2,1)S(1)} %get-tuple-element.583), channel_id=1, source_target_pairs={{0,8},{8,0},{16,24},{24,16},{1,9},{9,1},{17,25},{25,17},{2,10},{10... | collective-permute-start | bytes 1130504 | tf_op jit(solution)/shard_map/ppermute | solution.py:956
  90.7 15.4 %collective-permute-start.31 = (bf16[368,512]{1,0:T(8,128)(2,1)S(1)}, bf16[368,512]{1,0:T(8,128)(2,1)S(1)}, u32[]{:S(2)}, u32[]{:S(2)}) collective-permute-start(bf16[368,512]{1,0:T(8,128)(2,1)S(1)} %get-tuple-element.584), channel_id=1, source_target_pairs={{0,16},{8,24},{16,0},{24,8},{1,17},{9,25},{17,1},{25,9},{2,18},{10... | collective-permute-start | bytes 1130504 | tf_op jit(solution)/shard_map/ppermute | solution.py:956
  91.9 11.4 %collective-permute-start.35 = (bf16[2,64,800]{2,1,0:T(8,128)(2,1)S(1)}, bf16[2,64,800]{2,1,0:T(8,128)(2,1)S(1)}, u32[]{:S(2)}, u32[]{:S(2)}) collective-permute-start(bf16[2,64,800]{2,1,0:T(8,128)(2,1)S(1)} %get-tuple-element.592), channel_id=1, source_target_pairs={{0,2},{1,3},{2,0},{3,1},{4,6},{5,7},{6,4},{7,5},{8,10},{9,11},{10,... | collective-permute-start | bytes 614408 | tf_op jit(solution)/shard_map/ppermute | solution.py:956
  95.3 9.5 %collective-permute-start.33 = (bf16[13,32,128]{2,1,0:T(8,128)(2,1)S(1)}, bf16[13,32,128]{2,1,0:T(8,128)(2,1)S(1)}, u32[]{:S(2)}, u32[]{:S(2)}) collective-permute-start(bf16[13,32,128]{2,1,0:T(8,128)(2,1)S(1)} %get-tuple-element.590), channel_id=1, source_target_pairs={{0,16},{8,24},{16,0},{24,8},{1,17},{9,25},{17,1},{25,9},{2,18},{10... | collective-permute-start | bytes 319496 | tf_op jit(solution)/shard_map/ppermute | solution.py:956
  96.8 12.5 %collective-permute-start.29 = (bf16[24,32,128]{2,1,0:T(8,128)(2,1)S(1)}, bf16[24,32,128]{2,1,0:T(8,128)(2,1)S(1)}, u32[]{:S(2)}, u32[]{:S(2)}) collective-permute-start(bf16[24,32,128]{2,1,0:T(8,128)(2,1)S(1)} %shard_map.367.refs_0_), channel_id=1, source_target_pairs={{0,4},{1,5},{2,6},{3,7},{4,0},{5,1},{6,2},{7,3},{8,12},{9,13},{10,... | collective-permute-start | bytes 589832 | tf_op jit(solution)/shard_map/ppermute | solution.py:956
  103.3 9.9 %collective-permute-start.37 = (bf16[368,512]{1,0:T(8,128)(2,1)S(1)}, bf16[368,512]{1,0:T(8,128)(2,1)S(1)}, u32[]{:S(2)}, u32[]{:S(2)}) collective-permute-start(bf16[368,512]{1,0:T(8,128)(2,1)S(1)} %get-tuple-element.601), channel_id=1, source_target_pairs={{0,24},{8,16},{16,8},{24,0},{1,25},{9,17},{17,9},{25,1},{2,26},{10... | collective-permute-start | bytes 1130504 | tf_op jit(solution)/shard_map/ppermute | solution.py:956
  104.9 7.1 %collective-permute-start.38 = (bf16[13,32,128]{2,1,0:T(8,128)(2,1)S(1)}, bf16[13,32,128]{2,1,0:T(8,128)(2,1)S(1)}, u32[]{:S(2)}, u32[]{:S(2)}) collective-permute-start(bf16[13,32,128]{2,1,0:T(8,128)(2,1)S(1)} %shard_map.370.refs_0_), channel_id=1, source_target_pairs={{0,4},{1,5},{2,6},{3,7},{4,0},{5,1},{6,2},{7,3},{8,12},{9,13},{10,... | collective-permute-start | bytes 319496 | tf_op jit(solution)/shard_map/ppermute | solution.py:956
  109.3 5.7 %collective-permute-start.36 = (bf16[24,32,128]{2,1,0:T(8,128)(2,1)S(1)}, bf16[24,32,128]{2,1,0:T(8,128)(2,1)S(1)}, u32[]{:S(2)}, u32[]{:S(2)}) collective-permute-start(bf16[24,32,128]{2,1,0:T(8,128)(2,1)S(1)} %shard_map.371.refs_0_), channel_id=1, source_target_pairs={{0,2},{1,3},{2,0},{3,1},{4,6},{5,7},{6,4},{7,5},{8,10},{9,11},{10,... | collective-permute-start | bytes 589832 | tf_op jit(solution)/shard_map/ppermute | solution.py:956
  112.0 5.9 %collective-permute-start.41 = (bf16[13,32,128]{2,1,0:T(8,128)(2,1)S(1)}, bf16[13,32,128]{2,1,0:T(8,128)(2,1)S(1)}, u32[]{:S(2)}, u32[]{:S(2)}) collective-permute-start(bf16[13,32,128]{2,1,0:T(8,128)(2,1)S(1)} %shard_map.372.refs_0_), channel_id=1, source_target_pairs={{0,16},{8,24},{16,0},{24,8},{1,17},{9,25},{17,1},{25,9},{2,18},{10... | collective-permute-start | bytes 319496 | tf_op jit(solution)/shard_map/ppermute | solution.py:956
  115.1 6.9 %collective-permute-start.40 = (bf16[12,64,128]{2,1,0:T(8,128)(2,1)S(1)}, bf16[12,64,128]{2,1,0:T(8,128)(2,1)S(1)}, u32[]{:S(2)}, u32[]{:S(2)}) collective-permute-start(bf16[12,64,128]{2,1,0:T(8,128)(2,1)S(1)} %get-tuple-element.613.refs_2_), channel_id=1, source_target_pairs={{0,8},{8,0},{16,24},{24,16},{1,9},{9,1},{17,25},{25,17},{2,10},{10... | collective-permute-start | bytes 589832 | tf_op jit(solution)/shard_map/ppermute | solution.py:956
  116.2 5.8 %collective-permute-start.39 = (bf16[12,64,128]{2,1,0:T(8,128)(2,1)S(1)}, bf16[12,64,128]{2,1,0:T(8,128)(2,1)S(1)}, u32[]{:S(2)}, u32[]{:S(2)}) collective-permute-start(bf16[12,64,128]{2,1,0:T(8,128)(2,1)S(1)} %get-tuple-element.611.refs_0_), channel_id=1, source_target_pairs={{0,16},{8,24},{16,0},{24,8},{1,17},{9,25},{17,1},{25,9},{2,18},{10... | collective-permute-start | bytes 589832 | tf_op jit(solution)/shard_map/ppermute | solution.py:956
  118.0 7.7 %collective-permute-start.46 = (bf16[13,64,128]{2,1,0:T(8,128)(2,1)S(1)}, bf16[13,64,128]{2,1,0:T(8,128)(2,1)S(1)}, u32[]{:S(2)}, u32[]{:S(2)}) collective-permute-start(bf16[13,64,128]{2,1,0:T(8,128)(2,1)S(1)} %shard_map.374.refs_0_), channel_id=1, source_target_pairs={{0,8},{8,0},{16,24},{24,16},{1,9},{9,1},{17,25},{25,17},{2,10},{10... | collective-permute-start | bytes 638984 | tf_op jit(solution)/shard_map/ppermute | solution.py:956
  119.1 7.6 %collective-permute-start.44 = (bf16[1,64,800]{2,1,0:T(8,128)(2,1)S(1)}, bf16[1,64,800]{2,1,0:T(8,128)(2,1)S(1)}, u32[]{:S(2)}, u32[]{:S(2)}) collective-permute-start(bf16[1,64,800]{2,1,0:T(8,128)(2,1)S(1)} %get-tuple-element.617), channel_id=1, source_target_pairs={{0,4},{1,5},{2,6},{3,7},{4,0},{5,1},{6,2},{7,3},{8,12},{9,13},{10,... | collective-permute-start | bytes 307208 | tf_op jit(solution)/shard_map/ppermute | solution.py:956
  121.0 6.6 %collective-permute-start.45 = (bf16[1,64,800]{2,1,0:T(8,128)(2,1)S(1)}, bf16[1,64,800]{2,1,0:T(8,128)(2,1)S(1)}, u32[]{:S(2)}, u32[]{:S(2)}) collective-permute-start(bf16[1,64,800]{2,1,0:T(8,128)(2,1)S(1)} %get-tuple-element.618), channel_id=1, source_target_pairs={{0,4},{1,5},{2,6},{3,7},{4,0},{5,1},{6,2},{7,3},{8,12},{9,13},{10,... | collective-permute-start | bytes 307208 | tf_op jit(solution)/shard_map/ppermute | solution.py:956
  122.1 9.1 %collective-permute-start.43 = (bf16[12,128,128]{2,1,0:T(8,128)(2,1)S(1)}, bf16[12,128,128]{2,1,0:T(8,128)(2,1)S(1)}, u32[]{:S(2)}, u32[]{:S(2)}) collective-permute-start(bf16[12,128,128]{2,1,0:T(8,128)(2,1)S(1)} %get-tuple-element.635.refs_2_), channel_id=1, source_target_pairs={{0,16},{8,24},{16,0},{24,8},{1,17},{9,25},{17,1},{25,9},{2,18},{10... | collective-permute-start | bytes 1179656 | tf_op jit(solution)/shard_map/ppermute | solution.py:956
  123.3 9.0 %collective-permute-start.42 = (bf16[12,128,128]{2,1,0:T(8,128)(2,1)S(1)}, bf16[12,128,128]{2,1,0:T(8,128)(2,1)S(1)}, u32[]{:S(2)}, u32[]{:S(2)}) collective-permute-start(bf16[12,128,128]{2,1,0:T(8,128)(2,1)S(1)} %get-tuple-element.633.refs_0_), channel_id=1, source_target_pairs={{0,8},{8,0},{16,24},{24,16},{1,9},{9,1},{17,25},{25,17},{2,10},{10... | collective-permute-start | bytes 1179656 | tf_op jit(solution)/shard_map/ppermute | solution.py:956
  125.7 9.3 %collective-permute-start.47 = (bf16[13,128,128]{2,1,0:T(8,128)(2,1)S(1)}, bf16[13,128,128]{2,1,0:T(8,128)(2,1)S(1)}, u32[]{:S(2)}, u32[]{:S(2)}) collective-permute-start(bf16[13,128,128]{2,1,0:T(8,128)(2,1)S(1)} %shard_map.376.refs_0_), channel_id=1, source_target_pairs={{0,2},{1,3},{2,0},{3,1},{4,6},{5,7},{6,4},{7,5},{8,10},{9,11},{10,... | collective-permute-start | bytes 1277960 | tf_op jit(solution)/shard_map/ppermute | solution.py:956
  132.4 3.9 %collective-permute-start.49 = (bf16[12,256,128]{2,1,0:T(8,128)(2,1)S(1)}, bf16[12,256,128]{2,1,0:T(8,128)(2,1)S(1)}, u32[]{:S(2)}, u32[]{:S(2)}) collective-permute-start(bf16[12,256,128]{2,1,0:T(8,128)(2,1)S(1)} %get-tuple-element.647.refs_0_), channel_id=1, source_target_pairs={{0,1},{1,0},{2,3},{3,2},{4,5},{5,4},{6,7},{7,6},{8,9},{9,8},{10,11... | collective-permute-start | bytes 2359304 | tf_op jit(solution)/shard_map/ppermute | solution.py:956
  132.5 3.8 %collective-permute-start.50 = (bf16[12,256,128]{2,1,0:T(8,128)(2,1)S(1)}, bf16[12,256,128]{2,1,0:T(8,128)(2,1)S(1)}, u32[]{:S(2)}, u32[]{:S(2)}) collective-permute-start(bf16[12,256,128]{2,1,0:T(8,128)(2,1)S(1)} %get-tuple-element.648.refs_1_), channel_id=1, source_target_pairs={{0,1},{1,0},{2,3},{3,2},{4,5},{5,4},{6,7},{7,6},{8,9},{9,8},{10,11... | collective-permute-start | bytes 2359304 | tf_op jit(solution)/shard_map/ppermute | solution.py:956
  135.0 3.1 %collective-permute-start.48 = (bf16[13,256,128]{2,1,0:T(8,128)(2,1)S(1)}, bf16[13,256,128]{2,1,0:T(8,128)(2,1)S(1)}, u32[]{:S(2)}, u32[]{:S(2)}) collective-permute-start(bf16[13,256,128]{2,1,0:T(8,128)(2,1)S(1)} %shard_map.381.refs_0_.refs_1_), channel_id=1, source_target_pairs={{0,1},{1,0},{2,3},{3,2},{4,5},{5,4},{6,7},{7,6},{8,9},{9,8},{10,11... | collective-permute-start | bytes 2555912 | tf_op jit(solution)/shard_map/ppermute | solution.py:956
